TPU v7x, 32 devices: a whole 2x2x4 slice. The times are simulated.
32 devices in a mesh: ens: 2 (over y), lat: 8 (over z, x), lev: 2 (over core).
Axes of the slice: x: 2, y: 2, z: 4, core: 2. Of those that a mesh axis runs over, the one named last changes fastest.
Arguments:
- constituent_densities: float32 [32, 4, 32, 1152], P('ens', 'lev', 'lat'), parts along dimension 0, may hold values from -6 to 6
- thermal_state: float32 [8, 32, 1152], P(('ens', 'lev'), 'lat'), parts along dimension 0, may hold values from 0.5 to 1.5
- integer_boxes_traversed: int32 [8, 32, 1152], P(('ens', 'lev'), 'lat'), parts along dimension 0, may hold values from 0 to 2
- partial_crossing_share: float32 [8, 32, 1152], P(('ens', 'lev'), 'lat'), parts along dimension 0, may hold values from 0 to 1
- northward_crossing_share: float32 [8, 32, 1152], P(('ens', 'lev'), 'lat'), parts along dimension 0, may hold values from -0.9 to 0.9
- higher_donor_stratum: int32 [8, 32, 1152], P('ens', 'lat', 'lev'), parts along dimension 0, may hold values from 0 to 2
- deeper_donor_share: float32 [8, 32, 1152], P('ens', 'lat', 'lev'), parts along dimension 0, may hold values from 0 to 1
- napierian_thickness_quotient: float32 [8, 32, 1152], P('ens', 'lat', 'lev'), parts along dimension 0, may hold values from 0.1 to 1
- ground_gravity_height: float32 [64, 1152], P(('ens', 'lat'), 'lev'), parts along dimension 0, may hold values from 0 to 2
Outputs:
- tracers_out: float32 [32, 4, 32, 1152], P('ens', 'lev', 'lat'), parts along dimension 0
- temperature_out: float32 [8, 32, 1152], P(('ens', 'lev'), 'lat'), parts along dimension 0
- geopotential: float32 [8, 32, 1152], P(('ens', 'lev'), 'lat'), parts along dimension 0
There are 2 independent parts, one for each index of `ens`. A program takes and returns all parts, laid end to end along the dimension named above; each array names one. Nothing has to cross between parts.
All inputs are finite; a program needn't handle non-finite values.
Results may differ from a plain program's by a relative error of at most 0.0003.
Values sent between devices are 32-bit elements; how exact they have to be, the bound alone decides.
No kernel may reach another device: no remote copies, remote signals or barrier semaphores. Data moves between devices by JAX's collectives and lax.ppermute only.
A program may use at most 64 MiB of HBM per device.

v0:
```python
import math

import jax
import jax.numpy as jnp
from jax import lax
from jax.sharding import PartitionSpec as P

NMAX = 2


def padded_2(array, sides, width):
    for axis, dim in sides:
        size, length = (lax.axis_size(axis), array.shape[dim])
        up = [(i, (i + 1) % size) for i in range(size - 1)]
        down = [(j, i) for i, j in up]
        last = lax.slice_in_dim(array, length - width, length, axis=dim)
        initial = lax.slice_in_dim(array, 0, width, axis=dim)
        before = lax.ppermute(last, axis, up)
        after = lax.ppermute(initial, axis, down)
        array = jnp.concatenate([before, array, after], axis=dim)
    return array


def shift_lon(values, offset):
    return jnp.roll(values, offset, axis=-1)


def pad_poles(values, factor):
    row_count = values.shape[-2]
    lon_count = values.shape[-1]
    south_rows = factor * shift_lon(jnp.flip(values[..., 0:3, :], -2), lon_count // 2)
    north_rows = factor * shift_lon(
        jnp.flip(values[..., row_count - 3 : row_count, :], -2), lon_count // 2
    )
    return jnp.concatenate([south_rows, values, north_rows], axis=-2)


def advect(padded, courant_y, whole_cells, fraction, first_row, lat_total):
    row_count = padded.shape[-2] - 6
    cell_values = padded[..., 3 : row_count + 3, :]
    west_edge = 7.0 / 12.0 * (shift_lon(cell_values, 1) + cell_values) - 1.0 / 12.0 * (
        shift_lon(cell_values, 2) + shift_lon(cell_values, -1)
    )
    east_edge = shift_lon(west_edge, -1)
    gradient = east_edge - west_edge
    parabola = 6.0 * cell_values - 3.0 * (west_edge + east_edge)
    crossed = jnp.zeros_like(cell_values)
    upwind_edge = jnp.zeros_like(cell_values)
    upwind_gradient = jnp.zeros_like(cell_values)
    upwind_parabola = jnp.zeros_like(cell_values)
    for offset in range(1, NMAX + 2):
        if offset <= NMAX:
            crossed = crossed + jnp.where(
                whole_cells >= offset, shift_lon(cell_values, offset), 0.0
            )
        landing = whole_cells == offset - 1
        upwind_edge = upwind_edge + jnp.where(landing, shift_lon(east_edge, offset), 0.0)
        upwind_gradient = upwind_gradient + jnp.where(landing, shift_lon(gradient, offset), 0.0)
        upwind_parabola = upwind_parabola + jnp.where(landing, shift_lon(parabola, offset), 0.0)
    zonal_flux = crossed + fraction * (
        upwind_edge
        - 0.5 * fraction * (upwind_gradient - (1.0 - 2.0 * fraction / 3.0) * upwind_parabola)
    )
    zonal_change = shift_lon(zonal_flux, -1) - zonal_flux
    face_values = 7.0 / 12.0 * (
        padded[..., 1 : row_count + 4, :] + padded[..., 2 : row_count + 5, :]
    ) - 1.0 / 12.0 * (padded[..., 0 : row_count + 3, :] + padded[..., 3 : row_count + 6, :])
    low_edge = face_values[..., 0 : row_count + 2, :]
    high_edge = face_values[..., 1 : row_count + 3, :]
    centers = padded[..., 2 : row_count + 4, :]
    incline = high_edge - low_edge
    curvature = 6.0 * centers - 3.0 * (low_edge + high_edge)
    courant = courant_y[..., 2 : row_count + 3, :]
    magnitude = jnp.abs(courant)
    northward = courant * (
        high_edge[..., 0 : row_count + 1, :]
        - 0.5
        * magnitude
        * (
            incline[..., 0 : row_count + 1, :]
            - (1.0 - 2.0 * magnitude / 3.0) * curvature[..., 0 : row_count + 1, :]
        )
    )
    southward = courant * (
        low_edge[..., 1 : row_count + 2, :]
        + 0.5
        * magnitude
        * (
            incline[..., 1 : row_count + 2, :]
            + (1.0 - 2.0 * magnitude / 3.0) * curvature[..., 1 : row_count + 2, :]
        )
    )
    face_flux = jnp.where(courant >= 0.0, northward, southward)
    face_rows = jnp.arange(row_count + 1, dtype=jnp.int32) + first_row
    face_cosine = jnp.sin(
        math.pi * jnp.minimum(face_rows, lat_total - face_rows).astype(jnp.float32) / lat_total
    )
    center_rows = (jnp.arange(row_count, dtype=jnp.int32) + first_row).astype(jnp.float32) + 0.5
    center_cosine = jnp.sin(math.pi * center_rows / lat_total)
    weighted = face_flux * face_cosine[:, None]
    meridional_change = (weighted[..., 1:, :] - weighted[..., :-1, :]) / center_cosine[:, None]
    return cell_values - zonal_change - meridional_change


def remap(source, level_index, weight):
    level_count = source.shape[1]
    remapped = jnp.zeros((source.shape[0],) + weight.shape, jnp.float32)
    for level in range(level_count - 1):
        blended = (1.0 - weight) * source[:, level][:, None] + weight * source[:, level + 1][
            :, None
        ]
        remapped = remapped + jnp.where(level_index == level, blended, 0.0)
    return remapped


def layer_thickness(remapped, napierian_thickness_quotient):
    return remapped[-1] * (1.0 + 0.608 * remapped[0]) * napierian_thickness_quotient


def deeper_sum(thickness):
    return jnp.flip(jnp.cumsum(jnp.flip(thickness, 0), 0), 0) - thickness


def on_device(
    constituent_densities,
    thermal_state,
    integer_boxes_traversed,
    partial_crossing_share,
    northward_crossing_share,
    higher_donor_stratum,
    deeper_donor_share,
    napierian_thickness_quotient,
    ground_gravity_height,
):
    field_count = constituent_densities.shape[0] + 1
    constituent_arrays = jnp.concatenate([constituent_densities, thermal_state[None]], axis=0)
    stacked = jnp.concatenate([constituent_arrays, northward_crossing_share[None]], axis=0)
    band_rows = stacked.shape[2]
    lat_count = lax.axis_size("lat")
    lat_index = lax.axis_index("lat")
    lat_total = band_rows * lat_count
    extended = padded_2(stacked, (("lat", 2),), 3)
    factors = jnp.concatenate(
        [jnp.ones((field_count,), jnp.float32), -jnp.ones((1,), jnp.float32)]
    )[:, None, None, None]
    polar = pad_poles(stacked, factors)
    south_rim = jnp.where(lat_index == 0, polar[:, :, 0:3, :], extended[:, :, 0:3, :])
    north_rim = jnp.where(
        lat_index == lat_count - 1,
        polar[:, :, band_rows + 3 :, :],
        extended[:, :, band_rows + 3 :, :],
    )
    extended = jnp.concatenate([south_rim, extended[:, :, 3 : band_rows + 3, :], north_rim], axis=2)
    advected = advect(
        extended[:field_count],
        extended[field_count],
        integer_boxes_traversed,
        partial_crossing_share,
        lat_index * band_rows,
        lat_total,
    )
    columns = lax.all_to_all(advected, "lev", split_axis=3, concat_axis=1, tiled=True)
    remapped = remap(columns, higher_donor_stratum, deeper_donor_share)
    thickness = layer_thickness(remapped, napierian_thickness_quotient)
    geopotential = ground_gravity_height + deeper_sum(thickness) + 0.5 * thickness
    stacked_back = jnp.concatenate([remapped, geopotential[None]], axis=0)
    returned = lax.all_to_all(stacked_back, "lev", split_axis=1, concat_axis=3, tiled=True)
    return (returned[: field_count - 1], returned[field_count - 1], returned[field_count])


def solution(mesh):
    return jax.shard_map(
        on_device,
        mesh=mesh,
        in_specs=(
            P("ens", "lev", "lat", None),
            P(("ens", "lev"), "lat", None),
            P(("ens", "lev"), "lat", None),
            P(("ens", "lev"), "lat", None),
            P(("ens", "lev"), "lat", None),
            P("ens", "lat", "lev"),
            P("ens", "lat", "lev"),
            P("ens", "lat", "lev"),
            P(("ens", "lat"), "lev"),
        ),
        out_specs=(
            P("ens", "lev", "lat", None),
            P(("ens", "lev"), "lat", None),
            P(("ens", "lev"), "lat", None),
        ),
        check_vma=False,
    )
```

profile of v0, /device:TPU:9, one launch (start us, length us, event | category | flops | bytes accessed | tf_op | source)
XLA Modules:
  0.0 84.0 jit_solution(2997605423662641399)
XLA Ops:
  0.6 0.8 copy.41
  1.5 0.8 copy.38
  2.3 1.2 %constant_dynamic-update-slice_fusion = (f32[17,2,4,1152]{3,0,2,1:T(8,128)S(1)}, f32[16,2,4,1152]{3,0,2,1:T(8,128)S(1)}) fusion(f32[16,2,4,1152]{3,2,1,0:T(4,128)} %param.9), kind=kLoop, calls=%fused_computation.99 | loop fusion | bytes 1769472
  3.5 0.8 copy-done
  4.3 0.1 pad_maximum_fusion.10
  4.4 1.2 %fusion.47 = (f32[18,2,3,1152]{3,0,2,1:T(8,128)}, f32[18,2,3,1152]{3,0,2,1:T(8,128)}) fusion(f32[18,2,4,1152]{3,0,2,1:T(8,128)S(1)} %pad_maximum_fusion.10), kind=kLoop, calls=%fused_computation.108 | loop fusion | bytes 1990656 | tf_op jit(solution)/shard_map/slice | solution.py:16
  5.6 3.1 %collective-permute-start = (f32[18,2,3,1152]{3,0,2,1:T(8,128)}, f32[18,2,3,1152]{3,0,2,1:T(8,128)}, u32[]{:S(2)}, u32[]{:S(2)}) collective-permute-start(f32[18,2,3,1152]{3,0,2,1:T(8,128)} %get-tuple-element.15), channel_id=1, source_target_pairs={{0,2},{2,4},{4,6},{6,8},{8,10},{10,12},{12,14},{1,3},{3,5},{5,7},{... | collective-permute-start | bytes 1493000 | tf_op jit(solution)/shard_map/ppermute | solution.py:18
  8.7 3.1 %collective-permute-start.1 = (f32[18,2,3,1152]{3,0,2,1:T(8,128)}, f32[18,2,3,1152]{3,0,2,1:T(8,128)}, u32[]{:S(2)}, u32[]{:S(2)}) collective-permute-start(f32[18,2,3,1152]{3,0,2,1:T(8,128)} %get-tuple-element.16), channel_id=1, source_target_pairs={{2,0},{4,2},{6,4},{8,6},{10,8},{12,10},{14,12},{3,1},{5,3},{7,5},{... | collective-permute-start | bytes 1493000 | tf_op jit(solution)/shard_map/ppermute | solution.py:19
  11.8 1.3 %fusion.46 = (f32[18,2,3,576]{3,0,2,1:T(8,128)}, f32[18,2,3,576]{3,0,2,1:T(8,128)}, f32[18,2,3,576]{3,0,2,1:T(8,128)}, f32[18,2,3,576]{3,0,2,1:T(8,128)}) fusion(f32[18,2,4,1152]{3,0,2,1:T(8,128)S(1)} %pad_maximum_fusion.10), kind=kLoop, calls=%fused_computation.107 | loop fusion | bytes 1990656 | tf_op jit(solution)/shard_map/jit(_roll_static)/slice | solution.py:25
  13.1 0.1 dynamic-update-slice.1
  13.3 0.1 fusion.44
  13.4 0.3 fusion.45
  13.7 0.1 slice.299
  13.8 0.2 copy-done.16
  14.0 0.6 fusion.18
  14.6 0.0 copy-done.15
  14.6 1.2 %slice.307 = f32[17,2,4,1150]{3,0,2,1:T(8,128)} slice(f32[17,2,4,1152]{3,0,2,1:T(8,128)S(1)} %fusion.18), slice={[0:17], [0:2], [0:4], [1:1151]} | slice | bytes 1251200 | tf_op jit(solution)/shard_map/jit(_roll_static)/slice | solution.py:25
  15.9 0.3 slice.303
  16.2 1.2 %slice.310 = f32[17,2,4,1149]{3,0,2,1:T(8,128)} slice(f32[17,2,4,1152]{3,0,2,1:T(8,128)S(1)} %fusion.18), slice={[0:17], [0:2], [0:4], [1:1150]} | slice | bytes 1250112 | tf_op jit(solution)/shard_map/jit(_roll_static)/slice | solution.py:25
  17.4 0.8 fusion.35
  18.1 0.8 fusion.36
  18.9 0.2 multiply_subtract_fusion
  19.1 0.7 slice.311
  19.9 0.7 slice.313
  20.6 0.7 slice.315
  21.3 0.7 slice.317
  22.0 0.7 slice.319
  22.8 0.8 slice.321
  23.6 0.8 broadcast_multiply_fusion
  24.4 0.8 broadcast_compare_fusion.8
  25.2 4.1 %fusion.23 = f32[17,2,4,1152]{3,0,2,1:T(8,128)S(1)} fusion(f32[17,2,4,1150]{3,0,2,1:T(8,128)} %slice.307, f32[17,2,4,2]{3,0,2,1:T(8,128)} %fusion.35, f32[17,2,4,1149]{3,0,2,1:T(8,128)} %slice.310, f32[17,2,4,3]{3,0,2,1:T(8,128)} %fusion.36, f32[17,2,4,1151]{3,0,2,1:T(8,128)S(1)} %bitcast.43, f32[17,2,4,1]{3,0,2,1:T(8,128)} %slice.311, ...), kind=kLoop, calls=%fused_computation.43 | loop fusion | flops 5326848 | bytes 7676928 | tf_op jit(solution)/shard_map/add | solution.py:60
  29.4 0.8 %copy-done.2 = f32[17,2,4,1152]{3,0,2,1:T(8,128)} copy-done((f32[17,2,4,1152]{3,0,2,1:T(8,128)}, f32[17,2,4,1152]{3,0,2,1:T(8,128)S(1)}, u32[]{:S(2)}) %copy-start.2) | copy-done | bytes 626712
  30.3 0.3 slice.323
  30.6 0.8 slice.264
  31.4 0.8 slice.262
  32.2 0.8 slice.269
  33.1 3.7 %collective-permute-done = f32[18,2,3,1152]{3,0,2,1:T(8,128)} collective-permute-done((f32[18,2,3,1152]{3,0,2,1:T(8,128)}, f32[18,2,3,1152]{3,0,2,1:T(8,128)}, u32[]{:S(2)}, u32[]{:S(2)}) %collective-permute-start) | collective-permute-done | bytes 497696 | tf_op jit(solution)/shard_map/ppermute | solution.py:18
  36.8 2.9 %collective-permute-done.1 = f32[18,2,3,1152]{3,0,2,1:T(8,128)} collective-permute-done((f32[18,2,3,1152]{3,0,2,1:T(8,128)}, f32[18,2,3,1152]{3,0,2,1:T(8,128)}, u32[]{:S(2)}, u32[]{:S(2)}) %collective-permute-start.1) | collective-permute-done | bytes 497696 | tf_op jit(solution)/shard_map/ppermute | solution.py:19
  39.7 1.7 %fusion.33 = (f32[18,2,3,1152]{3,0,2,1:T(8,128)S(1)}, f32[18,2,3,1152]{3,0,2,1:T(8,128)S(1)}) fusion(f32[18,2,3,1152]{3,0,2,1:T(8,128)} %collective-permute-done, f32[18,2,3,576]{3,0,2,1:T(8,128)S(1)} %copy-done.9, f32[18,2,3,576]{3,0,2,1:T(8,128)S(1)} %copy-done.10, f32[18]{0:T(128)S(1)} %copy-done.21, pred[]{:T(512)S(6)} %eq.42, ...), kind=kLoop, calls=%fused_computation.68 | loop fusion | flops 746496 | bytes 2986058 | tf_op jit(solution)/shard_map/jit(_where)/select_n | solution.py:147
  41.5 0.2 pad_maximum_fusion
  41.7 0.1 pad_maximum_fusion.12
  41.8 0.1 fusion.49
  42.0 0.4 fusion.2
  42.3 0.2 slice_subtract_fusion
  42.6 0.5 fusion.10
  43.2 0.6 copy-done.3
  43.8 0.3 fusion.16
  44.1 3.6 %copy.47 = f32[17,2,4,1152]{0,2,1,3:T(4,128)} copy(f32[17,2,4,1152]{3,0,2,1:T(8,128)S(1)} %fusion.16) | data formatting | bytes 1253376 | tf_op jit(solution)/shard_map/sub | solution.py:102
  47.7 7.3 %reshape.42 = f32[2,1,78336]{2,1,0:T(1,128)S(1)} reshape(f32[1152,2,4,17]{3,2,1,0:T(4,128)} %bitcast.38) | data formatting | bytes 1253376
  55.0 4.4 %all_to_all.33 = f32[2,1,78336]{2,1,0:T(1,128)S(1)} all-to-all(f32[2,1,78336]{2,1,0:T(1,128)S(1)} %reshape.42), channel_id=1, replica_groups=mesh['ens'=2,'lat'=8,'lev'=2] {'lev'}, dimensions={0} | all-to-all | bytes 1253376 | tf_op jit(solution)/shard_map/all_to_all | solution.py:162
  59.4 0.5 broadcast.94
  59.9 2.6 %reduce = f32[2,78336]{1,0:T(2,128)S(1)} reduce(f32[2,1,78336]{2,1,0:T(1,128)S(1)} %all_to_all.33, f32[]{:T(128)} %broadcast.94), dimensions={1}, to_apply=%all_to_all.24.reduce_sub_computation | reduce | bytes 1253380 | tf_op jit(solution)/shard_map/all_to_all | solution.py:162
  62.5 8.3 %reshape.43 = f32[1152,2,4,17]{3,2,1,0:T(4,128)} reshape(f32[2,78336]{1,0:T(2,128)S(1)} %reduce) | data formatting | bytes 1253376
  70.8 3.9 %copy.48 = f32[17,2,4,2,576]{4,2,1,3,0:T(4,128)S(1)} copy(f32[17,2,4,2,576]{0,2,1,4,3:T(4,128)} %bitcast.39) | data formatting | bytes 1253376 | tf_op jit(solution)/shard_map/all_to_all | solution.py:162
  74.7 0.1 slice_bitcast_fusion.3
  74.8 0.7 select_add_fusion
  75.5 0.0 copy-done.18
  75.6 0.7 pad_maximum_fusion.11
  76.3 4.2 %all_to_all.34 = f32[18,4,4,576]{3,2,0,1:T(4,128)S(1)} all-to-all(f32[18,4,4,576]{3,2,0,1:T(4,128)S(1)} %pad_maximum_fusion.11), channel_id=1, replica_groups=mesh['ens'=2,'lat'=8,'lev'=2] {'lev'}, dimensions={1} | all-to-all | bytes 1327104 | tf_op jit(solution)/shard_map/all_to_all | solution.py:167
  80.6 0.1 slice.350
  80.6 0.5 copy.50
  81.1 1.4 %slice.294 = f32[16,2,4,1152]{3,2,1,0:T(4,128)} reshape(f32[16,2,4,2,576]{4,3,2,1,0:T(2,128)S(1)} %copy.50) | data formatting | bytes 1179648 | tf_op jit(solution)/shard_map/slice | solution.py:168
  82.6 0.7 squeeze.12
  83.3 0.7 squeeze.13
  (58 shorter events, 0.5 us)
Async XLA Ops:
  1.4 2.1 %copy-start.13 = (f32[1,2,4,1152]{3,0,2,1:T(1,128)}, f32[1,2,4,1152]{3,0,2,1:T(1,128)S(1)}, u32[]{:S(2)}) copy-start(f32[1,2,4,1152]{3,0,2,1:T(1,128)S(1)} %copy.41) | copy-start | bytes 110596
  2.3 10.8 %copy-start.11 = (f32[1,2,4,1152]{3,0,2,1:T(1,128)}, f32[1,2,4,1152]{3,0,2,1:T(1,128)S(1)}, u32[]{:S(2)}) copy-start(f32[1,2,4,1152]{3,0,2,1:T(1,128)S(1)} %copy.38) | copy-start | bytes 110596
  3.5 0.8 copy-start
  5.6 31.2 %collective-permute-start = (f32[18,2,3,1152]{3,0,2,1:T(8,128)}, f32[18,2,3,1152]{3,0,2,1:T(8,128)}, u32[]{:S(2)}, u32[]{:S(2)}) collective-permute-start(f32[18,2,3,1152]{3,0,2,1:T(8,128)} %get-tuple-element.15), channel_id=1, source_target_pairs={{0,2},{2,4},{4,6},{6,8},{8,10},{10,12},{12,14},{1,3},{3,5},{5,7},{... | collective-permute-start | bytes 1493000 | tf_op jit(solution)/shard_map/ppermute | solution.py:18
  8.7 31.0 %collective-permute-start.1 = (f32[18,2,3,1152]{3,0,2,1:T(8,128)}, f32[18,2,3,1152]{3,0,2,1:T(8,128)}, u32[]{:S(2)}, u32[]{:S(2)}) collective-permute-start(f32[18,2,3,1152]{3,0,2,1:T(8,128)} %get-tuple-element.16), channel_id=1, source_target_pairs={{2,0},{4,2},{6,4},{8,6},{10,8},{12,10},{14,12},{3,1},{5,3},{7,5},{... | collective-permute-start | bytes 1493000 | tf_op jit(solution)/shard_map/ppermute | solution.py:19
  13.3 0.7 copy-start.16
  13.7 0.9 %copy-start.4 = (f32[17,2,4,1151]{3,0,2,1:T(8,128)}, f32[17,2,4,1151]{3,0,2,1:T(8,128)S(1)}, u32[]{:S(2)}) copy-start(f32[17,2,4,1151]{3,0,2,1:T(8,128)S(1)} %get-tuple-element.9) | copy-start | bytes 1878436
  13.8 0.9 %copy-start.15 = (f32[17,2,4,2]{3,0,2,1:T(8,128)}, f32[17,2,4,2]{3,0,2,1:T(8,128)S(1)}, u32[]{:S(2)}) copy-start(f32[17,2,4,2]{3,0,2,1:T(8,128)S(1)} %slice.299) | copy-start | bytes 3268
  29.3 0.9 %copy-start.2 = (f32[17,2,4,1152]{3,0,2,1:T(8,128)}, f32[17,2,4,1152]{3,0,2,1:T(8,128)S(1)}, u32[]{:S(2)}) copy-start(f32[17,2,4,1152]{3,0,2,1:T(8,128)S(1)} %fusion.23) | copy-start | bytes 1880068
  29.3 1.3 %copy-start.8 = (f32[18,2,3,576]{3,0,2,1:T(8,128)S(1)}, f32[18,2,3,576]{3,0,2,1:T(8,128)}, u32[]{:S(2)}) copy-start(f32[18,2,3,576]{3,0,2,1:T(8,128)} %get-tuple-element.14) | copy-start | bytes 746500
  29.3 2.0 %copy-start.7 = (f32[18,2,3,576]{3,0,2,1:T(8,128)S(1)}, f32[18,2,3,576]{3,0,2,1:T(8,128)}, u32[]{:S(2)}) copy-start(f32[18,2,3,576]{3,0,2,1:T(8,128)} %get-tuple-element.11) | copy-start | bytes 746500
  30.3 1.9 %copy-start.6 = (f32[18,2,3,576]{3,0,2,1:T(8,128)S(1)}, f32[18,2,3,576]{3,0,2,1:T(8,128)}, u32[]{:S(2)}) copy-start(f32[18,2,3,576]{3,0,2,1:T(8,128)} %get-tuple-element.12) | copy-start | bytes 746500
  30.6 2.4 %copy-start.5 = (f32[18,2,3,576]{3,0,2,1:T(8,128)S(1)}, f32[18,2,3,576]{3,0,2,1:T(8,128)}, u32[]{:S(2)}) copy-start(f32[18,2,3,576]{3,0,2,1:T(8,128)} %get-tuple-element.13) | copy-start | bytes 746500
  30.6 2.4 %copy-start.19 = (s32[4,4,576]{2,1,0:T(4,128)S(1)}, s32[4,4,576]{2,1,0:T(4,128)}, u32[]{:S(2)}) copy-start(s32[4,4,576]{2,1,0:T(4,128)} %param.14) | copy-start | bytes 110596
  30.6 2.4 %copy-start.17 = (f32[4,4,576]{2,1,0:T(4,128)S(1)}, f32[4,4,576]{2,1,0:T(4,128)}, u32[]{:S(2)}) copy-start(f32[4,4,576]{2,1,0:T(4,128)} %param.15) | copy-start | bytes 110596
  30.6 9.1 %copy-start.21 = (f32[18]{0:T(128)S(1)}, f32[18]{0:T(128)}, u32[]{:S(2)}) copy-start(f32[18]{0:T(128)} %constant.32.clone.1) | copy-start | bytes 220
  31.4 8.3 %copy-start.9 = (f32[18,2,3,576]{3,0,2,1:T(8,128)S(1)}, f32[18,2,3,576]{3,0,2,1:T(8,128)}, u32[]{:S(2)}) copy-start(f32[18,2,3,576]{3,0,2,1:T(8,128)} %slice.264) | copy-start | bytes 746500
  32.2 7.6 %copy-start.10 = (f32[18,2,3,576]{3,0,2,1:T(8,128)S(1)}, f32[18,2,3,576]{3,0,2,1:T(8,128)}, u32[]{:S(2)}) copy-start(f32[18,2,3,576]{3,0,2,1:T(8,128)} %slice.262) | copy-start | bytes 746500
  33.0 8.4 %copy-start.1 = (f32[16,2,4,1152]{3,0,2,1:T(8,128)S(1)}, f32[16,2,4,1152]{3,0,2,1:T(8,128)}, u32[]{:S(2)}) copy-start(f32[16,2,4,1152]{3,0,2,1:T(8,128)} %copy-done) | copy-start | bytes 1769476
  33.0 8.4 %copy-start.12 = (f32[1,2,4,1152]{3,0,2,1:T(1,128)S(1)}, f32[1,2,4,1152]{3,0,2,1:T(1,128)}, u32[]{:S(2)}) copy-start(f32[1,2,4,1152]{3,0,2,1:T(1,128)} %copy-done.11) | copy-start | bytes 110596
  33.1 8.4 %copy-start.14 = (f32[1,2,4,1152]{3,0,2,1:T(1,128)S(1)}, f32[1,2,4,1152]{3,0,2,1:T(1,128)}, u32[]{:S(2)}) copy-start(f32[1,2,4,1152]{3,0,2,1:T(1,128)} %copy-done.13) | copy-start | bytes 110596
  42.6 1.2 %copy-start.3 = (f32[17,2,4,1152]{3,0,2,1:T(8,128)S(1)}, f32[17,2,4,1152]{3,0,2,1:T(8,128)}, u32[]{:S(2)}) copy-start(f32[17,2,4,1152]{3,0,2,1:T(8,128)} %copy-done.2) | copy-start | bytes 1880068
  74.7 0.8 copy-start.18
  74.7 0.8 copy-start.20
where the time goes:
time: 84.8 us; the launch traced here: 84 us
  local copies, waits for them, and re-layouts  45.6 us (54%)
  other arithmetic  15.8 us (19%)
  blocking collectives  8.64 us (10%)
  waiting for transfers between devices  6.64 us (8%)
  starting transfers between devices  6.17 us (7%)
  between operations  1.15 us (1%)
    unnamed x47, local copies, waits for them, and re-layouts  19.5 us
    slice x20, local copies, waits for them, and re-layouts, shift_lon(): return jnp.roll(values, offset, axis=-1)  11.6 us
    all_to_all x1, blocking collectives, on_device(): lax.all_to_all(advected, 'lev', split_axis=3, concat_axis=1, tiled=True)  4.4 us
    all_to_all x2, local copies, waits for them, and re-layouts, on_device(): lax.all_to_all(advected, 'lev', split_axis=3, concat_axis=1, tiled=True)  4.38 us
    all_to_all x1, blocking collectives, on_device(): lax.all_to_all(stacked_back, 'lev', split_axis=1, concat_axis=3, tiled=True)  4.24 us
    add x1, other arithmetic, advect(): crossed + fraction * (upwind_edge - 0.5 * fraction * (upwind_gradient - (...  4.12 us
    ppermute x1, waiting for transfers between devices, padded_2(): before = lax.ppermute(last, axis, up)  3.7 us
    sub x1, local copies, waits for them, and re-layouts, advect(): return cell_values - zonal_change - meridional_change  3.61 us
  transfers between devices with their start and end apart: 2, of which 2 were waited for; matrix products, arithmetic and copies ran while one was open for 24% of the time, Pallas kernels for 0%

commit v1 on v0

v1 whole, which is shorter than its diff:
```python
import functools
import math

import jax
import jax.numpy as jnp
import numpy as np
from jax import lax
from jax.experimental import pallas as pl
from jax.experimental.pallas import tpu as pltpu
from jax.sharding import PartitionSpec as P

ROWS = 4
LEVELS = 2
LANE = 128


def lane_view(values):
    rows, lons = values.shape[-2:]
    lead = math.prod(values.shape[:-2])
    chunks = lons // LANE
    return (
        values.reshape(lead, rows, chunks, LANE)
        .transpose(0, 2, 1, 3)
        .reshape(lead * chunks * rows, LANE)
    )


def from_lane_view(values, shape):
    rows, lons = shape[-2:]
    lead = math.prod(shape[:-2])
    chunks = lons // LANE
    return values.reshape(lead, chunks, rows, LANE).transpose(0, 2, 1, 3).reshape(shape)


def lanes(chunk):
    return pl.ds(chunk * LANE, LANE)


def parity():
    return lax.rem(lax.axis_index("lat"), 2)


def pack_kernel(chunks, fields, x, t, c, edge, relay0, relay1, near, near_t):
    odd = parity()
    relay = (relay0, relay1)
    stride = LEVELS * ROWS * chunks
    for d in range(3):
        row = jnp.where(odd == 1, 1 + d, 2 - d)
        for chunk in range(chunks):
            for lev in range(LEVELS):
                start = lev * ROWS * chunks + chunk * ROWS + row
                relay[lev][d, :, lanes(chunk)] = x[pl.ds(start, fields, stride=stride), :]
            edge[pl.ds(2 * d, 2), lanes(chunk)] = t[
                pl.ds(chunk * ROWS + row, 2, stride=ROWS * chunks), :
            ]
    row = jnp.where(odd == 1, 0, ROWS - 1)
    for chunk in range(chunks):
        for lev in range(LEVELS):
            start = lev * ROWS * chunks + chunk * ROWS + row
            near[lev, :, lanes(chunk)] = x[pl.ds(start, fields, stride=stride), :]
        near_t[:, lanes(chunk)] = t[pl.ds(chunk * ROWS + row, 2, stride=ROWS * chunks), :]
        edge[pl.ds(6, 2), lanes(chunk)] = c[
            pl.ds(chunk * ROWS + ROWS - 1, 2, stride=ROWS * chunks), :
        ]


def parabola_weights(share):
    half = 0.5 * share
    curve = half * (1.0 - share * (2.0 / 3.0))
    right = (1.0 - half - 3.0 * curve) * (1.0 / 12.0)
    left = (half - 3.0 * curve) * (1.0 / 12.0)
    return (
        -share * left,
        share * (7.0 * left - right),
        share * (7.0 * (left + right) + 6.0 * curve),
        share * (7.0 * right - left),
        -share * right,
    )


def face_weights(courant):
    t = parabola_weights(jnp.abs(courant))
    north = courant >= 0.0
    zero = jnp.zeros_like(courant)
    return (
        jnp.where(north, t[0], zero),
        jnp.where(north, t[1], -t[4]),
        jnp.where(north, t[2], -t[3]),
        jnp.where(north, t[3], -t[2]),
        jnp.where(north, t[4], -t[1]),
        jnp.where(north, zero, -t[0]),
    )


def halo_terms(j):
    south = [(0, d, -(j + d)) for d in range(1, 4 - j)]
    north = [(1, d, ROWS - 1 - j + d) for d in range(1, j + 1)]
    return south + north


def spread(row, like):
    return jnp.broadcast_to(row, like.shape)


def pre_kernel(
    chunks, fields, last, scale, x, t, c, n, f, edge_near, edge_far,
    pre, pre_t, halo_w, q, qt, zonal_w, own_w,
):
    lat = lax.axis_index("lat")
    odd = lax.rem(lat, 2)
    lons = chunks * LANE
    stride = LEVELS * ROWS * chunks

    def row_of(ref, j):
        return jnp.concatenate(
            [ref[pl.ds(k * ROWS + j, LEVELS, stride=ROWS * chunks), :] for k in range(chunks)],
            axis=1,
        )

    for j in range(ROWS):
        qt[j] = row_of(t, j)
        for lev in range(LEVELS):
            for chunk in range(chunks):
                start = lev * ROWS * chunks + chunk * ROWS + j
                q[lev, j, :, lanes(chunk)] = x[pl.ds(start, fields, stride=stride), :]

    courants = [row_of(c, j) for j in range(ROWS)]
    below = jnp.where(odd == 1, edge_near[6:8, :], edge_far[6:8, :])
    below = jnp.where(lat == 0, -pltpu.roll(courants[0], lons // 2, 1), below)
    faces = [face_weights(v) for v in [below] + courants]
    for j in range(ROWS):
        low = scale[lat * 2 * ROWS + 2 * j]
        high = scale[lat * 2 * ROWS + 2 * j + 1]
        lower, upper = faces[j], faces[j + 1]

        def weight(offset):
            total = None
            if offset <= 2:
                total = low * lower[offset + 3]
            if offset >= -2:
                part = high * upper[offset + 2]
                total = -part if total is None else total - part
            return total

        for r in range(ROWS):
            own_w[j, r] = weight(r - j)
        for k, (_, _, offset) in enumerate(halo_terms(j)):
            halo_w[3 * j + k] = weight(offset)

    for j in range(ROWS):
        whole = row_of(n, j)
        s = parabola_weights(row_of(f, j))
        zero = jnp.zeros_like(s[0])
        one = jnp.ones_like(s[0])
        n0, n1 = whole == 0, whole == 1

        def pick(a, b, d):
            return jnp.where(n0, a, jnp.where(n1, b, d))

        zonal_w[j, 0] = pick(s[4], zero, zero)
        zonal_w[j, 1] = pick(s[3], s[4], zero)
        zonal_w[j, 2] = pick(s[2], s[3] + one, s[4] + one)
        zonal_w[j, 3] = pick(s[1], s[2], s[3] + one)
        zonal_w[j, 4] = pick(s[0], s[1], s[2])
        zonal_w[j, 5] = pick(zero, s[0], s[1])
        zonal_w[j, 6] = pick(zero, zero, s[0])

    def shifted(values, k):
        return values if k == 0 else pltpu.roll(values, (-k) % lons, 1)

    for j in range(ROWS):
        v = qt[j]
        flux = zonal_w[j, 1] * v
        for k in (0, 2, 3, 4, 5, 6):
            flux = flux + zonal_w[j, k] * shifted(v, 1 - k)
        total = v - (shifted(flux, 1) - flux)
        for r in range(ROWS):
            total = total + own_w[j, r] * qt[r]
        pre_t[j] = total

    for lev in range(LEVELS):

        @pl.loop(0, ROWS)
        def _(j):
            for g in range(fields // 8):
                span = pl.ds(8 * g, 8)
                v = q[lev, j, span, :]
                flux = spread(zonal_w[j, 1, lev : lev + 1, :], v) * v
                for k in (0, 2, 3, 4, 5, 6):
                    flux = flux + spread(zonal_w[j, k, lev : lev + 1, :], v) * shifted(v, 1 - k)
                total = v - (shifted(flux, 1) - flux)
                for r in range(ROWS):
                    total = total + spread(own_w[j, r, lev : lev + 1, :], v) * q[lev, r, span, :]
                pre[lev, j, span, :] = total

    def pole(side):
        for j in range(ROWS):
            for k, (where, d, _) in enumerate(halo_terms(j)):
                if where != side:
                    continue
                r = d - 1 if side == 0 else ROWS - d
                w = halo_w[3 * j + k]
                pre_t[j] = pre_t[j] + w * pltpu.roll(qt[r], lons // 2, 1)
                for lev in range(LEVELS):
                    for g in range(fields // 8):
                        span = pl.ds(8 * g, 8)
                        v = pltpu.roll(q[lev, r, span, :], lons // 2, 1)
                        pre[lev, j, span, :] = (
                            pre[lev, j, span, :] + spread(w[lev : lev + 1, :], v) * v
                        )
                halo_w[3 * j + k] = jnp.zeros_like(w)

    @pl.when(lat == 0)
    def _():
        pole(0)

    @pl.when(lat == last)
    def _():
        pole(1)


def fin_kernel(
    chunks, fields, pre, pre_t, halo_w, relay0, relay1, far0, far1, near, near_t, edge_near,
    edge_far, adv, adv_t,
):
    odd = parity()
    relay, far = (relay0, relay1), (far0, far1)

    def near_row(lev, d, lane):
        return near[lev, :, lane] if d == 1 else relay[lev][d - 2, :, lane]

    def far_row(lev, d, lane):
        return far[lev][3 - d, :, lane]

    def near_edge(d):
        return near_t[...] if d == 1 else edge_near[pl.ds(2 * (d - 2), 2), :]

    def far_edge(d):
        return edge_far[pl.ds(2 * (3 - d), 2), :]

    def body(rows, edges):
        for j in range(ROWS):
            total = pre_t[j]
            for k, (side, d, _) in enumerate(halo_terms(j)):
                total = total + halo_w[3 * j + k] * edges[side](d)
            for lev in range(LEVELS):
                adv_t[lev, j : j + 1, :] = total[lev : lev + 1, :]
            for lev in range(LEVELS):
                for chunk in range(chunks):
                    lane = lanes(chunk)
                    total = pre[lev, j, :, lane]
                    for k, (side, d, _) in enumerate(halo_terms(j)):
                        w = halo_w[3 * j + k, lev : lev + 1, lane]
                        total = total + spread(w, total) * rows[side](lev, d, lane)
                    adv[lev, j, :, lane] = total

    @pl.when(odd == 1)
    def _():
        body((near_row, far_row), (near_edge, far_edge))

    @pl.when(odd == 0)
    def _():
        body((far_row, near_row), (far_edge, near_edge))


def remap_kernel(
    chunks, fields, levels, adv_own, adv_peer, t_own, t_peer, columns,
    out, out_t, out_phi, weights, vapour, thick,
):
    group = lax.axis_index("lev")
    stride = LEVELS * ROWS * chunks
    sources = [(adv_own, t_own, lev, group * LEVELS + lev) for lev in range(LEVELS)]
    sources += [(adv_peer, t_peer, lev, (1 - group) * LEVELS + lev) for lev in range(LEVELS)]

    for s, (adv, _, lev, _) in enumerate(sources):
        for j in range(ROWS):
            vapour[s, j : j + 1, :] = adv[lev, j, 0:1, :]
    for k in range(levels):
        upper = columns[k]
        share = columns[levels + k]
        water = None
        heat = None
        for s, (_, temp, lev, level) in enumerate(sources):
            at = level.astype(jnp.float32)
            w = jnp.where(
                upper == at, 1.0 - share, jnp.where(upper + 1.0 == at, share, 0.0)
            )
            weights[k, s] = w
            water = w * vapour[s] if water is None else water + w * vapour[s]
            heat = w * temp[lev] if heat is None else heat + w * temp[lev]
        thick[k] = heat * (1.0 + 0.608 * water) * columns[2 * levels + k]
        thick[levels + k] = heat
    deeper = columns[3 * levels]
    for k in range(levels - 1, -1, -1):
        layer = thick[k]
        thick[k] = deeper + 0.5 * layer
        deeper = deeper + layer
    for lev in range(LEVELS):
        phi = thick[group * LEVELS + lev]
        heat = thick[levels + group * LEVELS + lev]
        for chunk in range(chunks):
            at = pl.ds((lev * chunks + chunk) * ROWS, ROWS)
            lane = slice(chunk * LANE, (chunk + 1) * LANE)
            out_phi[at, :] = phi[:, lane]
            out_t[at, :] = heat[:, lane]

    for j in range(ROWS):
        for chunk in range(chunks):
            lane = lanes(chunk)
            values = [adv[lev, j, :, lane] for adv, _, lev, _ in sources]
            for lev in range(LEVELS):
                k = group * LEVELS + lev
                total = None
                for s, v in enumerate(values):
                    part = spread(weights[k, s, j : j + 1, lane], v) * v
                    total = part if total is None else total + part
                start = (lev * chunks + chunk) * ROWS + j
                out[pl.ds(start, fields, stride=stride), :] = total


def call(kernel, outs, scratch=(), specs=None, cost=(0, 0), limit=16):
    return pl.pallas_call(
        kernel,
        out_shape=tuple(jax.ShapeDtypeStruct(s, jnp.float32) for s in outs),
        scratch_shapes=[pltpu.VMEM(s, jnp.float32) for s in scratch],
        compiler_params=pltpu.CompilerParams(vmem_limit_bytes=limit * 2**20),
        cost_estimate=pl.CostEstimate(flops=cost[0], bytes_accessed=cost[1], transcendentals=0),
        **({} if specs is None else {"in_specs": specs}),
    )


def on_device(
    constituent_densities,
    thermal_state,
    integer_boxes_traversed,
    partial_crossing_share,
    northward_crossing_share,
    higher_donor_stratum,
    deeper_donor_share,
    napierian_thickness_quotient,
    ground_gravity_height,
):
    fields, _, _, lons = constituent_densities.shape
    levels = higher_donor_stratum.shape[0]
    chunks = lons // LANE
    bands = lax.axis_size("lat")
    lat_total = bands * ROWS

    pairs = [(i, i ^ 1) for i in range(bands)]
    relays = [(i, i + 2) for i in range(0, bands - 2, 2)] + [(i, i - 2) for i in range(3, bands, 2)]
    cores = [(0, 1), (1, 0)]

    def swap(v):
        return lax.ppermute(v, "lat", pairs)

    def pass_on(v):
        return lax.ppermute(v, "lat", relays)

    def other_core(v):
        return lax.ppermute(v, "lev", cores)

    face = np.arange(lat_total + 1)
    face_sine = np.sin(math.pi * np.minimum(face, lat_total - face) / lat_total)
    face_sine[[0, -1]] = 0.0
    row_sine = np.sin(math.pi * (np.arange(lat_total) + 0.5) / lat_total)
    scale = np.stack([face_sine[:-1] / row_sine, face_sine[1:] / row_sine], 1)
    scale = jnp.asarray(scale.reshape(-1).astype(np.float32))

    x = lane_view(constituent_densities)
    t, n, f, c = (
        lane_view(v)
        for v in (
            thermal_state,
            integer_boxes_traversed,
            partial_crossing_share,
            northward_crossing_share,
        )
    )
    relay_shape = (3, fields, lons)
    field_shape = (LEVELS, ROWS, fields, lons)
    row = (LEVELS, lons)
    edge, relay0, relay1, near, near_t = call(
        functools.partial(pack_kernel, chunks, fields),
        [(8, lons), relay_shape, relay_shape, (LEVELS, fields, lons), row],
        cost=(0, 1400000),
    )(x, t, c)

    edge_near = swap(edge)
    relay0_near = swap(relay0)
    relay1_near = swap(relay1)
    near_near = swap(near)
    near_t_near = swap(near_t)
    edge_far = pass_on(edge_near)
    relay0_far = pass_on(relay0_near)
    relay1_far = pass_on(relay1_near)

    columns = jnp.concatenate(
        [
            higher_donor_stratum.astype(jnp.float32),
            deeper_donor_share,
            napierian_thickness_quotient,
            ground_gravity_height[None],
        ],
        axis=0,
    )
    peer_columns = other_core(columns)
    columns = jnp.where(
        lax.axis_index("lev") == 0,
        jnp.concatenate([columns, peer_columns], -1),
        jnp.concatenate([peer_columns, columns], -1),
    )

    vmem = pl.BlockSpec(memory_space=pltpu.VMEM)
    pre, pre_t, halo_w = call(
        functools.partial(pre_kernel, chunks, fields, bands - 1),
        [field_shape, (ROWS,) + row, (3 * ROWS,) + row],
        [field_shape, (ROWS,) + row, (ROWS, 7) + row, (ROWS, ROWS) + row],
        [pl.BlockSpec(memory_space=pltpu.SMEM)] + [vmem] * 7,
        cost=(20000000, 3000000),
    )(scale, x, t, c, n, f, edge_near, edge_far)

    adv, adv_t = call(
        functools.partial(fin_kernel, chunks, fields),
        [field_shape, (LEVELS, ROWS, lons)],
        cost=(2000000, 3000000),
    )(
        pre, pre_t, halo_w, relay0_near, relay1_near, relay0_far, relay1_far,
        near_near, near_t_near, edge_near, edge_far,
    )
    peer = other_core(adv)
    peer_t = other_core(adv_t)
    out, out_t, phi = call(
        functools.partial(remap_kernel, chunks, fields, levels),
        [x.shape, t.shape, t.shape],
        [(levels, 2 * LEVELS, ROWS, lons), (2 * LEVELS, ROWS, lons), (2 * levels, ROWS, lons)],
        cost=(3000000, 3000000),
    )(adv, peer, adv_t, peer_t, columns)
    return (
        from_lane_view(out, constituent_densities.shape),
        from_lane_view(out_t, thermal_state.shape),
        from_lane_view(phi, thermal_state.shape),
    )


def solution(mesh):
    return jax.shard_map(
        on_device,
        mesh=mesh,
        in_specs=(
            P("ens", "lev", "lat", None),
            P(("ens", "lev"), "lat", None),
            P(("ens", "lev"), "lat", None),
            P(("ens", "lev"), "lat", None),
            P(("ens", "lev"), "lat", None),
            P("ens", "lat", "lev"),
            P("ens", "lat", "lev"),
            P("ens", "lat", "lev"),
            P(("ens", "lat"), "lev"),
        ),
        out_specs=(
            P("ens", "lev", "lat", None),
            P(("ens", "lev"), "lat", None),
            P(("ens", "lev"), "lat", None),
        ),
        check_vma=False,
    )
```

time: 84.8 us -> 42.2 us (0.50)
  the two profiles are of different devices: /device:TPU:9 before, /device:TPU:0 now
where the time goes in v1:
time: 42.2 us; the launch traced here: 41.7 us
  starting transfers between devices  17 us (40%)
  waiting for transfers between devices  11.3 us (27%)
  local copies, waits for them, and re-layouts  7.54 us (18%)
  Pallas kernels  4.75 us (11%)
  between operations  0.93 us (2%)
    ppermute x3, starting transfers between devices, pass_on(): return lax.ppermute(v, 'lat', relays)  11.1 us
    ppermute x5, waiting for transfers between devices, swap(): return lax.ppermute(v, 'lat', pairs)  9.7 us
    ppermute x5, starting transfers between devices, swap(): return lax.ppermute(v, 'lat', pairs)  5.24 us
    pallas_call x1, Pallas kernels, on_device(): call(functools.partial(pre_kernel, chunks, fields, bands - 1), [field_sha...  4.03 us
    unnamed x18, local copies, waits for them, and re-layouts  3.35 us
    reshape x6, local copies, waits for them, and re-layouts, from_lane_view(): values.reshape(lead, chunks, rows, LANE).transpose(0, 2, 1, 3)  2.43 us
    reshape x5, local copies, waits for them, and re-layouts, lane_view(): values.reshape(lead, rows, chunks, LANE).transpose(0, 2, 1, 3)  1.45 us
    ppermute x3, waiting for transfers between devices, other_core(): return lax.ppermute(v, 'lev', cores)  0.87 us
  transfers between devices with their start and end apart: 11, of which 4 were waited for; matrix products, arithmetic and copies ran while one was open for 1% of the time, Pallas kernels for 10%

profile of v1, /device:TPU:0, one launch (start us, length us, event | category | flops | bytes accessed | tf_op | source)
XLA Modules:
  0.0 41.7 jit_solution(14649329538219857197)
XLA Ops:
  0.6 1.4 %reshape.54 = f32[32,4,9,128]{3,2,1,0:T(8,128)S(1)} reshape(f32[16,2,4,1152]{3,2,1,0:T(4,128)} %param.10) | data formatting | bytes 1179648 | tf_op jit(solution)/shard_map/reshape | solution.py:22
  2.0 0.0 copy-start.5
  2.0 0.2 copy.21
  2.3 0.5 %copy-done.5 = f32[2,4,1152]{2,1,0:T(4,128)S(1)} copy-done((f32[2,4,1152]{2,1,0:T(4,128)S(1)}, f32[2,4,1152]{2,1,0:T(4,128)}, u32[]{:S(2)}) %copy-start.5) | copy-done | bytes 36888
  2.8 0.0 copy-start.6
  2.8 0.7 %copy-done.6 = f32[2,4,1152]{2,1,0:T(4,128)S(1)} copy-done((f32[2,4,1152]{2,1,0:T(4,128)S(1)}, f32[2,4,1152]{2,1,0:T(4,128)}, u32[]{:S(2)}) %copy-start.6) | copy-done | bytes 36888
  3.6 0.0 copy-start.7
  3.6 0.2 shard_map.121
  3.8 3.0 %collective-permute-start.2 = (f32[3,16,1152]{2,1,0:T(8,128)S(1)}, f32[3,16,1152]{2,1,0:T(8,128)S(1)}, u32[]{:S(2)}, u32[]{:S(2)}) collective-permute-start(f32[3,16,1152]{2,1,0:T(8,128)S(1)} %get-tuple-element.20), channel_id=1, source_target_pairs={{0,2},{2,0},{4,6},{6,4},{8,10},{10,8},{12,14},{14,12},{1,3},{3,1},... | collective-permute-start | bytes 663560 | tf_op jit(solution)/shard_map/ppermute | solution.py:354
  6.8 0.1 collective-permute-start.3
  6.9 6.2 %collective-permute-done.2.relay0 = f32[3,16,1152]{2,1,0:T(8,128)S(1)} collective-permute-done((f32[3,16,1152]{2,1,0:T(8,128)S(1)}, f32[3,16,1152]{2,1,0:T(8,128)S(1)}, u32[]{:S(2)}, u32[]{:S(2)}) %collective-permute-start.2) | collective-permute-done | bytes 221216 | tf_op jit(solution)/shard_map/ppermute | solution.py:354
  13.0 4.0 %collective-permute-start.4 = (f32[3,16,1152]{2,1,0:T(8,128)S(1)}, f32[3,16,1152]{2,1,0:T(8,128)S(1)}, u32[]{:S(2)}, u32[]{:S(2)}) collective-permute-start(f32[3,16,1152]{2,1,0:T(8,128)S(1)} %collective-permute-done.2.relay0), channel_id=1, source_target_pairs={{0,4},{4,8},{8,12},{6,2},{10,6},{14,10},{1,5},{5,9},{9,13},{7,3},{... | collective-permute-start | bytes 663560 | tf_op jit(solution)/shard_map/ppermute | solution.py:357
  17.1 0.0 collective-permute-done.3.relay1
  17.1 3.6 %collective-permute-start.5 = (f32[3,16,1152]{2,1,0:T(8,128)S(1)}, f32[3,16,1152]{2,1,0:T(8,128)S(1)}, u32[]{:S(2)}, u32[]{:S(2)}) collective-permute-start(f32[3,16,1152]{2,1,0:T(8,128)S(1)} %collective-permute-done.3.relay1), channel_id=1, source_target_pairs={{0,4},{4,8},{8,12},{6,2},{10,6},{14,10},{1,5},{5,9},{9,13},{7,3},{... | collective-permute-start | bytes 663560 | tf_op jit(solution)/shard_map/ppermute | solution.py:357
  20.7 0.1 collective-permute-start.6
  20.8 2.0 %collective-permute-start = (f32[8,1152]{1,0:T(8,128)S(1)}, f32[8,1152]{1,0:T(8,128)S(1)}, u32[]{:S(2)}, u32[]{:S(2)}) collective-permute-start(f32[8,1152]{1,0:T(8,128)S(1)} %get-tuple-element.16), channel_id=1, source_target_pairs={{0,2},{2,0},{4,6},{6,4},{8,10},{10,8},{12,14},{14,12},{1,3},{3,1},... | collective-permute-start | bytes 110600 | tf_op jit(solution)/shard_map/ppermute | solution.py:354
  22.8 3.5 %collective-permute-done.edge_near = f32[8,1152]{1,0:T(8,128)S(1)} collective-permute-done((f32[8,1152]{1,0:T(8,128)S(1)}, f32[8,1152]{1,0:T(8,128)S(1)}, u32[]{:S(2)}, u32[]{:S(2)}) %collective-permute-start) | collective-permute-done | bytes 36896 | tf_op jit(solution)/shard_map/ppermute | solution.py:354
  26.3 3.5 %collective-permute-start.1 = (f32[8,1152]{1,0:T(8,128)S(1)}, f32[8,1152]{1,0:T(8,128)S(1)}, u32[]{:S(2)}, u32[]{:S(2)}) collective-permute-start(f32[8,1152]{1,0:T(8,128)S(1)} %collective-permute-done.edge_near), channel_id=1, source_target_pairs={{0,4},{4,8},{8,12},{6,2},{10,6},{14,10},{1,5},{5,9},{9,13},{7,3},{... | collective-permute-start | bytes 110600 | tf_op jit(solution)/shard_map/ppermute | solution.py:357
  29.8 0.1 collective-permute-start.7
  29.8 0.0 copy-done.7
  29.9 0.0 copy-start.8
  29.9 0.7 %copy-done.8 = f32[2,4,1152]{2,1,0:T(4,128)S(1)} copy-done((f32[2,4,1152]{2,1,0:T(4,128)S(1)}, f32[2,4,1152]{2,1,0:T(4,128)}, u32[]{:S(2)}) %copy-start.8) | copy-done | bytes 36888
  30.7 0.7 %collective-permute-done.1.edge_far = f32[8,1152]{1,0:T(8,128)S(1)} collective-permute-done((f32[8,1152]{1,0:T(8,128)S(1)}, f32[8,1152]{1,0:T(8,128)S(1)}, u32[]{:S(2)}, u32[]{:S(2)}) %collective-permute-start.1) | collective-permute-done | bytes 36896 | tf_op jit(solution)/shard_map/ppermute | solution.py:357
  31.4 0.0 copy-start
  31.4 0.7 %copy-done = f32[64]{0:T(128)S(1)} copy-done((f32[64]{0:T(128)S(1)}, f32[64]{0:T(128)}, u32[]{:S(2)}) %copy-start) | copy-done | bytes 280
  32.0 4.0 %shard_map.122 = (f32[2,4,16,1152]{3,2,1,0:T(8,128)S(1)}, f32[4,2,1152]{2,1,0:T(2,128)S(1)}, f32[12,2,1152]{2,1,0:T(2,128)S(1)}) custom-call(f32[64]{0:T(128)S(1)} %copy-done, f32[1152,128]{1,0:T(8,128)S(1)} %bitcast.24, f32[72,128]{1,0:T(8,128)S(1)} %bitcast.27, f32[72,128]{1,0:T(8,128)S(1)} %bitcast.29, s32[72,128]{1,0:T(8,128)S(1)} %bitcast.30, ...), custom_call_target="tpu_custom_call" | custom-call | flops 20000000 | bytes 3000000 | tf_op jit(solution)/shard_map/pallas_call | solution.py:414
  36.1 0.0 collective-permute-done.7.near_t
  36.1 0.0 collective-permute-done.6.near
  36.1 0.0 collective-permute-done.4.far0
  36.1 0.0 collective-permute-done.5.far1
  36.1 0.0 copy-start.3
  36.1 0.0 copy-start.4
  36.1 0.3 shard_map.123
  36.4 0.0 copy-start.1
  36.4 0.0 copy-start.2
  36.4 0.1 collective-permute-start.8
  36.5 0.4 copy-done.3
  36.9 0.0 copy-done.4
  36.9 0.3 copy-done.1
  37.2 0.0 copy-done.2
  37.2 0.1 collective-permute-start.10
  37.3 0.5 %collective-permute-start.9 = (f32[2,4,1152]{2,1,0:T(4,128)S(1)}, f32[2,4,1152]{2,1,0:T(4,128)S(1)}, u32[]{:S(2)}, u32[]{:S(2)}) collective-permute-start(f32[2,4,1152]{2,1,0:T(4,128)S(1)} %get-tuple-element.25.t_own), channel_id=1, source_target_pairs={{0,1},{1,0},{2,3},{3,2},{4,5},{5,4},{6,7},{7,6},{8,9},{9,8},{10,11... | collective-permute-start | bytes 110600 | tf_op jit(solution)/shard_map/ppermute | solution.py:360
  37.8 0.9 %collective-permute-done.10 = f32[13,4,576]{2,1,0:T(4,128)S(1)} collective-permute-done((f32[13,4,576]{2,1,0:T(4,128)S(1)}, f32[13,4,576]{2,1,0:T(4,128)S(1)}, u32[]{:S(2)}, u32[]{:S(2)}) %collective-permute-start.10) | collective-permute-done | bytes 119840 | tf_op jit(solution)/shard_map/ppermute | solution.py:360
  38.7 0.2 maximum_select_fusion.columns
  38.9 0.0 collective-permute-done.9.t_peer
  38.9 0.0 collective-permute-done.8.adv_peer
  38.9 0.3 shard_map.124
  39.2 0.1 copy.32
  39.4 1.0 %reshape.65 = f32[16,2,4,1152]{3,2,1,0:T(4,128)} reshape(f32[32,4,9,128]{3,2,1,0:T(8,128)S(1)} %bitcast.34) | data formatting | bytes 1179648 | tf_op jit(solution)/shard_map/reshape | solution.py:32
  40.4 0.6 %reshape.67 = f32[2,4,1152]{2,1,0:T(4,128)} reshape(f32[2,4,9,128]{3,2,1,0:T(8,128)S(1)} %bitcast.36) | data formatting | bytes 73728 | tf_op jit(solution)/shard_map/reshape | solution.py:32
  41.0 0.6 %reshape.69 = f32[2,4,1152]{2,1,0:T(4,128)} reshape(f32[2,4,9,128]{3,2,1,0:T(8,128)S(1)} %bitcast.37) | data formatting | bytes 73728 | tf_op jit(solution)/shard_map/reshape | solution.py:32
  (12 shorter events, 0.2 us)
Async XLA Ops:
  2.0 0.8 %copy-start.5 = (f32[2,4,1152]{2,1,0:T(4,128)S(1)}, f32[2,4,1152]{2,1,0:T(4,128)}, u32[]{:S(2)}) copy-start(f32[2,4,1152]{2,1,0:T(4,128)} %param.11) | copy-start | bytes 110596
  2.8 0.8 %copy-start.6 = (f32[2,4,1152]{2,1,0:T(4,128)S(1)}, f32[2,4,1152]{2,1,0:T(4,128)}, u32[]{:S(2)}) copy-start(f32[2,4,1152]{2,1,0:T(4,128)} %param.14) | copy-start | bytes 110596
  3.6 26.2 %copy-start.7 = (s32[2,4,1152]{2,1,0:T(4,128)S(1)}, s32[2,4,1152]{2,1,0:T(4,128)}, u32[]{:S(2)}) copy-start(s32[2,4,1152]{2,1,0:T(4,128)} %param.12) | copy-start | bytes 110596
  3.8 9.3 %collective-permute-start.2 = (f32[3,16,1152]{2,1,0:T(8,128)S(1)}, f32[3,16,1152]{2,1,0:T(8,128)S(1)}, u32[]{:S(2)}, u32[]{:S(2)}) collective-permute-start(f32[3,16,1152]{2,1,0:T(8,128)S(1)} %get-tuple-element.20), channel_id=1, source_target_pairs={{0,2},{2,0},{4,6},{6,4},{8,10},{10,8},{12,14},{14,12},{1,3},{3,1},... | collective-permute-start | bytes 663560 | tf_op jit(solution)/shard_map/ppermute | solution.py:354
  6.8 10.3 %collective-permute-start.3 = (f32[3,16,1152]{2,1,0:T(8,128)S(1)}, f32[3,16,1152]{2,1,0:T(8,128)S(1)}, u32[]{:S(2)}, u32[]{:S(2)}) collective-permute-start(f32[3,16,1152]{2,1,0:T(8,128)S(1)} %get-tuple-element.21), channel_id=1, source_target_pairs={{0,2},{2,0},{4,6},{6,4},{8,10},{10,8},{12,14},{14,12},{1,3},{3,1},... | collective-permute-start | bytes 663560 | tf_op jit(solution)/shard_map/ppermute | solution.py:354
  13.0 23.1 %collective-permute-start.4 = (f32[3,16,1152]{2,1,0:T(8,128)S(1)}, f32[3,16,1152]{2,1,0:T(8,128)S(1)}, u32[]{:S(2)}, u32[]{:S(2)}) collective-permute-start(f32[3,16,1152]{2,1,0:T(8,128)S(1)} %collective-permute-done.2.relay0), channel_id=1, source_target_pairs={{0,4},{4,8},{8,12},{6,2},{10,6},{14,10},{1,5},{5,9},{9,13},{7,3},{... | collective-permute-start | bytes 663560 | tf_op jit(solution)/shard_map/ppermute | solution.py:357
  17.1 19.0 %collective-permute-start.5 = (f32[3,16,1152]{2,1,0:T(8,128)S(1)}, f32[3,16,1152]{2,1,0:T(8,128)S(1)}, u32[]{:S(2)}, u32[]{:S(2)}) collective-permute-start(f32[3,16,1152]{2,1,0:T(8,128)S(1)} %collective-permute-done.3.relay1), channel_id=1, source_target_pairs={{0,4},{4,8},{8,12},{6,2},{10,6},{14,10},{1,5},{5,9},{9,13},{7,3},{... | collective-permute-start | bytes 663560 | tf_op jit(solution)/shard_map/ppermute | solution.py:357
  20.7 15.4 %collective-permute-start.6 = (f32[2,16,1152]{2,1,0:T(8,128)S(1)}, f32[2,16,1152]{2,1,0:T(8,128)S(1)}, u32[]{:S(2)}, u32[]{:S(2)}) collective-permute-start(f32[2,16,1152]{2,1,0:T(8,128)S(1)} %get-tuple-element.22), channel_id=1, source_target_pairs={{0,2},{2,0},{4,6},{6,4},{8,10},{10,8},{12,14},{14,12},{1,3},{3,1},... | collective-permute-start | bytes 442376 | tf_op jit(solution)/shard_map/ppermute | solution.py:354
  20.8 5.5 %collective-permute-start = (f32[8,1152]{1,0:T(8,128)S(1)}, f32[8,1152]{1,0:T(8,128)S(1)}, u32[]{:S(2)}, u32[]{:S(2)}) collective-permute-start(f32[8,1152]{1,0:T(8,128)S(1)} %get-tuple-element.16), channel_id=1, source_target_pairs={{0,2},{2,0},{4,6},{6,4},{8,10},{10,8},{12,14},{14,12},{1,3},{3,1},... | collective-permute-start | bytes 110600 | tf_op jit(solution)/shard_map/ppermute | solution.py:354
  26.3 5.1 %collective-permute-start.1 = (f32[8,1152]{1,0:T(8,128)S(1)}, f32[8,1152]{1,0:T(8,128)S(1)}, u32[]{:S(2)}, u32[]{:S(2)}) collective-permute-start(f32[8,1152]{1,0:T(8,128)S(1)} %collective-permute-done.edge_near), channel_id=1, source_target_pairs={{0,4},{4,8},{8,12},{6,2},{10,6},{14,10},{1,5},{5,9},{9,13},{7,3},{... | collective-permute-start | bytes 110600 | tf_op jit(solution)/shard_map/ppermute | solution.py:357
  29.8 6.3 %collective-permute-start.7 = (f32[2,1152]{1,0:T(2,128)S(1)}, f32[2,1152]{1,0:T(2,128)S(1)}, u32[]{:S(2)}, u32[]{:S(2)}) collective-permute-start(f32[2,1152]{1,0:T(2,128)S(1)} %get-tuple-element.23), channel_id=1, source_target_pairs={{0,2},{2,0},{4,6},{6,4},{8,10},{10,8},{12,14},{14,12},{1,3},{3,1},... | collective-permute-start | bytes 27656 | tf_op jit(solution)/shard_map/ppermute | solution.py:354
  29.9 0.8 %copy-start.8 = (f32[2,4,1152]{2,1,0:T(4,128)S(1)}, f32[2,4,1152]{2,1,0:T(4,128)}, u32[]{:S(2)}) copy-start(f32[2,4,1152]{2,1,0:T(4,128)} %param.13) | copy-start | bytes 110596
  31.4 0.7 %copy-start = (f32[64]{0:T(128)S(1)}, f32[64]{0:T(128)}, u32[]{:S(2)}) copy-start(f32[64]{0:T(128)} %constant.8.clone.scale) | copy-start | bytes 772
  36.1 0.8 %copy-start.3 = (s32[4,4,576]{2,1,0:T(4,128)S(1)}, s32[4,4,576]{2,1,0:T(4,128)}, u32[]{:S(2)}) copy-start(s32[4,4,576]{2,1,0:T(4,128)} %param.15) | copy-start | bytes 110596
  36.1 0.8 %copy-start.4 = (f32[4,576]{1,0:T(4,128)S(1)}, f32[4,576]{1,0:T(4,128)}, u32[]{:S(2)}) copy-start(f32[4,576]{1,0:T(4,128)} %param.18) | copy-start | bytes 27652
  36.4 0.8 %copy-start.1 = (f32[4,4,576]{2,1,0:T(4,128)S(1)}, f32[4,4,576]{2,1,0:T(4,128)}, u32[]{:S(2)}) copy-start(f32[4,4,576]{2,1,0:T(4,128)} %param.17) | copy-start | bytes 110596
  36.4 0.8 %copy-start.2 = (f32[4,4,576]{2,1,0:T(4,128)S(1)}, f32[4,4,576]{2,1,0:T(4,128)}, u32[]{:S(2)}) copy-start(f32[4,4,576]{2,1,0:T(4,128)} %param.16) | copy-start | bytes 110596
  36.4 2.5 %collective-permute-start.8 = (f32[2,4,16,1152]{3,2,1,0:T(8,128)S(1)}, f32[2,4,16,1152]{3,2,1,0:T(8,128)S(1)}, u32[]{:S(2)}, u32[]{:S(2)}) collective-permute-start(f32[2,4,16,1152]{3,2,1,0:T(8,128)S(1)} %get-tuple-element.24.adv_own), channel_id=1, source_target_pairs={{0,1},{1,0},{2,3},{3,2},{4,5},{5,4},{6,7},{7,6},{8,9},{9,8},{10,11... | collective-permute-start | bytes 1769480 | tf_op jit(solution)/shard_map/ppermute | solution.py:360
  37.2 1.4 %collective-permute-start.10 = (f32[13,4,576]{2,1,0:T(4,128)S(1)}, f32[13,4,576]{2,1,0:T(4,128)S(1)}, u32[]{:S(2)}, u32[]{:S(2)}) collective-permute-start(f32[13,4,576]{2,1,0:T(4,128)S(1)} %pad_maximum_fusion), channel_id=1, source_target_pairs={{0,1},{1,0},{2,3},{3,2},{4,5},{5,4},{6,7},{7,6},{8,9},{9,8},{10,11... | collective-permute-start | bytes 359432 | tf_op jit(solution)/shard_map/ppermute | solution.py:360
  37.3 1.6 %collective-permute-start.9 = (f32[2,4,1152]{2,1,0:T(4,128)S(1)}, f32[2,4,1152]{2,1,0:T(4,128)S(1)}, u32[]{:S(2)}, u32[]{:S(2)}) collective-permute-start(f32[2,4,1152]{2,1,0:T(4,128)S(1)} %get-tuple-element.25.t_own), channel_id=1, source_target_pairs={{0,1},{1,0},{2,3},{3,2},{4,5},{5,4},{6,7},{7,6},{8,9},{9,8},{10,11... | collective-permute-start | bytes 110600 | tf_op jit(solution)/shard_map/ppermute | solution.py:360

commit v2 on v0

v2 whole, which is shorter than its diff:
```python
import functools
import math

import jax
import jax.numpy as jnp
import numpy as np
from jax import lax
from jax.experimental import pallas as pl
from jax.experimental.pallas import tpu as pltpu
from jax.sharding import PartitionSpec as P

ROWS = 4
LEVELS = 2
LANE = 128
SPLIT = 4


def lanes(chunk):
    return pl.ds(chunk * LANE, LANE)


def parity():
    return lax.rem(lax.axis_index("lat"), 2)


def both(odd, body):
    @pl.when(odd == 1)
    def _():
        body(True)

    @pl.when(odd == 0)
    def _():
        body(False)


def pack_kernel(fields, x, relay):
    def body(odd):
        for d in range(1, 4):
            row = d - 1 if odd else ROWS - d
            for f in range(fields):
                for lev in range(LEVELS):
                    relay[d - 1, lev, f : f + 1, :] = x[f, lev, row : row + 1, :]

    both(parity(), body)


def edge_kernel(t, c, edge):
    def body(odd):
        for lev in range(LEVELS):
            for d in range(1, 4):
                row = d - 1 if odd else ROWS - d
                at = 2 * (d - 1) + lev
                edge[at : at + 1, :] = t[lev, row : row + 1, :]
            edge[6 + lev : 7 + lev, :] = c[lev, ROWS - 1 : ROWS, :]

    both(parity(), body)


def parabola_weights(share):
    half = 0.5 * share
    curve = half * (1.0 - share * (2.0 / 3.0))
    right = (1.0 - half - 3.0 * curve) * (1.0 / 12.0)
    left = (half - 3.0 * curve) * (1.0 / 12.0)
    return (
        -share * left,
        share * (7.0 * left - right),
        share * (7.0 * (left + right) + 6.0 * curve),
        share * (7.0 * right - left),
        -share * right,
    )


def face_weights(courant):
    t = parabola_weights(jnp.abs(courant))
    north = courant >= 0.0
    zero = jnp.zeros_like(courant)
    return (
        jnp.where(north, t[0], zero),
        jnp.where(north, t[1], -t[4]),
        jnp.where(north, t[2], -t[3]),
        jnp.where(north, t[3], -t[2]),
        jnp.where(north, t[4], -t[1]),
        jnp.where(north, zero, -t[0]),
    )


def row_weights(c, below, scale, lat):
    row = lax.broadcasted_iota(jnp.int32, c.shape, 0)

    def by_row(parts):
        total = parts[ROWS - 1]
        for j in range(ROWS - 2, -1, -1):
            total = jnp.where(row == j, parts[j], total)
        return total

    low = by_row([jnp.full(c.shape, scale[lat * 2 * ROWS + 2 * j]) for j in range(ROWS)])
    high = by_row([jnp.full(c.shape, scale[lat * 2 * ROWS + 2 * j + 1]) for j in range(ROWS)])
    lower = face_weights(jnp.concatenate([below, c[: ROWS - 1]], axis=0))
    upper = face_weights(c)
    offsets = {}
    for o in range(-3, 4):
        total = jnp.zeros_like(c)
        if o <= 2:
            total = total + low * lower[o + 3]
        if o >= -2:
            total = total - high * upper[o + 2]
        offsets[o] = total
    zero = jnp.zeros_like(c)
    return [by_row([offsets.get(r - j, zero) for j in range(ROWS)]) for r in range(-3, ROWS + 3)]


def weights_kernel(last, scale, c, c_near, edge_far, out):
    lat = lax.axis_index("lat")
    odd = lax.rem(lat, 2)
    for lev in range(LEVELS):
        own = c[lev]
        below = jnp.where(odd == 1, c_near[lev, ROWS - 1 : ROWS, :], edge_far[6 + lev : 7 + lev, :])
        below = jnp.where(lat == 0, -pltpu.roll(own, own.shape[1] // 2, 1)[0:1], below)
        for r, w in enumerate(row_weights(own, below, scale, lat)):
            if r < 3:
                w = jnp.where(lat == 0, 0.0, w)
            if r >= ROWS + 3:
                w = jnp.where(lat == last, 0.0, w)
            out[r, lev] = w


def zonal_kernel(fields, last, scale, x, t, c, n, f, zon, zon_t, w):
    lat = lax.axis_index("lat")
    lons = x.shape[-1]

    def shifted(values, k):
        return values if k == 0 else pltpu.roll(values, (-k) % lons, 1)

    def advance(v, lev):
        flux = w[lev, 1] * v
        for k in (0, 2, 3, 4, 5, 6):
            flux = flux + w[lev, k] * shifted(v, 1 - k)
        return v - (shifted(flux, 1) - flux)

    for lev in range(LEVELS):
        whole = n[lev]
        s = parabola_weights(f[lev])
        zero = jnp.zeros_like(s[0])
        n0, n1 = whole == 0, whole == 1

        def pick(a, b, d):
            return jnp.where(n0, a, jnp.where(n1, b, d))

        w[lev, 0] = pick(s[4], zero, zero)
        w[lev, 1] = pick(s[3], s[4], zero)
        w[lev, 2] = pick(s[2], s[3] + 1.0, s[4] + 1.0)
        w[lev, 3] = pick(s[1], s[2], s[3] + 1.0)
        w[lev, 4] = pick(s[0], s[1], s[2])
        w[lev, 5] = pick(zero, s[0], s[1])
        w[lev, 6] = pick(zero, zero, s[0])

        @pl.loop(0, fields)
        def _(i):
            zon[i, lev] = advance(x[i, lev], lev)

        zon_t[lev] = advance(t[lev], lev)

    def pole(side):
        for lev in range(LEVELS):
            own = c[lev]
            below = -pltpu.roll(own, lons // 2, 1)[0:1]
            weights = row_weights(own, below, scale, lat)
            for d in range(1, 4):
                r = d - 1 if side == 0 else ROWS - d
                at = 3 - d if side == 0 else ROWS + 2 + d
                w[lev, d] = weights[at]
                w[lev, d + 3] = jnp.broadcast_to(t[lev, r : r + 1, :], own.shape)

            for d in range(1, 4):
                zon_t[lev] = zon_t[lev] + w[lev, d] * pltpu.roll(w[lev, d + 3], lons // 2, 1)

            @pl.loop(0, fields)
            def _(i):
                total = zon[i, lev]
                v = pltpu.roll(x[i, lev], lons // 2, 1)
                for d in range(1, 4):
                    r = d - 1 if side == 0 else ROWS - d
                    total = total + w[lev, d] * jnp.broadcast_to(v[r : r + 1], v.shape)
                zon[i, lev] = total

    @pl.when(lat == 0)
    def _():
        pole(0)

    @pl.when(lat == last)
    def _():
        pole(1)


def fin_kernel(fields, with_t, *refs):
    if with_t:
        x, zon, near, far, w, t, zon_t, t_near, edge_far, adv, adv_t = refs
    else:
        x, zon, near, far, w, adv = refs
    chunks = w.shape[-1] // LANE

    def body(odd):
        south_near = odd

        def halo(row, near_row, far_row):
            if 0 <= row < ROWS:
                return None
            d = -row if row < 0 else row - ROWS + 1
            if (row < 0) == south_near:
                return near_row(ROWS - d if south_near else d - 1)
            return far_row(d)

        for lev in range(LEVELS):
            for chunk in range(chunks):
                lane = lanes(chunk)
                weights = [w[r, lev, :, lane] for r in range(ROWS + 6)]

                def total_of(first, own_row, near_row, far_row):
                    total = first
                    for r in range(-3, ROWS + 3):
                        if 0 <= r < ROWS:
                            v = own_row(r)
                        else:
                            v = halo(r, near_row, far_row)
                        total = total + weights[r + 3] * jnp.broadcast_to(v, total.shape)
                    return total

                for f in range(fields):
                    adv[f, lev, :, lane] = total_of(
                        zon[f, lev, :, lane],
                        lambda r: x[f, lev, r : r + 1, lane],
                        lambda r: near[f, lev, r : r + 1, lane],
                        lambda d: far[d - 1, lev, f : f + 1, lane],
                    )
                if with_t:
                    adv_t[lev, :, lane] = total_of(
                        zon_t[lev, :, lane],
                        lambda r: t[lev, r : r + 1, lane],
                        lambda r: t_near[lev, r : r + 1, lane],
                        lambda d: edge_far[2 * (d - 1) + lev : 2 * (d - 1) + lev + 1, lane],
                    )

    both(parity(), body)


def remap_kernel(parts, levels, *refs):
    own, peer = refs[:parts], refs[parts : 2 * parts]
    t_own, t_peer, columns, out, out_t, out_phi, weights, vapour, thick = refs[2 * parts :]
    group = lax.axis_index("lev")
    chunks = out.shape[-1] // LANE
    sources = [(own, t_own, lev, group * LEVELS + lev) for lev in range(LEVELS)]
    sources += [(peer, t_peer, lev, (1 - group) * LEVELS + lev) for lev in range(LEVELS)]

    for k in range(levels):
        upper = columns[k]
        share = columns[levels + k]
        water = None
        heat = None
        for s, (adv, temp, lev, level) in enumerate(sources):
            at = level.astype(jnp.float32)
            w = jnp.where(upper == at, 1.0 - share, jnp.where(upper + 1.0 == at, share, 0.0))
            weights[k, s] = w
            water = w * adv[0][0, lev] if water is None else water + w * adv[0][0, lev]
            heat = w * temp[lev] if heat is None else heat + w * temp[lev]
        thick[k] = heat * (1.0 + 0.608 * water) * columns[2 * levels + k]
        thick[levels + k] = heat
    deeper = columns[3 * levels]
    for k in range(levels - 1, -1, -1):
        layer = thick[k]
        thick[k] = deeper + 0.5 * layer
        deeper = deeper + layer
    for lev in range(LEVELS):
        out_phi[lev] = thick[group * LEVELS + lev]
        out_t[lev] = thick[levels + group * LEVELS + lev]

    for chunk in range(chunks):
        lane = lanes(chunk)
        ws = [
            [weights[group * LEVELS + lev, s, :, lane] for s in range(2 * LEVELS)]
            for lev in range(LEVELS)
        ]
        field = 0
        for part in range(parts):
            for f in range(own[part].shape[0]):
                values = [adv[part][f, lev, :, lane] for adv, _, lev, _ in sources]
                for lev in range(LEVELS):
                    total = ws[lev][0] * values[0]
                    for s in range(1, 2 * LEVELS):
                        total = total + ws[lev][s] * values[s]
                    out[field, lev, :, lane] = total
                field += 1


def call(kernel, outs, scratch=(), specs=None, cost=(0, 0), limit=12):
    single = not isinstance(outs, list)
    shapes = tuple(jax.ShapeDtypeStruct(s, jnp.float32) for s in ([outs] if single else outs))
    return pl.pallas_call(
        kernel,
        out_shape=shapes[0] if single else shapes,
        scratch_shapes=[pltpu.VMEM(s, jnp.float32) for s in scratch],
        compiler_params=pltpu.CompilerParams(vmem_limit_bytes=limit * 2**20),
        cost_estimate=pl.CostEstimate(flops=cost[0], bytes_accessed=cost[1], transcendentals=0),
        **({} if specs is None else {"in_specs": specs}),
    )


def on_device(
    constituent_densities,
    thermal_state,
    integer_boxes_traversed,
    partial_crossing_share,
    northward_crossing_share,
    higher_donor_stratum,
    deeper_donor_share,
    napierian_thickness_quotient,
    ground_gravity_height,
):
    x, t, c = constituent_densities, thermal_state, northward_crossing_share
    fields, _, _, lons = x.shape
    levels = higher_donor_stratum.shape[0]
    bands = lax.axis_size("lat")
    lat_total = bands * ROWS

    pairs = [(i, i ^ 1) for i in range(bands)]
    relays = [(i, i + 2) for i in range(0, bands - 2, 2)] + [(i, i - 2) for i in range(3, bands, 2)]
    cores = [(0, 1), (1, 0)]

    def swap(v):
        return lax.ppermute(v, "lat", pairs)

    def pass_on(v):
        return lax.ppermute(v, "lat", relays)

    def other_core(v):
        return lax.ppermute(v, "lev", cores)

    face = np.arange(lat_total + 1)
    face_sine = np.sin(math.pi * np.minimum(face, lat_total - face) / lat_total)
    row_sine = np.sin(math.pi * (np.arange(lat_total) + 0.5) / lat_total)
    scale = np.stack([face_sine[:-1] / row_sine, face_sine[1:] / row_sine], 1)
    scale = jnp.asarray(scale.reshape(-1).astype(np.float32))

    smem, vmem = pl.BlockSpec(memory_space=pltpu.SMEM), pl.BlockSpec(memory_space=pltpu.VMEM)
    each = fields // SPLIT
    xs = [x[i * each : (i + 1) * each] for i in range(SPLIT)]
    t_near, c_near = swap(t), swap(c)
    near = [swap(v) for v in xs]

    zon, zon_t = call(
        functools.partial(zonal_kernel, fields, bands - 1),
        [x.shape, t.shape],
        [(LEVELS, 7, ROWS, lons)],
        [smem] + [vmem] * 5,
        cost=(4000000000, 3000000),
    )(scale, x, t, c, integer_boxes_traversed, partial_crossing_share)

    edge_far = pass_on(call(edge_kernel, (8, lons))(t_near, c_near))
    far = [
        pass_on(call(functools.partial(pack_kernel, each), (3, LEVELS, each, lons))(v)) for v in near
    ]

    columns = jnp.concatenate(
        [
            higher_donor_stratum.astype(jnp.float32),
            deeper_donor_share,
            napierian_thickness_quotient,
            ground_gravity_height[None],
        ],
        axis=0,
    )
    peer_columns = other_core(columns)
    columns = jnp.where(
        lax.axis_index("lev") == 0,
        jnp.concatenate([columns, peer_columns], -1),
        jnp.concatenate([peer_columns, columns], -1),
    )

    weights = call(
        functools.partial(weights_kernel, bands - 1),
        (ROWS + 6, LEVELS, ROWS, lons),
        (),
        [smem] + [vmem] * 3,
        cost=(400000000, 3000000),
    )(scale, c, c_near, edge_far)

    advected = []
    for i in range(SPLIT):
        args = [xs[i], zon[i * each : (i + 1) * each], near[i], far[i], weights]
        outs = [xs[i].shape]
        if i == 0:
            args += [t, zon_t, t_near, edge_far]
            outs.append(t.shape)
        advected += call(functools.partial(fin_kernel, each, i == 0), outs, cost=(200000000, 1000000))(
            *args
        )
    adv_t = advected.pop(1)
    peer = [other_core(v) for v in advected]
    peer_t = other_core(adv_t)
    return call(
        functools.partial(remap_kernel, SPLIT, levels),
        [x.shape, t.shape, t.shape],
        [(levels, 2 * LEVELS, ROWS, lons), (2 * LEVELS, ROWS, lons), (2 * levels, ROWS, lons)],
        cost=(3000000, 3000000),
    )(*advected, *peer, adv_t, peer_t, columns)


def solution(mesh):
    return jax.shard_map(
        on_device,
        mesh=mesh,
        in_specs=(
            P("ens", "lev", "lat", None),
            P(("ens", "lev"), "lat", None),
            P(("ens", "lev"), "lat", None),
            P(("ens", "lev"), "lat", None),
            P(("ens", "lev"), "lat", None),
            P("ens", "lat", "lev"),
            P("ens", "lat", "lev"),
            P("ens", "lat", "lev"),
            P(("ens", "lat"), "lev"),
        ),
        out_specs=(
            P("ens", "lev", "lat", None),
            P(("ens", "lev"), "lat", None),
            P(("ens", "lev"), "lat", None),
        ),
        check_vma=False,
    )
```

time: 84.8 us -> 38.7 us (0.46)
  the two profiles are of different devices: /device:TPU:9 before, /device:TPU:0 now
where the time goes in v2:
time: 38.7 us; the launch traced here: 38.4 us
  starting transfers between devices  20.3 us (52%)
  Pallas kernels  14 us (36%)
  waiting for transfers between devices  1.65 us (4%)
  local copies, waits for them, and re-layouts  1.26 us (3%)
  between operations  1 us (3%)
    ppermute x5, starting transfers between devices, pass_on(): return lax.ppermute(v, 'lat', relays)  11.7 us
    pallas_call x1, Pallas kernels, on_device(): call(functools.partial(zonal_kernel, fields, bands - 1), [x.shape, t.shap...  10.6 us
    ppermute x6, starting transfers between devices, swap(): return lax.ppermute(v, 'lat', pairs)  7.23 us
    ppermute x6, starting transfers between devices, other_core(): return lax.ppermute(v, 'lev', cores)  1.34 us
    pallas_call x1, Pallas kernels, on_device(): call(functools.partial(remap_kernel, SPLIT, levels), [x.shape, t.shape, t...  1.23 us
    slice x1, local copies, waits for them, and re-layouts, on_device(): xs = [x[i * each:(i + 1) * each] for i in range(SPLIT)]  1.17 us
    pallas_call x4, Pallas kernels, on_device(): call(functools.partial(fin_kernel, each, i == 0), outs, cost=(200000000,...  1 us
    ppermute x5, waiting for transfers between devices, pass_on(): return lax.ppermute(v, 'lat', relays)  0.93 us
  transfers between devices with their start and end apart: 17, of which 2 were waited for; matrix products, arithmetic and copies ran while one was open for 4% of the time, Pallas kernels for 33%

profile of v2, /device:TPU:0, one launch (start us, length us, event | category | flops | bytes accessed | tf_op | source)
XLA Modules:
  0.0 38.4 jit_solution(489250800403479942)
XLA Ops:
  0.6 0.0 copy-start.4
  0.6 0.0 copy-start
  0.7 0.0 copy-start.1
  0.7 0.0 copy-start.2
  0.7 0.0 copy-start.3
  0.7 3.0 %collective-permute-start.2 = (f32[2,4,1152]{2,1,0:T(4,128)}, f32[2,4,1152]{2,1,0:T(4,128)S(1)}, u32[]{:S(2)}, u32[]{:S(2)}) collective-permute-start(f32[2,4,1152]{2,1,0:T(4,128)} %c.3), channel_id=1, source_target_pairs={{0,2},{2,0},{4,6},{6,4},{8,10},{10,8},{12,14},{14,12},{1,3},{3,1},... | collective-permute-start | bytes 110600 | tf_op jit(solution)/shard_map/ppermute | solution.py:329
  3.7 1.2 %fusion.1 = (f32[4,2,4,1152]{3,2,1,0:T(4,128)S(1)}, f32[4,2,4,1152]{3,2,1,0:T(4,128)S(1)}, f32[4,2,4,1152]{3,2,1,0:T(4,128)S(1)}, f32[4,2,4,1152]{3,2,1,0:T(4,128)S(1)}) fusion(f32[16,2,4,1152]{3,2,1,0:T(4,128)} %x.1), kind=kLoop, calls=%fused_computation.3 | loop fusion | bytes 1179648 | tf_op jit(solution)/shard_map/slice | solution.py:345
  4.9 0.2 collective-permute-start
  5.0 0.0 copy-done.1
  5.0 1.9 %collective-permute-start.3 = (f32[2,4,1152]{2,1,0:T(4,128)S(1)}, f32[2,4,1152]{2,1,0:T(4,128)S(1)}, u32[]{:S(2)}, u32[]{:S(2)}) collective-permute-start(f32[2,4,1152]{2,1,0:T(4,128)S(1)} %copy-done.1), channel_id=1, source_target_pairs={{0,2},{2,0},{4,6},{6,4},{8,10},{10,8},{12,14},{14,12},{1,3},{3,1},... | collective-permute-start | bytes 110600 | tf_op jit(solution)/shard_map/ppermute | solution.py:329
  7.0 0.1 collective-permute-start.5
  7.0 0.0 copy-start.5
  7.0 1.9 %collective-permute-start.7 = (f32[4,2,4,1152]{3,2,1,0:T(4,128)S(1)}, f32[4,2,4,1152]{3,2,1,0:T(4,128)S(1)}, u32[]{:S(2)}, u32[]{:S(2)}) collective-permute-start(f32[4,2,4,1152]{3,2,1,0:T(4,128)S(1)} %get-tuple-element.18.refs_0_), channel_id=1, source_target_pairs={{0,2},{2,0},{4,6},{6,4},{8,10},{10,8},{12,14},{14,12},{1,3},{3,1},... | collective-permute-start | bytes 442376 | tf_op jit(solution)/shard_map/ppermute | solution.py:329
  9.0 0.0 collective-permute-done.2.c.c_near
  9.0 0.0 copy-start.8
  9.0 0.1 collective-permute-start.9
  9.1 0.0 copy-done.4
  9.1 0.0 copy-done
  9.1 0.0 copy-done.2
  9.1 0.0 copy-done.3
  9.1 0.0 copy-done.5
  9.1 10.6 %shard_map.121 = (f32[16,2,4,1152]{3,2,1,0:T(4,128)S(1)}, f32[2,4,1152]{2,1,0:T(4,128)S(1)}) custom-call(f32[64]{0:T(128)S(1)} %copy-done.5, f32[16,2,4,1152]{3,2,1,0:T(4,128)S(1)} %copy-done, f32[2,4,1152]{2,1,0:T(4,128)S(1)} %copy-done.1, f32[2,4,1152]{2,1,0:T(4,128)S(1)} %copy-done.4, s32[2,4,1152]{2,1,0:T(4,128)S(1)} %copy-done.2, ...), custom_call_target="tpu_custom_call" | custom-call | flops 4000000000 | bytes 3000000 | tf_op jit(solution)/shard_map/pallas_call | solution.py:349
  19.8 0.0 copy-done.8
  19.8 0.0 copy-start.6
  19.8 0.0 copy-start.7
  19.8 0.0 copy-start.9
  19.8 0.0 collective-permute-done.3.t.refs_7_
  19.9 1.3 %collective-permute-start.4 = (f32[8,1152]{1,0:T(8,128)S(1)}, f32[8,1152]{1,0:T(8,128)S(1)}, u32[]{:S(2)}, u32[]{:S(2)}) collective-permute-start(f32[8,1152]{1,0:T(8,128)S(1)} %shard_map.123), channel_id=1, source_target_pairs={{0,4},{4,8},{8,12},{6,2},{10,6},{14,10},{1,5},{5,9},{9,13},{7,3},{... | collective-permute-start | bytes 110600 | tf_op jit(solution)/shard_map/ppermute | solution.py:332
  21.2 0.0 copy-done.6
  21.2 0.0 copy-done.7
  21.2 0.0 copy-done.9
  21.3 0.0 collective-permute-done.x.refs_2_
  21.3 0.1 collective-permute-start.16
  21.4 0.0 collective-permute-done.5.x.refs_2_
  21.4 3.1 %collective-permute-start.1 = (f32[3,2,4,1152]{3,2,1,0:T(4,128)S(1)}, f32[3,2,4,1152]{3,2,1,0:T(4,128)S(1)}, u32[]{:S(2)}, u32[]{:S(2)}) collective-permute-start(f32[3,2,4,1152]{3,2,1,0:T(4,128)S(1)} %shard_map.122), channel_id=1, source_target_pairs={{0,4},{4,8},{8,12},{6,2},{10,6},{14,10},{1,5},{5,9},{9,13},{7,3},{... | collective-permute-start | bytes 331784 | tf_op jit(solution)/shard_map/ppermute | solution.py:332
  24.6 0.0 collective-permute-done.7.x.refs_2_
  24.6 3.5 %collective-permute-start.6 = (f32[3,2,4,1152]{3,2,1,0:T(4,128)S(1)}, f32[3,2,4,1152]{3,2,1,0:T(4,128)S(1)}, u32[]{:S(2)}, u32[]{:S(2)}) collective-permute-start(f32[3,2,4,1152]{3,2,1,0:T(4,128)S(1)} %shard_map.126), channel_id=1, source_target_pairs={{0,4},{4,8},{8,12},{6,2},{10,6},{14,10},{1,5},{5,9},{9,13},{7,3},{... | collective-permute-start | bytes 331784 | tf_op jit(solution)/shard_map/ppermute | solution.py:332
  28.1 0.0 collective-permute-done.9.x.refs_2_
  28.1 1.9 %collective-permute-start.8 = (f32[3,2,4,1152]{3,2,1,0:T(4,128)S(1)}, f32[3,2,4,1152]{3,2,1,0:T(4,128)S(1)}, u32[]{:S(2)}, u32[]{:S(2)}) collective-permute-start(f32[3,2,4,1152]{3,2,1,0:T(4,128)S(1)} %shard_map.128), channel_id=1, source_target_pairs={{0,4},{4,8},{8,12},{6,2},{10,6},{14,10},{1,5},{5,9},{9,13},{7,3},{... | collective-permute-start | bytes 331784 | tf_op jit(solution)/shard_map/ppermute | solution.py:332
  30.1 0.0 collective-permute-done.4.edge_far.refs_8_
  30.1 1.9 %collective-permute-start.10 = (f32[3,2,4,1152]{3,2,1,0:T(4,128)S(1)}, f32[3,2,4,1152]{3,2,1,0:T(4,128)S(1)}, u32[]{:S(2)}, u32[]{:S(2)}) collective-permute-start(f32[3,2,4,1152]{3,2,1,0:T(4,128)S(1)} %shard_map.130), channel_id=1, source_target_pairs={{0,4},{4,8},{8,12},{6,2},{10,6},{14,10},{1,5},{5,9},{9,13},{7,3},{... | collective-permute-start | bytes 331784 | tf_op jit(solution)/shard_map/ppermute | solution.py:332
  32.1 0.9 %shard_map.124.refs_4_ = f32[10,2,4,1152]{3,2,1,0:T(4,128)S(1)} custom-call(f32[64]{0:T(128)S(1)} %copy-done.5, f32[2,4,1152]{2,1,0:T(4,128)S(1)} %copy-done.4, f32[2,4,1152]{2,1,0:T(4,128)S(1)} %collective-permute-done.2.c.c_near, f32[8,1152]{1,0:T(8,128)S(1)} %collective-permute-done.4.edge_far.refs_8_), custom_call_target="tpu_custom_call" | custom-call | flops 400000000 | bytes 3000000 | tf_op jit(solution)/shard_map/pallas_call | solution.py:378
  33.0 0.0 collective-permute-done.1.refs_3_
  33.0 0.3 shard_map.125
  33.3 0.1 collective-permute-start.11
  33.4 0.0 collective-permute-done.6.refs_3_
  33.4 0.2 shard_map.127.refs_1_
  33.7 0.5 %collective-permute-start.12 = (f32[4,2,4,1152]{3,2,1,0:T(4,128)S(1)}, f32[4,2,4,1152]{3,2,1,0:T(4,128)S(1)}, u32[]{:S(2)}, u32[]{:S(2)}) collective-permute-start(f32[4,2,4,1152]{3,2,1,0:T(4,128)S(1)} %shard_map.127.refs_1_), channel_id=1, source_target_pairs={{0,1},{1,0},{2,3},{3,2},{4,5},{5,4},{6,7},{7,6},{8,9},{9,8},{10,11... | collective-permute-start | bytes 442376 | tf_op jit(solution)/shard_map/ppermute | solution.py:335
  34.2 0.0 collective-permute-done.8.refs_3_
  34.2 0.2 shard_map.129.refs_2_
  34.4 0.1 collective-permute-start.13
  34.5 0.9 %collective-permute-done.10.refs_3_ = f32[3,2,4,1152]{3,2,1,0:T(4,128)S(1)} collective-permute-done((f32[3,2,4,1152]{3,2,1,0:T(4,128)S(1)}, f32[3,2,4,1152]{3,2,1,0:T(4,128)S(1)}, u32[]{:S(2)}, u32[]{:S(2)}) %collective-permute-start.10) | collective-permute-done | bytes 110624 | tf_op jit(solution)/shard_map/ppermute | solution.py:332
  35.5 0.2 shard_map.131.refs_3_
  35.7 0.1 collective-permute-start.14
  35.8 0.0 collective-permute-done.16
  35.8 0.5 %collective-permute-start.15 = (f32[2,4,1152]{2,1,0:T(4,128)S(1)}, f32[2,4,1152]{2,1,0:T(4,128)S(1)}, u32[]{:S(2)}, u32[]{:S(2)}) collective-permute-start(f32[2,4,1152]{2,1,0:T(4,128)S(1)} %get-tuple-element.10.refs_8_), channel_id=1, source_target_pairs={{0,1},{1,0},{2,3},{3,2},{4,5},{5,4},{6,7},{7,6},{8,9},{9,8},{10,11... | collective-permute-start | bytes 110600 | tf_op jit(solution)/shard_map/ppermute | solution.py:335
  36.3 0.2 maximum_select_fusion.refs_10_
  36.5 0.7 %collective-permute-done.15.refs_9_ = f32[2,4,1152]{2,1,0:T(4,128)S(1)} collective-permute-done((f32[2,4,1152]{2,1,0:T(4,128)S(1)}, f32[2,4,1152]{2,1,0:T(4,128)S(1)}, u32[]{:S(2)}, u32[]{:S(2)}) %collective-permute-start.15) | collective-permute-done | bytes 36896 | tf_op jit(solution)/shard_map/ppermute | solution.py:335
  37.2 0.0 collective-permute-done.11.refs_4_
  37.2 0.0 collective-permute-done.12.refs_5_
  37.2 0.0 collective-permute-done.13.refs_6_
  37.2 0.0 collective-permute-done.14.refs_7_
  37.2 1.2 %shard_map.132 = (f32[16,2,4,1152]{3,2,1,0:T(4,128)}, f32[2,4,1152]{2,1,0:T(4,128)}, f32[2,4,1152]{2,1,0:T(4,128)}) custom-call(f32[4,2,4,1152]{3,2,1,0:T(4,128)S(1)} %get-tuple-element.9.refs_0_, f32[4,2,4,1152]{3,2,1,0:T(4,128)S(1)} %shard_map.127.refs_1_, f32[4,2,4,1152]{3,2,1,0:T(4,128)S(1)} %shard_map.129.refs_2_, ...), custom_call_target="tpu_custom_call" | custom-call | flops 3000000 | bytes 3000000 | tf_op jit(solution)/shard_map/pallas_call | solution.py:399
  (8 shorter events, 0.3 us)
Async XLA Ops:
  0.6 8.5 %copy-start.4 = (f32[2,4,1152]{2,1,0:T(4,128)S(1)}, f32[2,4,1152]{2,1,0:T(4,128)}, u32[]{:S(2)}) copy-start(f32[2,4,1152]{2,1,0:T(4,128)} %c.3) | copy-start | bytes 110596
  0.6 8.5 %copy-start = (f32[16,2,4,1152]{3,2,1,0:T(4,128)S(1)}, f32[16,2,4,1152]{3,2,1,0:T(4,128)}, u32[]{:S(2)}) copy-start(f32[16,2,4,1152]{3,2,1,0:T(4,128)} %x.1) | copy-start | bytes 1769476
  0.7 4.4 %copy-start.1 = (f32[2,4,1152]{2,1,0:T(4,128)S(1)}, f32[2,4,1152]{2,1,0:T(4,128)}, u32[]{:S(2)}) copy-start(f32[2,4,1152]{2,1,0:T(4,128)} %refs_5_.1) | copy-start | bytes 110596
  0.7 8.4 %copy-start.2 = (s32[2,4,1152]{2,1,0:T(4,128)S(1)}, s32[2,4,1152]{2,1,0:T(4,128)}, u32[]{:S(2)}) copy-start(s32[2,4,1152]{2,1,0:T(4,128)} %n.1) | copy-start | bytes 110596
  0.7 8.4 %copy-start.3 = (f32[2,4,1152]{2,1,0:T(4,128)S(1)}, f32[2,4,1152]{2,1,0:T(4,128)}, u32[]{:S(2)}) copy-start(f32[2,4,1152]{2,1,0:T(4,128)} %f.1) | copy-start | bytes 110596
  0.7 8.3 %collective-permute-start.2 = (f32[2,4,1152]{2,1,0:T(4,128)}, f32[2,4,1152]{2,1,0:T(4,128)S(1)}, u32[]{:S(2)}, u32[]{:S(2)}) collective-permute-start(f32[2,4,1152]{2,1,0:T(4,128)} %c.3), channel_id=1, source_target_pairs={{0,2},{2,0},{4,6},{6,4},{8,10},{10,8},{12,14},{14,12},{1,3},{3,1},... | collective-permute-start | bytes 110600 | tf_op jit(solution)/shard_map/ppermute | solution.py:329
  4.9 16.4 %collective-permute-start = (f32[4,2,4,1152]{3,2,1,0:T(4,128)S(1)}, f32[4,2,4,1152]{3,2,1,0:T(4,128)S(1)}, u32[]{:S(2)}, u32[]{:S(2)}) collective-permute-start(f32[4,2,4,1152]{3,2,1,0:T(4,128)S(1)} %get-tuple-element.17.refs_0_), channel_id=1, source_target_pairs={{0,2},{2,0},{4,6},{6,4},{8,10},{10,8},{12,14},{14,12},{1,3},{3,1},... | collective-permute-start | bytes 442376 | tf_op jit(solution)/shard_map/ppermute | solution.py:329
  5.0 14.8 %collective-permute-start.3 = (f32[2,4,1152]{2,1,0:T(4,128)S(1)}, f32[2,4,1152]{2,1,0:T(4,128)S(1)}, u32[]{:S(2)}, u32[]{:S(2)}) collective-permute-start(f32[2,4,1152]{2,1,0:T(4,128)S(1)} %copy-done.1), channel_id=1, source_target_pairs={{0,2},{2,0},{4,6},{6,4},{8,10},{10,8},{12,14},{14,12},{1,3},{3,1},... | collective-permute-start | bytes 110600 | tf_op jit(solution)/shard_map/ppermute | solution.py:329
  7.0 14.4 %collective-permute-start.5 = (f32[4,2,4,1152]{3,2,1,0:T(4,128)S(1)}, f32[4,2,4,1152]{3,2,1,0:T(4,128)S(1)}, u32[]{:S(2)}, u32[]{:S(2)}) collective-permute-start(f32[4,2,4,1152]{3,2,1,0:T(4,128)S(1)} %get-tuple-element.16.refs_0_), channel_id=1, source_target_pairs={{0,2},{2,0},{4,6},{6,4},{8,10},{10,8},{12,14},{14,12},{1,3},{3,1},... | collective-permute-start | bytes 442376 | tf_op jit(solution)/shard_map/ppermute | solution.py:329
  7.0 2.1 %copy-start.5 = (f32[64]{0:T(128)S(1)}, f32[64]{0:T(128)}, u32[]{:S(2)}) copy-start(f32[64]{0:T(128)} %constant.8.clone.scale) | copy-start | bytes 772
  7.0 17.5 %collective-permute-start.7 = (f32[4,2,4,1152]{3,2,1,0:T(4,128)S(1)}, f32[4,2,4,1152]{3,2,1,0:T(4,128)S(1)}, u32[]{:S(2)}, u32[]{:S(2)}) collective-permute-start(f32[4,2,4,1152]{3,2,1,0:T(4,128)S(1)} %get-tuple-element.18.refs_0_), channel_id=1, source_target_pairs={{0,2},{2,0},{4,6},{6,4},{8,10},{10,8},{12,14},{14,12},{1,3},{3,1},... | collective-permute-start | bytes 442376 | tf_op jit(solution)/shard_map/ppermute | solution.py:329
  9.0 10.8 %copy-start.8 = (s32[4,4,576]{2,1,0:T(4,128)S(1)}, s32[4,4,576]{2,1,0:T(4,128)}, u32[]{:S(2)}) copy-start(s32[4,4,576]{2,1,0:T(4,128)} %param.15) | copy-start | bytes 110596
  9.0 19.1 %collective-permute-start.9 = (f32[4,2,4,1152]{3,2,1,0:T(4,128)S(1)}, f32[4,2,4,1152]{3,2,1,0:T(4,128)S(1)}, u32[]{:S(2)}, u32[]{:S(2)}) collective-permute-start(f32[4,2,4,1152]{3,2,1,0:T(4,128)S(1)} %get-tuple-element.15.refs_0_), channel_id=1, source_target_pairs={{0,2},{2,0},{4,6},{6,4},{8,10},{10,8},{12,14},{14,12},{1,3},{3,1},... | collective-permute-start | bytes 442376 | tf_op jit(solution)/shard_map/ppermute | solution.py:329
  19.8 1.4 %copy-start.6 = (f32[4,4,576]{2,1,0:T(4,128)S(1)}, f32[4,4,576]{2,1,0:T(4,128)}, u32[]{:S(2)}) copy-start(f32[4,4,576]{2,1,0:T(4,128)} %param.17) | copy-start | bytes 110596
  19.8 1.4 %copy-start.7 = (f32[4,4,576]{2,1,0:T(4,128)S(1)}, f32[4,4,576]{2,1,0:T(4,128)}, u32[]{:S(2)}) copy-start(f32[4,4,576]{2,1,0:T(4,128)} %param.16) | copy-start | bytes 110596
  19.8 1.4 %copy-start.9 = (f32[4,576]{1,0:T(4,128)S(1)}, f32[4,576]{1,0:T(4,128)}, u32[]{:S(2)}) copy-start(f32[4,576]{1,0:T(4,128)} %param.18) | copy-start | bytes 27652
  19.9 10.2 %collective-permute-start.4 = (f32[8,1152]{1,0:T(8,128)S(1)}, f32[8,1152]{1,0:T(8,128)S(1)}, u32[]{:S(2)}, u32[]{:S(2)}) collective-permute-start(f32[8,1152]{1,0:T(8,128)S(1)} %shard_map.123), channel_id=1, source_target_pairs={{0,4},{4,8},{8,12},{6,2},{10,6},{14,10},{1,5},{5,9},{9,13},{7,3},{... | collective-permute-start | bytes 110600 | tf_op jit(solution)/shard_map/ppermute | solution.py:332
  21.3 14.5 %collective-permute-start.16 = (f32[13,4,576]{2,1,0:T(4,128)S(1)}, f32[13,4,576]{2,1,0:T(4,128)S(1)}, u32[]{:S(2)}, u32[]{:S(2)}) collective-permute-start(f32[13,4,576]{2,1,0:T(4,128)S(1)} %pad_maximum_fusion), channel_id=1, source_target_pairs={{0,1},{1,0},{2,3},{3,2},{4,5},{5,4},{6,7},{7,6},{8,9},{9,8},{10,11... | collective-permute-start | bytes 359432 | tf_op jit(solution)/shard_map/ppermute | solution.py:335
  21.4 11.6 %collective-permute-start.1 = (f32[3,2,4,1152]{3,2,1,0:T(4,128)S(1)}, f32[3,2,4,1152]{3,2,1,0:T(4,128)S(1)}, u32[]{:S(2)}, u32[]{:S(2)}) collective-permute-start(f32[3,2,4,1152]{3,2,1,0:T(4,128)S(1)} %shard_map.122), channel_id=1, source_target_pairs={{0,4},{4,8},{8,12},{6,2},{10,6},{14,10},{1,5},{5,9},{9,13},{7,3},{... | collective-permute-start | bytes 331784 | tf_op jit(solution)/shard_map/ppermute | solution.py:332
  24.6 8.8 %collective-permute-start.6 = (f32[3,2,4,1152]{3,2,1,0:T(4,128)S(1)}, f32[3,2,4,1152]{3,2,1,0:T(4,128)S(1)}, u32[]{:S(2)}, u32[]{:S(2)}) collective-permute-start(f32[3,2,4,1152]{3,2,1,0:T(4,128)S(1)} %shard_map.126), channel_id=1, source_target_pairs={{0,4},{4,8},{8,12},{6,2},{10,6},{14,10},{1,5},{5,9},{9,13},{7,3},{... | collective-permute-start | bytes 331784 | tf_op jit(solution)/shard_map/ppermute | solution.py:332
  28.1 6.1 %collective-permute-start.8 = (f32[3,2,4,1152]{3,2,1,0:T(4,128)S(1)}, f32[3,2,4,1152]{3,2,1,0:T(4,128)S(1)}, u32[]{:S(2)}, u32[]{:S(2)}) collective-permute-start(f32[3,2,4,1152]{3,2,1,0:T(4,128)S(1)} %shard_map.128), channel_id=1, source_target_pairs={{0,4},{4,8},{8,12},{6,2},{10,6},{14,10},{1,5},{5,9},{9,13},{7,3},{... | collective-permute-start | bytes 331784 | tf_op jit(solution)/shard_map/ppermute | solution.py:332
  30.1 5.3 %collective-permute-start.10 = (f32[3,2,4,1152]{3,2,1,0:T(4,128)S(1)}, f32[3,2,4,1152]{3,2,1,0:T(4,128)S(1)}, u32[]{:S(2)}, u32[]{:S(2)}) collective-permute-start(f32[3,2,4,1152]{3,2,1,0:T(4,128)S(1)} %shard_map.130), channel_id=1, source_target_pairs={{0,4},{4,8},{8,12},{6,2},{10,6},{14,10},{1,5},{5,9},{9,13},{7,3},{... | collective-permute-start | bytes 331784 | tf_op jit(solution)/shard_map/ppermute | solution.py:332
  33.3 3.9 %collective-permute-start.11 = (f32[4,2,4,1152]{3,2,1,0:T(4,128)S(1)}, f32[4,2,4,1152]{3,2,1,0:T(4,128)S(1)}, u32[]{:S(2)}, u32[]{:S(2)}) collective-permute-start(f32[4,2,4,1152]{3,2,1,0:T(4,128)S(1)} %get-tuple-element.9.refs_0_), channel_id=1, source_target_pairs={{0,1},{1,0},{2,3},{3,2},{4,5},{5,4},{6,7},{7,6},{8,9},{9,8},{10,11... | collective-permute-start | bytes 442376 | tf_op jit(solution)/shard_map/ppermute | solution.py:335
  33.7 3.5 %collective-permute-start.12 = (f32[4,2,4,1152]{3,2,1,0:T(4,128)S(1)}, f32[4,2,4,1152]{3,2,1,0:T(4,128)S(1)}, u32[]{:S(2)}, u32[]{:S(2)}) collective-permute-start(f32[4,2,4,1152]{3,2,1,0:T(4,128)S(1)} %shard_map.127.refs_1_), channel_id=1, source_target_pairs={{0,1},{1,0},{2,3},{3,2},{4,5},{5,4},{6,7},{7,6},{8,9},{9,8},{10,11... | collective-permute-start | bytes 442376 | tf_op jit(solution)/shard_map/ppermute | solution.py:335
  34.4 2.8 %collective-permute-start.13 = (f32[4,2,4,1152]{3,2,1,0:T(4,128)S(1)}, f32[4,2,4,1152]{3,2,1,0:T(4,128)S(1)}, u32[]{:S(2)}, u32[]{:S(2)}) collective-permute-start(f32[4,2,4,1152]{3,2,1,0:T(4,128)S(1)} %shard_map.129.refs_2_), channel_id=1, source_target_pairs={{0,1},{1,0},{2,3},{3,2},{4,5},{5,4},{6,7},{7,6},{8,9},{9,8},{10,11... | collective-permute-start | bytes 442376 | tf_op jit(solution)/shard_map/ppermute | solution.py:335
  35.7 1.5 %collective-permute-start.14 = (f32[4,2,4,1152]{3,2,1,0:T(4,128)S(1)}, f32[4,2,4,1152]{3,2,1,0:T(4,128)S(1)}, u32[]{:S(2)}, u32[]{:S(2)}) collective-permute-start(f32[4,2,4,1152]{3,2,1,0:T(4,128)S(1)} %shard_map.131.refs_3_), channel_id=1, source_target_pairs={{0,1},{1,0},{2,3},{3,2},{4,5},{5,4},{6,7},{7,6},{8,9},{9,8},{10,11... | collective-permute-start | bytes 442376 | tf_op jit(solution)/shard_map/ppermute | solution.py:335
  35.8 1.4 %collective-permute-start.15 = (f32[2,4,1152]{2,1,0:T(4,128)S(1)}, f32[2,4,1152]{2,1,0:T(4,128)S(1)}, u32[]{:S(2)}, u32[]{:S(2)}) collective-permute-start(f32[2,4,1152]{2,1,0:T(4,128)S(1)} %get-tuple-element.10.refs_8_), channel_id=1, source_target_pairs={{0,1},{1,0},{2,3},{3,2},{4,5},{5,4},{6,7},{7,6},{8,9},{9,8},{10,11... | collective-permute-start | bytes 110600 | tf_op jit(solution)/shard_map/ppermute | solution.py:335

commit v3 on v2

v3 whole, which is shorter than its diff:
```python
import functools
import math

import jax
import jax.numpy as jnp
import numpy as np
from jax import lax
from jax.experimental import pallas as pl
from jax.experimental.pallas import tpu as pltpu
from jax.sharding import PartitionSpec as P

ROWS = 4
LEVELS = 2
LANE = 128


def lanes(chunk):
    return pl.ds(chunk * LANE, LANE)


def parity():
    return lax.rem(lax.axis_index("lat"), 2)


def both(odd, body):
    @pl.when(odd == 1)
    def _():
        body(True)

    @pl.when(odd == 0)
    def _():
        body(False)


def copy_kernel(x, out):
    out[...] = x[: out.shape[0]]


def side_rows(to_north):
    return (ROWS - 1, ROWS - 2, ROWS - 3) if to_north else (0, 1, 2)


def gather_rows(rows, x, t, out):
    count = out.shape[1]
    skip = x.shape[0] - count
    for d, row in enumerate(rows):
        for lev in range(LEVELS):
            at = d * LEVELS + lev
            for f in range(count):
                out[at, f : f + 1, :] = x[skip + f, lev, row : row + 1, :]
            out[3 * LEVELS, at : at + 1, :] = t[lev, row : row + 1, :]


def near_kernel(x, t, out):
    both(parity(), lambda odd: gather_rows(side_rows(not odd), x, t, out))


def relay_kernel(swapped, x, t, relay, out):
    def body(odd):
        for d, row in enumerate(side_rows(not odd)):
            for lev in range(LEVELS):
                for f in range(swapped.shape[0]):
                    relay[d * LEVELS + lev, f : f + 1, :] = swapped[f, lev, row : row + 1, :]
        gather_rows(side_rows(odd), x, t, out)

    both(parity(), body)


def parabola_weights(share):
    half = 0.5 * share
    curve = half * (1.0 - share * (2.0 / 3.0))
    right = (1.0 - half - 3.0 * curve) * (1.0 / 12.0)
    left = (half - 3.0 * curve) * (1.0 / 12.0)
    return (
        -share * left,
        share * (7.0 * left - right),
        share * (7.0 * (left + right) + 6.0 * curve),
        share * (7.0 * right - left),
        -share * right,
    )


def face_weights(courant):
    t = parabola_weights(jnp.abs(courant))
    north = courant >= 0.0
    zero = jnp.zeros_like(courant)
    return (
        jnp.where(north, t[0], zero),
        jnp.where(north, t[1], -t[4]),
        jnp.where(north, t[2], -t[3]),
        jnp.where(north, t[3], -t[2]),
        jnp.where(north, t[4], -t[1]),
        jnp.where(north, zero, -t[0]),
    )


def row_weights(c, below, scale, lat):
    row = lax.broadcasted_iota(jnp.int32, c.shape, 0)

    def by_row(parts):
        total = parts[ROWS - 1]
        for j in range(ROWS - 2, -1, -1):
            total = jnp.where(row == j, parts[j], total)
        return total

    low = by_row([jnp.full(c.shape, scale[lat * 2 * ROWS + 2 * j]) for j in range(ROWS)])
    high = by_row([jnp.full(c.shape, scale[lat * 2 * ROWS + 2 * j + 1]) for j in range(ROWS)])
    lower = face_weights(jnp.concatenate([below, c[: ROWS - 1]], axis=0))
    upper = face_weights(c)
    offsets = {}
    for o in range(-3, 4):
        total = jnp.zeros_like(c)
        if o <= 2:
            total = total + low * lower[o + 3]
        if o >= -2:
            total = total - high * upper[o + 2]
        offsets[o] = total
    zero = jnp.zeros_like(c)
    return [by_row([offsets.get(r - j, zero) for j in range(ROWS)]) for r in range(-3, ROWS + 3)]


def weights_kernel(fields, last, scale, c, c_near, c_far, x, t, zon_in, zon_t_in, relay, out, zon, zon_t):
    lat = lax.axis_index("lat")
    odd = lax.rem(lat, 2)
    lons = x.shape[-1]
    for lev in range(LEVELS):
        own = c[lev]
        north_row = slice(ROWS - 1, ROWS)
        below = jnp.where(odd == 1, c_near[lev, north_row, :], c_far[lev, north_row, :])
        below = jnp.where(lat == 0, -pltpu.roll(own, lons // 2, 1)[0:1], below)
        for r, w in enumerate(row_weights(own, below, scale, lat)):
            out[r, lev] = w

    def pole(rows):
        for lev in range(LEVELS):
            for source, at in rows:
                v = pltpu.roll(t[lev], lons // 2, 1)
                v = jnp.broadcast_to(v[source : source + 1], v.shape)
                zon_t[lev] = zon_t[lev] + out[at, lev] * v

            @pl.loop(0, fields)
            def _(i):
                total = zon[i, lev]
                v = pltpu.roll(x[i, lev], lons // 2, 1)
                for source, at in rows:
                    total = total + out[at, lev] * jnp.broadcast_to(v[source : source + 1], v.shape)
                zon[i, lev] = total

            for _, at in rows:
                out[at, lev] = jnp.zeros_like(out[at, lev])

    @pl.when(lat == 0)
    def _():
        pole([(d - 1, 3 - d) for d in range(1, 4)])

    @pl.when(lat == last)
    def _():
        pole([(ROWS - d, ROWS + 2 + d) for d in range(1, 4)])


def zonal_kernel(fields, x, t, n, f, zon, zon_t, w):
    lons = x.shape[-1]

    def shifted(values, k):
        return values if k == 0 else pltpu.roll(values, (-k) % lons, 1)

    def advance(v):
        flux = w[1] * v
        for k in (0, 2, 3, 4, 5, 6):
            flux = flux + w[k] * shifted(v, 1 - k)
        return v - (shifted(flux, 1) - flux)

    def stacked(ref):
        return jnp.concatenate([ref[lev] for lev in range(LEVELS)], axis=0)

    whole = stacked(n)
    s = parabola_weights(stacked(f))
    zero = jnp.zeros_like(s[0])
    n0, n1 = whole == 0, whole == 1

    def pick(a, b, d):
        return jnp.where(n0, a, jnp.where(n1, b, d))

    w[0] = pick(s[4], zero, zero)
    w[1] = pick(s[3], s[4], zero)
    w[2] = pick(s[2], s[3] + 1.0, s[4] + 1.0)
    w[3] = pick(s[1], s[2], s[3] + 1.0)
    w[4] = pick(s[0], s[1], s[2])
    w[5] = pick(zero, s[0], s[1])
    w[6] = pick(zero, zero, s[0])

    total = advance(stacked(t))
    for lev in range(LEVELS):
        zon_t[lev] = total[lev * ROWS : (lev + 1) * ROWS]

    @pl.loop(0, fields, step=2)
    def _(start):
        for i in (start, start + 1):
            total = advance(stacked(x.at[i]))
            for lev in range(LEVELS):
                zon[i, lev] = total[lev * ROWS : (lev + 1) * ROWS]


def fin_kernel(skip, count, direct, *refs):
    if direct:
        x, zon, near, far, w, t, zon_t, adv, adv_t = refs
    else:
        x, zon, near, far, w, adv = refs
    chunks = w.shape[-1] // LANE

    def body(odd):
        for lev in range(LEVELS):
            for chunk in range(chunks):
                lane = lanes(chunk)
                weights = [w[r, lev, :, lane] for r in range(ROWS + 6)]

                def total_of(total, own_row, near_row, far_row):
                    for r in range(-3, ROWS + 3):
                        if 0 <= r < ROWS:
                            v = own_row(r)
                        else:
                            d = -r if r < 0 else r - ROWS + 1
                            v = near_row(d) if (r < 0) == odd else far_row(d)
                        total = total + weights[r + 3] * jnp.broadcast_to(v, total.shape)
                    return total

                def gathered(ref, f):
                    return lambda d: ref[(d - 1) * LEVELS + lev, f : f + 1, lane]

                def swapped(ref, f):
                    def row_at(d):
                        row = side_rows(odd)[d - 1]
                        return ref[f, lev, row : row + 1, lane]

                    return row_at

                def gathered_t(ref):
                    def row_at(d):
                        at = (d - 1) * LEVELS + lev
                        return ref[3 * LEVELS, at : at + 1, lane]

                    return row_at

                for f in range(count):
                    adv[f, lev, :, lane] = total_of(
                        zon[skip + f, lev, :, lane],
                        lambda r: x[skip + f, lev, r : r + 1, lane],
                        gathered(near, f) if direct else swapped(near, f),
                        gathered(far, f),
                    )
                if direct:
                    adv_t[lev, :, lane] = total_of(
                        zon_t[lev, :, lane],
                        lambda r: t[lev, r : r + 1, lane],
                        gathered_t(near),
                        gathered_t(far),
                    )

    both(parity(), body)


def remap_kernel(parts, levels, *refs):
    own, peer = refs[:parts], refs[parts : 2 * parts]
    t_own, t_peer, columns, out, out_t, out_phi, weights, vapour, thick = refs[2 * parts :]
    group = lax.axis_index("lev")
    chunks = out.shape[-1] // LANE
    sources = [(own, t_own, lev, group * LEVELS + lev) for lev in range(LEVELS)]
    sources += [(peer, t_peer, lev, (1 - group) * LEVELS + lev) for lev in range(LEVELS)]

    for k in range(levels):
        upper = columns[k]
        share = columns[levels + k]
        water = None
        heat = None
        for s, (adv, temp, lev, level) in enumerate(sources):
            at = level.astype(jnp.float32)
            w = jnp.where(upper == at, 1.0 - share, jnp.where(upper + 1.0 == at, share, 0.0))
            weights[k, s] = w
            water = w * adv[0][0, lev] if water is None else water + w * adv[0][0, lev]
            heat = w * temp[lev] if heat is None else heat + w * temp[lev]
        thick[k] = heat * (1.0 + 0.608 * water) * columns[2 * levels + k]
        thick[levels + k] = heat
    deeper = columns[3 * levels]
    for k in range(levels - 1, -1, -1):
        layer = thick[k]
        thick[k] = deeper + 0.5 * layer
        deeper = deeper + layer
    for lev in range(LEVELS):
        out_phi[lev] = thick[group * LEVELS + lev]
        out_t[lev] = thick[levels + group * LEVELS + lev]

    for chunk in range(chunks):
        lane = lanes(chunk)
        ws = [
            [weights[group * LEVELS + lev, s, :, lane] for s in range(2 * LEVELS)]
            for lev in range(LEVELS)
        ]
        field = 0
        for part in range(parts):
            for f in range(own[part].shape[0]):
                values = [adv[part][f, lev, :, lane] for adv, _, lev, _ in sources]
                for lev in range(LEVELS):
                    total = ws[lev][0] * values[0]
                    for s in range(1, 2 * LEVELS):
                        total = total + ws[lev][s] * values[s]
                    out[field, lev, :, lane] = total
                field += 1


def call(kernel, outs, scratch=(), specs=None, cost=(0, 0), limit=12, aliases=None):
    single = not isinstance(outs, list)
    shapes = tuple(jax.ShapeDtypeStruct(s, jnp.float32) for s in ([outs] if single else outs))
    return pl.pallas_call(
        kernel,
        out_shape=shapes[0] if single else shapes,
        scratch_shapes=[pltpu.VMEM(s, jnp.float32) for s in scratch],
        compiler_params=pltpu.CompilerParams(vmem_limit_bytes=limit * 2**20),
        cost_estimate=pl.CostEstimate(flops=cost[0], bytes_accessed=cost[1], transcendentals=0),
        input_output_aliases=aliases or {},
        **({} if specs is None else {"in_specs": specs}),
    )


def on_device(
    constituent_densities,
    thermal_state,
    integer_boxes_traversed,
    partial_crossing_share,
    northward_crossing_share,
    higher_donor_stratum,
    deeper_donor_share,
    napierian_thickness_quotient,
    ground_gravity_height,
):
    x, t, c = constituent_densities, thermal_state, northward_crossing_share
    fields, _, _, lons = x.shape
    levels = higher_donor_stratum.shape[0]
    bands = lax.axis_size("lat")
    lat_total = bands * ROWS

    pairs = [(i, i ^ 1) for i in range(bands)]
    across = [(i, i + 1 if i % 2 else i - 1) for i in range(1, bands - 1)]
    relays = [(i, i + 2) for i in range(0, bands - 2, 2)] + [(i, i - 2) for i in range(3, bands, 2)]
    cores = [(0, 1), (1, 0)]

    def swap(v):
        return lax.ppermute(v, "lat", pairs)

    def exchange_across(v):
        return lax.ppermute(v, "lat", across)

    def pass_on(v):
        return lax.ppermute(v, "lat", relays)

    def other_core(v):
        return lax.ppermute(v, "lev", cores)

    face = np.arange(lat_total + 1)
    face_sine = np.sin(math.pi * np.minimum(face, lat_total - face) / lat_total)
    row_sine = np.sin(math.pi * (np.arange(lat_total) + 0.5) / lat_total)
    scale = np.stack([face_sine[:-1] / row_sine, face_sine[1:] / row_sine], 1)
    scale = jnp.asarray(scale.reshape(-1).astype(np.float32))

    smem, vmem = pl.BlockSpec(memory_space=pltpu.SMEM), pl.BlockSpec(memory_space=pltpu.VMEM)
    direct = fields // 2
    swapped = fields - direct
    direct_shape = (3 * LEVELS + 1, direct, lons)

    c_near = swap(c)
    near_a = swap(call(copy_kernel, (swapped,) + x.shape[1:])(x))
    near_b = swap(call(near_kernel, direct_shape)(x, t))
    c_far = exchange_across(c)

    zon, zon_t = call(
        functools.partial(zonal_kernel, fields),
        [x.shape, t.shape],
        [(7, LEVELS * ROWS, lons)],
        cost=(4000000000, 3000000),
    )(x, t, integer_boxes_traversed, partial_crossing_share)

    relay, direct_rows = call(relay_kernel, [(3 * LEVELS, swapped, lons), direct_shape])(near_a, x, t)
    far_a = pass_on(relay)
    far_b = exchange_across(direct_rows)

    columns = jnp.concatenate(
        [
            higher_donor_stratum.astype(jnp.float32),
            deeper_donor_share,
            napierian_thickness_quotient,
            ground_gravity_height[None],
        ],
        axis=0,
    )
    peer_columns = other_core(columns)
    columns = jnp.where(
        lax.axis_index("lev") == 0,
        jnp.concatenate([columns, peer_columns], -1),
        jnp.concatenate([peer_columns, columns], -1),
    )

    weights, zon, zon_t = call(
        functools.partial(weights_kernel, fields, bands - 1),
        [(ROWS + 6, LEVELS, ROWS, lons), x.shape, t.shape],
        (),
        [smem] + [vmem] * 8,
        cost=(2000000000, 3000000),
        aliases={6: 1, 7: 2},
    )(scale, c, c_near, c_far, x, t, zon, zon_t, relay)

    adv_a = call(
        functools.partial(fin_kernel, 0, swapped, False),
        (swapped,) + x.shape[1:],
        cost=(200000000, 1000000),
    )(x, zon, near_a, far_a, weights)
    peer_a = other_core(adv_a)
    adv_b, adv_t = call(
        functools.partial(fin_kernel, swapped, direct, True),
        [(direct,) + x.shape[1:], t.shape],
        cost=(200000000, 1000000),
    )(x, zon, near_b, far_b, weights, t, zon_t)
    peer_b = other_core(adv_b)
    peer_t = other_core(adv_t)
    return call(
        functools.partial(remap_kernel, 2, levels),
        [x.shape, t.shape, t.shape],
        [(levels, 2 * LEVELS, ROWS, lons), (2 * LEVELS, ROWS, lons), (2 * levels, ROWS, lons)],
        cost=(3000000, 3000000),
    )(adv_a, adv_b, peer_a, peer_b, adv_t, peer_t, columns)


def solution(mesh):
    return jax.shard_map(
        on_device,
        mesh=mesh,
        in_specs=(
            P("ens", "lev", "lat", None),
            P(("ens", "lev"), "lat", None),
            P(("ens", "lev"), "lat", None),
            P(("ens", "lev"), "lat", None),
            P(("ens", "lev"), "lat", None),
            P("ens", "lat", "lev"),
            P("ens", "lat", "lev"),
            P("ens", "lat", "lev"),
            P(("ens", "lat"), "lev"),
        ),
        out_specs=(
            P("ens", "lev", "lat", None),
            P(("ens", "lev"), "lat", None),
            P(("ens", "lev"), "lat", None),
        ),
        check_vma=False,
    )
```

time: 38.7 us -> 34.7 us (0.90)
  Pallas kernels: 14 us -> 8.59 us
  waiting for transfers between devices: 1.65 us -> 5.59 us
  starting transfers between devices: 20.3 us -> 17.3 us
  local copies, waits for them, and re-layouts: 1.26 us -> 1.76 us
    pallas_call x12 -> x8, Pallas kernels: 14 us -> 8.59 us  [the longest x1 3.84 us: on_device(): call(functools.partial(weights_kernel, fields, bands - 1), [(ROWS + 6, LE...]
    ppermute x5 -> x1, starting transfers between devices: 11.7 us -> 6.65 us  [pass_on(): return lax.ppermute(v, 'lat', relays)]
    ppermute x6 -> x3, waiting for transfers between devices: 0.02 us -> 4.67 us  [swap(): return lax.ppermute(v, 'lat', pairs)]
    unnamed x20, local copies, waits for them, and re-layouts: 0.05 us -> 1.76 us
    ppermute x0 -> x2, starting transfers between devices: none -> 1.33 us  [exchange_across(): return lax.ppermute(v, 'lat', across)]
    slice x2 -> x0, local copies, waits for them, and re-layouts: 1.22 us -> none  [the longest x1 1.17 us: on_device(): xs = [x[i * each:(i + 1) * each] for i in range(SPLIT)]]
    ppermute x5 -> x1, waiting for transfers between devices: 0.93 us -> 0.01 us  [pass_on(): return lax.ppermute(v, 'lat', relays)]
    ppermute x6 -> x3, starting transfers between devices: 7.23 us -> 8.08 us  [swap(): return lax.ppermute(v, 'lat', pairs)]
  transfers between devices with their start and end apart: 17 -> 10, of which waited for: 2 -> 2; matrix products, arithmetic and copies ran while one was open for 4% -> 1% of each run, Pallas kernels for 33% -> 22%
where the time goes in v3:
time: 34.7 us; the launch traced here: 34.3 us
  starting transfers between devices  17.3 us (50%)
  Pallas kernels  8.59 us (25%)
  waiting for transfers between devices  5.59 us (16%)
  local copies, waits for them, and re-layouts  1.76 us (5%)
  between operations  0.84 us (2%)
    ppermute x3, starting transfers between devices, swap(): return lax.ppermute(v, 'lat', pairs)  8.08 us
    ppermute x1, starting transfers between devices, pass_on(): return lax.ppermute(v, 'lat', relays)  6.65 us
    ppermute x3, waiting for transfers between devices, swap(): return lax.ppermute(v, 'lat', pairs)  4.67 us
    pallas_call x1, Pallas kernels, on_device(): call(functools.partial(weights_kernel, fields, bands - 1), [(ROWS + 6, LE...  3.84 us
    pallas_call x1, Pallas kernels, on_device(): call(functools.partial(zonal_kernel, fields), [x.shape, t.shape], [(7, LE...  2.34 us
    unnamed x20, local copies, waits for them, and re-layouts  1.76 us
    ppermute x2, starting transfers between devices, exchange_across(): return lax.ppermute(v, 'lat', across)  1.33 us
    pallas_call x1, Pallas kernels, on_device(): call(functools.partial(remap_kernel, 2, levels), [x.shape, t.shape, t.sha...  1.22 us
  transfers between devices with their start and end apart: 10, of which 2 were waited for; matrix products, arithmetic and copies ran while one was open for 1% of the time, Pallas kernels for 22%

profile of v3, /device:TPU:0, one launch (start us, length us, event | category | flops | bytes accessed | tf_op | source)
XLA Modules:
  0.0 34.3 jit_solution(15099916142056034922)
XLA Ops:
  0.6 3.0 %collective-permute-start = (f32[2,4,1152]{2,1,0:T(4,128)}, f32[2,4,1152]{2,1,0:T(4,128)S(1)}, u32[]{:S(2)}, u32[]{:S(2)}) collective-permute-start(f32[2,4,1152]{2,1,0:T(4,128)} %c.1), channel_id=1, source_target_pairs={{0,2},{2,0},{4,6},{6,4},{8,10},{10,8},{12,14},{14,12},{1,3},{3,1},... | collective-permute-start | bytes 110600 | tf_op jit(solution)/shard_map/ppermute | solution.py:347
  3.6 0.7 %collective-permute-start.1 = (f32[2,4,1152]{2,1,0:T(4,128)}, f32[2,4,1152]{2,1,0:T(4,128)S(1)}, u32[]{:S(2)}, u32[]{:S(2)}) collective-permute-start(f32[2,4,1152]{2,1,0:T(4,128)} %c.1), channel_id=1, source_target_pairs={{2,4},{4,2},{6,8},{8,6},{10,12},{12,10},{3,5},{5,3},{7,9},{9,7},{1... | collective-permute-start | bytes 110600 | tf_op jit(solution)/shard_map/ppermute | solution.py:350
  4.3 0.0 copy-start
  4.3 1.1 %copy-done = f32[16,2,4,1152]{3,2,1,0:T(4,128)S(1)} copy-done((f32[16,2,4,1152]{3,2,1,0:T(4,128)S(1)}, f32[16,2,4,1152]{3,2,1,0:T(4,128)}, u32[]{:S(2)}) %copy-start) | copy-done | bytes 589848
  5.4 0.0 copy-start.1
  5.4 0.0 copy-start.8
  5.4 4.4 %collective-permute-start.2 = (f32[8,2,4,1152]{3,2,1,0:T(4,128)S(1)}, f32[8,2,4,1152]{3,2,1,0:T(4,128)S(1)}, u32[]{:S(2)}, u32[]{:S(2)}) collective-permute-start(f32[8,2,4,1152]{3,2,1,0:T(4,128)S(1)} %shard_map.122), channel_id=1, source_target_pairs={{0,2},{2,0},{4,6},{6,4},{8,10},{10,8},{12,14},{14,12},{1,3},{3,1},... | collective-permute-start | bytes 884744 | tf_op jit(solution)/shard_map/ppermute | solution.py:347
  9.8 0.0 copy-done.1
  9.8 0.1 shard_map.126
  9.8 0.0 copy-start.2
  9.8 0.0 copy-start.3
  9.9 0.7 %collective-permute-start.4 = (f32[7,8,1152]{2,1,0:T(8,128)S(1)}, f32[7,8,1152]{2,1,0:T(8,128)S(1)}, u32[]{:S(2)}, u32[]{:S(2)}) collective-permute-start(f32[7,8,1152]{2,1,0:T(8,128)S(1)} %shard_map.126), channel_id=1, source_target_pairs={{0,2},{2,0},{4,6},{6,4},{8,10},{10,8},{12,14},{14,12},{1,3},{3,1},... | collective-permute-start | bytes 774152 | tf_op jit(solution)/shard_map/ppermute | solution.py:347
  10.6 0.0 copy-done.8
  10.6 0.0 copy-done.2
  10.6 0.0 copy-done.3
  10.6 2.3 %shard_map.121 = (f32[16,2,4,1152]{3,2,1,0:T(4,128)S(1)}, f32[2,4,1152]{2,1,0:T(4,128)S(1)}) custom-call(f32[16,2,4,1152]{3,2,1,0:T(4,128)S(1)} %copy-done, f32[2,4,1152]{2,1,0:T(4,128)S(1)} %copy-done.1, s32[2,4,1152]{2,1,0:T(4,128)S(1)} %copy-done.2, f32[2,4,1152]{2,1,0:T(4,128)S(1)} %copy-done.3), custom_call_target="tpu_custom_call" | custom-call | flops 4000000000 | bytes 3000000 | tf_op jit(solution)/shard_map/pallas_call | solution.py:374
  13.0 0.0 copy-start.6
  13.0 0.0 copy-start.7
  13.0 4.7 %collective-permute-done.2.swapped.refs_2_ = f32[8,2,4,1152]{3,2,1,0:T(4,128)S(1)} collective-permute-done((f32[8,2,4,1152]{3,2,1,0:T(4,128)S(1)}, f32[8,2,4,1152]{3,2,1,0:T(4,128)S(1)}, u32[]{:S(2)}, u32[]{:S(2)}) %collective-permute-start.2) | collective-permute-done | bytes 294944 | tf_op jit(solution)/shard_map/ppermute | solution.py:347
  17.7 0.0 copy-start.9
  17.7 0.1 shard_map.123
  17.8 0.7 %collective-permute-start.5 = (f32[7,8,1152]{2,1,0:T(8,128)S(1)}, f32[7,8,1152]{2,1,0:T(8,128)S(1)}, u32[]{:S(2)}, u32[]{:S(2)}) collective-permute-start(f32[7,8,1152]{2,1,0:T(8,128)S(1)} %get-tuple-element.17), channel_id=1, source_target_pairs={{2,4},{4,2},{6,8},{8,6},{10,12},{12,10},{3,5},{5,3},{7,9},{9,7},{1... | collective-permute-start | bytes 774152 | tf_op jit(solution)/shard_map/ppermute | solution.py:350
  18.5 6.7 %collective-permute-start.3 = (f32[6,8,1152]{2,1,0:T(8,128)S(1)}, f32[6,8,1152]{2,1,0:T(8,128)S(1)}, u32[]{:S(2)}, u32[]{:S(2)}) collective-permute-start(f32[6,8,1152]{2,1,0:T(8,128)S(1)} %get-tuple-element.14.relay), channel_id=1, source_target_pairs={{0,4},{4,8},{8,12},{6,2},{10,6},{14,10},{1,5},{5,9},{9,13},{7,3},{... | collective-permute-start | bytes 663560 | tf_op jit(solution)/shard_map/ppermute | solution.py:353
  25.2 0.0 copy-done.6
  25.2 0.0 copy-done.7
  25.2 0.0 copy-done.9
  25.2 0.0 copy-start.4
  25.2 0.0 collective-permute-done.c_near
  25.2 0.1 collective-permute-start.9
  25.3 0.0 collective-permute-done.1.c_far
  25.3 0.0 copy-start.5
  25.3 0.6 %copy-done.4 = f32[2,4,1152]{2,1,0:T(4,128)S(1)} copy-done((f32[2,4,1152]{2,1,0:T(4,128)S(1)}, f32[2,4,1152]{2,1,0:T(4,128)}, u32[]{:S(2)}) %copy-start.4) | copy-done | bytes 36888
  26.0 0.0 copy-done.5
  26.0 3.8 %shard_map.124 = (f32[10,2,4,1152]{3,2,1,0:T(4,128)S(1)}, f32[16,2,4,1152]{3,2,1,0:T(4,128)S(1)}, f32[2,4,1152]{2,1,0:T(4,128)S(1)}) custom-call(f32[64]{0:T(128)S(1)} %copy-done.5, f32[2,4,1152]{2,1,0:T(4,128)S(1)} %copy-done.4, f32[2,4,1152]{2,1,0:T(4,128)S(1)} %collective-permute-done.c_near, ...), custom_call_target="tpu_custom_call", output_to_operand_aliasing={{1}: (6, {}), {2}: (7, {})} | custom-call | flops 2000000000 | bytes 3000000 | tf_op jit(solution)/shard_map/pallas_call | solution.py:401
  29.8 0.0 collective-permute-done.3.refs_3_
  29.9 0.5 %shard_map.125.refs_0_ = f32[8,2,4,1152]{3,2,1,0:T(4,128)S(1)} custom-call(f32[16,2,4,1152]{3,2,1,0:T(4,128)S(1)} %copy-done, f32[16,2,4,1152]{3,2,1,0:T(4,128)S(1)} %get-tuple-element.15.refs_1_, f32[8,2,4,1152]{3,2,1,0:T(4,128)S(1)} %collective-permute-done.2.swapped.refs_2_, f32[6,8,1152]{2,1,0:T(8,128)S(1)} %collective-permute-done.3.refs_3_, ...), custom_call_target="tpu_custom_call" | custom-call | flops 200000000 | bytes 1000000 | tf_op jit(solution)/shard_map/pallas_call | solution.py:410
  30.3 0.5 %collective-permute-start.6 = (f32[8,2,4,1152]{3,2,1,0:T(4,128)S(1)}, f32[8,2,4,1152]{3,2,1,0:T(4,128)S(1)}, u32[]{:S(2)}, u32[]{:S(2)}) collective-permute-start(f32[8,2,4,1152]{3,2,1,0:T(4,128)S(1)} %shard_map.125.refs_0_), channel_id=1, source_target_pairs={{0,1},{1,0},{2,3},{3,2},{4,5},{5,4},{6,7},{7,6},{8,9},{9,8},{10,11... | collective-permute-start | bytes 884744 | tf_op jit(solution)/shard_map/ppermute | solution.py:356
  30.9 0.0 collective-permute-done.4.refs_2_
  30.9 0.0 collective-permute-done.5.refs_3_
  30.9 0.5 %shard_map.127 = (f32[8,2,4,1152]{3,2,1,0:T(4,128)S(1)}, f32[2,4,1152]{2,1,0:T(4,128)S(1)}) custom-call(f32[16,2,4,1152]{3,2,1,0:T(4,128)S(1)} %copy-done, f32[16,2,4,1152]{3,2,1,0:T(4,128)S(1)} %get-tuple-element.15.refs_1_, f32[7,8,1152]{2,1,0:T(8,128)S(1)} %collective-permute-done.4.refs_2_, f32[7,8,1152]{2,1,0:T(8,128)S(1)} %collective-permute-done.5.refs_3_, ...), custom_call_target="tpu_custom_call" | custom-call | flops 200000000 | bytes 1000000 | tf_op jit(solution)/shard_map/pallas_call | solution.py:416
  31.4 0.1 collective-permute-start.7
  31.5 0.5 %collective-permute-start.8 = (f32[2,4,1152]{2,1,0:T(4,128)S(1)}, f32[2,4,1152]{2,1,0:T(4,128)S(1)}, u32[]{:S(2)}, u32[]{:S(2)}) collective-permute-start(f32[2,4,1152]{2,1,0:T(4,128)S(1)} %get-tuple-element.20.refs_4_), channel_id=1, source_target_pairs={{0,1},{1,0},{2,3},{3,2},{4,5},{5,4},{6,7},{7,6},{8,9},{9,8},{10,11... | collective-permute-start | bytes 110600 | tf_op jit(solution)/shard_map/ppermute | solution.py:356
  32.0 0.0 collective-permute-done.9
  32.0 0.2 maximum_select_fusion.refs_6_
  32.2 0.9 %collective-permute-done.8.refs_5_ = f32[2,4,1152]{2,1,0:T(4,128)S(1)} collective-permute-done((f32[2,4,1152]{2,1,0:T(4,128)S(1)}, f32[2,4,1152]{2,1,0:T(4,128)S(1)}, u32[]{:S(2)}, u32[]{:S(2)}) %collective-permute-start.8) | collective-permute-done | bytes 36896 | tf_op jit(solution)/shard_map/ppermute | solution.py:356
  33.1 0.0 collective-permute-done.6.refs_2_
  33.1 0.0 collective-permute-done.7.refs_3_
  33.1 1.2 %shard_map.128 = (f32[16,2,4,1152]{3,2,1,0:T(4,128)}, f32[2,4,1152]{2,1,0:T(4,128)}, f32[2,4,1152]{2,1,0:T(4,128)}) custom-call(f32[8,2,4,1152]{3,2,1,0:T(4,128)S(1)} %shard_map.125.refs_0_, f32[8,2,4,1152]{3,2,1,0:T(4,128)S(1)} %get-tuple-element.19.refs_1_, f32[8,2,4,1152]{3,2,1,0:T(4,128)S(1)} %collective-permute-done.6.refs_2_, ...), custom_call_target="tpu_custom_call" | custom-call | flops 3000000 | bytes 3000000 | tf_op jit(solution)/shard_map/pallas_call | solution.py:423
  (3 shorter events, 0.1 us)
Async XLA Ops:
  0.6 24.6 %collective-permute-start = (f32[2,4,1152]{2,1,0:T(4,128)}, f32[2,4,1152]{2,1,0:T(4,128)S(1)}, u32[]{:S(2)}, u32[]{:S(2)}) collective-permute-start(f32[2,4,1152]{2,1,0:T(4,128)} %c.1), channel_id=1, source_target_pairs={{0,2},{2,0},{4,6},{6,4},{8,10},{10,8},{12,14},{14,12},{1,3},{3,1},... | collective-permute-start | bytes 110600 | tf_op jit(solution)/shard_map/ppermute | solution.py:347
  3.6 21.7 %collective-permute-start.1 = (f32[2,4,1152]{2,1,0:T(4,128)}, f32[2,4,1152]{2,1,0:T(4,128)S(1)}, u32[]{:S(2)}, u32[]{:S(2)}) collective-permute-start(f32[2,4,1152]{2,1,0:T(4,128)} %c.1), channel_id=1, source_target_pairs={{2,4},{4,2},{6,8},{8,6},{10,12},{12,10},{3,5},{5,3},{7,9},{9,7},{1... | collective-permute-start | bytes 110600 | tf_op jit(solution)/shard_map/ppermute | solution.py:350
  4.3 1.1 %copy-start = (f32[16,2,4,1152]{3,2,1,0:T(4,128)S(1)}, f32[16,2,4,1152]{3,2,1,0:T(4,128)}, u32[]{:S(2)}) copy-start(f32[16,2,4,1152]{3,2,1,0:T(4,128)} %refs_0_.3) | copy-start | bytes 1769476
  5.4 4.4 %copy-start.1 = (f32[2,4,1152]{2,1,0:T(4,128)S(1)}, f32[2,4,1152]{2,1,0:T(4,128)}, u32[]{:S(2)}) copy-start(f32[2,4,1152]{2,1,0:T(4,128)} %refs_5_.1) | copy-start | bytes 110596
  5.4 5.2 %copy-start.8 = (s32[4,4,576]{2,1,0:T(4,128)S(1)}, s32[4,4,576]{2,1,0:T(4,128)}, u32[]{:S(2)}) copy-start(s32[4,4,576]{2,1,0:T(4,128)} %param.15) | copy-start | bytes 110596
  5.4 12.3 %collective-permute-start.2 = (f32[8,2,4,1152]{3,2,1,0:T(4,128)S(1)}, f32[8,2,4,1152]{3,2,1,0:T(4,128)S(1)}, u32[]{:S(2)}, u32[]{:S(2)}) collective-permute-start(f32[8,2,4,1152]{3,2,1,0:T(4,128)S(1)} %shard_map.122), channel_id=1, source_target_pairs={{0,2},{2,0},{4,6},{6,4},{8,10},{10,8},{12,14},{14,12},{1,3},{3,1},... | collective-permute-start | bytes 884744 | tf_op jit(solution)/shard_map/ppermute | solution.py:347
  9.8 0.8 %copy-start.2 = (s32[2,4,1152]{2,1,0:T(4,128)S(1)}, s32[2,4,1152]{2,1,0:T(4,128)}, u32[]{:S(2)}) copy-start(s32[2,4,1152]{2,1,0:T(4,128)} %n.1) | copy-start | bytes 110596
  9.8 0.8 %copy-start.3 = (f32[2,4,1152]{2,1,0:T(4,128)S(1)}, f32[2,4,1152]{2,1,0:T(4,128)}, u32[]{:S(2)}) copy-start(f32[2,4,1152]{2,1,0:T(4,128)} %f.1) | copy-start | bytes 110596
  9.9 21.0 %collective-permute-start.4 = (f32[7,8,1152]{2,1,0:T(8,128)S(1)}, f32[7,8,1152]{2,1,0:T(8,128)S(1)}, u32[]{:S(2)}, u32[]{:S(2)}) collective-permute-start(f32[7,8,1152]{2,1,0:T(8,128)S(1)} %shard_map.126), channel_id=1, source_target_pairs={{0,2},{2,0},{4,6},{6,4},{8,10},{10,8},{12,14},{14,12},{1,3},{3,1},... | collective-permute-start | bytes 774152 | tf_op jit(solution)/shard_map/ppermute | solution.py:347
  13.0 12.2 %copy-start.6 = (f32[4,4,576]{2,1,0:T(4,128)S(1)}, f32[4,4,576]{2,1,0:T(4,128)}, u32[]{:S(2)}) copy-start(f32[4,4,576]{2,1,0:T(4,128)} %param.17) | copy-start | bytes 110596
  13.0 12.2 %copy-start.7 = (f32[4,4,576]{2,1,0:T(4,128)S(1)}, f32[4,4,576]{2,1,0:T(4,128)}, u32[]{:S(2)}) copy-start(f32[4,4,576]{2,1,0:T(4,128)} %param.16) | copy-start | bytes 110596
  17.7 7.5 %copy-start.9 = (f32[4,576]{1,0:T(4,128)S(1)}, f32[4,576]{1,0:T(4,128)}, u32[]{:S(2)}) copy-start(f32[4,576]{1,0:T(4,128)} %param.18) | copy-start | bytes 27652
  17.8 13.1 %collective-permute-start.5 = (f32[7,8,1152]{2,1,0:T(8,128)S(1)}, f32[7,8,1152]{2,1,0:T(8,128)S(1)}, u32[]{:S(2)}, u32[]{:S(2)}) collective-permute-start(f32[7,8,1152]{2,1,0:T(8,128)S(1)} %get-tuple-element.17), channel_id=1, source_target_pairs={{2,4},{4,2},{6,8},{8,6},{10,12},{12,10},{3,5},{5,3},{7,9},{9,7},{1... | collective-permute-start | bytes 774152 | tf_op jit(solution)/shard_map/ppermute | solution.py:350
  18.5 11.4 %collective-permute-start.3 = (f32[6,8,1152]{2,1,0:T(8,128)S(1)}, f32[6,8,1152]{2,1,0:T(8,128)S(1)}, u32[]{:S(2)}, u32[]{:S(2)}) collective-permute-start(f32[6,8,1152]{2,1,0:T(8,128)S(1)} %get-tuple-element.14.relay), channel_id=1, source_target_pairs={{0,4},{4,8},{8,12},{6,2},{10,6},{14,10},{1,5},{5,9},{9,13},{7,3},{... | collective-permute-start | bytes 663560 | tf_op jit(solution)/shard_map/ppermute | solution.py:353
  25.2 0.8 %copy-start.4 = (f32[2,4,1152]{2,1,0:T(4,128)S(1)}, f32[2,4,1152]{2,1,0:T(4,128)}, u32[]{:S(2)}) copy-start(f32[2,4,1152]{2,1,0:T(4,128)} %c.1) | copy-start | bytes 110596
  25.2 6.7 %collective-permute-start.9 = (f32[13,4,576]{2,1,0:T(4,128)S(1)}, f32[13,4,576]{2,1,0:T(4,128)S(1)}, u32[]{:S(2)}, u32[]{:S(2)}) collective-permute-start(f32[13,4,576]{2,1,0:T(4,128)S(1)} %pad_maximum_fusion), channel_id=1, source_target_pairs={{0,1},{1,0},{2,3},{3,2},{4,5},{5,4},{6,7},{7,6},{8,9},{9,8},{10,11... | collective-permute-start | bytes 359432 | tf_op jit(solution)/shard_map/ppermute | solution.py:356
  25.3 0.7 %copy-start.5 = (f32[64]{0:T(128)S(1)}, f32[64]{0:T(128)}, u32[]{:S(2)}) copy-start(f32[64]{0:T(128)} %constant.8.clone.scale) | copy-start | bytes 772
  30.3 2.8 %collective-permute-start.6 = (f32[8,2,4,1152]{3,2,1,0:T(4,128)S(1)}, f32[8,2,4,1152]{3,2,1,0:T(4,128)S(1)}, u32[]{:S(2)}, u32[]{:S(2)}) collective-permute-start(f32[8,2,4,1152]{3,2,1,0:T(4,128)S(1)} %shard_map.125.refs_0_), channel_id=1, source_target_pairs={{0,1},{1,0},{2,3},{3,2},{4,5},{5,4},{6,7},{7,6},{8,9},{9,8},{10,11... | collective-permute-start | bytes 884744 | tf_op jit(solution)/shard_map/ppermute | solution.py:356
  31.4 1.7 %collective-permute-start.7 = (f32[8,2,4,1152]{3,2,1,0:T(4,128)S(1)}, f32[8,2,4,1152]{3,2,1,0:T(4,128)S(1)}, u32[]{:S(2)}, u32[]{:S(2)}) collective-permute-start(f32[8,2,4,1152]{3,2,1,0:T(4,128)S(1)} %get-tuple-element.19.refs_1_), channel_id=1, source_target_pairs={{0,1},{1,0},{2,3},{3,2},{4,5},{5,4},{6,7},{7,6},{8,9},{9,8},{10,11... | collective-permute-start | bytes 884744 | tf_op jit(solution)/shard_map/ppermute | solution.py:356
  31.5 1.6 %collective-permute-start.8 = (f32[2,4,1152]{2,1,0:T(4,128)S(1)}, f32[2,4,1152]{2,1,0:T(4,128)S(1)}, u32[]{:S(2)}, u32[]{:S(2)}) collective-permute-start(f32[2,4,1152]{2,1,0:T(4,128)S(1)} %get-tuple-element.20.refs_4_), channel_id=1, source_target_pairs={{0,1},{1,0},{2,3},{3,2},{4,5},{5,4},{6,7},{7,6},{8,9},{9,8},{10,11... | collective-permute-start | bytes 110600 | tf_op jit(solution)/shard_map/ppermute | solution.py:356

commit v4 on v3

--- a/solution.py
+++ b/solution.py
@@ -51,17 +51,12 @@
             out[3 * LEVELS, at : at + 1, :] = t[lev, row : row + 1, :]
 
 
-def near_kernel(x, t, out):
-    both(parity(), lambda odd: gather_rows(side_rows(not odd), x, t, out))
-
-
-def relay_kernel(swapped, x, t, relay, out):
+def relay_kernel(swapped, relay):
     def body(odd):
         for d, row in enumerate(side_rows(not odd)):
             for lev in range(LEVELS):
                 for f in range(swapped.shape[0]):
                     relay[d * LEVELS + lev, f : f + 1, :] = swapped[f, lev, row : row + 1, :]
-        gather_rows(side_rows(odd), x, t, out)
 
     both(parity(), body)
 
@@ -119,35 +114,49 @@
     return [by_row([offsets.get(r - j, zero) for j in range(ROWS)]) for r in range(-3, ROWS + 3)]
 
 
-def weights_kernel(fields, last, scale, c, c_near, c_far, x, t, zon_in, zon_t_in, relay, out, zon, zon_t):
+def stacked(ref):
+    return jnp.concatenate([ref[lev] for lev in range(LEVELS)], axis=0)
+
+
+def weights_kernel(
+    fields, last, scale, c, c_south, x, t, zon_in, zon_t_in, relay, out, zon, zon_t, direct, ws
+):
     lat = lax.axis_index("lat")
     odd = lax.rem(lat, 2)
     lons = x.shape[-1]
+    both(odd, lambda is_odd: gather_rows(side_rows(is_odd), x, t, direct))
     for lev in range(LEVELS):
         own = c[lev]
-        north_row = slice(ROWS - 1, ROWS)
-        below = jnp.where(odd == 1, c_near[lev, north_row, :], c_far[lev, north_row, :])
+        below = c_south[lev, ROWS - 1 : ROWS, :]
         below = jnp.where(lat == 0, -pltpu.roll(own, lons // 2, 1)[0:1], below)
         for r, w in enumerate(row_weights(own, below, scale, lat)):
             out[r, lev] = w
 
     def pole(rows):
-        for lev in range(LEVELS):
-            for source, at in rows:
-                v = pltpu.roll(t[lev], lons // 2, 1)
-                v = jnp.broadcast_to(v[source : source + 1], v.shape)
-                zon_t[lev] = zon_t[lev] + out[at, lev] * v
-
-            @pl.loop(0, fields)
-            def _(i):
-                total = zon[i, lev]
-                v = pltpu.roll(x[i, lev], lons // 2, 1)
-                for source, at in rows:
-                    total = total + out[at, lev] * jnp.broadcast_to(v[source : source + 1], v.shape)
-                zon[i, lev] = total
-
-            for _, at in rows:
+        for k, (_, at) in enumerate(rows):
+            ws[k] = stacked(out.at[at])
+            for lev in range(LEVELS):
                 out[at, lev] = jnp.zeros_like(out[at, lev])
+
+        def beyond(ref):
+            v = pltpu.roll(stacked(ref), lons // 2, 1)
+            total = jnp.zeros_like(v)
+            for k, (source, _) in enumerate(rows):
+                both_rows = [
+                    jnp.broadcast_to(v[r : r + 1], (ROWS, lons))
+                    for r in range(source, LEVELS * ROWS, ROWS)
+                ]
+                total = total + ws[k] * jnp.concatenate(both_rows, axis=0)
+            return [total[lev * ROWS : (lev + 1) * ROWS] for lev in range(LEVELS)]
+
+        for lev, part in enumerate(beyond(t)):
+            zon_t[lev] = zon_t[lev] + part
+
+        @pl.loop(0, fields, step=2)
+        def _(start):
+            for i in (start, start + 1):
+                for lev, part in enumerate(beyond(x.at[i])):
+                    zon[i, lev] = zon[i, lev] + part
 
     @pl.when(lat == 0)
     def _():
@@ -158,8 +167,10 @@
         pole([(ROWS - d, ROWS + 2 + d) for d in range(1, 4)])
 
 
-def zonal_kernel(fields, x, t, n, f, zon, zon_t, w):
+def zonal_kernel(fields, x, t, n, f, c, zon, zon_t, near, c_copy, w):
     lons = x.shape[-1]
+    c_copy[...] = c[...]
+    both(parity(), lambda odd: gather_rows(side_rows(not odd), x, t, near))
 
     def shifted(values, k):
         return values if k == 0 else pltpu.roll(values, (-k) % lons, 1)
@@ -169,9 +180,6 @@
         for k in (0, 2, 3, 4, 5, 6):
             flux = flux + w[k] * shifted(v, 1 - k)
         return v - (shifted(flux, 1) - flux)
-
-    def stacked(ref):
-        return jnp.concatenate([ref[lev] for lev in range(LEVELS)], axis=0)
 
     whole = stacked(n)
     s = parabola_weights(stacked(f))
@@ -203,9 +211,9 @@
 
 def fin_kernel(skip, count, direct, *refs):
     if direct:
-        x, zon, near, far, w, t, zon_t, adv, adv_t = refs
+        x, zon, near, far, w, t, zon_t, adv = refs
     else:
-        x, zon, near, far, w, adv = refs
+        x, zon, near, far, w, _, adv = refs
     chunks = w.shape[-1] // LANE
 
     def body(odd):
@@ -249,7 +257,7 @@
                         gathered(far, f),
                     )
                 if direct:
-                    adv_t[lev, :, lane] = total_of(
+                    adv[count, lev, :, lane] = total_of(
                         zon_t[lev, :, lane],
                         lambda r: t[lev, r : r + 1, lane],
                         gathered_t(near),
@@ -259,25 +267,69 @@
     both(parity(), body)
 
 
-def remap_kernel(parts, levels, *refs):
-    own, peer = refs[:parts], refs[parts : 2 * parts]
-    t_own, t_peer, columns, out, out_t, out_phi, weights, vapour, thick = refs[2 * parts :]
+def mix_kernel(levels, columns, weights):
     group = lax.axis_index("lev")
-    chunks = out.shape[-1] // LANE
-    sources = [(own, t_own, lev, group * LEVELS + lev) for lev in range(LEVELS)]
-    sources += [(peer, t_peer, lev, (1 - group) * LEVELS + lev) for lev in range(LEVELS)]
-
     for k in range(levels):
         upper = columns[k]
         share = columns[levels + k]
-        water = None
-        heat = None
-        for s, (adv, temp, lev, level) in enumerate(sources):
+        for s in range(2 * LEVELS):
+            level = (group if s < LEVELS else 1 - group) * LEVELS + s % LEVELS
             at = level.astype(jnp.float32)
-            w = jnp.where(upper == at, 1.0 - share, jnp.where(upper + 1.0 == at, share, 0.0))
-            weights[k, s] = w
-            water = w * adv[0][0, lev] if water is None else water + w * adv[0][0, lev]
-            heat = w * temp[lev] if heat is None else heat + w * temp[lev]
+            weights[k, s] = jnp.where(
+                upper == at, 1.0 - share, jnp.where(upper + 1.0 == at, share, 0.0)
+            )
+
+
+def mixed(weights, values):
+    total = weights[0] * values[0]
+    for w, v in zip(weights[1:], values[1:]):
+        total = total + w * v
+    return total
+
+
+def remap_fields(skip, count, own, peer, weights, out, buffer, sems):
+    group = lax.axis_index("lev")
+    chunks = out.shape[-1] // LANE
+    copies = []
+    step = 4
+    for first in range(0, count, step):
+        for chunk in range(chunks):
+            lane = lanes(chunk)
+            ws = [
+                [weights[group * LEVELS + lev, s, :, lane] for s in range(2 * LEVELS)]
+                for lev in range(LEVELS)
+            ]
+            for f in range(first, first + step):
+                values = [adv[f, lev, :, lane] for adv in (own, peer) for lev in range(LEVELS)]
+                for lev in range(LEVELS):
+                    buffer[f, lev, :, lane] = mixed(ws[lev], values)
+        copy = pltpu.make_async_copy(
+            buffer.at[pl.ds(first, step)],
+            out.at[pl.ds(skip + first, step)],
+            sems.at[first // step],
+        )
+        copy.start()
+        copies.append(copy)
+    return copies
+
+
+def remap_first_kernel(count, own, peer, weights, out, buffer, sems):
+    for copy in remap_fields(0, count, own, peer, weights, out, buffer, sems):
+        copy.wait()
+
+
+def remap_last_kernel(
+    skip, count, levels, own, peer, first_own, first_peer, weights, columns, out_in,
+    out, out_t, out_phi, buffer, thick, sems,
+):
+    group = lax.axis_index("lev")
+    copies = remap_fields(skip, count, own, peer, weights, out, buffer, sems)
+    vapour = [adv[0, lev] for adv in (first_own, first_peer) for lev in range(LEVELS)]
+    temp = [adv[count, lev] for adv in (own, peer) for lev in range(LEVELS)]
+    for k in range(levels):
+        ws = [weights[k, s] for s in range(2 * LEVELS)]
+        water = mixed(ws, vapour)
+        heat = mixed(ws, temp)
         thick[k] = heat * (1.0 + 0.608 * water) * columns[2 * levels + k]
         thick[levels + k] = heat
     deeper = columns[3 * levels]
@@ -288,36 +340,24 @@
     for lev in range(LEVELS):
         out_phi[lev] = thick[group * LEVELS + lev]
         out_t[lev] = thick[levels + group * LEVELS + lev]
-
-    for chunk in range(chunks):
-        lane = lanes(chunk)
-        ws = [
-            [weights[group * LEVELS + lev, s, :, lane] for s in range(2 * LEVELS)]
-            for lev in range(LEVELS)
-        ]
-        field = 0
-        for part in range(parts):
-            for f in range(own[part].shape[0]):
-                values = [adv[part][f, lev, :, lane] for adv, _, lev, _ in sources]
-                for lev in range(LEVELS):
-                    total = ws[lev][0] * values[0]
-                    for s in range(1, 2 * LEVELS):
-                        total = total + ws[lev][s] * values[s]
-                    out[field, lev, :, lane] = total
-                field += 1
-
-
-def call(kernel, outs, scratch=(), specs=None, cost=(0, 0), limit=12, aliases=None):
+    for copy in copies:
+        copy.wait()
+
+
+def call(kernel, outs, scratch=(), specs=None, cost=(0, 0), limit=12, aliases=None, out_specs=None):
     single = not isinstance(outs, list)
     shapes = tuple(jax.ShapeDtypeStruct(s, jnp.float32) for s in ([outs] if single else outs))
+    extra = {} if specs is None else {"in_specs": specs}
+    if out_specs is not None:
+        extra["out_specs"] = out_specs
     return pl.pallas_call(
         kernel,
         out_shape=shapes[0] if single else shapes,
-        scratch_shapes=[pltpu.VMEM(s, jnp.float32) for s in scratch],
+        scratch_shapes=[pltpu.VMEM(s, jnp.float32) if isinstance(s, tuple) else s for s in scratch],
         compiler_params=pltpu.CompilerParams(vmem_limit_bytes=limit * 2**20),
         cost_estimate=pl.CostEstimate(flops=cost[0], bytes_accessed=cost[1], transcendentals=0),
         input_output_aliases=aliases or {},
-        **({} if specs is None else {"in_specs": specs}),
+        **extra,
     )
 
 
@@ -340,6 +380,7 @@
 
     pairs = [(i, i ^ 1) for i in range(bands)]
     across = [(i, i + 1 if i % 2 else i - 1) for i in range(1, bands - 1)]
+    north = [(i, i + 1) for i in range(bands - 1)]
     relays = [(i, i + 2) for i in range(0, bands - 2, 2)] + [(i, i - 2) for i in range(3, bands, 2)]
     cores = [(0, 1), (1, 0)]
 
@@ -366,21 +407,18 @@
     swapped = fields - direct
     direct_shape = (3 * LEVELS + 1, direct, lons)
 
-    c_near = swap(c)
     near_a = swap(call(copy_kernel, (swapped,) + x.shape[1:])(x))
-    near_b = swap(call(near_kernel, direct_shape)(x, t))
-    c_far = exchange_across(c)
-
-    zon, zon_t = call(
+    zon, zon_t, near_rows, c_copy = call(
         functools.partial(zonal_kernel, fields),
-        [x.shape, t.shape],
+        [x.shape, t.shape, direct_shape, c.shape],
         [(7, LEVELS * ROWS, lons)],
         cost=(4000000000, 3000000),
-    )(x, t, integer_boxes_traversed, partial_crossing_share)
-
-    relay, direct_rows = call(relay_kernel, [(3 * LEVELS, swapped, lons), direct_shape])(near_a, x, t)
+    )(x, t, integer_boxes_traversed, partial_crossing_share, c)
+    c_south = lax.ppermute(c_copy, "lat", north)
+    near_b = swap(near_rows)
+
+    relay = call(relay_kernel, (3 * LEVELS, swapped, lons))(near_a)
     far_a = pass_on(relay)
-    far_b = exchange_across(direct_rows)
 
     columns = jnp.concatenate(
         [
@@ -398,34 +436,53 @@
         jnp.concatenate([peer_columns, columns], -1),
     )
 
-    weights, zon, zon_t = call(
+    weights, zon, zon_t, far_rows = call(
         functools.partial(weights_kernel, fields, bands - 1),
-        [(ROWS + 6, LEVELS, ROWS, lons), x.shape, t.shape],
-        (),
-        [smem] + [vmem] * 8,
+        [(ROWS + 6, LEVELS, ROWS, lons), x.shape, t.shape, direct_shape],
+        [(3, LEVELS * ROWS, lons)],
+        [smem] + [vmem] * 7,
         cost=(2000000000, 3000000),
-        aliases={6: 1, 7: 2},
-    )(scale, c, c_near, c_far, x, t, zon, zon_t, relay)
+        aliases={5: 1, 6: 2},
+    )(scale, c, c_south, x, t, zon, zon_t, relay)
+    far_b = exchange_across(far_rows)
+    mix = call(
+        functools.partial(mix_kernel, levels), (levels, 2 * LEVELS, ROWS, lons), cost=(400000000, 1000000)
+    )(columns)
 
     adv_a = call(
         functools.partial(fin_kernel, 0, swapped, False),
         (swapped,) + x.shape[1:],
         cost=(200000000, 1000000),
-    )(x, zon, near_a, far_a, weights)
+    )(x, zon, near_a, far_a, weights, mix)
     peer_a = other_core(adv_a)
-    adv_b, adv_t = call(
+    adv_b = call(
         functools.partial(fin_kernel, swapped, direct, True),
-        [(direct,) + x.shape[1:], t.shape],
+        (direct + 1,) + x.shape[1:],
         cost=(200000000, 1000000),
     )(x, zon, near_b, far_b, weights, t, zon_t)
     peer_b = other_core(adv_b)
-    peer_t = other_core(adv_t)
+
+    anywhere = pl.BlockSpec(memory_space=pl.ANY)
+    out = call(
+        functools.partial(remap_first_kernel, swapped),
+        x.shape,
+        [(swapped,) + x.shape[1:], pltpu.SemaphoreType.DMA((swapped // 4,))],
+        cost=(200000000, 1000000),
+        out_specs=anywhere,
+    )(adv_a, peer_a, mix)
     return call(
-        functools.partial(remap_kernel, 2, levels),
+        functools.partial(remap_last_kernel, swapped, direct, levels),
         [x.shape, t.shape, t.shape],
-        [(levels, 2 * LEVELS, ROWS, lons), (2 * LEVELS, ROWS, lons), (2 * levels, ROWS, lons)],
-        cost=(3000000, 3000000),
-    )(adv_a, adv_b, peer_a, peer_b, adv_t, peer_t, columns)
+        [
+            (direct,) + x.shape[1:],
+            (2 * levels, ROWS, lons),
+            pltpu.SemaphoreType.DMA((direct // 4,)),
+        ],
+        [vmem] * 6 + [anywhere],
+        cost=(200000000, 1000000),
+        aliases={6: 0},
+        out_specs=(anywhere, vmem, vmem),
+    )(adv_b, peer_b, adv_a, peer_a, mix, columns, out)
 
 
 def solution(mesh):

time: 34.7 us -> 33.3 us (0.960)
  the two profiles are of different devices: /device:TPU:0 before, /device:TPU:9 now
where the time goes in v4:
time: 33.3 us; the launch traced here: 33 us
  starting transfers between devices  13.9 us (42%)
  waiting for transfers between devices  9.59 us (29%)
  Pallas kernels  6.64 us (20%)
  local copies, waits for them, and re-layouts  1.75 us (5%)
  between operations  0.86 us (3%)
    ppermute x1, waiting for transfers between devices, exchange_across(): return lax.ppermute(v, 'lat', across)  8.03 us
    ppermute x1, starting transfers between devices, pass_on(): return lax.ppermute(v, 'lat', relays)  3.2 us
    ppermute x2, starting transfers between devices, swap(): return lax.ppermute(v, 'lat', pairs)  3.17 us
    ppermute x3, starting transfers between devices, other_core(): return lax.ppermute(v, 'lev', cores)  2.9 us
    ppermute x1, starting transfers between devices, on_device(): c_south = lax.ppermute(c_copy, 'lat', north)  2.69 us
    pallas_call x1, Pallas kernels, on_device(): call(functools.partial(zonal_kernel, fields), [x.shape, t.shape, direct_s...  2.44 us
    ppermute x1, starting transfers between devices, exchange_across(): return lax.ppermute(v, 'lat', across)  1.92 us
    unnamed x22, local copies, waits for them, and re-layouts  1.75 us
  transfers between devices with their start and end apart: 8, of which 2 were waited for; matrix products, arithmetic and copies ran while one was open for 1% of the time, Pallas kernels for 16%

profile of v4, /device:TPU:9, one launch (start us, length us, event | category | flops | bytes accessed | tf_op | source)
XLA Modules:
  0.0 33.0 jit_solution(11798595590998924316)
XLA Ops:
  0.6 0.0 copy-start
  0.6 1.1 %copy-done = f32[16,2,4,1152]{3,2,1,0:T(4,128)S(1)} copy-done((f32[16,2,4,1152]{3,2,1,0:T(4,128)S(1)}, f32[16,2,4,1152]{3,2,1,0:T(4,128)}, u32[]{:S(2)}) %copy-start) | copy-done | bytes 589848
  1.7 0.0 copy-start.2
  1.7 0.0 copy-start.3
  1.7 0.0 copy-start.4
  1.7 0.0 copy-start.5
  1.7 0.0 copy-start.9
  1.8 1.3 %collective-permute-start.1 = (f32[8,2,4,1152]{3,2,1,0:T(4,128)S(1)}, f32[8,2,4,1152]{3,2,1,0:T(4,128)S(1)}, u32[]{:S(2)}, u32[]{:S(2)}) collective-permute-start(f32[8,2,4,1152]{3,2,1,0:T(4,128)S(1)} %shard_map.122), channel_id=1, source_target_pairs={{0,2},{2,0},{4,6},{6,4},{8,10},{10,8},{12,14},{14,12},{1,3},{3,1},... | collective-permute-start | bytes 884744 | tf_op jit(solution)/shard_map/ppermute | solution.py:388
  3.0 0.0 copy-done.2
  3.0 0.0 copy-done.3
  3.0 0.0 copy-done.4
  3.0 0.0 copy-done.5
  3.0 0.0 copy-start.7
  3.1 0.0 copy-start.8
  3.1 0.0 copy-start.10
  3.1 2.4 %shard_map.121 = (f32[16,2,4,1152]{3,2,1,0:T(4,128)S(1)}, f32[2,4,1152]{2,1,0:T(4,128)S(1)}, f32[7,8,1152]{2,1,0:T(8,128)S(1)}, f32[2,4,1152]{2,1,0:T(4,128)S(1)}) custom-call(f32[16,2,4,1152]{3,2,1,0:T(4,128)S(1)} %copy-done, f32[2,4,1152]{2,1,0:T(4,128)S(1)} %copy-done.2, s32[2,4,1152]{2,1,0:T(4,128)S(1)} %copy-done.3, f32[2,4,1152]{2,1,0:T(4,128)S(1)} %copy-done.4, ...), custom_call_target="tpu_custom_call" | custom-call | flops 4000000000 | bytes 3000000 | tf_op jit(solution)/shard_map/pallas_call | solution.py:411
  5.5 0.0 copy-start.1
  5.5 2.7 %collective-permute-start = (f32[2,4,1152]{2,1,0:T(4,128)S(1)}, f32[2,4,1152]{2,1,0:T(4,128)S(1)}, u32[]{:S(2)}, u32[]{:S(2)}) collective-permute-start(f32[2,4,1152]{2,1,0:T(4,128)S(1)} %get-tuple-element.11), channel_id=1, source_target_pairs={{0,2},{2,4},{4,6},{6,8},{8,10},{10,12},{12,14},{1,3},{3,5},{5,7},{... | collective-permute-start | bytes 110600 | tf_op jit(solution)/shard_map/ppermute | solution.py:417
  8.2 1.9 %collective-permute-start.2 = (f32[7,8,1152]{2,1,0:T(8,128)S(1)}, f32[7,8,1152]{2,1,0:T(8,128)S(1)}, u32[]{:S(2)}, u32[]{:S(2)}) collective-permute-start(f32[7,8,1152]{2,1,0:T(8,128)S(1)} %get-tuple-element.15), channel_id=1, source_target_pairs={{0,2},{2,0},{4,6},{6,4},{8,10},{10,8},{12,14},{14,12},{1,3},{3,1},... | collective-permute-start | bytes 774152 | tf_op jit(solution)/shard_map/ppermute | solution.py:388
  10.1 0.0 copy-done.9
  10.1 0.0 copy-done.7
  10.2 0.0 copy-done.8
  10.2 0.0 copy-done.10
  10.2 1.6 %collective-permute-start.6 = (f32[13,4,576]{2,1,0:T(4,128)S(1)}, f32[13,4,576]{2,1,0:T(4,128)S(1)}, u32[]{:S(2)}, u32[]{:S(2)}) collective-permute-start(f32[13,4,576]{2,1,0:T(4,128)S(1)} %pad_maximum_fusion), channel_id=1, source_target_pairs={{0,1},{1,0},{2,3},{3,2},{4,5},{5,4},{6,7},{7,6},{8,9},{9,8},{10,11... | collective-permute-start | bytes 359432 | tf_op jit(solution)/shard_map/ppermute | solution.py:397
  11.8 0.0 collective-permute-done.1.swapped.refs_2_
  11.8 0.1 shard_map.123.relay
  11.9 3.2 %collective-permute-start.5 = (f32[6,8,1152]{2,1,0:T(8,128)S(1)}, f32[6,8,1152]{2,1,0:T(8,128)S(1)}, u32[]{:S(2)}, u32[]{:S(2)}) collective-permute-start(f32[6,8,1152]{2,1,0:T(8,128)S(1)} %shard_map.123.relay), channel_id=1, source_target_pairs={{0,4},{4,8},{8,12},{6,2},{10,6},{14,10},{1,5},{5,9},{9,13},{7,3},{... | collective-permute-start | bytes 663560 | tf_op jit(solution)/shard_map/ppermute | solution.py:394
  15.1 0.0 collective-permute-done.c_south
  15.1 0.0 copy-start.6
  15.1 0.0 copy-done.1
  15.1 0.6 %copy-done.6 = f32[64]{0:T(128)S(1)} copy-done((f32[64]{0:T(128)S(1)}, f32[64]{0:T(128)}, u32[]{:S(2)}) %copy-start.6) | copy-done | bytes 280
  15.8 0.9 %shard_map.124 = (f32[10,2,4,1152]{3,2,1,0:T(4,128)S(1)}, f32[16,2,4,1152]{3,2,1,0:T(4,128)S(1)}, f32[2,4,1152]{2,1,0:T(4,128)S(1)}, f32[7,8,1152]{2,1,0:T(8,128)S(1)}) custom-call(f32[64]{0:T(128)S(1)} %copy-done.6, f32[2,4,1152]{2,1,0:T(4,128)S(1)} %copy-done.5, ...), custom_call_target="tpu_custom_call", output_to_operand_aliasing={{1}: (5, {}), {2}: (6, {})} | custom-call | flops 2000000000 | bytes 3000000 | tf_op jit(solution)/shard_map/pallas_call | solution.py:439
  16.7 1.9 %collective-permute-start.3 = (f32[7,8,1152]{2,1,0:T(8,128)S(1)}, f32[7,8,1152]{2,1,0:T(8,128)S(1)}, u32[]{:S(2)}, u32[]{:S(2)}) collective-permute-start(f32[7,8,1152]{2,1,0:T(8,128)S(1)} %get-tuple-element.16), channel_id=1, source_target_pairs={{2,4},{4,2},{6,8},{8,6},{10,12},{12,10},{3,5},{5,3},{7,9},{9,7},{1... | collective-permute-start | bytes 774152 | tf_op jit(solution)/shard_map/ppermute | solution.py:391
  18.6 0.0 collective-permute-done.6
  18.6 0.2 maximum_select_fusion.columns
  18.8 0.1 shard_map.126.refs_5_.weights
  18.9 0.0 collective-permute-done.2.refs_2_
  18.9 8.0 %collective-permute-done.3.refs_3_ = f32[7,8,1152]{2,1,0:T(8,128)S(1)} collective-permute-done((f32[7,8,1152]{2,1,0:T(8,128)S(1)}, f32[7,8,1152]{2,1,0:T(8,128)S(1)}, u32[]{:S(2)}, u32[]{:S(2)}) %collective-permute-start.3) | collective-permute-done | bytes 258080 | tf_op jit(solution)/shard_map/ppermute | solution.py:391
  27.0 0.4 %shard_map.125.own = f32[9,2,4,1152]{3,2,1,0:T(4,128)S(1)} custom-call(f32[16,2,4,1152]{3,2,1,0:T(4,128)S(1)} %copy-done.1, f32[16,2,4,1152]{3,2,1,0:T(4,128)S(1)} %get-tuple-element.14.refs_1_, f32[7,8,1152]{2,1,0:T(8,128)S(1)} %collective-permute-done.2.refs_2_, f32[7,8,1152]{2,1,0:T(8,128)S(1)} %collective-permute-done.3.refs_3_, ...), custom_call_target="tpu_custom_call" | custom-call | flops 200000000 | bytes 1000000 | tf_op jit(solution)/shard_map/pallas_call | solution.py:458
  27.4 1.2 %collective-permute-start.4 = (f32[9,2,4,1152]{3,2,1,0:T(4,128)S(1)}, f32[9,2,4,1152]{3,2,1,0:T(4,128)S(1)}, u32[]{:S(2)}, u32[]{:S(2)}) collective-permute-start(f32[9,2,4,1152]{3,2,1,0:T(4,128)S(1)} %shard_map.125.own), channel_id=1, source_target_pairs={{0,1},{1,0},{2,3},{3,2},{4,5},{5,4},{6,7},{7,6},{8,9},{9,8},{10,11... | collective-permute-start | bytes 995336 | tf_op jit(solution)/shard_map/ppermute | solution.py:397
  28.6 0.0 collective-permute-done.5.refs_3_
  28.6 0.4 %shard_map.127.own.first_own = f32[8,2,4,1152]{3,2,1,0:T(4,128)S(1)} custom-call(f32[16,2,4,1152]{3,2,1,0:T(4,128)S(1)} %copy-done.1, f32[16,2,4,1152]{3,2,1,0:T(4,128)S(1)} %get-tuple-element.14.refs_1_, f32[8,2,4,1152]{3,2,1,0:T(4,128)S(1)} %collective-permute-done.1.swapped.refs_2_, f32[6,8,1152]{2,1,0:T(8,128)S(1)} %collective-permute-done.5.refs_3_, ...), custom_call_target="tpu_custom_call" | custom-call | flops 200000000 | bytes 1000000 | tf_op jit(solution)/shard_map/pallas_call | solution.py:452
  29.0 0.1 collective-permute-start.7
  29.1 1.5 %collective-permute-done.7.peer.first_peer = f32[8,2,4,1152]{3,2,1,0:T(4,128)S(1)} collective-permute-done((f32[8,2,4,1152]{3,2,1,0:T(4,128)S(1)}, f32[8,2,4,1152]{3,2,1,0:T(4,128)S(1)}, u32[]{:S(2)}, u32[]{:S(2)}) %collective-permute-start.7) | collective-permute-done | bytes 294944 | tf_op jit(solution)/shard_map/ppermute | solution.py:397
  30.7 0.8 %shard_map.128.out_in = f32[16,2,4,1152]{3,2,1,0:T(4,128)} custom-call(f32[8,2,4,1152]{3,2,1,0:T(4,128)S(1)} %shard_map.127.own.first_own, f32[8,2,4,1152]{3,2,1,0:T(4,128)S(1)} %collective-permute-done.7.peer.first_peer, f32[4,4,4,1152]{3,2,1,0:T(4,128)S(1)} %shard_map.126.refs_5_.weights), custom_call_target="tpu_custom_call" | custom-call | flops 200000000 | bytes 1000000 | tf_op jit(solution)/shard_map/pallas_call | solution.py:466
  31.5 0.0 collective-permute-done.4.peer
  31.5 1.5 %shard_map.129 = (f32[16,2,4,1152]{3,2,1,0:T(4,128)}, f32[2,4,1152]{2,1,0:T(4,128)}, f32[2,4,1152]{2,1,0:T(4,128)}) custom-call(f32[9,2,4,1152]{3,2,1,0:T(4,128)S(1)} %shard_map.125.own, f32[9,2,4,1152]{3,2,1,0:T(4,128)S(1)} %collective-permute-done.4.peer, f32[8,2,4,1152]{3,2,1,0:T(4,128)S(1)} %shard_map.127.own.first_own, ...), custom_call_target="tpu_custom_call", output_to_operand_aliasing={{0}: (6, {})} | custom-call | flops 200000000 | bytes 1000000 | tf_op jit(solution)/shard_map/pallas_call | solution.py:473
  (3 shorter events, 0.1 us)
Async XLA Ops:
  0.6 1.1 %copy-start = (f32[16,2,4,1152]{3,2,1,0:T(4,128)S(1)}, f32[16,2,4,1152]{3,2,1,0:T(4,128)}, u32[]{:S(2)}) copy-start(f32[16,2,4,1152]{3,2,1,0:T(4,128)} %refs_0_.3) | copy-start | bytes 1769476
  1.7 1.3 %copy-start.2 = (f32[2,4,1152]{2,1,0:T(4,128)S(1)}, f32[2,4,1152]{2,1,0:T(4,128)}, u32[]{:S(2)}) copy-start(f32[2,4,1152]{2,1,0:T(4,128)} %refs_5_.1) | copy-start | bytes 110596
  1.7 1.3 %copy-start.3 = (s32[2,4,1152]{2,1,0:T(4,128)S(1)}, s32[2,4,1152]{2,1,0:T(4,128)}, u32[]{:S(2)}) copy-start(s32[2,4,1152]{2,1,0:T(4,128)} %n.1) | copy-start | bytes 110596
  1.7 1.3 %copy-start.4 = (f32[2,4,1152]{2,1,0:T(4,128)S(1)}, f32[2,4,1152]{2,1,0:T(4,128)}, u32[]{:S(2)}) copy-start(f32[2,4,1152]{2,1,0:T(4,128)} %f.1) | copy-start | bytes 110596
  1.7 1.3 %copy-start.5 = (f32[2,4,1152]{2,1,0:T(4,128)S(1)}, f32[2,4,1152]{2,1,0:T(4,128)}, u32[]{:S(2)}) copy-start(f32[2,4,1152]{2,1,0:T(4,128)} %c.3) | copy-start | bytes 110596
  1.7 8.4 %copy-start.9 = (s32[4,4,576]{2,1,0:T(4,128)S(1)}, s32[4,4,576]{2,1,0:T(4,128)}, u32[]{:S(2)}) copy-start(s32[4,4,576]{2,1,0:T(4,128)} %param.15) | copy-start | bytes 110596
  1.8 10.0 %collective-permute-start.1 = (f32[8,2,4,1152]{3,2,1,0:T(4,128)S(1)}, f32[8,2,4,1152]{3,2,1,0:T(4,128)S(1)}, u32[]{:S(2)}, u32[]{:S(2)}) collective-permute-start(f32[8,2,4,1152]{3,2,1,0:T(4,128)S(1)} %shard_map.122), channel_id=1, source_target_pairs={{0,2},{2,0},{4,6},{6,4},{8,10},{10,8},{12,14},{14,12},{1,3},{3,1},... | collective-permute-start | bytes 884744 | tf_op jit(solution)/shard_map/ppermute | solution.py:388
  3.0 7.1 %copy-start.7 = (f32[4,4,576]{2,1,0:T(4,128)S(1)}, f32[4,4,576]{2,1,0:T(4,128)}, u32[]{:S(2)}) copy-start(f32[4,4,576]{2,1,0:T(4,128)} %param.17) | copy-start | bytes 110596
  3.1 7.1 %copy-start.8 = (f32[4,4,576]{2,1,0:T(4,128)S(1)}, f32[4,4,576]{2,1,0:T(4,128)}, u32[]{:S(2)}) copy-start(f32[4,4,576]{2,1,0:T(4,128)} %param.16) | copy-start | bytes 110596
  3.1 7.1 %copy-start.10 = (f32[4,576]{1,0:T(4,128)S(1)}, f32[4,576]{1,0:T(4,128)}, u32[]{:S(2)}) copy-start(f32[4,576]{1,0:T(4,128)} %param.18) | copy-start | bytes 27652
  5.5 9.6 %copy-start.1 = (f32[16,2,4,1152]{3,2,1,0:T(4,128)S(1)}, f32[16,2,4,1152]{3,2,1,0:T(4,128)}, u32[]{:S(2)}) copy-start(f32[16,2,4,1152]{3,2,1,0:T(4,128)} %refs_0_.3) | copy-start | bytes 1769476
  5.5 9.6 %collective-permute-start = (f32[2,4,1152]{2,1,0:T(4,128)S(1)}, f32[2,4,1152]{2,1,0:T(4,128)S(1)}, u32[]{:S(2)}, u32[]{:S(2)}) collective-permute-start(f32[2,4,1152]{2,1,0:T(4,128)S(1)} %get-tuple-element.11), channel_id=1, source_target_pairs={{0,2},{2,4},{4,6},{6,8},{8,10},{10,12},{12,14},{1,3},{3,5},{5,7},{... | collective-permute-start | bytes 110600 | tf_op jit(solution)/shard_map/ppermute | solution.py:417
  8.2 10.7 %collective-permute-start.2 = (f32[7,8,1152]{2,1,0:T(8,128)S(1)}, f32[7,8,1152]{2,1,0:T(8,128)S(1)}, u32[]{:S(2)}, u32[]{:S(2)}) collective-permute-start(f32[7,8,1152]{2,1,0:T(8,128)S(1)} %get-tuple-element.15), channel_id=1, source_target_pairs={{0,2},{2,0},{4,6},{6,4},{8,10},{10,8},{12,14},{14,12},{1,3},{3,1},... | collective-permute-start | bytes 774152 | tf_op jit(solution)/shard_map/ppermute | solution.py:388
  10.2 8.4 %collective-permute-start.6 = (f32[13,4,576]{2,1,0:T(4,128)S(1)}, f32[13,4,576]{2,1,0:T(4,128)S(1)}, u32[]{:S(2)}, u32[]{:S(2)}) collective-permute-start(f32[13,4,576]{2,1,0:T(4,128)S(1)} %pad_maximum_fusion), channel_id=1, source_target_pairs={{0,1},{1,0},{2,3},{3,2},{4,5},{5,4},{6,7},{7,6},{8,9},{9,8},{10,11... | collective-permute-start | bytes 359432 | tf_op jit(solution)/shard_map/ppermute | solution.py:397
  11.9 16.7 %collective-permute-start.5 = (f32[6,8,1152]{2,1,0:T(8,128)S(1)}, f32[6,8,1152]{2,1,0:T(8,128)S(1)}, u32[]{:S(2)}, u32[]{:S(2)}) collective-permute-start(f32[6,8,1152]{2,1,0:T(8,128)S(1)} %shard_map.123.relay), channel_id=1, source_target_pairs={{0,4},{4,8},{8,12},{6,2},{10,6},{14,10},{1,5},{5,9},{9,13},{7,3},{... | collective-permute-start | bytes 663560 | tf_op jit(solution)/shard_map/ppermute | solution.py:394
  15.1 0.7 %copy-start.6 = (f32[64]{0:T(128)S(1)}, f32[64]{0:T(128)}, u32[]{:S(2)}) copy-start(f32[64]{0:T(128)} %constant.8.clone.scale) | copy-start | bytes 772
  16.7 10.3 %collective-permute-start.3 = (f32[7,8,1152]{2,1,0:T(8,128)S(1)}, f32[7,8,1152]{2,1,0:T(8,128)S(1)}, u32[]{:S(2)}, u32[]{:S(2)}) collective-permute-start(f32[7,8,1152]{2,1,0:T(8,128)S(1)} %get-tuple-element.16), channel_id=1, source_target_pairs={{2,4},{4,2},{6,8},{8,6},{10,12},{12,10},{3,5},{5,3},{7,9},{9,7},{1... | collective-permute-start | bytes 774152 | tf_op jit(solution)/shard_map/ppermute | solution.py:391
  27.4 4.1 %collective-permute-start.4 = (f32[9,2,4,1152]{3,2,1,0:T(4,128)S(1)}, f32[9,2,4,1152]{3,2,1,0:T(4,128)S(1)}, u32[]{:S(2)}, u32[]{:S(2)}) collective-permute-start(f32[9,2,4,1152]{3,2,1,0:T(4,128)S(1)} %shard_map.125.own), channel_id=1, source_target_pairs={{0,1},{1,0},{2,3},{3,2},{4,5},{5,4},{6,7},{7,6},{8,9},{9,8},{10,11... | collective-permute-start | bytes 995336 | tf_op jit(solution)/shard_map/ppermute | solution.py:397
  29.0 1.6 %collective-permute-start.7 = (f32[8,2,4,1152]{3,2,1,0:T(4,128)S(1)}, f32[8,2,4,1152]{3,2,1,0:T(4,128)S(1)}, u32[]{:S(2)}, u32[]{:S(2)}) collective-permute-start(f32[8,2,4,1152]{3,2,1,0:T(4,128)S(1)} %shard_map.127.own.first_own), channel_id=1, source_target_pairs={{0,1},{1,0},{2,3},{3,2},{4,5},{5,4},{6,7},{7,6},{8,9},{9,8},{10,11... | collective-permute-start | bytes 884744 | tf_op jit(solution)/shard_map/ppermute | solution.py:397

commit v5 on v4

--- a/solution.py
+++ b/solution.py
@@ -13,6 +13,8 @@
 LEVELS = 2
 LANE = 128
 
+COST = dict(zonal=10000, relay=10000, weights=1, mix=1, fin_b=1, fin_a=1, first=1, last=1)
+
 
 def lanes(chunk):
     return pl.ds(chunk * LANE, LANE)
@@ -33,25 +35,28 @@
 
 
 def copy_kernel(x, out):
-    out[...] = x[: out.shape[0]]
+    skip = x.shape[0] - out.shape[0]
+    out[...] = x[skip:]
 
 
 def side_rows(to_north):
     return (ROWS - 1, ROWS - 2, ROWS - 3) if to_north else (0, 1, 2)
 
 
-def gather_rows(rows, x, t, out):
+def gather_rows(rows, x, t, c, out):
     count = out.shape[1]
-    skip = x.shape[0] - count
+    last = 3 * LEVELS
     for d, row in enumerate(rows):
         for lev in range(LEVELS):
             at = d * LEVELS + lev
             for f in range(count):
-                out[at, f : f + 1, :] = x[skip + f, lev, row : row + 1, :]
-            out[3 * LEVELS, at : at + 1, :] = t[lev, row : row + 1, :]
-
-
-def relay_kernel(swapped, relay):
+                out[at, f : f + 1, :] = x[f, lev, row : row + 1, :]
+            out[last, at : at + 1, :] = t[lev, row : row + 1, :]
+    for lev in range(LEVELS):
+        out[last, last + lev : last + lev + 1, :] = c[lev, ROWS - 1 : ROWS, :]
+
+
+def relay_kernel(swapped, zon_t, relay):
     def body(odd):
         for d, row in enumerate(side_rows(not odd)):
             for lev in range(LEVELS):
@@ -90,7 +95,7 @@
 
 
 def row_weights(c, below, scale, lat):
-    row = lax.broadcasted_iota(jnp.int32, c.shape, 0)
+    row = lax.broadcasted_iota(jnp.int32, c.shape, 0) % ROWS
 
     def by_row(parts):
         total = parts[ROWS - 1]
@@ -100,7 +105,7 @@
 
     low = by_row([jnp.full(c.shape, scale[lat * 2 * ROWS + 2 * j]) for j in range(ROWS)])
     high = by_row([jnp.full(c.shape, scale[lat * 2 * ROWS + 2 * j + 1]) for j in range(ROWS)])
-    lower = face_weights(jnp.concatenate([below, c[: ROWS - 1]], axis=0))
+    lower = face_weights(below)
     upper = face_weights(c)
     offsets = {}
     for o in range(-3, 4):
@@ -119,18 +124,22 @@
 
 
 def weights_kernel(
-    fields, last, scale, c, c_south, x, t, zon_in, zon_t_in, relay, out, zon, zon_t, direct, ws
+    fields, last, scale, c, near, far, x, t, zon_in, zon_t_in, mix, out, zon, zon_t, ws
 ):
     lat = lax.axis_index("lat")
     odd = lax.rem(lat, 2)
     lons = x.shape[-1]
-    both(odd, lambda is_odd: gather_rows(side_rows(is_odd), x, t, direct))
+    block = 3 * LEVELS
+    parts = []
     for lev in range(LEVELS):
         own = c[lev]
-        below = c_south[lev, ROWS - 1 : ROWS, :]
-        below = jnp.where(lat == 0, -pltpu.roll(own, lons // 2, 1)[0:1], below)
-        for r, w in enumerate(row_weights(own, below, scale, lat)):
-            out[r, lev] = w
+        at = slice(block + lev, block + lev + 1)
+        south = jnp.where(odd == 1, near[block, at, :], far[block, at, :])
+        south = jnp.where(lat == 0, -pltpu.roll(own, lons // 2, 1)[0:1], south)
+        parts += [south, own[: ROWS - 1]]
+    for r, w in enumerate(row_weights(stacked(c), jnp.concatenate(parts, axis=0), scale, lat)):
+        for lev in range(LEVELS):
+            out[r, lev] = w[lev * ROWS : (lev + 1) * ROWS]
 
     def pole(rows):
         for k, (_, at) in enumerate(rows):
@@ -167,10 +176,17 @@
         pole([(ROWS - d, ROWS + 2 + d) for d in range(1, 4)])
 
 
-def zonal_kernel(fields, x, t, n, f, c, zon, zon_t, near, c_copy, w):
+def zonal_kernel(
+    fields, x, t, n, f, c, upper, share, quotient, ground, zon, zon_t, near, far, columns, w
+):
     lons = x.shape[-1]
-    c_copy[...] = c[...]
-    both(parity(), lambda odd: gather_rows(side_rows(not odd), x, t, near))
+    pack_columns(upper, share, quotient, ground, columns)
+
+    def gather(odd):
+        gather_rows(side_rows(not odd), x, t, c, near)
+        gather_rows(side_rows(odd), x, t, c, far)
+
+    both(parity(), gather)
 
     def shifted(values, k):
         return values if k == 0 else pltpu.roll(values, (-k) % lons, 1)
@@ -211,9 +227,9 @@
 
 def fin_kernel(skip, count, direct, *refs):
     if direct:
-        x, zon, near, far, w, t, zon_t, adv = refs
+        x, zon, near, far, w, t, zon_t, _, adv = refs
     else:
-        x, zon, near, far, w, _, adv = refs
+        x, zon, near, far, w, adv = refs
     chunks = w.shape[-1] // LANE
 
     def body(odd):
@@ -267,6 +283,14 @@
     both(parity(), body)
 
 
+def pack_columns(upper, share, quotient, ground, out):
+    levels = upper.shape[0]
+    out[:levels] = upper[...].astype(jnp.float32)
+    out[levels : 2 * levels] = share[...]
+    out[2 * levels : 3 * levels] = quotient[...]
+    out[3 * levels] = ground[...]
+
+
 def mix_kernel(levels, columns, weights):
     group = lax.axis_index("lev")
     for k in range(levels):
@@ -287,12 +311,12 @@
     return total
 
 
-def remap_fields(skip, count, own, peer, weights, out, buffer, sems):
+def remap_fields(skip, own, peer, weights, out, buffer, sems):
     group = lax.axis_index("lev")
     chunks = out.shape[-1] // LANE
     copies = []
     step = 4
-    for first in range(0, count, step):
+    for first in range(0, buffer.shape[0], step):
         for chunk in range(chunks):
             lane = lanes(chunk)
             ws = [
@@ -313,18 +337,17 @@
     return copies
 
 
-def remap_first_kernel(count, own, peer, weights, out, buffer, sems):
-    for copy in remap_fields(0, count, own, peer, weights, out, buffer, sems):
+def remap_last_kernel(skip, own, peer, weights, out_in, out, buffer, sems):
+    for copy in remap_fields(skip, own, peer, weights, out, buffer, sems):
         copy.wait()
 
 
-def remap_last_kernel(
-    skip, count, levels, own, peer, first_own, first_peer, weights, columns, out_in,
-    out, out_t, out_phi, buffer, thick, sems,
+def remap_first_kernel(
+    levels, own, peer, weights, columns, out, out_t, out_phi, buffer, thick, sems, column_sems
 ):
     group = lax.axis_index("lev")
-    copies = remap_fields(skip, count, own, peer, weights, out, buffer, sems)
-    vapour = [adv[0, lev] for adv in (first_own, first_peer) for lev in range(LEVELS)]
+    count = buffer.shape[0]
+    vapour = [adv[0, lev] for adv in (own, peer) for lev in range(LEVELS)]
     temp = [adv[count, lev] for adv in (own, peer) for lev in range(LEVELS)]
     for k in range(levels):
         ws = [weights[k, s] for s in range(2 * LEVELS)]
@@ -337,14 +360,19 @@
         layer = thick[k]
         thick[k] = deeper + 0.5 * layer
         deeper = deeper + layer
-    for lev in range(LEVELS):
-        out_phi[lev] = thick[group * LEVELS + lev]
-        out_t[lev] = thick[levels + group * LEVELS + lev]
+    copies = [
+        pltpu.make_async_copy(
+            thick.at[pl.ds(at + group * LEVELS, LEVELS)], target, column_sems.at[i]
+        )
+        for i, (at, target) in enumerate(((0, out_phi), (levels, out_t)))
+    ]
     for copy in copies:
+        copy.start()
+    for copy in copies + remap_fields(0, own, peer, weights, out, buffer, sems):
         copy.wait()
 
 
-def call(kernel, outs, scratch=(), specs=None, cost=(0, 0), limit=12, aliases=None, out_specs=None):
+def call(kernel, outs, scratch=(), specs=None, cost=0, limit=12, aliases=None, out_specs=None):
     single = not isinstance(outs, list)
     shapes = tuple(jax.ShapeDtypeStruct(s, jnp.float32) for s in ([outs] if single else outs))
     extra = {} if specs is None else {"in_specs": specs}
@@ -355,7 +383,7 @@
         out_shape=shapes[0] if single else shapes,
         scratch_shapes=[pltpu.VMEM(s, jnp.float32) if isinstance(s, tuple) else s for s in scratch],
         compiler_params=pltpu.CompilerParams(vmem_limit_bytes=limit * 2**20),
-        cost_estimate=pl.CostEstimate(flops=cost[0], bytes_accessed=cost[1], transcendentals=0),
+        cost_estimate=pl.CostEstimate(flops=cost * 10**6, bytes_accessed=1000, transcendentals=0),
         input_output_aliases=aliases or {},
         **extra,
     )
@@ -380,7 +408,6 @@
 
     pairs = [(i, i ^ 1) for i in range(bands)]
     across = [(i, i + 1 if i % 2 else i - 1) for i in range(1, bands - 1)]
-    north = [(i, i + 1) for i in range(bands - 1)]
     relays = [(i, i + 2) for i in range(0, bands - 2, 2)] + [(i, i - 2) for i in range(3, bands, 2)]
     cores = [(0, 1), (1, 0)]
 
@@ -408,27 +435,34 @@
     direct_shape = (3 * LEVELS + 1, direct, lons)
 
     near_a = swap(call(copy_kernel, (swapped,) + x.shape[1:])(x))
-    zon, zon_t, near_rows, c_copy = call(
+    zon, zon_t, near_rows, far_rows, columns = call(
         functools.partial(zonal_kernel, fields),
-        [x.shape, t.shape, direct_shape, c.shape],
+        [
+            x.shape,
+            t.shape,
+            direct_shape,
+            direct_shape,
+            (3 * levels + 1,) + ground_gravity_height.shape,
+        ],
         [(7, LEVELS * ROWS, lons)],
-        cost=(4000000000, 3000000),
-    )(x, t, integer_boxes_traversed, partial_crossing_share, c)
-    c_south = lax.ppermute(c_copy, "lat", north)
+        cost=COST["zonal"],
+    )(
+        x,
+        t,
+        integer_boxes_traversed,
+        partial_crossing_share,
+        c,
+        higher_donor_stratum,
+        deeper_donor_share,
+        napierian_thickness_quotient,
+        ground_gravity_height,
+    )
+    far_b = exchange_across(far_rows)
     near_b = swap(near_rows)
 
-    relay = call(relay_kernel, (3 * LEVELS, swapped, lons))(near_a)
+    relay = call(relay_kernel, (3 * LEVELS, swapped, lons), cost=COST["relay"])(near_a, zon_t)
     far_a = pass_on(relay)
 
-    columns = jnp.concatenate(
-        [
-            higher_donor_stratum.astype(jnp.float32),
-            deeper_donor_share,
-            napierian_thickness_quotient,
-            ground_gravity_height[None],
-        ],
-        axis=0,
-    )
     peer_columns = other_core(columns)
     columns = jnp.where(
         lax.axis_index("lev") == 0,
@@ -436,53 +470,54 @@
         jnp.concatenate([peer_columns, columns], -1),
     )
 
-    weights, zon, zon_t, far_rows = call(
+    mix = call(
+        functools.partial(mix_kernel, levels), (levels, 2 * LEVELS, ROWS, lons), cost=COST["mix"]
+    )(columns)
+    weights, zon, zon_t = call(
         functools.partial(weights_kernel, fields, bands - 1),
-        [(ROWS + 6, LEVELS, ROWS, lons), x.shape, t.shape, direct_shape],
+        [(ROWS + 6, LEVELS, ROWS, lons), x.shape, t.shape],
         [(3, LEVELS * ROWS, lons)],
-        [smem] + [vmem] * 7,
-        cost=(2000000000, 3000000),
-        aliases={5: 1, 6: 2},
-    )(scale, c, c_south, x, t, zon, zon_t, relay)
-    far_b = exchange_across(far_rows)
-    mix = call(
-        functools.partial(mix_kernel, levels), (levels, 2 * LEVELS, ROWS, lons), cost=(400000000, 1000000)
-    )(columns)
-
+        [smem] + [vmem] * 8,
+        cost=COST["weights"],
+        aliases={6: 1, 7: 2},
+    )(scale, c, near_b, far_b, x, t, zon, zon_t, mix)
+
+    adv_b = call(
+        functools.partial(fin_kernel, 0, direct, True),
+        (direct + 1,) + x.shape[1:],
+        cost=COST["fin_b"],
+    )(x, zon, near_b, far_b, weights, t, zon_t, mix)
+    peer_b = other_core(adv_b)
     adv_a = call(
-        functools.partial(fin_kernel, 0, swapped, False),
+        functools.partial(fin_kernel, direct, swapped, False),
         (swapped,) + x.shape[1:],
-        cost=(200000000, 1000000),
-    )(x, zon, near_a, far_a, weights, mix)
+        cost=COST["fin_a"],
+    )(x, zon, near_a, far_a, weights)
     peer_a = other_core(adv_a)
-    adv_b = call(
-        functools.partial(fin_kernel, swapped, direct, True),
-        (direct + 1,) + x.shape[1:],
-        cost=(200000000, 1000000),
-    )(x, zon, near_b, far_b, weights, t, zon_t)
-    peer_b = other_core(adv_b)
 
     anywhere = pl.BlockSpec(memory_space=pl.ANY)
-    out = call(
-        functools.partial(remap_first_kernel, swapped),
-        x.shape,
-        [(swapped,) + x.shape[1:], pltpu.SemaphoreType.DMA((swapped // 4,))],
-        cost=(200000000, 1000000),
-        out_specs=anywhere,
-    )(adv_a, peer_a, mix)
-    return call(
-        functools.partial(remap_last_kernel, swapped, direct, levels),
+    out, out_t, out_phi = call(
+        functools.partial(remap_first_kernel, levels),
         [x.shape, t.shape, t.shape],
         [
             (direct,) + x.shape[1:],
             (2 * levels, ROWS, lons),
             pltpu.SemaphoreType.DMA((direct // 4,)),
+            pltpu.SemaphoreType.DMA((2,)),
         ],
-        [vmem] * 6 + [anywhere],
-        cost=(200000000, 1000000),
-        aliases={6: 0},
-        out_specs=(anywhere, vmem, vmem),
-    )(adv_b, peer_b, adv_a, peer_a, mix, columns, out)
+        cost=COST["first"],
+        out_specs=(anywhere,) * 3,
+    )(adv_b, peer_b, mix, columns)
+    out = call(
+        functools.partial(remap_last_kernel, direct),
+        x.shape,
+        [(swapped,) + x.shape[1:], pltpu.SemaphoreType.DMA((swapped // 4,))],
+        [vmem] * 3 + [anywhere],
+        cost=COST["last"],
+        aliases={3: 0},
+        out_specs=anywhere,
+    )(adv_a, peer_a, mix, out)
+    return out, out_t, out_phi
 
 
 def solution(mesh):

time: 33.3 us -> 28.1 us (0.84)
  the two profiles are of different devices: /device:TPU:9 before, /device:TPU:0 now
where the time goes in v5:
time: 28.1 us; the launch traced here: 27.9 us
  starting transfers between devices  9.29 us (33%)
  waiting for transfers between devices  9.29 us (33%)
  Pallas kernels  7.13 us (25%)
  local copies, waits for them, and re-layouts  1.1 us (4%)
  between operations  0.85 us (3%)
    ppermute x2, waiting for transfers between devices, swap(): return lax.ppermute(v, 'lat', pairs)  8.67 us
    ppermute x1, starting transfers between devices, pass_on(): return lax.ppermute(v, 'lat', relays)  4.19 us
    ppermute x2, starting transfers between devices, swap(): return lax.ppermute(v, 'lat', pairs)  3.75 us
    pallas_call x1, Pallas kernels, on_device(): call(functools.partial(zonal_kernel, fields), [x.shape, t.shape, direct_s...  2.5 us
    pallas_call x1, Pallas kernels, on_device(): call(functools.partial(weights_kernel, fields, bands - 1), [(ROWS + 6, LE...  1.77 us
    unnamed x22, local copies, waits for them, and re-layouts  1.1 us
    pallas_call x1, Pallas kernels, on_device(): call(functools.partial(remap_first_kernel, levels), [x.shape, t.shape, t....  0.91 us
    pallas_call x1, Pallas kernels, on_device(): call(functools.partial(remap_last_kernel, direct), x.shape, [(swapped,) +...  0.83 us
  transfers between devices with their start and end apart: 7, of which 3 were waited for; matrix products, arithmetic and copies ran while one was open for 1% of the time, Pallas kernels for 22%

profile of v5, /device:TPU:0, one launch (start us, length us, event | category | flops | bytes accessed | tf_op | source)
XLA Modules:
  0.0 27.9 jit_solution(17255372693537234649)
XLA Ops:
  0.6 0.0 copy-start
  0.6 1.1 %copy-done = f32[16,2,4,1152]{3,2,1,0:T(4,128)S(1)} copy-done((f32[16,2,4,1152]{3,2,1,0:T(4,128)S(1)}, f32[16,2,4,1152]{3,2,1,0:T(4,128)}, u32[]{:S(2)}) %copy-start) | copy-done | bytes 589848
  1.7 0.0 copy-start.2
  1.7 0.0 copy-start.3
  1.7 0.0 copy-start.5
  1.7 0.0 copy-start.6
  1.7 0.0 copy-start.7
  1.7 0.0 copy-start.8
  1.7 0.0 copy-start.9
  1.7 0.0 copy-start.10
  1.8 3.0 %collective-permute-start.3 = (f32[8,2,4,1152]{3,2,1,0:T(4,128)S(1)}, f32[8,2,4,1152]{3,2,1,0:T(4,128)S(1)}, u32[]{:S(2)}, u32[]{:S(2)}) collective-permute-start(f32[8,2,4,1152]{3,2,1,0:T(4,128)S(1)} %shard_map.124), channel_id=1, source_target_pairs={{0,2},{2,0},{4,6},{6,4},{8,10},{10,8},{12,14},{14,12},{1,3},{3,1},... | collective-permute-start | bytes 884744 | tf_op jit(solution)/shard_map/ppermute | solution.py:415
  4.8 0.0 copy-done.2
  4.8 0.0 copy-done.3
  4.8 0.0 copy-done.5
  4.8 0.0 copy-done.6
  4.8 0.0 copy-done.7
  4.8 0.0 copy-done.8
  4.8 0.0 copy-done.9
  4.8 0.0 copy-done.10
  4.8 2.5 %shard_map.121 = (f32[16,2,4,1152]{3,2,1,0:T(4,128)S(1)}, f32[2,4,1152]{2,1,0:T(4,128)S(1)}, f32[7,8,1152]{2,1,0:T(8,128)S(1)}, f32[7,8,1152]{2,1,0:T(8,128)S(1)}, f32[13,4,576]{2,1,0:T(4,128)S(1)}) custom-call(f32[16,2,4,1152]{3,2,1,0:T(4,128)S(1)} %copy-done, f32[2,4,1152]{2,1,0:T(4,128)S(1)} %copy-done.2, s32[2,4,1152]{2,1,0:T(4,128)S(1)} %copy-done.8, ...), custom_call_target="tpu_custom_call" | custom-call | flops 10000000000 | bytes 1000 | tf_op jit(solution)/shard_map/pallas_call | solution.py:438
  7.3 0.1 collective-permute-start.2
  7.4 0.7 %collective-permute-start = (f32[7,8,1152]{2,1,0:T(8,128)S(1)}, f32[7,8,1152]{2,1,0:T(8,128)S(1)}, u32[]{:S(2)}, u32[]{:S(2)}) collective-permute-start(f32[7,8,1152]{2,1,0:T(8,128)S(1)} %get-tuple-element.14), channel_id=1, source_target_pairs={{0,2},{2,0},{4,6},{6,4},{8,10},{10,8},{12,14},{14,12},{1,3},{3,1},... | collective-permute-start | bytes 774152 | tf_op jit(solution)/shard_map/ppermute | solution.py:415
  8.2 0.7 %collective-permute-start.1 = (f32[7,8,1152]{2,1,0:T(8,128)S(1)}, f32[7,8,1152]{2,1,0:T(8,128)S(1)}, u32[]{:S(2)}, u32[]{:S(2)}) collective-permute-start(f32[7,8,1152]{2,1,0:T(8,128)S(1)} %get-tuple-element.15), channel_id=1, source_target_pairs={{2,4},{4,2},{6,8},{8,6},{10,12},{12,10},{3,5},{5,3},{7,9},{9,7},{1... | collective-permute-start | bytes 774152 | tf_op jit(solution)/shard_map/ppermute | solution.py:418
  8.9 3.8 %collective-permute-done.3.swapped.refs_2_ = f32[8,2,4,1152]{3,2,1,0:T(4,128)S(1)} collective-permute-done((f32[8,2,4,1152]{3,2,1,0:T(4,128)S(1)}, f32[8,2,4,1152]{3,2,1,0:T(4,128)S(1)}, u32[]{:S(2)}, u32[]{:S(2)}) %collective-permute-start.3) | collective-permute-done | bytes 294944 | tf_op jit(solution)/shard_map/ppermute | solution.py:415
  12.6 0.1 shard_map.125
  12.7 0.0 copy-start.1
  12.7 4.2 %collective-permute-start.4 = (f32[6,8,1152]{2,1,0:T(8,128)S(1)}, f32[6,8,1152]{2,1,0:T(8,128)S(1)}, u32[]{:S(2)}, u32[]{:S(2)}) collective-permute-start(f32[6,8,1152]{2,1,0:T(8,128)S(1)} %shard_map.125), channel_id=1, source_target_pairs={{0,4},{4,8},{8,12},{6,2},{10,6},{14,10},{1,5},{5,9},{9,13},{7,3},{... | collective-permute-start | bytes 663560 | tf_op jit(solution)/shard_map/ppermute | solution.py:421
  16.9 0.0 collective-permute-done.2
  16.9 0.2 maximum_select_fusion.columns
  17.1 0.1 shard_map.122.mix.refs_7_.weights
  17.2 0.0 copy-start.4
  17.2 4.9 %collective-permute-done.near.refs_2_ = f32[7,8,1152]{2,1,0:T(8,128)S(1)} collective-permute-done((f32[7,8,1152]{2,1,0:T(8,128)S(1)}, f32[7,8,1152]{2,1,0:T(8,128)S(1)}, u32[]{:S(2)}, u32[]{:S(2)}) %collective-permute-start) | collective-permute-done | bytes 258080 | tf_op jit(solution)/shard_map/ppermute | solution.py:415
  22.1 0.0 collective-permute-done.1.far.refs_3_
  22.1 0.0 copy-done.1
  22.1 0.0 copy-done.4
  22.1 1.8 %shard_map.123 = (f32[10,2,4,1152]{3,2,1,0:T(4,128)S(1)}, f32[16,2,4,1152]{3,2,1,0:T(4,128)S(1)}, f32[2,4,1152]{2,1,0:T(4,128)S(1)}) custom-call(f32[64]{0:T(128)S(1)} %copy-done.4, f32[2,4,1152]{2,1,0:T(4,128)S(1)} %copy-done.3, f32[7,8,1152]{2,1,0:T(8,128)S(1)} %collective-permute-done.near.refs_2_, ...), custom_call_target="tpu_custom_call", output_to_operand_aliasing={{1}: (6, {}), {2}: (7, {})} | custom-call | flops 1000000 | bytes 1000 | tf_op jit(solution)/shard_map/pallas_call | solution.py:476
  23.9 0.5 %shard_map.127.own = f32[9,2,4,1152]{3,2,1,0:T(4,128)S(1)} custom-call(f32[16,2,4,1152]{3,2,1,0:T(4,128)S(1)} %copy-done.1, f32[16,2,4,1152]{3,2,1,0:T(4,128)S(1)} %get-tuple-element.19.refs_1_, f32[7,8,1152]{2,1,0:T(8,128)S(1)} %collective-permute-done.near.refs_2_, f32[7,8,1152]{2,1,0:T(8,128)S(1)} %collective-permute-done.1.far.refs_3_, ...), custom_call_target="tpu_custom_call" | custom-call | flops 1000000 | bytes 1000 | tf_op jit(solution)/shard_map/pallas_call | solution.py:485
  24.4 0.1 collective-permute-start.6
  24.5 0.0 collective-permute-done.4.refs_3_
  24.5 0.5 %shard_map.126.own = f32[8,2,4,1152]{3,2,1,0:T(4,128)S(1)} custom-call(f32[16,2,4,1152]{3,2,1,0:T(4,128)S(1)} %copy-done.1, f32[16,2,4,1152]{3,2,1,0:T(4,128)S(1)} %get-tuple-element.19.refs_1_, f32[8,2,4,1152]{3,2,1,0:T(4,128)S(1)} %collective-permute-done.3.swapped.refs_2_, f32[6,8,1152]{2,1,0:T(8,128)S(1)} %collective-permute-done.4.refs_3_, ...), custom_call_target="tpu_custom_call" | custom-call | flops 1000000 | bytes 1000 | tf_op jit(solution)/shard_map/pallas_call | solution.py:491
  25.0 0.5 %collective-permute-start.5 = (f32[8,2,4,1152]{3,2,1,0:T(4,128)S(1)}, f32[8,2,4,1152]{3,2,1,0:T(4,128)S(1)}, u32[]{:S(2)}, u32[]{:S(2)}) collective-permute-start(f32[8,2,4,1152]{3,2,1,0:T(4,128)S(1)} %shard_map.126.own), channel_id=1, source_target_pairs={{0,1},{1,0},{2,3},{3,2},{4,5},{5,4},{6,7},{7,6},{8,9},{9,8},{10,11... | collective-permute-start | bytes 884744 | tf_op jit(solution)/shard_map/ppermute | solution.py:424
  25.5 0.6 %collective-permute-done.6.peer = f32[9,2,4,1152]{3,2,1,0:T(4,128)S(1)} collective-permute-done((f32[9,2,4,1152]{3,2,1,0:T(4,128)S(1)}, f32[9,2,4,1152]{3,2,1,0:T(4,128)S(1)}, u32[]{:S(2)}, u32[]{:S(2)}) %collective-permute-start.6) | collective-permute-done | bytes 331808 | tf_op jit(solution)/shard_map/ppermute | solution.py:424
  26.1 0.9 %shard_map.128 = (f32[16,2,4,1152]{3,2,1,0:T(4,128)}, f32[2,4,1152]{2,1,0:T(4,128)}, f32[2,4,1152]{2,1,0:T(4,128)}) custom-call(f32[9,2,4,1152]{3,2,1,0:T(4,128)S(1)} %shard_map.127.own, f32[9,2,4,1152]{3,2,1,0:T(4,128)S(1)} %collective-permute-done.6.peer, f32[4,4,4,1152]{3,2,1,0:T(4,128)S(1)} %shard_map.122.mix.refs_7_.weights, ...), custom_call_target="tpu_custom_call" | custom-call | flops 1000000 | bytes 1000 | tf_op jit(solution)/shard_map/pallas_call | solution.py:499
  27.0 0.0 collective-permute-done.5.peer
  27.0 0.8 %shard_map.129 = f32[16,2,4,1152]{3,2,1,0:T(4,128)} custom-call(f32[8,2,4,1152]{3,2,1,0:T(4,128)S(1)} %shard_map.126.own, f32[8,2,4,1152]{3,2,1,0:T(4,128)S(1)} %collective-permute-done.5.peer, f32[4,4,4,1152]{3,2,1,0:T(4,128)S(1)} %shard_map.122.mix.refs_7_.weights, f32[16,2,4,1152]{3,2,1,0:T(4,128)} %get-tuple-element.22.out_in), custom_call_target="tpu_custom_call", output_to_operand_aliasing={{}: (3, {})} | custom-call | flops 1000000 | bytes 1000 | tf_op jit(solution)/shard_map/pallas_call | solution.py:511
  (1 shorter events, 0.0 us)
Async XLA Ops:
  0.6 1.1 %copy-start = (f32[16,2,4,1152]{3,2,1,0:T(4,128)S(1)}, f32[16,2,4,1152]{3,2,1,0:T(4,128)}, u32[]{:S(2)}) copy-start(f32[16,2,4,1152]{3,2,1,0:T(4,128)} %refs_0_.3) | copy-start | bytes 1769476
  1.7 3.1 %copy-start.2 = (f32[2,4,1152]{2,1,0:T(4,128)S(1)}, f32[2,4,1152]{2,1,0:T(4,128)}, u32[]{:S(2)}) copy-start(f32[2,4,1152]{2,1,0:T(4,128)} %refs_5_.1) | copy-start | bytes 110596
  1.7 3.1 %copy-start.3 = (f32[2,4,1152]{2,1,0:T(4,128)S(1)}, f32[2,4,1152]{2,1,0:T(4,128)}, u32[]{:S(2)}) copy-start(f32[2,4,1152]{2,1,0:T(4,128)} %c.3) | copy-start | bytes 110596
  1.7 3.1 %copy-start.5 = (s32[4,4,576]{2,1,0:T(4,128)S(1)}, s32[4,4,576]{2,1,0:T(4,128)}, u32[]{:S(2)}) copy-start(s32[4,4,576]{2,1,0:T(4,128)} %upper.1) | copy-start | bytes 110596
  1.7 3.1 %copy-start.6 = (f32[4,4,576]{2,1,0:T(4,128)S(1)}, f32[4,4,576]{2,1,0:T(4,128)}, u32[]{:S(2)}) copy-start(f32[4,4,576]{2,1,0:T(4,128)} %share.1) | copy-start | bytes 110596
  1.7 3.1 %copy-start.7 = (f32[4,4,576]{2,1,0:T(4,128)S(1)}, f32[4,4,576]{2,1,0:T(4,128)}, u32[]{:S(2)}) copy-start(f32[4,4,576]{2,1,0:T(4,128)} %quotient.1) | copy-start | bytes 110596
  1.7 3.1 %copy-start.8 = (s32[2,4,1152]{2,1,0:T(4,128)S(1)}, s32[2,4,1152]{2,1,0:T(4,128)}, u32[]{:S(2)}) copy-start(s32[2,4,1152]{2,1,0:T(4,128)} %n.1) | copy-start | bytes 110596
  1.7 3.1 %copy-start.9 = (f32[2,4,1152]{2,1,0:T(4,128)S(1)}, f32[2,4,1152]{2,1,0:T(4,128)}, u32[]{:S(2)}) copy-start(f32[2,4,1152]{2,1,0:T(4,128)} %f.1) | copy-start | bytes 110596
  1.7 3.1 %copy-start.10 = (f32[4,576]{1,0:T(4,128)S(1)}, f32[4,576]{1,0:T(4,128)}, u32[]{:S(2)}) copy-start(f32[4,576]{1,0:T(4,128)} %ground.1) | copy-start | bytes 27652
  1.8 10.8 %collective-permute-start.3 = (f32[8,2,4,1152]{3,2,1,0:T(4,128)S(1)}, f32[8,2,4,1152]{3,2,1,0:T(4,128)S(1)}, u32[]{:S(2)}, u32[]{:S(2)}) collective-permute-start(f32[8,2,4,1152]{3,2,1,0:T(4,128)S(1)} %shard_map.124), channel_id=1, source_target_pairs={{0,2},{2,0},{4,6},{6,4},{8,10},{10,8},{12,14},{14,12},{1,3},{3,1},... | collective-permute-start | bytes 884744 | tf_op jit(solution)/shard_map/ppermute | solution.py:415
  7.3 9.6 %collective-permute-start.2 = (f32[13,4,576]{2,1,0:T(4,128)S(1)}, f32[13,4,576]{2,1,0:T(4,128)S(1)}, u32[]{:S(2)}, u32[]{:S(2)}) collective-permute-start(f32[13,4,576]{2,1,0:T(4,128)S(1)} %get-tuple-element.18), channel_id=1, source_target_pairs={{0,1},{1,0},{2,3},{3,2},{4,5},{5,4},{6,7},{7,6},{8,9},{9,8},{10,11... | collective-permute-start | bytes 359432 | tf_op jit(solution)/shard_map/ppermute | solution.py:424
  7.4 14.7 %collective-permute-start = (f32[7,8,1152]{2,1,0:T(8,128)S(1)}, f32[7,8,1152]{2,1,0:T(8,128)S(1)}, u32[]{:S(2)}, u32[]{:S(2)}) collective-permute-start(f32[7,8,1152]{2,1,0:T(8,128)S(1)} %get-tuple-element.14), channel_id=1, source_target_pairs={{0,2},{2,0},{4,6},{6,4},{8,10},{10,8},{12,14},{14,12},{1,3},{3,1},... | collective-permute-start | bytes 774152 | tf_op jit(solution)/shard_map/ppermute | solution.py:415
  8.2 13.9 %collective-permute-start.1 = (f32[7,8,1152]{2,1,0:T(8,128)S(1)}, f32[7,8,1152]{2,1,0:T(8,128)S(1)}, u32[]{:S(2)}, u32[]{:S(2)}) collective-permute-start(f32[7,8,1152]{2,1,0:T(8,128)S(1)} %get-tuple-element.15), channel_id=1, source_target_pairs={{2,4},{4,2},{6,8},{8,6},{10,12},{12,10},{3,5},{5,3},{7,9},{9,7},{1... | collective-permute-start | bytes 774152 | tf_op jit(solution)/shard_map/ppermute | solution.py:418
  12.7 9.4 %copy-start.1 = (f32[16,2,4,1152]{3,2,1,0:T(4,128)S(1)}, f32[16,2,4,1152]{3,2,1,0:T(4,128)}, u32[]{:S(2)}) copy-start(f32[16,2,4,1152]{3,2,1,0:T(4,128)} %refs_0_.3) | copy-start | bytes 1769476
  12.7 11.8 %collective-permute-start.4 = (f32[6,8,1152]{2,1,0:T(8,128)S(1)}, f32[6,8,1152]{2,1,0:T(8,128)S(1)}, u32[]{:S(2)}, u32[]{:S(2)}) collective-permute-start(f32[6,8,1152]{2,1,0:T(8,128)S(1)} %shard_map.125), channel_id=1, source_target_pairs={{0,4},{4,8},{8,12},{6,2},{10,6},{14,10},{1,5},{5,9},{9,13},{7,3},{... | collective-permute-start | bytes 663560 | tf_op jit(solution)/shard_map/ppermute | solution.py:421
  17.2 4.9 %copy-start.4 = (f32[64]{0:T(128)S(1)}, f32[64]{0:T(128)}, u32[]{:S(2)}) copy-start(f32[64]{0:T(128)} %constant.8.clone.scale) | copy-start | bytes 772
  24.4 1.7 %collective-permute-start.6 = (f32[9,2,4,1152]{3,2,1,0:T(4,128)S(1)}, f32[9,2,4,1152]{3,2,1,0:T(4,128)S(1)}, u32[]{:S(2)}, u32[]{:S(2)}) collective-permute-start(f32[9,2,4,1152]{3,2,1,0:T(4,128)S(1)} %shard_map.127.own), channel_id=1, source_target_pairs={{0,1},{1,0},{2,3},{3,2},{4,5},{5,4},{6,7},{7,6},{8,9},{9,8},{10,11... | collective-permute-start | bytes 995336 | tf_op jit(solution)/shard_map/ppermute | solution.py:424
  25.0 2.1 %collective-permute-start.5 = (f32[8,2,4,1152]{3,2,1,0:T(4,128)S(1)}, f32[8,2,4,1152]{3,2,1,0:T(4,128)S(1)}, u32[]{:S(2)}, u32[]{:S(2)}) collective-permute-start(f32[8,2,4,1152]{3,2,1,0:T(4,128)S(1)} %shard_map.126.own), channel_id=1, source_target_pairs={{0,1},{1,0},{2,3},{3,2},{4,5},{5,4},{6,7},{7,6},{8,9},{9,8},{10,11... | collective-permute-start | bytes 884744 | tf_op jit(solution)/shard_map/ppermute | solution.py:424

commit v6 on v5

--- a/solution.py
+++ b/solution.py
@@ -13,7 +13,7 @@
 LEVELS = 2
 LANE = 128
 
-COST = dict(zonal=10000, relay=10000, weights=1, mix=1, fin_b=1, fin_a=1, first=1, last=1)
+COST = dict(zonal=10000, relay=10000, early=1, patch=1, fin_b=1, fin_a=1, remap=1)
 
 
 def lanes(chunk):
@@ -123,20 +123,19 @@
     return jnp.concatenate([ref[lev] for lev in range(LEVELS)], axis=0)
 
 
-def weights_kernel(
-    fields, last, scale, c, near, far, x, t, zon_in, zon_t_in, mix, out, zon, zon_t, ws
+def early_kernel(
+    fields, levels, last, scale, columns, c, x, t, zon_in, zon_t_in, mix, out, zon, zon_t, ws
 ):
     lat = lax.axis_index("lat")
-    odd = lax.rem(lat, 2)
     lons = x.shape[-1]
-    block = 3 * LEVELS
+    mix_weights(levels, columns, mix)
     parts = []
     for lev in range(LEVELS):
         own = c[lev]
-        at = slice(block + lev, block + lev + 1)
-        south = jnp.where(odd == 1, near[block, at, :], far[block, at, :])
-        south = jnp.where(lat == 0, -pltpu.roll(own, lons // 2, 1)[0:1], south)
-        parts += [south, own[: ROWS - 1]]
+        parts += [
+            jnp.where(lat == 0, -pltpu.roll(own, lons // 2, 1)[0:1], 0.0),
+            own[: ROWS - 1],
+        ]
     for r, w in enumerate(row_weights(stacked(c), jnp.concatenate(parts, axis=0), scale, lat)):
         for lev in range(LEVELS):
             out[r, lev] = w[lev * ROWS : (lev + 1) * ROWS]
@@ -176,6 +175,20 @@
         pole([(ROWS - d, ROWS + 2 + d) for d in range(1, 4)])
 
 
+def patch_kernel(scale, near, far, weights_in, weights):
+    lat = lax.axis_index("lat")
+    odd = lax.rem(lat, 2)
+    block = 3 * LEVELS
+    rows = slice(block, block + LEVELS)
+    below = jnp.where(odd == 1, near[block, rows, :], far[block, rows, :])
+    below = jnp.where(lat == 0, 0.0, below)
+    low = scale[lat * 2 * ROWS]
+    for r, part in enumerate(face_weights(below)):
+        part = low * part
+        for lev in range(LEVELS):
+            weights[r, lev, 0:1, :] = weights[r, lev, 0:1, :] + part[lev : lev + 1]
+
+
 def zonal_kernel(
     fields, x, t, n, f, c, upper, share, quotient, ground, zon, zon_t, near, far, columns, w
 ):
@@ -227,7 +240,7 @@
 
 def fin_kernel(skip, count, direct, *refs):
     if direct:
-        x, zon, near, far, w, t, zon_t, _, adv = refs
+        x, zon, near, far, w, t, zon_t, adv = refs
     else:
         x, zon, near, far, w, adv = refs
     chunks = w.shape[-1] // LANE
@@ -291,7 +304,7 @@
     out[3 * levels] = ground[...]
 
 
-def mix_kernel(levels, columns, weights):
+def mix_weights(levels, columns, weights):
     group = lax.axis_index("lev")
     for k in range(levels):
         upper = columns[k]
@@ -311,12 +324,23 @@
     return total
 
 
-def remap_fields(skip, own, peer, weights, out, buffer, sems):
+def remap_kernel(
+    levels, own_b, peer_b, own_a, peer_a, weights, columns,
+    out, out_t, out_phi, buffer, thick, sems, column_sems,
+):
     group = lax.axis_index("lev")
     chunks = out.shape[-1] // LANE
     copies = []
     step = 4
-    for first in range(0, buffer.shape[0], step):
+    count = own_b.shape[0] - 1
+
+    def send(source, target, sem):
+        copy = pltpu.make_async_copy(source, target, sem)
+        copy.start()
+        copies.append(copy)
+
+    def blend(first):
+        own, peer, skip = (own_b, peer_b, 0) if first < count else (own_a, peer_a, count)
         for chunk in range(chunks):
             lane = lanes(chunk)
             ws = [
@@ -324,31 +348,17 @@
                 for lev in range(LEVELS)
             ]
             for f in range(first, first + step):
-                values = [adv[f, lev, :, lane] for adv in (own, peer) for lev in range(LEVELS)]
+                values = [adv[f - skip, lev, :, lane] for adv in (own, peer) for lev in range(LEVELS)]
                 for lev in range(LEVELS):
                     buffer[f, lev, :, lane] = mixed(ws[lev], values)
-        copy = pltpu.make_async_copy(
-            buffer.at[pl.ds(first, step)],
-            out.at[pl.ds(skip + first, step)],
-            sems.at[first // step],
-        )
-        copy.start()
-        copies.append(copy)
-    return copies
-
-
-def remap_last_kernel(skip, own, peer, weights, out_in, out, buffer, sems):
-    for copy in remap_fields(skip, own, peer, weights, out, buffer, sems):
-        copy.wait()
-
-
-def remap_first_kernel(
-    levels, own, peer, weights, columns, out, out_t, out_phi, buffer, thick, sems, column_sems
-):
-    group = lax.axis_index("lev")
-    count = buffer.shape[0]
-    vapour = [adv[0, lev] for adv in (own, peer) for lev in range(LEVELS)]
-    temp = [adv[count, lev] for adv in (own, peer) for lev in range(LEVELS)]
+        send(buffer.at[pl.ds(first, step)], out.at[pl.ds(first, step)], sems.at[first // step])
+
+    fields = buffer.shape[0]
+    for first in range(0, fields - step, step):
+        blend(first)
+
+    vapour = [adv[0, lev] for adv in (own_b, peer_b) for lev in range(LEVELS)]
+    temp = [adv[count, lev] for adv in (own_b, peer_b) for lev in range(LEVELS)]
     for k in range(levels):
         ws = [weights[k, s] for s in range(2 * LEVELS)]
         water = mixed(ws, vapour)
@@ -360,15 +370,11 @@
         layer = thick[k]
         thick[k] = deeper + 0.5 * layer
         deeper = deeper + layer
-    copies = [
-        pltpu.make_async_copy(
-            thick.at[pl.ds(at + group * LEVELS, LEVELS)], target, column_sems.at[i]
-        )
-        for i, (at, target) in enumerate(((0, out_phi), (levels, out_t)))
-    ]
+    mine = group * LEVELS
+    send(thick.at[pl.ds(mine, LEVELS)], out_phi, column_sems.at[0])
+    send(thick.at[pl.ds(levels + mine, LEVELS)], out_t, column_sems.at[1])
+    blend(fields - step)
     for copy in copies:
-        copy.start()
-    for copy in copies + remap_fields(0, own, peer, weights, out, buffer, sems):
         copy.wait()
 
 
@@ -470,23 +476,33 @@
         jnp.concatenate([peer_columns, columns], -1),
     )
 
-    mix = call(
-        functools.partial(mix_kernel, levels), (levels, 2 * LEVELS, ROWS, lons), cost=COST["mix"]
-    )(columns)
-    weights, zon, zon_t = call(
-        functools.partial(weights_kernel, fields, bands - 1),
-        [(ROWS + 6, LEVELS, ROWS, lons), x.shape, t.shape],
+    mix, weights, zon, zon_t = call(
+        functools.partial(early_kernel, fields, levels, bands - 1),
+        [
+            (levels, 2 * LEVELS, ROWS, lons),
+            (ROWS + 6, LEVELS, ROWS, lons),
+            x.shape,
+            t.shape,
+        ],
         [(3, LEVELS * ROWS, lons)],
-        [smem] + [vmem] * 8,
-        cost=COST["weights"],
-        aliases={6: 1, 7: 2},
-    )(scale, c, near_b, far_b, x, t, zon, zon_t, mix)
+        [smem] + [vmem] * 6,
+        cost=COST["early"],
+        aliases={5: 2, 6: 3},
+    )(scale, columns, c, x, t, zon, zon_t)
+    weights = call(
+        patch_kernel,
+        weights.shape,
+        (),
+        [smem] + [vmem] * 3,
+        cost=COST["patch"],
+        aliases={3: 0},
+    )(scale, near_b, far_b, weights)
 
     adv_b = call(
         functools.partial(fin_kernel, 0, direct, True),
         (direct + 1,) + x.shape[1:],
         cost=COST["fin_b"],
-    )(x, zon, near_b, far_b, weights, t, zon_t, mix)
+    )(x, zon, near_b, far_b, weights, t, zon_t)
     peer_b = other_core(adv_b)
     adv_a = call(
         functools.partial(fin_kernel, direct, swapped, False),
@@ -496,28 +512,18 @@
     peer_a = other_core(adv_a)
 
     anywhere = pl.BlockSpec(memory_space=pl.ANY)
-    out, out_t, out_phi = call(
-        functools.partial(remap_first_kernel, levels),
+    return call(
+        functools.partial(remap_kernel, levels),
         [x.shape, t.shape, t.shape],
         [
-            (direct,) + x.shape[1:],
+            x.shape,
             (2 * levels, ROWS, lons),
-            pltpu.SemaphoreType.DMA((direct // 4,)),
+            pltpu.SemaphoreType.DMA((fields // 4,)),
             pltpu.SemaphoreType.DMA((2,)),
         ],
-        cost=COST["first"],
+        cost=COST["remap"],
         out_specs=(anywhere,) * 3,
-    )(adv_b, peer_b, mix, columns)
-    out = call(
-        functools.partial(remap_last_kernel, direct),
-        x.shape,
-        [(swapped,) + x.shape[1:], pltpu.SemaphoreType.DMA((swapped // 4,))],
-        [vmem] * 3 + [anywhere],
-        cost=COST["last"],
-        aliases={3: 0},
-        out_specs=anywhere,
-    )(adv_a, peer_a, mix, out)
-    return out, out_t, out_phi
+    )(adv_b, peer_b, adv_a, peer_a, mix, columns)
 
 
 def solution(mesh):

time: 28.1 us -> 27 us (0.961)
  waiting for transfers between devices: 9.29 us -> 7.5 us
  local copies, waits for them, and re-layouts: 1.1 us -> 1.74 us
    ppermute x2, waiting for transfers between devices: 8.67 us -> 6.28 us  [swap(): return lax.ppermute(v, 'lat', pairs)]
    unnamed x22, local copies, waits for them, and re-layouts: 1.1 us -> 1.74 us
    ppermute x3, waiting for transfers between devices: 0.61 us -> 1.21 us  [other_core(): return lax.ppermute(v, 'lev', cores)]
    pallas_call x4 -> x3, Pallas kernels: 3.58 us -> 3.54 us  [the longest x1 1.82 us: on_device(): call(functools.partial(early_kernel, fields, levels, bands - 1), [(levels...]
  transfers between devices with their start and end apart: 7 -> 7, of which waited for: 3 -> 4; matrix products, arithmetic and copies ran while one was open for 1% -> 1% of each run, Pallas kernels for 22% -> 22%
where the time goes in v6:
time: 27 us; the launch traced here: 26.6 us
  starting transfers between devices  9.29 us (34%)
  waiting for transfers between devices  7.5 us (28%)
  Pallas kernels  7.08 us (26%)
  local copies, waits for them, and re-layouts  1.74 us (6%)
  between operations  0.84 us (3%)
    ppermute x2, waiting for transfers between devices, swap(): return lax.ppermute(v, 'lat', pairs)  6.28 us
    ppermute x1, starting transfers between devices, pass_on(): return lax.ppermute(v, 'lat', relays)  4.19 us
    ppermute x2, starting transfers between devices, swap(): return lax.ppermute(v, 'lat', pairs)  3.75 us
    pallas_call x1, Pallas kernels, on_device(): call(functools.partial(zonal_kernel, fields), [x.shape, t.shape, direct_s...  2.5 us
    pallas_call x1, Pallas kernels, on_device(): call(functools.partial(early_kernel, fields, levels, bands - 1), [(levels...  1.82 us
    unnamed x22, local copies, waits for them, and re-layouts  1.74 us
    ppermute x3, waiting for transfers between devices, other_core(): return lax.ppermute(v, 'lev', cores)  1.21 us
    pallas_call x1, Pallas kernels, on_device(): call(functools.partial(remap_kernel, levels), [x.shape, t.shape, t.shape]...  1.07 us
  transfers between devices with their start and end apart: 7, of which 4 were waited for; matrix products, arithmetic and copies ran while one was open for 1% of the time, Pallas kernels for 22%

profile of v6, /device:TPU:0, one launch (start us, length us, event | category | flops | bytes accessed | tf_op | source)
XLA Modules:
  0.0 26.6 jit_solution(13971433801912682010)
XLA Ops:
  0.6 0.0 copy-start
  0.6 1.1 %copy-done = f32[16,2,4,1152]{3,2,1,0:T(4,128)S(1)} copy-done((f32[16,2,4,1152]{3,2,1,0:T(4,128)S(1)}, f32[16,2,4,1152]{3,2,1,0:T(4,128)}, u32[]{:S(2)}) %copy-start) | copy-done | bytes 589848
  1.7 0.0 copy-start.2
  1.7 0.0 copy-start.3
  1.7 0.0 copy-start.5
  1.7 0.0 copy-start.6
  1.7 0.0 copy-start.7
  1.7 0.0 copy-start.8
  1.7 0.0 copy-start.9
  1.7 0.0 copy-start.10
  1.8 3.0 %collective-permute-start.4 = (f32[8,2,4,1152]{3,2,1,0:T(4,128)S(1)}, f32[8,2,4,1152]{3,2,1,0:T(4,128)S(1)}, u32[]{:S(2)}, u32[]{:S(2)}) collective-permute-start(f32[8,2,4,1152]{3,2,1,0:T(4,128)S(1)} %shard_map.125), channel_id=1, source_target_pairs={{0,2},{2,0},{4,6},{6,4},{8,10},{10,8},{12,14},{14,12},{1,3},{3,1},... | collective-permute-start | bytes 884744 | tf_op jit(solution)/shard_map/ppermute | solution.py:421
  4.8 0.0 copy-done.2
  4.8 0.0 copy-done.3
  4.8 0.0 copy-done.5
  4.8 0.0 copy-done.6
  4.8 0.0 copy-done.7
  4.8 0.0 copy-done.8
  4.8 0.0 copy-done.9
  4.8 0.0 copy-done.10
  4.8 2.5 %shard_map.121 = (f32[16,2,4,1152]{3,2,1,0:T(4,128)S(1)}, f32[2,4,1152]{2,1,0:T(4,128)S(1)}, f32[7,8,1152]{2,1,0:T(8,128)S(1)}, f32[7,8,1152]{2,1,0:T(8,128)S(1)}, f32[13,4,576]{2,1,0:T(4,128)S(1)}) custom-call(f32[16,2,4,1152]{3,2,1,0:T(4,128)S(1)} %copy-done, f32[2,4,1152]{2,1,0:T(4,128)S(1)} %copy-done.2, s32[2,4,1152]{2,1,0:T(4,128)S(1)} %copy-done.8, ...), custom_call_target="tpu_custom_call" | custom-call | flops 10000000000 | bytes 1000 | tf_op jit(solution)/shard_map/pallas_call | solution.py:444
  7.3 0.1 collective-permute-start
  7.4 0.7 %collective-permute-start.1 = (f32[7,8,1152]{2,1,0:T(8,128)S(1)}, f32[7,8,1152]{2,1,0:T(8,128)S(1)}, u32[]{:S(2)}, u32[]{:S(2)}) collective-permute-start(f32[7,8,1152]{2,1,0:T(8,128)S(1)} %get-tuple-element.16), channel_id=1, source_target_pairs={{0,2},{2,0},{4,6},{6,4},{8,10},{10,8},{12,14},{14,12},{1,3},{3,1},... | collective-permute-start | bytes 774152 | tf_op jit(solution)/shard_map/ppermute | solution.py:421
  8.2 0.7 %collective-permute-start.2 = (f32[7,8,1152]{2,1,0:T(8,128)S(1)}, f32[7,8,1152]{2,1,0:T(8,128)S(1)}, u32[]{:S(2)}, u32[]{:S(2)}) collective-permute-start(f32[7,8,1152]{2,1,0:T(8,128)S(1)} %get-tuple-element.17), channel_id=1, source_target_pairs={{2,4},{4,2},{6,8},{8,6},{10,12},{12,10},{3,5},{5,3},{7,9},{9,7},{1... | collective-permute-start | bytes 774152 | tf_op jit(solution)/shard_map/ppermute | solution.py:424
  8.9 3.8 %collective-permute-done.4.swapped.refs_2_ = f32[8,2,4,1152]{3,2,1,0:T(4,128)S(1)} collective-permute-done((f32[8,2,4,1152]{3,2,1,0:T(4,128)S(1)}, f32[8,2,4,1152]{3,2,1,0:T(4,128)S(1)}, u32[]{:S(2)}, u32[]{:S(2)}) %collective-permute-start.4) | collective-permute-done | bytes 294944 | tf_op jit(solution)/shard_map/ppermute | solution.py:421
  12.6 0.0 copy-start.1
  12.6 0.1 shard_map.126
  12.7 4.2 %collective-permute-start.5 = (f32[6,8,1152]{2,1,0:T(8,128)S(1)}, f32[6,8,1152]{2,1,0:T(8,128)S(1)}, u32[]{:S(2)}, u32[]{:S(2)}) collective-permute-start(f32[6,8,1152]{2,1,0:T(8,128)S(1)} %shard_map.126), channel_id=1, source_target_pairs={{0,4},{4,8},{8,12},{6,2},{10,6},{14,10},{1,5},{5,9},{9,13},{7,3},{... | collective-permute-start | bytes 663560 | tf_op jit(solution)/shard_map/ppermute | solution.py:427
  16.9 0.0 collective-permute-done
  16.9 0.2 maximum_select_fusion.columns
  17.1 0.0 copy-start.4
  17.1 0.0 copy-done.1
  17.1 0.6 %copy-done.4 = f32[64]{0:T(128)S(1)} copy-done((f32[64]{0:T(128)S(1)}, f32[64]{0:T(128)}, u32[]{:S(2)}) %copy-start.4) | copy-done | bytes 280
  17.8 1.8 %shard_map.122 = (f32[4,4,4,1152]{3,2,1,0:T(4,128)S(1)}, f32[10,2,4,1152]{3,2,1,0:T(4,128)S(1)}, f32[16,2,4,1152]{3,2,1,0:T(4,128)S(1)}, f32[2,4,1152]{2,1,0:T(4,128)S(1)}) custom-call(f32[64]{0:T(128)S(1)} %copy-done.4, f32[13,4,1152]{2,1,0:T(4,128)S(1)} %maximum_select_fusion.columns, ...), custom_call_target="tpu_custom_call", output_to_operand_aliasing={{2}: (5, {}), {3}: (6, {})} | custom-call | flops 1000000 | bytes 1000 | tf_op jit(solution)/shard_map/pallas_call | solution.py:479
  19.6 2.5 %collective-permute-done.1.near.refs_2_ = f32[7,8,1152]{2,1,0:T(8,128)S(1)} collective-permute-done((f32[7,8,1152]{2,1,0:T(8,128)S(1)}, f32[7,8,1152]{2,1,0:T(8,128)S(1)}, u32[]{:S(2)}, u32[]{:S(2)}) %collective-permute-start.1) | collective-permute-done | bytes 258080 | tf_op jit(solution)/shard_map/ppermute | solution.py:421
  22.1 0.0 collective-permute-done.2.far.refs_3_
  22.1 0.6 %shard_map.123.refs_4_ = f32[10,2,4,1152]{3,2,1,0:T(4,128)S(1)} custom-call(f32[64]{0:T(128)S(1)} %copy-done.4, f32[7,8,1152]{2,1,0:T(8,128)S(1)} %collective-permute-done.1.near.refs_2_, f32[7,8,1152]{2,1,0:T(8,128)S(1)} %collective-permute-done.2.far.refs_3_, f32[10,2,4,1152]{3,2,1,0:T(4,128)S(1)} %get-tuple-element.18.weights_in), custom_call_target="tpu_custom_call", output_to_operand_aliasing={{}: (3, {})} | custom-call | flops 1000000 | bytes 1000 | tf_op jit(solution)/shard_map/pallas_call | solution.py:492
  22.8 0.5 %shard_map.124.own_b = f32[9,2,4,1152]{3,2,1,0:T(4,128)S(1)} custom-call(f32[16,2,4,1152]{3,2,1,0:T(4,128)S(1)} %copy-done.1, f32[16,2,4,1152]{3,2,1,0:T(4,128)S(1)} %get-tuple-element.15.refs_1_, f32[7,8,1152]{2,1,0:T(8,128)S(1)} %collective-permute-done.1.near.refs_2_, f32[7,8,1152]{2,1,0:T(8,128)S(1)} %collective-permute-done.2.far.refs_3_, ...), custom_call_target="tpu_custom_call" | custom-call | flops 1000000 | bytes 1000 | tf_op jit(solution)/shard_map/pallas_call | solution.py:501
  23.3 0.1 collective-permute-start.3
  23.3 0.0 collective-permute-done.5.refs_3_
  23.4 0.5 %shard_map.127.own_a = f32[8,2,4,1152]{3,2,1,0:T(4,128)S(1)} custom-call(f32[16,2,4,1152]{3,2,1,0:T(4,128)S(1)} %copy-done.1, f32[16,2,4,1152]{3,2,1,0:T(4,128)S(1)} %get-tuple-element.15.refs_1_, f32[8,2,4,1152]{3,2,1,0:T(4,128)S(1)} %collective-permute-done.4.swapped.refs_2_, f32[6,8,1152]{2,1,0:T(8,128)S(1)} %collective-permute-done.5.refs_3_, ...), custom_call_target="tpu_custom_call" | custom-call | flops 1000000 | bytes 1000 | tf_op jit(solution)/shard_map/pallas_call | solution.py:507
  23.8 0.5 %collective-permute-start.6 = (f32[8,2,4,1152]{3,2,1,0:T(4,128)S(1)}, f32[8,2,4,1152]{3,2,1,0:T(4,128)S(1)}, u32[]{:S(2)}, u32[]{:S(2)}) collective-permute-start(f32[8,2,4,1152]{3,2,1,0:T(4,128)S(1)} %shard_map.127.own_a), channel_id=1, source_target_pairs={{0,1},{1,0},{2,3},{3,2},{4,5},{5,4},{6,7},{7,6},{8,9},{9,8},{10,11... | collective-permute-start | bytes 884744 | tf_op jit(solution)/shard_map/ppermute | solution.py:430
  24.4 0.6 %collective-permute-done.3.peer_b = f32[9,2,4,1152]{3,2,1,0:T(4,128)S(1)} collective-permute-done((f32[9,2,4,1152]{3,2,1,0:T(4,128)S(1)}, f32[9,2,4,1152]{3,2,1,0:T(4,128)S(1)}, u32[]{:S(2)}, u32[]{:S(2)}) %collective-permute-start.3) | collective-permute-done | bytes 331808 | tf_op jit(solution)/shard_map/ppermute | solution.py:430
  25.0 0.6 %collective-permute-done.6.peer_a = f32[8,2,4,1152]{3,2,1,0:T(4,128)S(1)} collective-permute-done((f32[8,2,4,1152]{3,2,1,0:T(4,128)S(1)}, f32[8,2,4,1152]{3,2,1,0:T(4,128)S(1)}, u32[]{:S(2)}, u32[]{:S(2)}) %collective-permute-start.6) | collective-permute-done | bytes 294944 | tf_op jit(solution)/shard_map/ppermute | solution.py:430
  25.6 1.1 %shard_map.128 = (f32[16,2,4,1152]{3,2,1,0:T(4,128)}, f32[2,4,1152]{2,1,0:T(4,128)}, f32[2,4,1152]{2,1,0:T(4,128)}) custom-call(f32[9,2,4,1152]{3,2,1,0:T(4,128)S(1)} %shard_map.124.own_b, f32[9,2,4,1152]{3,2,1,0:T(4,128)S(1)} %collective-permute-done.3.peer_b, f32[8,2,4,1152]{3,2,1,0:T(4,128)S(1)} %shard_map.127.own_a, ...), custom_call_target="tpu_custom_call" | custom-call | flops 1000000 | bytes 1000 | tf_op jit(solution)/shard_map/pallas_call | solution.py:515
  (1 shorter events, 0.0 us)
Async XLA Ops:
  0.6 1.1 %copy-start = (f32[16,2,4,1152]{3,2,1,0:T(4,128)S(1)}, f32[16,2,4,1152]{3,2,1,0:T(4,128)}, u32[]{:S(2)}) copy-start(f32[16,2,4,1152]{3,2,1,0:T(4,128)} %refs_0_.3) | copy-start | bytes 1769476
  1.7 3.1 %copy-start.2 = (f32[2,4,1152]{2,1,0:T(4,128)S(1)}, f32[2,4,1152]{2,1,0:T(4,128)}, u32[]{:S(2)}) copy-start(f32[2,4,1152]{2,1,0:T(4,128)} %refs_5_.1) | copy-start | bytes 110596
  1.7 3.1 %copy-start.3 = (f32[2,4,1152]{2,1,0:T(4,128)S(1)}, f32[2,4,1152]{2,1,0:T(4,128)}, u32[]{:S(2)}) copy-start(f32[2,4,1152]{2,1,0:T(4,128)} %c.3) | copy-start | bytes 110596
  1.7 3.1 %copy-start.5 = (s32[4,4,576]{2,1,0:T(4,128)S(1)}, s32[4,4,576]{2,1,0:T(4,128)}, u32[]{:S(2)}) copy-start(s32[4,4,576]{2,1,0:T(4,128)} %upper.1) | copy-start | bytes 110596
  1.7 3.1 %copy-start.6 = (f32[4,4,576]{2,1,0:T(4,128)S(1)}, f32[4,4,576]{2,1,0:T(4,128)}, u32[]{:S(2)}) copy-start(f32[4,4,576]{2,1,0:T(4,128)} %share.1) | copy-start | bytes 110596
  1.7 3.1 %copy-start.7 = (f32[4,4,576]{2,1,0:T(4,128)S(1)}, f32[4,4,576]{2,1,0:T(4,128)}, u32[]{:S(2)}) copy-start(f32[4,4,576]{2,1,0:T(4,128)} %quotient.1) | copy-start | bytes 110596
  1.7 3.1 %copy-start.8 = (s32[2,4,1152]{2,1,0:T(4,128)S(1)}, s32[2,4,1152]{2,1,0:T(4,128)}, u32[]{:S(2)}) copy-start(s32[2,4,1152]{2,1,0:T(4,128)} %n.1) | copy-start | bytes 110596
  1.7 3.1 %copy-start.9 = (f32[2,4,1152]{2,1,0:T(4,128)S(1)}, f32[2,4,1152]{2,1,0:T(4,128)}, u32[]{:S(2)}) copy-start(f32[2,4,1152]{2,1,0:T(4,128)} %f.1) | copy-start | bytes 110596
  1.7 3.1 %copy-start.10 = (f32[4,576]{1,0:T(4,128)S(1)}, f32[4,576]{1,0:T(4,128)}, u32[]{:S(2)}) copy-start(f32[4,576]{1,0:T(4,128)} %ground.1) | copy-start | bytes 27652
  1.8 10.8 %collective-permute-start.4 = (f32[8,2,4,1152]{3,2,1,0:T(4,128)S(1)}, f32[8,2,4,1152]{3,2,1,0:T(4,128)S(1)}, u32[]{:S(2)}, u32[]{:S(2)}) collective-permute-start(f32[8,2,4,1152]{3,2,1,0:T(4,128)S(1)} %shard_map.125), channel_id=1, source_target_pairs={{0,2},{2,0},{4,6},{6,4},{8,10},{10,8},{12,14},{14,12},{1,3},{3,1},... | collective-permute-start | bytes 884744 | tf_op jit(solution)/shard_map/ppermute | solution.py:421
  7.3 9.6 %collective-permute-start = (f32[13,4,576]{2,1,0:T(4,128)S(1)}, f32[13,4,576]{2,1,0:T(4,128)S(1)}, u32[]{:S(2)}, u32[]{:S(2)}) collective-permute-start(f32[13,4,576]{2,1,0:T(4,128)S(1)} %get-tuple-element.12), channel_id=1, source_target_pairs={{0,1},{1,0},{2,3},{3,2},{4,5},{5,4},{6,7},{7,6},{8,9},{9,8},{10,11... | collective-permute-start | bytes 359432 | tf_op jit(solution)/shard_map/ppermute | solution.py:430
  7.4 14.7 %collective-permute-start.1 = (f32[7,8,1152]{2,1,0:T(8,128)S(1)}, f32[7,8,1152]{2,1,0:T(8,128)S(1)}, u32[]{:S(2)}, u32[]{:S(2)}) collective-permute-start(f32[7,8,1152]{2,1,0:T(8,128)S(1)} %get-tuple-element.16), channel_id=1, source_target_pairs={{0,2},{2,0},{4,6},{6,4},{8,10},{10,8},{12,14},{14,12},{1,3},{3,1},... | collective-permute-start | bytes 774152 | tf_op jit(solution)/shard_map/ppermute | solution.py:421
  8.2 13.9 %collective-permute-start.2 = (f32[7,8,1152]{2,1,0:T(8,128)S(1)}, f32[7,8,1152]{2,1,0:T(8,128)S(1)}, u32[]{:S(2)}, u32[]{:S(2)}) collective-permute-start(f32[7,8,1152]{2,1,0:T(8,128)S(1)} %get-tuple-element.17), channel_id=1, source_target_pairs={{2,4},{4,2},{6,8},{8,6},{10,12},{12,10},{3,5},{5,3},{7,9},{9,7},{1... | collective-permute-start | bytes 774152 | tf_op jit(solution)/shard_map/ppermute | solution.py:424
  12.6 4.5 %copy-start.1 = (f32[16,2,4,1152]{3,2,1,0:T(4,128)S(1)}, f32[16,2,4,1152]{3,2,1,0:T(4,128)}, u32[]{:S(2)}) copy-start(f32[16,2,4,1152]{3,2,1,0:T(4,128)} %refs_0_.3) | copy-start | bytes 1769476
  12.7 10.7 %collective-permute-start.5 = (f32[6,8,1152]{2,1,0:T(8,128)S(1)}, f32[6,8,1152]{2,1,0:T(8,128)S(1)}, u32[]{:S(2)}, u32[]{:S(2)}) collective-permute-start(f32[6,8,1152]{2,1,0:T(8,128)S(1)} %shard_map.126), channel_id=1, source_target_pairs={{0,4},{4,8},{8,12},{6,2},{10,6},{14,10},{1,5},{5,9},{9,13},{7,3},{... | collective-permute-start | bytes 663560 | tf_op jit(solution)/shard_map/ppermute | solution.py:427
  17.1 0.7 %copy-start.4 = (f32[64]{0:T(128)S(1)}, f32[64]{0:T(128)}, u32[]{:S(2)}) copy-start(f32[64]{0:T(128)} %constant.8.clone.scale) | copy-start | bytes 772
  23.3 1.7 %collective-permute-start.3 = (f32[9,2,4,1152]{3,2,1,0:T(4,128)S(1)}, f32[9,2,4,1152]{3,2,1,0:T(4,128)S(1)}, u32[]{:S(2)}, u32[]{:S(2)}) collective-permute-start(f32[9,2,4,1152]{3,2,1,0:T(4,128)S(1)} %shard_map.124.own_b), channel_id=1, source_target_pairs={{0,1},{1,0},{2,3},{3,2},{4,5},{5,4},{6,7},{7,6},{8,9},{9,8},{10,11... | collective-permute-start | bytes 995336 | tf_op jit(solution)/shard_map/ppermute | solution.py:430
  23.8 1.7 %collective-permute-start.6 = (f32[8,2,4,1152]{3,2,1,0:T(4,128)S(1)}, f32[8,2,4,1152]{3,2,1,0:T(4,128)S(1)}, u32[]{:S(2)}, u32[]{:S(2)}) collective-permute-start(f32[8,2,4,1152]{3,2,1,0:T(4,128)S(1)} %shard_map.127.own_a), channel_id=1, source_target_pairs={{0,1},{1,0},{2,3},{3,2},{4,5},{5,4},{6,7},{7,6},{8,9},{9,8},{10,11... | collective-permute-start | bytes 884744 | tf_op jit(solution)/shard_map/ppermute | solution.py:430

commit v7 on v6

--- a/solution.py
+++ b/solution.py
@@ -13,7 +13,7 @@
 LEVELS = 2
 LANE = 128
 
-COST = dict(zonal=10000, relay=10000, early=1, patch=1, fin_b=1, fin_a=1, remap=1)
+COST = dict(zonal=10000, relay=10000, early=1, patch=1, fin_b=1, fin_a=1, first=1, last=1)
 
 
 def lanes(chunk):
@@ -34,9 +34,16 @@
         body(False)
 
 
-def copy_kernel(x, out):
-    skip = x.shape[0] - out.shape[0]
-    out[...] = x[skip:]
+def copy_kernel(x, out, sems):
+    count = out.shape[0]
+    skip = x.shape[0] - count
+    copies = [
+        pltpu.make_async_copy(x.at[skip + i], out.at[i], sems.at[i]) for i in range(count)
+    ]
+    for copy in copies:
+        copy.start()
+    for copy in copies:
+        copy.wait()
 
 
 def side_rows(to_north):
@@ -124,11 +131,12 @@
 
 
 def early_kernel(
-    fields, levels, last, scale, columns, c, x, t, zon_in, zon_t_in, mix, out, zon, zon_t, ws
+    fields, levels, last, scale, columns, c, x, t, zon_in, zon_t_in, mix, out, zon, zon_t, factor, ws
 ):
     lat = lax.axis_index("lat")
     lons = x.shape[-1]
     mix_weights(levels, columns, mix)
+    factor[...] = jnp.full(factor.shape, jnp.where(lat == 0, 0.0, scale[lat * 2 * ROWS]))
     parts = []
     for lev in range(LEVELS):
         own = c[lev]
@@ -175,16 +183,12 @@
         pole([(ROWS - d, ROWS + 2 + d) for d in range(1, 4)])
 
 
-def patch_kernel(scale, near, far, weights_in, weights):
-    lat = lax.axis_index("lat")
-    odd = lax.rem(lat, 2)
+def patch_kernel(factor, near, far, weights_in, weights):
     block = 3 * LEVELS
     rows = slice(block, block + LEVELS)
-    below = jnp.where(odd == 1, near[block, rows, :], far[block, rows, :])
-    below = jnp.where(lat == 0, 0.0, below)
-    low = scale[lat * 2 * ROWS]
+    below = jnp.where(parity() == 1, near[block, rows, :], far[block, rows, :])
     for r, part in enumerate(face_weights(below)):
-        part = low * part
+        part = factor[...] * part
         for lev in range(LEVELS):
             weights[r, lev, 0:1, :] = weights[r, lev, 0:1, :] + part[lev : lev + 1]
 
@@ -324,41 +328,24 @@
     return total
 
 
-def remap_kernel(
-    levels, own_b, peer_b, own_a, peer_a, weights, columns,
-    out, out_t, out_phi, buffer, thick, sems, column_sems,
-):
+def blend(own, peer, weights, out, fields, skip=0):
     group = lax.axis_index("lev")
-    chunks = out.shape[-1] // LANE
-    copies = []
-    step = 4
-    count = own_b.shape[0] - 1
-
-    def send(source, target, sem):
-        copy = pltpu.make_async_copy(source, target, sem)
-        copy.start()
-        copies.append(copy)
-
-    def blend(first):
-        own, peer, skip = (own_b, peer_b, 0) if first < count else (own_a, peer_a, count)
-        for chunk in range(chunks):
-            lane = lanes(chunk)
-            ws = [
-                [weights[group * LEVELS + lev, s, :, lane] for s in range(2 * LEVELS)]
-                for lev in range(LEVELS)
-            ]
-            for f in range(first, first + step):
-                values = [adv[f - skip, lev, :, lane] for adv in (own, peer) for lev in range(LEVELS)]
-                for lev in range(LEVELS):
-                    buffer[f, lev, :, lane] = mixed(ws[lev], values)
-        send(buffer.at[pl.ds(first, step)], out.at[pl.ds(first, step)], sems.at[first // step])
-
-    fields = buffer.shape[0]
-    for first in range(0, fields - step, step):
-        blend(first)
-
-    vapour = [adv[0, lev] for adv in (own_b, peer_b) for lev in range(LEVELS)]
-    temp = [adv[count, lev] for adv in (own_b, peer_b) for lev in range(LEVELS)]
+    for chunk in range(own.shape[-1] // LANE):
+        lane = lanes(chunk)
+        ws = [
+            [weights[group * LEVELS + lev, s, :, lane] for s in range(2 * LEVELS)]
+            for lev in range(LEVELS)
+        ]
+        for f in fields:
+            values = [adv[f, lev, :, lane] for adv in (own, peer) for lev in range(LEVELS)]
+            for lev in range(LEVELS):
+                out[skip + f, lev, :, lane] = mixed(ws[lev], values)
+
+
+def remap_first_kernel(levels, own, peer, weights, columns, out, thick):
+    count = out.shape[0]
+    vapour = [adv[0, lev] for adv in (own, peer) for lev in range(LEVELS)]
+    temp = [adv[count, lev] for adv in (own, peer) for lev in range(LEVELS)]
     for k in range(levels):
         ws = [weights[k, s] for s in range(2 * LEVELS)]
         water = mixed(ws, vapour)
@@ -370,10 +357,29 @@
         layer = thick[k]
         thick[k] = deeper + 0.5 * layer
         deeper = deeper + layer
+    blend(own, peer, weights, out, range(count))
+
+
+def remap_last_kernel(levels, own, peer, weights, first, thick, out, out_t, out_phi, buffer, sems):
+    group = lax.axis_index("lev")
+    count = first.shape[0]
+    copies = []
+
+    def send(source, target):
+        copy = pltpu.make_async_copy(source, target, sems.at[len(copies)])
+        copy.start()
+        copies.append(copy)
+
+    half = count // 2
+    for start in (0, half):
+        send(first.at[pl.ds(start, half)], out.at[pl.ds(start, half)])
     mine = group * LEVELS
-    send(thick.at[pl.ds(mine, LEVELS)], out_phi, column_sems.at[0])
-    send(thick.at[pl.ds(levels + mine, LEVELS)], out_t, column_sems.at[1])
-    blend(fields - step)
+    send(thick.at[pl.ds(mine, LEVELS)], out_phi)
+    send(thick.at[pl.ds(levels + mine, LEVELS)], out_t)
+    step = 2
+    for start in range(0, buffer.shape[0], step):
+        blend(own, peer, weights, buffer, range(start, start + step))
+        send(buffer.at[pl.ds(start, step)], out.at[pl.ds(count + start, step)])
     for copy in copies:
         copy.wait()
 
@@ -440,7 +446,14 @@
     swapped = fields - direct
     direct_shape = (3 * LEVELS + 1, direct, lons)
 
-    near_a = swap(call(copy_kernel, (swapped,) + x.shape[1:])(x))
+    payload = call(
+        copy_kernel,
+        (swapped,) + x.shape[1:],
+        [pltpu.SemaphoreType.DMA((swapped,))],
+        [pl.BlockSpec(memory_space=pltpu.HBM)],
+        limit=60,
+    )(x)
+    near_a = swap(payload)
     zon, zon_t, near_rows, far_rows, columns = call(
         functools.partial(zonal_kernel, fields),
         [
@@ -476,13 +489,14 @@
         jnp.concatenate([peer_columns, columns], -1),
     )
 
-    mix, weights, zon, zon_t = call(
+    mix, weights, zon, zon_t, factor = call(
         functools.partial(early_kernel, fields, levels, bands - 1),
         [
             (levels, 2 * LEVELS, ROWS, lons),
             (ROWS + 6, LEVELS, ROWS, lons),
             x.shape,
             t.shape,
+            (LEVELS, lons),
         ],
         [(3, LEVELS * ROWS, lons)],
         [smem] + [vmem] * 6,
@@ -492,11 +506,9 @@
     weights = call(
         patch_kernel,
         weights.shape,
-        (),
-        [smem] + [vmem] * 3,
         cost=COST["patch"],
         aliases={3: 0},
-    )(scale, near_b, far_b, weights)
+    )(factor, near_b, far_b, weights)
 
     adv_b = call(
         functools.partial(fin_kernel, 0, direct, True),
@@ -512,18 +524,18 @@
     peer_a = other_core(adv_a)
 
     anywhere = pl.BlockSpec(memory_space=pl.ANY)
+    first, thick = call(
+        functools.partial(remap_first_kernel, levels),
+        [(direct,) + x.shape[1:], (2 * levels, ROWS, lons)],
+        cost=COST["first"],
+    )(adv_b, peer_b, mix, columns)
     return call(
-        functools.partial(remap_kernel, levels),
+        functools.partial(remap_last_kernel, levels),
         [x.shape, t.shape, t.shape],
-        [
-            x.shape,
-            (2 * levels, ROWS, lons),
-            pltpu.SemaphoreType.DMA((fields // 4,)),
-            pltpu.SemaphoreType.DMA((2,)),
-        ],
-        cost=COST["remap"],
+        [(swapped,) + x.shape[1:], pltpu.SemaphoreType.DMA((4 + swapped // 2,))],
+        cost=COST["last"],
         out_specs=(anywhere,) * 3,
-    )(adv_b, peer_b, adv_a, peer_a, mix, columns)
+    )(adv_a, peer_a, mix, first, thick)
 
 
 def solution(mesh):

time: 27 us -> 27.1 us (level)
  Pallas kernels: 7.08 us -> 8.27 us
  local copies, waits for them, and re-layouts: 1.74 us -> 0.69 us
  starting transfers between devices: 9.29 us -> 8.51 us
  waiting for transfers between devices: 7.5 us -> 8.26 us
    pallas_call x3 -> x4, Pallas kernels: 1.74 us -> 2.91 us  [the longest x1 1.72 us: on_device(): call(copy_kernel, (swapped,) + x.shape[1:], [pltpu.SemaphoreType.DMA((swa...]
    unnamed x22 -> x20, local copies, waits for them, and re-layouts: 1.74 us -> 0.69 us
    ppermute x2, waiting for transfers between devices: 6.28 us -> 7.26 us  [swap(): return lax.ppermute(v, 'lat', pairs)]
    ppermute x2, starting transfers between devices: 3.75 us -> 3.11 us  [swap(): return lax.ppermute(v, 'lat', pairs)]
  transfers between devices with their start and end apart: 7 -> 7, of which waited for: 4 -> 4; matrix products, arithmetic and copies ran while one was open for 1% -> 1% of each run, Pallas kernels for 22% -> 21%
where the time goes in v7:
time: 27.1 us; the launch traced here: 26.8 us
  starting transfers between devices  8.51 us (31%)
  Pallas kernels  8.27 us (31%)
  waiting for transfers between devices  8.26 us (30%)
  between operations  0.86 us (3%)
  local copies, waits for them, and re-layouts  0.69 us (3%)
    ppermute x2, waiting for transfers between devices, swap(): return lax.ppermute(v, 'lat', pairs)  7.26 us
    ppermute x1, starting transfers between devices, pass_on(): return lax.ppermute(v, 'lat', relays)  4.06 us
    ppermute x2, starting transfers between devices, swap(): return lax.ppermute(v, 'lat', pairs)  3.11 us
    pallas_call x1, Pallas kernels, on_device(): call(functools.partial(zonal_kernel, fields), [x.shape, t.shape, direct_s...  2.5 us
    pallas_call x1, Pallas kernels, on_device(): call(functools.partial(early_kernel, fields, levels, bands - 1), [(levels...  1.82 us
    pallas_call x1, Pallas kernels, on_device(): call(copy_kernel, (swapped,) + x.shape[1:], [pltpu.SemaphoreType.DMA((swa...  1.72 us
    ppermute x3, waiting for transfers between devices, other_core(): return lax.ppermute(v, 'lev', cores)  1 us
    pallas_call x1, Pallas kernels, on_device(): call(functools.partial(remap_last_kernel, levels), [x.shape, t.shape, t.s...  0.9 us
  transfers between devices with their start and end apart: 7, of which 4 were waited for; matrix products, arithmetic and copies ran while one was open for 1% of the time, Pallas kernels for 21%

profile of v7, /device:TPU:0, one launch (start us, length us, event | category | flops | bytes accessed | tf_op | source)
XLA Modules:
  0.0 26.8 jit_solution(18384823634160081517)
XLA Ops:
  0.6 0.0 copy-start
  0.6 0.0 copy-start.1
  0.7 0.0 copy-start.2
  0.7 0.0 copy-start.9
  0.7 0.0 copy-start.6
  0.7 0.0 copy-start.5
  0.7 0.0 copy-start.4
  0.7 0.0 copy-start.8
  0.7 0.0 copy-start.7
  0.7 1.7 %shard_map.123 = f32[8,2,4,1152]{3,2,1,0:T(4,128)} custom-call(f32[16,2,4,1152]{3,2,1,0:T(4,128)} %refs_0_.3), custom_call_target="tpu_custom_call" | custom-call | bytes 1000 | tf_op jit(solution)/shard_map/pallas_call | solution.py:449
  2.5 3.0 %collective-permute-start.1 = (f32[8,2,4,1152]{3,2,1,0:T(4,128)}, f32[8,2,4,1152]{3,2,1,0:T(4,128)S(1)}, u32[]{:S(2)}, u32[]{:S(2)}) collective-permute-start(f32[8,2,4,1152]{3,2,1,0:T(4,128)} %shard_map.123), channel_id=1, source_target_pairs={{0,2},{2,0},{4,6},{6,4},{8,10},{10,8},{12,14},{14,12},{1,3},{3,1},... | collective-permute-start | bytes 884744 | tf_op jit(solution)/shard_map/ppermute | solution.py:427
  5.5 0.0 copy-done
  5.5 0.0 copy-done.1
  5.5 0.0 copy-done.2
  5.5 0.0 copy-done.9
  5.5 0.0 copy-done.6
  5.5 0.0 copy-done.5
  5.5 0.0 copy-done.4
  5.5 0.0 copy-done.8
  5.5 0.0 copy-done.7
  5.5 2.5 %shard_map.121 = (f32[16,2,4,1152]{3,2,1,0:T(4,128)S(1)}, f32[2,4,1152]{2,1,0:T(4,128)S(1)}, f32[7,8,1152]{2,1,0:T(8,128)S(1)}, f32[7,8,1152]{2,1,0:T(8,128)S(1)}, f32[13,4,576]{2,1,0:T(4,128)S(1)}) custom-call(f32[16,2,4,1152]{3,2,1,0:T(4,128)S(1)} %copy-done, f32[2,4,1152]{2,1,0:T(4,128)S(1)} %copy-done.1, s32[2,4,1152]{2,1,0:T(4,128)S(1)} %copy-done.7, ...), custom_call_target="tpu_custom_call" | custom-call | flops 10000000000 | bytes 1000 | tf_op jit(solution)/shard_map/pallas_call | solution.py:457
  8.0 0.1 collective-permute-start
  8.1 0.1 collective-permute-start.3
  8.2 0.7 %collective-permute-start.4 = (f32[7,8,1152]{2,1,0:T(8,128)S(1)}, f32[7,8,1152]{2,1,0:T(8,128)S(1)}, u32[]{:S(2)}, u32[]{:S(2)}) collective-permute-start(f32[7,8,1152]{2,1,0:T(8,128)S(1)} %get-tuple-element.21), channel_id=1, source_target_pairs={{2,4},{4,2},{6,8},{8,6},{10,12},{12,10},{3,5},{5,3},{7,9},{9,7},{1... | collective-permute-start | bytes 774152 | tf_op jit(solution)/shard_map/ppermute | solution.py:430
  8.9 4.6 %collective-permute-done.1.swapped.refs_2_ = f32[8,2,4,1152]{3,2,1,0:T(4,128)S(1)} collective-permute-done((f32[8,2,4,1152]{3,2,1,0:T(4,128)}, f32[8,2,4,1152]{3,2,1,0:T(4,128)S(1)}, u32[]{:S(2)}, u32[]{:S(2)}) %collective-permute-start.1) | collective-permute-done | bytes 294944 | tf_op jit(solution)/shard_map/ppermute | solution.py:427
  13.5 0.1 shard_map.124
  13.6 4.1 %collective-permute-start.2 = (f32[6,8,1152]{2,1,0:T(8,128)S(1)}, f32[6,8,1152]{2,1,0:T(8,128)S(1)}, u32[]{:S(2)}, u32[]{:S(2)}) collective-permute-start(f32[6,8,1152]{2,1,0:T(8,128)S(1)} %shard_map.124), channel_id=1, source_target_pairs={{0,4},{4,8},{8,12},{6,2},{10,6},{14,10},{1,5},{5,9},{9,13},{7,3},{... | collective-permute-start | bytes 663560 | tf_op jit(solution)/shard_map/ppermute | solution.py:433
  17.6 0.0 collective-permute-done
  17.7 0.2 maximum_select_fusion.columns
  17.9 0.0 copy-start.3
  17.9 0.6 %copy-done.3 = f32[64]{0:T(128)S(1)} copy-done((f32[64]{0:T(128)S(1)}, f32[64]{0:T(128)}, u32[]{:S(2)}) %copy-start.3) | copy-done | bytes 280
  18.5 1.8 %shard_map.122 = (f32[4,4,4,1152]{3,2,1,0:T(4,128)S(1)}, f32[10,2,4,1152]{3,2,1,0:T(4,128)S(1)}, f32[16,2,4,1152]{3,2,1,0:T(4,128)S(1)}, f32[2,4,1152]{2,1,0:T(4,128)S(1)}, f32[2,1152]{1,0:T(2,128)S(1)}) custom-call(f32[64]{0:T(128)S(1)} %copy-done.3, f32[13,4,1152]{2,1,0:T(4,128)S(1)} %maximum_select_fusion.columns, ...), custom_call_target="tpu_custom_call", output_to_operand_aliasing={{2}: (5, {}), {3}: (6, {})} | custom-call | flops 1000000 | bytes 1000 | tf_op jit(solution)/shard_map/pallas_call | solution.py:492
  20.3 2.6 %collective-permute-done.3.near.refs_2_ = f32[7,8,1152]{2,1,0:T(8,128)S(1)} collective-permute-done((f32[7,8,1152]{2,1,0:T(8,128)S(1)}, f32[7,8,1152]{2,1,0:T(8,128)S(1)}, u32[]{:S(2)}, u32[]{:S(2)}) %collective-permute-start.3) | collective-permute-done | bytes 258080 | tf_op jit(solution)/shard_map/ppermute | solution.py:427
  23.0 0.0 collective-permute-done.4.far.refs_3_
  23.0 0.1 shard_map.125.refs_4_
  23.1 0.5 %shard_map.127.own = f32[9,2,4,1152]{3,2,1,0:T(4,128)S(1)} custom-call(f32[16,2,4,1152]{3,2,1,0:T(4,128)S(1)} %copy-done, f32[16,2,4,1152]{3,2,1,0:T(4,128)S(1)} %get-tuple-element.18.refs_1_, f32[7,8,1152]{2,1,0:T(8,128)S(1)} %collective-permute-done.3.near.refs_2_, f32[7,8,1152]{2,1,0:T(8,128)S(1)} %collective-permute-done.4.far.refs_3_, ...), custom_call_target="tpu_custom_call" | custom-call | flops 1000000 | bytes 1000 | tf_op jit(solution)/shard_map/pallas_call | solution.py:513
  23.6 0.1 collective-permute-start.6
  23.7 0.0 collective-permute-done.2.refs_3_
  23.7 0.5 %shard_map.126.own = f32[8,2,4,1152]{3,2,1,0:T(4,128)S(1)} custom-call(f32[16,2,4,1152]{3,2,1,0:T(4,128)S(1)} %copy-done, f32[16,2,4,1152]{3,2,1,0:T(4,128)S(1)} %get-tuple-element.18.refs_1_, f32[8,2,4,1152]{3,2,1,0:T(4,128)S(1)} %collective-permute-done.1.swapped.refs_2_, f32[6,8,1152]{2,1,0:T(8,128)S(1)} %collective-permute-done.2.refs_3_, ...), custom_call_target="tpu_custom_call" | custom-call | flops 1000000 | bytes 1000 | tf_op jit(solution)/shard_map/pallas_call | solution.py:519
  24.1 0.5 %collective-permute-start.5 = (f32[8,2,4,1152]{3,2,1,0:T(4,128)S(1)}, f32[8,2,4,1152]{3,2,1,0:T(4,128)S(1)}, u32[]{:S(2)}, u32[]{:S(2)}) collective-permute-start(f32[8,2,4,1152]{3,2,1,0:T(4,128)S(1)} %shard_map.126.own), channel_id=1, source_target_pairs={{0,1},{1,0},{2,3},{3,2},{4,5},{5,4},{6,7},{7,6},{8,9},{9,8},{10,11... | collective-permute-start | bytes 884744 | tf_op jit(solution)/shard_map/ppermute | solution.py:436
  24.7 0.6 %collective-permute-done.6.peer = f32[9,2,4,1152]{3,2,1,0:T(4,128)S(1)} collective-permute-done((f32[9,2,4,1152]{3,2,1,0:T(4,128)S(1)}, f32[9,2,4,1152]{3,2,1,0:T(4,128)S(1)}, u32[]{:S(2)}, u32[]{:S(2)}) %collective-permute-start.6) | collective-permute-done | bytes 331808 | tf_op jit(solution)/shard_map/ppermute | solution.py:436
  25.3 0.2 shard_map.128
  25.5 0.4 %collective-permute-done.5.peer = f32[8,2,4,1152]{3,2,1,0:T(4,128)S(1)} collective-permute-done((f32[8,2,4,1152]{3,2,1,0:T(4,128)S(1)}, f32[8,2,4,1152]{3,2,1,0:T(4,128)S(1)}, u32[]{:S(2)}, u32[]{:S(2)}) %collective-permute-start.5) | collective-permute-done | bytes 294944 | tf_op jit(solution)/shard_map/ppermute | solution.py:436
  25.9 0.9 %shard_map.129 = (f32[16,2,4,1152]{3,2,1,0:T(4,128)}, f32[2,4,1152]{2,1,0:T(4,128)}, f32[2,4,1152]{2,1,0:T(4,128)}) custom-call(f32[8,2,4,1152]{3,2,1,0:T(4,128)S(1)} %shard_map.126.own, f32[8,2,4,1152]{3,2,1,0:T(4,128)S(1)} %collective-permute-done.5.peer, f32[4,4,4,1152]{3,2,1,0:T(4,128)S(1)} %get-tuple-element.23.weights, ...), custom_call_target="tpu_custom_call" | custom-call | flops 1000000 | bytes 1000 | tf_op jit(solution)/shard_map/pallas_call | solution.py:532
Async XLA Ops:
  0.6 4.8 %copy-start = (f32[16,2,4,1152]{3,2,1,0:T(4,128)S(1)}, f32[16,2,4,1152]{3,2,1,0:T(4,128)}, u32[]{:S(2)}) copy-start(f32[16,2,4,1152]{3,2,1,0:T(4,128)} %refs_0_.3) | copy-start | bytes 1769476
  0.6 4.8 %copy-start.1 = (f32[2,4,1152]{2,1,0:T(4,128)S(1)}, f32[2,4,1152]{2,1,0:T(4,128)}, u32[]{:S(2)}) copy-start(f32[2,4,1152]{2,1,0:T(4,128)} %refs_5_.1) | copy-start | bytes 110596
  0.7 4.8 %copy-start.2 = (f32[2,4,1152]{2,1,0:T(4,128)S(1)}, f32[2,4,1152]{2,1,0:T(4,128)}, u32[]{:S(2)}) copy-start(f32[2,4,1152]{2,1,0:T(4,128)} %c.3) | copy-start | bytes 110596
  0.7 4.8 %copy-start.9 = (f32[4,576]{1,0:T(4,128)S(1)}, f32[4,576]{1,0:T(4,128)}, u32[]{:S(2)}) copy-start(f32[4,576]{1,0:T(4,128)} %ground.1) | copy-start | bytes 27652
  0.7 4.8 %copy-start.6 = (f32[4,4,576]{2,1,0:T(4,128)S(1)}, f32[4,4,576]{2,1,0:T(4,128)}, u32[]{:S(2)}) copy-start(f32[4,4,576]{2,1,0:T(4,128)} %quotient.1) | copy-start | bytes 110596
  0.7 4.8 %copy-start.5 = (f32[4,4,576]{2,1,0:T(4,128)S(1)}, f32[4,4,576]{2,1,0:T(4,128)}, u32[]{:S(2)}) copy-start(f32[4,4,576]{2,1,0:T(4,128)} %share.1) | copy-start | bytes 110596
  0.7 4.8 %copy-start.4 = (s32[4,4,576]{2,1,0:T(4,128)S(1)}, s32[4,4,576]{2,1,0:T(4,128)}, u32[]{:S(2)}) copy-start(s32[4,4,576]{2,1,0:T(4,128)} %upper.1) | copy-start | bytes 110596
  0.7 4.8 %copy-start.8 = (f32[2,4,1152]{2,1,0:T(4,128)S(1)}, f32[2,4,1152]{2,1,0:T(4,128)}, u32[]{:S(2)}) copy-start(f32[2,4,1152]{2,1,0:T(4,128)} %f.1) | copy-start | bytes 110596
  0.7 4.8 %copy-start.7 = (s32[2,4,1152]{2,1,0:T(4,128)S(1)}, s32[2,4,1152]{2,1,0:T(4,128)}, u32[]{:S(2)}) copy-start(s32[2,4,1152]{2,1,0:T(4,128)} %n.1) | copy-start | bytes 110596
  2.5 11.1 %collective-permute-start.1 = (f32[8,2,4,1152]{3,2,1,0:T(4,128)}, f32[8,2,4,1152]{3,2,1,0:T(4,128)S(1)}, u32[]{:S(2)}, u32[]{:S(2)}) collective-permute-start(f32[8,2,4,1152]{3,2,1,0:T(4,128)} %shard_map.123), channel_id=1, source_target_pairs={{0,2},{2,0},{4,6},{6,4},{8,10},{10,8},{12,14},{14,12},{1,3},{3,1},... | collective-permute-start | bytes 884744 | tf_op jit(solution)/shard_map/ppermute | solution.py:427
  8.0 9.6 %collective-permute-start = (f32[13,4,576]{2,1,0:T(4,128)S(1)}, f32[13,4,576]{2,1,0:T(4,128)S(1)}, u32[]{:S(2)}, u32[]{:S(2)}) collective-permute-start(f32[13,4,576]{2,1,0:T(4,128)S(1)} %get-tuple-element.15), channel_id=1, source_target_pairs={{0,1},{1,0},{2,3},{3,2},{4,5},{5,4},{6,7},{7,6},{8,9},{9,8},{10,11... | collective-permute-start | bytes 359432 | tf_op jit(solution)/shard_map/ppermute | solution.py:436
  8.1 14.9 %collective-permute-start.3 = (f32[7,8,1152]{2,1,0:T(8,128)S(1)}, f32[7,8,1152]{2,1,0:T(8,128)S(1)}, u32[]{:S(2)}, u32[]{:S(2)}) collective-permute-start(f32[7,8,1152]{2,1,0:T(8,128)S(1)} %get-tuple-element.20), channel_id=1, source_target_pairs={{0,2},{2,0},{4,6},{6,4},{8,10},{10,8},{12,14},{14,12},{1,3},{3,1},... | collective-permute-start | bytes 774152 | tf_op jit(solution)/shard_map/ppermute | solution.py:427
  8.2 14.8 %collective-permute-start.4 = (f32[7,8,1152]{2,1,0:T(8,128)S(1)}, f32[7,8,1152]{2,1,0:T(8,128)S(1)}, u32[]{:S(2)}, u32[]{:S(2)}) collective-permute-start(f32[7,8,1152]{2,1,0:T(8,128)S(1)} %get-tuple-element.21), channel_id=1, source_target_pairs={{2,4},{4,2},{6,8},{8,6},{10,12},{12,10},{3,5},{5,3},{7,9},{9,7},{1... | collective-permute-start | bytes 774152 | tf_op jit(solution)/shard_map/ppermute | solution.py:430
  13.6 10.1 %collective-permute-start.2 = (f32[6,8,1152]{2,1,0:T(8,128)S(1)}, f32[6,8,1152]{2,1,0:T(8,128)S(1)}, u32[]{:S(2)}, u32[]{:S(2)}) collective-permute-start(f32[6,8,1152]{2,1,0:T(8,128)S(1)} %shard_map.124), channel_id=1, source_target_pairs={{0,4},{4,8},{8,12},{6,2},{10,6},{14,10},{1,5},{5,9},{9,13},{7,3},{... | collective-permute-start | bytes 663560 | tf_op jit(solution)/shard_map/ppermute | solution.py:433
  17.9 0.7 %copy-start.3 = (f32[64]{0:T(128)S(1)}, f32[64]{0:T(128)}, u32[]{:S(2)}) copy-start(f32[64]{0:T(128)} %constant.8.clone.scale) | copy-start | bytes 772
  23.6 1.7 %collective-permute-start.6 = (f32[9,2,4,1152]{3,2,1,0:T(4,128)S(1)}, f32[9,2,4,1152]{3,2,1,0:T(4,128)S(1)}, u32[]{:S(2)}, u32[]{:S(2)}) collective-permute-start(f32[9,2,4,1152]{3,2,1,0:T(4,128)S(1)} %shard_map.127.own), channel_id=1, source_target_pairs={{0,1},{1,0},{2,3},{3,2},{4,5},{5,4},{6,7},{7,6},{8,9},{9,8},{10,11... | collective-permute-start | bytes 995336 | tf_op jit(solution)/shard_map/ppermute | solution.py:436
  24.1 1.7 %collective-permute-start.5 = (f32[8,2,4,1152]{3,2,1,0:T(4,128)S(1)}, f32[8,2,4,1152]{3,2,1,0:T(4,128)S(1)}, u32[]{:S(2)}, u32[]{:S(2)}) collective-permute-start(f32[8,2,4,1152]{3,2,1,0:T(4,128)S(1)} %shard_map.126.own), channel_id=1, source_target_pairs={{0,1},{1,0},{2,3},{3,2},{4,5},{5,4},{6,7},{7,6},{8,9},{9,8},{10,11... | collective-permute-start | bytes 884744 | tf_op jit(solution)/shard_map/ppermute | solution.py:436

commit v8 on v7

--- a/solution.py
+++ b/solution.py
@@ -34,16 +34,9 @@
         body(False)
 
 
-def copy_kernel(x, out, sems):
-    count = out.shape[0]
-    skip = x.shape[0] - count
-    copies = [
-        pltpu.make_async_copy(x.at[skip + i], out.at[i], sems.at[i]) for i in range(count)
-    ]
-    for copy in copies:
-        copy.start()
-    for copy in copies:
-        copy.wait()
+def copy_kernel(x, out):
+    skip = x.shape[0] - out.shape[0]
+    out[...] = x[skip:]
 
 
 def side_rows(to_north):
@@ -446,13 +439,7 @@
     swapped = fields - direct
     direct_shape = (3 * LEVELS + 1, direct, lons)
 
-    payload = call(
-        copy_kernel,
-        (swapped,) + x.shape[1:],
-        [pltpu.SemaphoreType.DMA((swapped,))],
-        [pl.BlockSpec(memory_space=pltpu.HBM)],
-        limit=60,
-    )(x)
+    payload = call(copy_kernel, (swapped,) + x.shape[1:])(x)
     near_a = swap(payload)
     zon, zon_t, near_rows, far_rows, columns = call(
         functools.partial(zonal_kernel, fields),

time: 27.1 us -> 26.2 us (0.967)
  Pallas kernels: 8.27 us -> 6.55 us
  local copies, waits for them, and re-layouts: 0.69 us -> 1.74 us
  waiting for transfers between devices: 8.26 us -> 7.28 us
  starting transfers between devices: 8.51 us -> 9.29 us
    pallas_call x1, Pallas kernels: 1.72 us -> 0.02 us  [on_device(): payload = call(copy_kernel, (swapped,) + x.shape[1:])(x)]
    unnamed x20 -> x22, local copies, waits for them, and re-layouts: 0.69 us -> 1.74 us
    ppermute x2, waiting for transfers between devices: 7.26 us -> 6.28 us  [swap(): return lax.ppermute(v, 'lat', pairs)]
    ppermute x2, starting transfers between devices: 3.11 us -> 3.75 us  [swap(): return lax.ppermute(v, 'lat', pairs)]
  transfers between devices with their start and end apart: 7 -> 7, of which waited for: 4 -> 4; matrix products, arithmetic and copies ran while one was open for 1% -> 1% of each run, Pallas kernels for 21% -> 22%
where the time goes in v8:
time: 26.2 us; the launch traced here: 25.9 us
  starting transfers between devices  9.29 us (35%)
  waiting for transfers between devices  7.28 us (28%)
  Pallas kernels  6.55 us (25%)
  local copies, waits for them, and re-layouts  1.74 us (7%)
  between operations  0.83 us (3%)
    ppermute x2, waiting for transfers between devices, swap(): return lax.ppermute(v, 'lat', pairs)  6.28 us
    ppermute x1, starting transfers between devices, pass_on(): return lax.ppermute(v, 'lat', relays)  4.19 us
    ppermute x2, starting transfers between devices, swap(): return lax.ppermute(v, 'lat', pairs)  3.75 us
    pallas_call x1, Pallas kernels, on_device(): call(functools.partial(zonal_kernel, fields), [x.shape, t.shape, direct_s...  2.5 us
    pallas_call x1, Pallas kernels, on_device(): call(functools.partial(early_kernel, fields, levels, bands - 1), [(levels...  1.82 us
    unnamed x22, local copies, waits for them, and re-layouts  1.74 us
    ppermute x3, waiting for transfers between devices, other_core(): return lax.ppermute(v, 'lev', cores)  0.99 us
    pallas_call x1, Pallas kernels, on_device(): call(functools.partial(remap_last_kernel, levels), [x.shape, t.shape, t.s...  0.9 us
  transfers between devices with their start and end apart: 7, of which 4 were waited for; matrix products, arithmetic and copies ran while one was open for 1% of the time, Pallas kernels for 22%

profile of v8, /device:TPU:0, one launch (start us, length us, event | category | flops | bytes accessed | tf_op | source)
XLA Modules:
  0.0 25.9 jit_solution(14479555362813334352)
XLA Ops:
  0.6 0.0 copy-start
  0.6 1.1 %copy-done = f32[16,2,4,1152]{3,2,1,0:T(4,128)S(1)} copy-done((f32[16,2,4,1152]{3,2,1,0:T(4,128)S(1)}, f32[16,2,4,1152]{3,2,1,0:T(4,128)}, u32[]{:S(2)}) %copy-start) | copy-done | bytes 589848
  1.7 0.0 copy-start.2
  1.7 0.0 copy-start.3
  1.7 0.0 copy-start.5
  1.7 0.0 copy-start.6
  1.7 0.0 copy-start.7
  1.7 0.0 copy-start.8
  1.7 0.0 copy-start.9
  1.7 0.0 copy-start.10
  1.8 3.0 %collective-permute-start.1 = (f32[8,2,4,1152]{3,2,1,0:T(4,128)S(1)}, f32[8,2,4,1152]{3,2,1,0:T(4,128)S(1)}, u32[]{:S(2)}, u32[]{:S(2)}) collective-permute-start(f32[8,2,4,1152]{3,2,1,0:T(4,128)S(1)} %shard_map.123), channel_id=1, source_target_pairs={{0,2},{2,0},{4,6},{6,4},{8,10},{10,8},{12,14},{14,12},{1,3},{3,1},... | collective-permute-start | bytes 884744 | tf_op jit(solution)/shard_map/ppermute | solution.py:420
  4.8 0.0 copy-done.2
  4.8 0.0 copy-done.3
  4.8 0.0 copy-done.5
  4.8 0.0 copy-done.6
  4.8 0.0 copy-done.7
  4.8 0.0 copy-done.8
  4.8 0.0 copy-done.9
  4.8 0.0 copy-done.10
  4.8 2.5 %shard_map.121 = (f32[16,2,4,1152]{3,2,1,0:T(4,128)S(1)}, f32[2,4,1152]{2,1,0:T(4,128)S(1)}, f32[7,8,1152]{2,1,0:T(8,128)S(1)}, f32[7,8,1152]{2,1,0:T(8,128)S(1)}, f32[13,4,576]{2,1,0:T(4,128)S(1)}) custom-call(f32[16,2,4,1152]{3,2,1,0:T(4,128)S(1)} %copy-done, f32[2,4,1152]{2,1,0:T(4,128)S(1)} %copy-done.2, s32[2,4,1152]{2,1,0:T(4,128)S(1)} %copy-done.8, ...), custom_call_target="tpu_custom_call" | custom-call | flops 10000000000 | bytes 1000 | tf_op jit(solution)/shard_map/pallas_call | solution.py:444
  7.3 0.1 collective-permute-start
  7.4 0.7 %collective-permute-start.3 = (f32[7,8,1152]{2,1,0:T(8,128)S(1)}, f32[7,8,1152]{2,1,0:T(8,128)S(1)}, u32[]{:S(2)}, u32[]{:S(2)}) collective-permute-start(f32[7,8,1152]{2,1,0:T(8,128)S(1)} %get-tuple-element.20), channel_id=1, source_target_pairs={{0,2},{2,0},{4,6},{6,4},{8,10},{10,8},{12,14},{14,12},{1,3},{3,1},... | collective-permute-start | bytes 774152 | tf_op jit(solution)/shard_map/ppermute | solution.py:420
  8.2 0.7 %collective-permute-start.4 = (f32[7,8,1152]{2,1,0:T(8,128)S(1)}, f32[7,8,1152]{2,1,0:T(8,128)S(1)}, u32[]{:S(2)}, u32[]{:S(2)}) collective-permute-start(f32[7,8,1152]{2,1,0:T(8,128)S(1)} %get-tuple-element.21), channel_id=1, source_target_pairs={{2,4},{4,2},{6,8},{8,6},{10,12},{12,10},{3,5},{5,3},{7,9},{9,7},{1... | collective-permute-start | bytes 774152 | tf_op jit(solution)/shard_map/ppermute | solution.py:423
  8.9 3.8 %collective-permute-done.1.swapped.refs_2_ = f32[8,2,4,1152]{3,2,1,0:T(4,128)S(1)} collective-permute-done((f32[8,2,4,1152]{3,2,1,0:T(4,128)S(1)}, f32[8,2,4,1152]{3,2,1,0:T(4,128)S(1)}, u32[]{:S(2)}, u32[]{:S(2)}) %collective-permute-start.1) | collective-permute-done | bytes 294944 | tf_op jit(solution)/shard_map/ppermute | solution.py:420
  12.6 0.0 copy-start.1
  12.6 0.1 shard_map.124
  12.7 4.2 %collective-permute-start.2 = (f32[6,8,1152]{2,1,0:T(8,128)S(1)}, f32[6,8,1152]{2,1,0:T(8,128)S(1)}, u32[]{:S(2)}, u32[]{:S(2)}) collective-permute-start(f32[6,8,1152]{2,1,0:T(8,128)S(1)} %shard_map.124), channel_id=1, source_target_pairs={{0,4},{4,8},{8,12},{6,2},{10,6},{14,10},{1,5},{5,9},{9,13},{7,3},{... | collective-permute-start | bytes 663560 | tf_op jit(solution)/shard_map/ppermute | solution.py:426
  16.9 0.0 collective-permute-done
  16.9 0.2 maximum_select_fusion.columns
  17.1 0.0 copy-start.4
  17.1 0.0 copy-done.1
  17.1 0.6 %copy-done.4 = f32[64]{0:T(128)S(1)} copy-done((f32[64]{0:T(128)S(1)}, f32[64]{0:T(128)}, u32[]{:S(2)}) %copy-start.4) | copy-done | bytes 280
  17.8 1.8 %shard_map.122 = (f32[4,4,4,1152]{3,2,1,0:T(4,128)S(1)}, f32[10,2,4,1152]{3,2,1,0:T(4,128)S(1)}, f32[16,2,4,1152]{3,2,1,0:T(4,128)S(1)}, f32[2,4,1152]{2,1,0:T(4,128)S(1)}, f32[2,1152]{1,0:T(2,128)S(1)}) custom-call(f32[64]{0:T(128)S(1)} %copy-done.4, f32[13,4,1152]{2,1,0:T(4,128)S(1)} %maximum_select_fusion.columns, ...), custom_call_target="tpu_custom_call", output_to_operand_aliasing={{2}: (5, {}), {3}: (6, {})} | custom-call | flops 1000000 | bytes 1000 | tf_op jit(solution)/shard_map/pallas_call | solution.py:479
  19.6 2.5 %collective-permute-done.3.near.refs_2_ = f32[7,8,1152]{2,1,0:T(8,128)S(1)} collective-permute-done((f32[7,8,1152]{2,1,0:T(8,128)S(1)}, f32[7,8,1152]{2,1,0:T(8,128)S(1)}, u32[]{:S(2)}, u32[]{:S(2)}) %collective-permute-start.3) | collective-permute-done | bytes 258080 | tf_op jit(solution)/shard_map/ppermute | solution.py:420
  22.1 0.0 collective-permute-done.4.far.refs_3_
  22.1 0.1 shard_map.125.refs_4_
  22.2 0.5 %shard_map.127.own = f32[9,2,4,1152]{3,2,1,0:T(4,128)S(1)} custom-call(f32[16,2,4,1152]{3,2,1,0:T(4,128)S(1)} %copy-done.1, f32[16,2,4,1152]{3,2,1,0:T(4,128)S(1)} %get-tuple-element.18.refs_1_, f32[7,8,1152]{2,1,0:T(8,128)S(1)} %collective-permute-done.3.near.refs_2_, f32[7,8,1152]{2,1,0:T(8,128)S(1)} %collective-permute-done.4.far.refs_3_, ...), custom_call_target="tpu_custom_call" | custom-call | flops 1000000 | bytes 1000 | tf_op jit(solution)/shard_map/pallas_call | solution.py:500
  22.7 0.1 collective-permute-start.6
  22.8 0.0 collective-permute-done.2.refs_3_
  22.8 0.5 %shard_map.126.own = f32[8,2,4,1152]{3,2,1,0:T(4,128)S(1)} custom-call(f32[16,2,4,1152]{3,2,1,0:T(4,128)S(1)} %copy-done.1, f32[16,2,4,1152]{3,2,1,0:T(4,128)S(1)} %get-tuple-element.18.refs_1_, f32[8,2,4,1152]{3,2,1,0:T(4,128)S(1)} %collective-permute-done.1.swapped.refs_2_, f32[6,8,1152]{2,1,0:T(8,128)S(1)} %collective-permute-done.2.refs_3_, ...), custom_call_target="tpu_custom_call" | custom-call | flops 1000000 | bytes 1000 | tf_op jit(solution)/shard_map/pallas_call | solution.py:506
  23.2 0.5 %collective-permute-start.5 = (f32[8,2,4,1152]{3,2,1,0:T(4,128)S(1)}, f32[8,2,4,1152]{3,2,1,0:T(4,128)S(1)}, u32[]{:S(2)}, u32[]{:S(2)}) collective-permute-start(f32[8,2,4,1152]{3,2,1,0:T(4,128)S(1)} %shard_map.126.own), channel_id=1, source_target_pairs={{0,1},{1,0},{2,3},{3,2},{4,5},{5,4},{6,7},{7,6},{8,9},{9,8},{10,11... | collective-permute-start | bytes 884744 | tf_op jit(solution)/shard_map/ppermute | solution.py:429
  23.8 0.6 %collective-permute-done.6.peer = f32[9,2,4,1152]{3,2,1,0:T(4,128)S(1)} collective-permute-done((f32[9,2,4,1152]{3,2,1,0:T(4,128)S(1)}, f32[9,2,4,1152]{3,2,1,0:T(4,128)S(1)}, u32[]{:S(2)}, u32[]{:S(2)}) %collective-permute-start.6) | collective-permute-done | bytes 331808 | tf_op jit(solution)/shard_map/ppermute | solution.py:429
  24.4 0.2 shard_map.128
  24.6 0.4 %collective-permute-done.5.peer = f32[8,2,4,1152]{3,2,1,0:T(4,128)S(1)} collective-permute-done((f32[8,2,4,1152]{3,2,1,0:T(4,128)S(1)}, f32[8,2,4,1152]{3,2,1,0:T(4,128)S(1)}, u32[]{:S(2)}, u32[]{:S(2)}) %collective-permute-start.5) | collective-permute-done | bytes 294944 | tf_op jit(solution)/shard_map/ppermute | solution.py:429
  25.0 0.9 %shard_map.129 = (f32[16,2,4,1152]{3,2,1,0:T(4,128)}, f32[2,4,1152]{2,1,0:T(4,128)}, f32[2,4,1152]{2,1,0:T(4,128)}) custom-call(f32[8,2,4,1152]{3,2,1,0:T(4,128)S(1)} %shard_map.126.own, f32[8,2,4,1152]{3,2,1,0:T(4,128)S(1)} %collective-permute-done.5.peer, f32[4,4,4,1152]{3,2,1,0:T(4,128)S(1)} %get-tuple-element.23.weights, ...), custom_call_target="tpu_custom_call" | custom-call | flops 1000000 | bytes 1000 | tf_op jit(solution)/shard_map/pallas_call | solution.py:519
  (1 shorter events, 0.0 us)
Async XLA Ops:
  0.6 1.1 %copy-start = (f32[16,2,4,1152]{3,2,1,0:T(4,128)S(1)}, f32[16,2,4,1152]{3,2,1,0:T(4,128)}, u32[]{:S(2)}) copy-start(f32[16,2,4,1152]{3,2,1,0:T(4,128)} %refs_0_.3) | copy-start | bytes 1769476
  1.7 3.1 %copy-start.2 = (f32[2,4,1152]{2,1,0:T(4,128)S(1)}, f32[2,4,1152]{2,1,0:T(4,128)}, u32[]{:S(2)}) copy-start(f32[2,4,1152]{2,1,0:T(4,128)} %refs_5_.1) | copy-start | bytes 110596
  1.7 3.1 %copy-start.3 = (f32[2,4,1152]{2,1,0:T(4,128)S(1)}, f32[2,4,1152]{2,1,0:T(4,128)}, u32[]{:S(2)}) copy-start(f32[2,4,1152]{2,1,0:T(4,128)} %c.3) | copy-start | bytes 110596
  1.7 3.1 %copy-start.5 = (s32[4,4,576]{2,1,0:T(4,128)S(1)}, s32[4,4,576]{2,1,0:T(4,128)}, u32[]{:S(2)}) copy-start(s32[4,4,576]{2,1,0:T(4,128)} %upper.1) | copy-start | bytes 110596
  1.7 3.1 %copy-start.6 = (f32[4,4,576]{2,1,0:T(4,128)S(1)}, f32[4,4,576]{2,1,0:T(4,128)}, u32[]{:S(2)}) copy-start(f32[4,4,576]{2,1,0:T(4,128)} %share.1) | copy-start | bytes 110596
  1.7 3.1 %copy-start.7 = (f32[4,4,576]{2,1,0:T(4,128)S(1)}, f32[4,4,576]{2,1,0:T(4,128)}, u32[]{:S(2)}) copy-start(f32[4,4,576]{2,1,0:T(4,128)} %quotient.1) | copy-start | bytes 110596
  1.7 3.1 %copy-start.8 = (s32[2,4,1152]{2,1,0:T(4,128)S(1)}, s32[2,4,1152]{2,1,0:T(4,128)}, u32[]{:S(2)}) copy-start(s32[2,4,1152]{2,1,0:T(4,128)} %n.1) | copy-start | bytes 110596
  1.7 3.1 %copy-start.9 = (f32[2,4,1152]{2,1,0:T(4,128)S(1)}, f32[2,4,1152]{2,1,0:T(4,128)}, u32[]{:S(2)}) copy-start(f32[2,4,1152]{2,1,0:T(4,128)} %f.1) | copy-start | bytes 110596
  1.7 3.1 %copy-start.10 = (f32[4,576]{1,0:T(4,128)S(1)}, f32[4,576]{1,0:T(4,128)}, u32[]{:S(2)}) copy-start(f32[4,576]{1,0:T(4,128)} %ground.1) | copy-start | bytes 27652
  1.8 10.8 %collective-permute-start.1 = (f32[8,2,4,1152]{3,2,1,0:T(4,128)S(1)}, f32[8,2,4,1152]{3,2,1,0:T(4,128)S(1)}, u32[]{:S(2)}, u32[]{:S(2)}) collective-permute-start(f32[8,2,4,1152]{3,2,1,0:T(4,128)S(1)} %shard_map.123), channel_id=1, source_target_pairs={{0,2},{2,0},{4,6},{6,4},{8,10},{10,8},{12,14},{14,12},{1,3},{3,1},... | collective-permute-start | bytes 884744 | tf_op jit(solution)/shard_map/ppermute | solution.py:420
  7.3 9.6 %collective-permute-start = (f32[13,4,576]{2,1,0:T(4,128)S(1)}, f32[13,4,576]{2,1,0:T(4,128)S(1)}, u32[]{:S(2)}, u32[]{:S(2)}) collective-permute-start(f32[13,4,576]{2,1,0:T(4,128)S(1)} %get-tuple-element.15), channel_id=1, source_target_pairs={{0,1},{1,0},{2,3},{3,2},{4,5},{5,4},{6,7},{7,6},{8,9},{9,8},{10,11... | collective-permute-start | bytes 359432 | tf_op jit(solution)/shard_map/ppermute | solution.py:429
  7.4 14.7 %collective-permute-start.3 = (f32[7,8,1152]{2,1,0:T(8,128)S(1)}, f32[7,8,1152]{2,1,0:T(8,128)S(1)}, u32[]{:S(2)}, u32[]{:S(2)}) collective-permute-start(f32[7,8,1152]{2,1,0:T(8,128)S(1)} %get-tuple-element.20), channel_id=1, source_target_pairs={{0,2},{2,0},{4,6},{6,4},{8,10},{10,8},{12,14},{14,12},{1,3},{3,1},... | collective-permute-start | bytes 774152 | tf_op jit(solution)/shard_map/ppermute | solution.py:420
  8.2 13.9 %collective-permute-start.4 = (f32[7,8,1152]{2,1,0:T(8,128)S(1)}, f32[7,8,1152]{2,1,0:T(8,128)S(1)}, u32[]{:S(2)}, u32[]{:S(2)}) collective-permute-start(f32[7,8,1152]{2,1,0:T(8,128)S(1)} %get-tuple-element.21), channel_id=1, source_target_pairs={{2,4},{4,2},{6,8},{8,6},{10,12},{12,10},{3,5},{5,3},{7,9},{9,7},{1... | collective-permute-start | bytes 774152 | tf_op jit(solution)/shard_map/ppermute | solution.py:423
  12.6 4.5 %copy-start.1 = (f32[16,2,4,1152]{3,2,1,0:T(4,128)S(1)}, f32[16,2,4,1152]{3,2,1,0:T(4,128)}, u32[]{:S(2)}) copy-start(f32[16,2,4,1152]{3,2,1,0:T(4,128)} %refs_0_.3) | copy-start | bytes 1769476
  12.7 10.1 %collective-permute-start.2 = (f32[6,8,1152]{2,1,0:T(8,128)S(1)}, f32[6,8,1152]{2,1,0:T(8,128)S(1)}, u32[]{:S(2)}, u32[]{:S(2)}) collective-permute-start(f32[6,8,1152]{2,1,0:T(8,128)S(1)} %shard_map.124), channel_id=1, source_target_pairs={{0,4},{4,8},{8,12},{6,2},{10,6},{14,10},{1,5},{5,9},{9,13},{7,3},{... | collective-permute-start | bytes 663560 | tf_op jit(solution)/shard_map/ppermute | solution.py:426
  17.1 0.7 %copy-start.4 = (f32[64]{0:T(128)S(1)}, f32[64]{0:T(128)}, u32[]{:S(2)}) copy-start(f32[64]{0:T(128)} %constant.8.clone.scale) | copy-start | bytes 772
  22.7 1.7 %collective-permute-start.6 = (f32[9,2,4,1152]{3,2,1,0:T(4,128)S(1)}, f32[9,2,4,1152]{3,2,1,0:T(4,128)S(1)}, u32[]{:S(2)}, u32[]{:S(2)}) collective-permute-start(f32[9,2,4,1152]{3,2,1,0:T(4,128)S(1)} %shard_map.127.own), channel_id=1, source_target_pairs={{0,1},{1,0},{2,3},{3,2},{4,5},{5,4},{6,7},{7,6},{8,9},{9,8},{10,11... | collective-permute-start | bytes 995336 | tf_op jit(solution)/shard_map/ppermute | solution.py:429
  23.2 1.7 %collective-permute-start.5 = (f32[8,2,4,1152]{3,2,1,0:T(4,128)S(1)}, f32[8,2,4,1152]{3,2,1,0:T(4,128)S(1)}, u32[]{:S(2)}, u32[]{:S(2)}) collective-permute-start(f32[8,2,4,1152]{3,2,1,0:T(4,128)S(1)} %shard_map.126.own), channel_id=1, source_target_pairs={{0,1},{1,0},{2,3},{3,2},{4,5},{5,4},{6,7},{7,6},{8,9},{9,8},{10,11... | collective-permute-start | bytes 884744 | tf_op jit(solution)/shard_map/ppermute | solution.py:429

commit v9 on v8

--- a/solution.py
+++ b/solution.py
@@ -13,7 +13,7 @@
 LEVELS = 2
 LANE = 128
 
-COST = dict(zonal=10000, relay=10000, early=1, patch=1, fin_b=1, fin_a=1, first=1, last=1)
+COST = dict(zonal=10000, relay=10000, mix=1, early=1, fin_b=1, fin_a=1, first=1, last=1)
 
 
 def lanes(chunk):
@@ -43,7 +43,7 @@
     return (ROWS - 1, ROWS - 2, ROWS - 3) if to_north else (0, 1, 2)
 
 
-def gather_rows(rows, x, t, c, out):
+def gather_rows(rows, x, t, out):
     count = out.shape[1]
     last = 3 * LEVELS
     for d, row in enumerate(rows):
@@ -52,8 +52,6 @@
             for f in range(count):
                 out[at, f : f + 1, :] = x[f, lev, row : row + 1, :]
             out[last, at : at + 1, :] = t[lev, row : row + 1, :]
-    for lev in range(LEVELS):
-        out[last, last + lev : last + lev + 1, :] = c[lev, ROWS - 1 : ROWS, :]
 
 
 def relay_kernel(swapped, zon_t, relay):
@@ -123,23 +121,44 @@
     return jnp.concatenate([ref[lev] for lev in range(LEVELS)], axis=0)
 
 
-def early_kernel(
-    fields, levels, last, scale, columns, c, x, t, zon_in, zon_t_in, mix, out, zon, zon_t, factor, ws
-):
+def mix_kernel(levels, columns, c, relay, mix, c_rows):
+    mix_weights(levels, columns, mix)
+    for lev in range(LEVELS):
+        c_rows[lev : lev + 1, :] = c[lev, ROWS - 1 : ROWS, :]
+
+
+def early_kernel(fields, last, scale, c, c_south, x, t, zon_in, zon_t_in, out, zon, zon_t, ws):
     lat = lax.axis_index("lat")
     lons = x.shape[-1]
-    mix_weights(levels, columns, mix)
-    factor[...] = jnp.full(factor.shape, jnp.where(lat == 0, 0.0, scale[lat * 2 * ROWS]))
     parts = []
     for lev in range(LEVELS):
         own = c[lev]
+        beyond_pole = -pltpu.roll(own, lons // 2, 1)[0:1]
         parts += [
-            jnp.where(lat == 0, -pltpu.roll(own, lons // 2, 1)[0:1], 0.0),
+            jnp.where(lat == 0, beyond_pole, c_south[lev : lev + 1, :]),
             own[: ROWS - 1],
         ]
     for r, w in enumerate(row_weights(stacked(c), jnp.concatenate(parts, axis=0), scale, lat)):
         for lev in range(LEVELS):
             out[r, lev] = w[lev * ROWS : (lev + 1) * ROWS]
+
+    for lev in range(LEVELS):
+        for chunk in range(lons // LANE):
+            lane = lanes(chunk)
+            weights = [out[r + 3, lev, :, lane] for r in range(ROWS)]
+
+            def with_own_rows(total, row_at):
+                for r, w in enumerate(weights):
+                    total = total + w * jnp.broadcast_to(row_at(r), total.shape)
+                return total
+
+            zon_t[lev, :, lane] = with_own_rows(
+                zon_t_in[lev, :, lane], lambda r: t[lev, r : r + 1, lane]
+            )
+            for i in range(fields):
+                zon[i, lev, :, lane] = with_own_rows(
+                    zon_in[i, lev, :, lane], lambda r: x[i, lev, r : r + 1, lane]
+                )
 
     def pole(rows):
         for k, (_, at) in enumerate(rows):
@@ -176,25 +195,15 @@
         pole([(ROWS - d, ROWS + 2 + d) for d in range(1, 4)])
 
 
-def patch_kernel(factor, near, far, weights_in, weights):
-    block = 3 * LEVELS
-    rows = slice(block, block + LEVELS)
-    below = jnp.where(parity() == 1, near[block, rows, :], far[block, rows, :])
-    for r, part in enumerate(face_weights(below)):
-        part = factor[...] * part
-        for lev in range(LEVELS):
-            weights[r, lev, 0:1, :] = weights[r, lev, 0:1, :] + part[lev : lev + 1]
-
-
 def zonal_kernel(
-    fields, x, t, n, f, c, upper, share, quotient, ground, zon, zon_t, near, far, columns, w
+    fields, x, t, n, f, upper, share, quotient, ground, zon, zon_t, near, far, columns, w
 ):
     lons = x.shape[-1]
     pack_columns(upper, share, quotient, ground, columns)
 
     def gather(odd):
-        gather_rows(side_rows(not odd), x, t, c, near)
-        gather_rows(side_rows(odd), x, t, c, far)
+        gather_rows(side_rows(not odd), x, t, near)
+        gather_rows(side_rows(odd), x, t, far)
 
     both(parity(), gather)
 
@@ -237,25 +246,24 @@
 
 def fin_kernel(skip, count, direct, *refs):
     if direct:
-        x, zon, near, far, w, t, zon_t, adv = refs
+        base, near, far, w, base_t, adv = refs
     else:
-        x, zon, near, far, w, adv = refs
+        base, near, far, w, adv = refs
     chunks = w.shape[-1] // LANE
 
     def body(odd):
         for lev in range(LEVELS):
             for chunk in range(chunks):
                 lane = lanes(chunk)
-                weights = [w[r, lev, :, lane] for r in range(ROWS + 6)]
-
-                def total_of(total, own_row, near_row, far_row):
-                    for r in range(-3, ROWS + 3):
-                        if 0 <= r < ROWS:
-                            v = own_row(r)
-                        else:
-                            d = -r if r < 0 else r - ROWS + 1
-                            v = near_row(d) if (r < 0) == odd else far_row(d)
-                        total = total + weights[r + 3] * jnp.broadcast_to(v, total.shape)
+                sides = [
+                    (w[3 - d, lev, :, lane], w[ROWS + 2 + d, lev, :, lane]) for d in range(1, 4)
+                ]
+
+                def total_of(total, near_row, far_row):
+                    for d, (south, north) in enumerate(sides, 1):
+                        for weight, is_near in ((south, odd), (north, not odd)):
+                            v = near_row(d) if is_near else far_row(d)
+                            total = total + weight * jnp.broadcast_to(v, total.shape)
                     return total
 
                 def gathered(ref, f):
@@ -277,15 +285,13 @@
 
                 for f in range(count):
                     adv[f, lev, :, lane] = total_of(
-                        zon[skip + f, lev, :, lane],
-                        lambda r: x[skip + f, lev, r : r + 1, lane],
+                        base[skip + f, lev, :, lane],
                         gathered(near, f) if direct else swapped(near, f),
                         gathered(far, f),
                     )
                 if direct:
                     adv[count, lev, :, lane] = total_of(
-                        zon_t[lev, :, lane],
-                        lambda r: t[lev, r : r + 1, lane],
+                        base_t[lev, :, lane],
                         gathered_t(near),
                         gathered_t(far),
                     )
@@ -457,7 +463,6 @@
         t,
         integer_boxes_traversed,
         partial_crossing_share,
-        c,
         higher_donor_stratum,
         deeper_donor_share,
         napierian_thickness_quotient,
@@ -476,38 +481,32 @@
         jnp.concatenate([peer_columns, columns], -1),
     )
 
-    mix, weights, zon, zon_t, factor = call(
-        functools.partial(early_kernel, fields, levels, bands - 1),
-        [
-            (levels, 2 * LEVELS, ROWS, lons),
-            (ROWS + 6, LEVELS, ROWS, lons),
-            x.shape,
-            t.shape,
-            (LEVELS, lons),
-        ],
+    mix, c_rows = call(
+        functools.partial(mix_kernel, levels),
+        [(levels, 2 * LEVELS, ROWS, lons), (LEVELS, lons)],
+        cost=COST["mix"],
+    )(columns, c, relay)
+    c_south = lax.ppermute(c_rows, "lat", [(i, i + 1) for i in range(bands - 1)])
+    weights, base, base_t = call(
+        functools.partial(early_kernel, fields, bands - 1),
+        [(ROWS + 6, LEVELS, ROWS, lons), x.shape, t.shape],
         [(3, LEVELS * ROWS, lons)],
         [smem] + [vmem] * 6,
         cost=COST["early"],
-        aliases={5: 2, 6: 3},
-    )(scale, columns, c, x, t, zon, zon_t)
-    weights = call(
-        patch_kernel,
-        weights.shape,
-        cost=COST["patch"],
-        aliases={3: 0},
-    )(factor, near_b, far_b, weights)
+        aliases={5: 1, 6: 2},
+    )(scale, c, c_south, x, t, zon, zon_t)
 
     adv_b = call(
         functools.partial(fin_kernel, 0, direct, True),
         (direct + 1,) + x.shape[1:],
         cost=COST["fin_b"],
-    )(x, zon, near_b, far_b, weights, t, zon_t)
+    )(base, near_b, far_b, weights, base_t)
     peer_b = other_core(adv_b)
     adv_a = call(
         functools.partial(fin_kernel, direct, swapped, False),
         (swapped,) + x.shape[1:],
         cost=COST["fin_a"],
-    )(x, zon, near_a, far_a, weights)
+    )(base, near_a, far_a, weights)
     peer_a = other_core(adv_a)
 
     anywhere = pl.BlockSpec(memory_space=pl.ANY)

time: 26.2 us -> 28.7 us (1.095)
  waiting for transfers between devices: 7.28 us -> 8.62 us
  starting transfers between devices: 9.29 us -> 10.6 us
  local copies, waits for them, and re-layouts: 1.74 us -> 1.1 us
  Pallas kernels: 6.55 us -> 7.09 us
    ppermute x0 -> x1, waiting for transfers between devices: none -> 3.79 us  [on_device(): lax.ppermute(c_rows, 'lat', [(i, i + 1) for i in range(bands - 1)])]
    ppermute x2, waiting for transfers between devices: 6.28 us -> 3.79 us  [swap(): return lax.ppermute(v, 'lat', pairs)]
    ppermute x0 -> x1, starting transfers between devices: none -> 1.29 us  [on_device(): lax.ppermute(c_rows, 'lat', [(i, i + 1) for i in range(bands - 1)])]
    pallas_call x2, Pallas kernels: 1.91 us -> 2.86 us  [the longest x1 2.79 us: on_device(): call(functools.partial(early_kernel, fields, bands - 1), [(ROWS + 6, LEVE...]
    unnamed x22, local copies, waits for them, and re-layouts: 1.74 us -> 1.1 us
  transfers between devices with their start and end apart: 7 -> 8, of which waited for: 4 -> 4; matrix products, arithmetic and copies ran while one was open for 1% -> 1% of each run, Pallas kernels for 22% -> 22%
where the time goes in v9:
time: 28.7 us; the launch traced here: 28.4 us
  starting transfers between devices  10.6 us (37%)
  waiting for transfers between devices  8.62 us (30%)
  Pallas kernels  7.09 us (25%)
  local copies, waits for them, and re-layouts  1.1 us (4%)
  between operations  0.86 us (3%)
    ppermute x1, starting transfers between devices, pass_on(): return lax.ppermute(v, 'lat', relays)  4.19 us
    ppermute x2, waiting for transfers between devices, swap(): return lax.ppermute(v, 'lat', pairs)  3.79 us
    ppermute x1, waiting for transfers between devices, on_device(): lax.ppermute(c_rows, 'lat', [(i, i + 1) for i in range(bands - 1)])  3.79 us
    ppermute x2, starting transfers between devices, swap(): return lax.ppermute(v, 'lat', pairs)  3.75 us
    pallas_call x1, Pallas kernels, on_device(): call(functools.partial(early_kernel, fields, bands - 1), [(ROWS + 6, LEVE...  2.79 us
    pallas_call x1, Pallas kernels, on_device(): call(functools.partial(zonal_kernel, fields), [x.shape, t.shape, direct_s...  2.49 us
    ppermute x1, starting transfers between devices, on_device(): lax.ppermute(c_rows, 'lat', [(i, i + 1) for i in range(bands - 1)])  1.29 us
    unnamed x22, local copies, waits for them, and re-layouts  1.1 us
  transfers between devices with their start and end apart: 8, of which 4 were waited for; matrix products, arithmetic and copies ran while one was open for 1% of the time, Pallas kernels for 22%

profile of v9, /device:TPU:0, one launch (start us, length us, event | category | flops | bytes accessed | tf_op | source)
XLA Modules:
  0.0 28.4 jit_solution(4399416744983953444)
XLA Ops:
  0.6 0.0 copy-start
  0.6 1.1 %copy-done = f32[16,2,4,1152]{3,2,1,0:T(4,128)S(1)} copy-done((f32[16,2,4,1152]{3,2,1,0:T(4,128)S(1)}, f32[16,2,4,1152]{3,2,1,0:T(4,128)}, u32[]{:S(2)}) %copy-start) | copy-done | bytes 589848
  1.7 0.0 copy-start.3
  1.7 0.0 copy-start.5
  1.7 0.0 copy-start.6
  1.7 0.0 copy-start.7
  1.7 0.0 copy-start.8
  1.7 0.0 copy-start.9
  1.7 0.0 copy-start.10
  1.8 3.0 %collective-permute-start.1 = (f32[8,2,4,1152]{3,2,1,0:T(4,128)S(1)}, f32[8,2,4,1152]{3,2,1,0:T(4,128)S(1)}, u32[]{:S(2)}, u32[]{:S(2)}) collective-permute-start(f32[8,2,4,1152]{3,2,1,0:T(4,128)S(1)} %shard_map.122), channel_id=1, source_target_pairs={{0,2},{2,0},{4,6},{6,4},{8,10},{10,8},{12,14},{14,12},{1,3},{3,1},... | collective-permute-start | bytes 884744 | tf_op jit(solution)/shard_map/ppermute | solution.py:426
  4.8 0.0 copy-done.3
  4.8 0.0 copy-done.5
  4.8 0.0 copy-done.6
  4.8 0.0 copy-done.7
  4.8 0.0 copy-done.8
  4.8 0.0 copy-done.9
  4.8 0.0 copy-done.10
  4.8 2.5 %shard_map.121 = (f32[16,2,4,1152]{3,2,1,0:T(4,128)S(1)}, f32[2,4,1152]{2,1,0:T(4,128)S(1)}, f32[7,8,1152]{2,1,0:T(8,128)S(1)}, f32[7,8,1152]{2,1,0:T(8,128)S(1)}, f32[13,4,576]{2,1,0:T(4,128)S(1)}) custom-call(f32[16,2,4,1152]{3,2,1,0:T(4,128)S(1)} %copy-done, f32[2,4,1152]{2,1,0:T(4,128)S(1)} %copy-done.3, s32[2,4,1152]{2,1,0:T(4,128)S(1)} %copy-done.8, ...), custom_call_target="tpu_custom_call" | custom-call | flops 10000000000 | bytes 1000 | tf_op jit(solution)/shard_map/pallas_call | solution.py:450
  7.3 0.1 collective-permute-start
  7.4 0.7 %collective-permute-start.5 = (f32[7,8,1152]{2,1,0:T(8,128)S(1)}, f32[7,8,1152]{2,1,0:T(8,128)S(1)}, u32[]{:S(2)}, u32[]{:S(2)}) collective-permute-start(f32[7,8,1152]{2,1,0:T(8,128)S(1)} %get-tuple-element.22), channel_id=1, source_target_pairs={{0,2},{2,0},{4,6},{6,4},{8,10},{10,8},{12,14},{14,12},{1,3},{3,1},... | collective-permute-start | bytes 774152 | tf_op jit(solution)/shard_map/ppermute | solution.py:426
  8.1 0.7 %collective-permute-start.6 = (f32[7,8,1152]{2,1,0:T(8,128)S(1)}, f32[7,8,1152]{2,1,0:T(8,128)S(1)}, u32[]{:S(2)}, u32[]{:S(2)}) collective-permute-start(f32[7,8,1152]{2,1,0:T(8,128)S(1)} %get-tuple-element.23), channel_id=1, source_target_pairs={{2,4},{4,2},{6,8},{8,6},{10,12},{12,10},{3,5},{5,3},{7,9},{9,7},{1... | collective-permute-start | bytes 774152 | tf_op jit(solution)/shard_map/ppermute | solution.py:429
  8.8 3.8 %collective-permute-done.1.swapped.refs_1_ = f32[8,2,4,1152]{3,2,1,0:T(4,128)S(1)} collective-permute-done((f32[8,2,4,1152]{3,2,1,0:T(4,128)S(1)}, f32[8,2,4,1152]{3,2,1,0:T(4,128)S(1)}, u32[]{:S(2)}, u32[]{:S(2)}) %collective-permute-start.1) | collective-permute-done | bytes 294944 | tf_op jit(solution)/shard_map/ppermute | solution.py:426
  12.6 0.0 copy-start.2
  12.6 0.1 shard_map.123.relay
  12.7 0.0 copy-start.1
  12.7 4.2 %collective-permute-start.3 = (f32[6,8,1152]{2,1,0:T(8,128)S(1)}, f32[6,8,1152]{2,1,0:T(8,128)S(1)}, u32[]{:S(2)}, u32[]{:S(2)}) collective-permute-start(f32[6,8,1152]{2,1,0:T(8,128)S(1)} %shard_map.123.relay), channel_id=1, source_target_pairs={{0,4},{4,8},{8,12},{6,2},{10,6},{14,10},{1,5},{5,9},{9,13},{7,3},{... | collective-permute-start | bytes 663560 | tf_op jit(solution)/shard_map/ppermute | solution.py:432
  16.9 0.0 collective-permute-done
  16.9 0.2 maximum_select_fusion.columns
  17.1 0.0 copy-done.2
  17.1 0.1 shard_map.124
  17.2 0.0 copy-start.4
  17.2 1.3 %collective-permute-start.2 = (f32[2,1152]{1,0:T(2,128)S(1)}, f32[2,1152]{1,0:T(2,128)S(1)}, u32[]{:S(2)}, u32[]{:S(2)}) collective-permute-start(f32[2,1152]{1,0:T(2,128)S(1)} %get-tuple-element.17), channel_id=1, source_target_pairs={{0,2},{2,4},{4,6},{6,8},{8,10},{10,12},{12,14},{1,3},{3,5},{5,7},{... | collective-permute-start | bytes 27656 | tf_op jit(solution)/shard_map/ppermute | solution.py:489
  18.5 3.8 %collective-permute-done.2.c_south = f32[2,1152]{1,0:T(2,128)S(1)} collective-permute-done((f32[2,1152]{1,0:T(2,128)S(1)}, f32[2,1152]{1,0:T(2,128)S(1)}, u32[]{:S(2)}, u32[]{:S(2)}) %collective-permute-start.2) | collective-permute-done | bytes 9248 | tf_op jit(solution)/shard_map/ppermute | solution.py:489
  22.3 0.0 copy-done.1
  22.3 0.0 copy-done.4
  22.3 2.8 %shard_map.125 = (f32[10,2,4,1152]{3,2,1,0:T(4,128)S(1)}, f32[16,2,4,1152]{3,2,1,0:T(4,128)S(1)}, f32[2,4,1152]{2,1,0:T(4,128)S(1)}) custom-call(f32[64]{0:T(128)S(1)} %copy-done.4, f32[2,4,1152]{2,1,0:T(4,128)S(1)} %copy-done.2, f32[2,1152]{1,0:T(2,128)S(1)} %collective-permute-done.2.c_south, ...), custom_call_target="tpu_custom_call", output_to_operand_aliasing={{1}: (5, {}), {2}: (6, {})} | custom-call | flops 1000000 | bytes 1000 | tf_op jit(solution)/shard_map/pallas_call | solution.py:490
  25.1 0.0 collective-permute-done.5.refs_1_
  25.1 0.0 collective-permute-done.6.refs_2_
  25.1 0.3 %shard_map.127.own = f32[9,2,4,1152]{3,2,1,0:T(4,128)S(1)} custom-call(f32[16,2,4,1152]{3,2,1,0:T(4,128)S(1)} %get-tuple-element.19.refs_0_, f32[7,8,1152]{2,1,0:T(8,128)S(1)} %collective-permute-done.5.refs_1_, f32[7,8,1152]{2,1,0:T(8,128)S(1)} %collective-permute-done.6.refs_2_, f32[10,2,4,1152]{3,2,1,0:T(4,128)S(1)} %get-tuple-element.20.refs_3_, ...), custom_call_target="tpu_custom_call" | custom-call | flops 1000000 | bytes 1000 | tf_op jit(solution)/shard_map/pallas_call | solution.py:499
  25.4 0.1 collective-permute-start.7
  25.5 0.0 collective-permute-done.3.refs_2_
  25.5 0.3 shard_map.126.own
  25.8 0.5 %collective-permute-start.4 = (f32[8,2,4,1152]{3,2,1,0:T(4,128)S(1)}, f32[8,2,4,1152]{3,2,1,0:T(4,128)S(1)}, u32[]{:S(2)}, u32[]{:S(2)}) collective-permute-start(f32[8,2,4,1152]{3,2,1,0:T(4,128)S(1)} %shard_map.126.own), channel_id=1, source_target_pairs={{0,1},{1,0},{2,3},{3,2},{4,5},{5,4},{6,7},{7,6},{8,9},{9,8},{10,11... | collective-permute-start | bytes 884744 | tf_op jit(solution)/shard_map/ppermute | solution.py:435
  26.3 0.8 %collective-permute-done.7.peer = f32[9,2,4,1152]{3,2,1,0:T(4,128)S(1)} collective-permute-done((f32[9,2,4,1152]{3,2,1,0:T(4,128)S(1)}, f32[9,2,4,1152]{3,2,1,0:T(4,128)S(1)}, u32[]{:S(2)}, u32[]{:S(2)}) %collective-permute-start.7) | collective-permute-done | bytes 331808 | tf_op jit(solution)/shard_map/ppermute | solution.py:435
  27.1 0.2 shard_map.128
  27.3 0.2 collective-permute-done.4.peer
  27.6 0.9 %shard_map.129 = (f32[16,2,4,1152]{3,2,1,0:T(4,128)}, f32[2,4,1152]{2,1,0:T(4,128)}, f32[2,4,1152]{2,1,0:T(4,128)}) custom-call(f32[8,2,4,1152]{3,2,1,0:T(4,128)S(1)} %shard_map.126.own, f32[8,2,4,1152]{3,2,1,0:T(4,128)S(1)} %collective-permute-done.4.peer, f32[4,4,4,1152]{3,2,1,0:T(4,128)S(1)} %get-tuple-element.21.weights, ...), custom_call_target="tpu_custom_call" | custom-call | flops 1000000 | bytes 1000 | tf_op jit(solution)/shard_map/pallas_call | solution.py:518
  (1 shorter events, 0.0 us)
Async XLA Ops:
  0.6 1.1 %copy-start = (f32[16,2,4,1152]{3,2,1,0:T(4,128)S(1)}, f32[16,2,4,1152]{3,2,1,0:T(4,128)}, u32[]{:S(2)}) copy-start(f32[16,2,4,1152]{3,2,1,0:T(4,128)} %x.5) | copy-start | bytes 1769476
  1.7 3.1 %copy-start.3 = (f32[2,4,1152]{2,1,0:T(4,128)S(1)}, f32[2,4,1152]{2,1,0:T(4,128)}, u32[]{:S(2)}) copy-start(f32[2,4,1152]{2,1,0:T(4,128)} %t.3) | copy-start | bytes 110596
  1.7 3.1 %copy-start.5 = (s32[4,4,576]{2,1,0:T(4,128)S(1)}, s32[4,4,576]{2,1,0:T(4,128)}, u32[]{:S(2)}) copy-start(s32[4,4,576]{2,1,0:T(4,128)} %upper.1) | copy-start | bytes 110596
  1.7 3.1 %copy-start.6 = (f32[4,4,576]{2,1,0:T(4,128)S(1)}, f32[4,4,576]{2,1,0:T(4,128)}, u32[]{:S(2)}) copy-start(f32[4,4,576]{2,1,0:T(4,128)} %share.1) | copy-start | bytes 110596
  1.7 3.1 %copy-start.7 = (f32[4,4,576]{2,1,0:T(4,128)S(1)}, f32[4,4,576]{2,1,0:T(4,128)}, u32[]{:S(2)}) copy-start(f32[4,4,576]{2,1,0:T(4,128)} %quotient.1) | copy-start | bytes 110596
  1.7 3.1 %copy-start.8 = (s32[2,4,1152]{2,1,0:T(4,128)S(1)}, s32[2,4,1152]{2,1,0:T(4,128)}, u32[]{:S(2)}) copy-start(s32[2,4,1152]{2,1,0:T(4,128)} %n.1) | copy-start | bytes 110596
  1.7 3.1 %copy-start.9 = (f32[2,4,1152]{2,1,0:T(4,128)S(1)}, f32[2,4,1152]{2,1,0:T(4,128)}, u32[]{:S(2)}) copy-start(f32[2,4,1152]{2,1,0:T(4,128)} %f.1) | copy-start | bytes 110596
  1.7 3.1 %copy-start.10 = (f32[4,576]{1,0:T(4,128)S(1)}, f32[4,576]{1,0:T(4,128)}, u32[]{:S(2)}) copy-start(f32[4,576]{1,0:T(4,128)} %ground.1) | copy-start | bytes 27652
  1.8 10.8 %collective-permute-start.1 = (f32[8,2,4,1152]{3,2,1,0:T(4,128)S(1)}, f32[8,2,4,1152]{3,2,1,0:T(4,128)S(1)}, u32[]{:S(2)}, u32[]{:S(2)}) collective-permute-start(f32[8,2,4,1152]{3,2,1,0:T(4,128)S(1)} %shard_map.122), channel_id=1, source_target_pairs={{0,2},{2,0},{4,6},{6,4},{8,10},{10,8},{12,14},{14,12},{1,3},{3,1},... | collective-permute-start | bytes 884744 | tf_op jit(solution)/shard_map/ppermute | solution.py:426
  7.3 9.6 %collective-permute-start = (f32[13,4,576]{2,1,0:T(4,128)S(1)}, f32[13,4,576]{2,1,0:T(4,128)S(1)}, u32[]{:S(2)}, u32[]{:S(2)}) collective-permute-start(f32[13,4,576]{2,1,0:T(4,128)S(1)} %get-tuple-element.15), channel_id=1, source_target_pairs={{0,1},{1,0},{2,3},{3,2},{4,5},{5,4},{6,7},{7,6},{8,9},{9,8},{10,11... | collective-permute-start | bytes 359432 | tf_op jit(solution)/shard_map/ppermute | solution.py:435
  7.4 17.7 %collective-permute-start.5 = (f32[7,8,1152]{2,1,0:T(8,128)S(1)}, f32[7,8,1152]{2,1,0:T(8,128)S(1)}, u32[]{:S(2)}, u32[]{:S(2)}) collective-permute-start(f32[7,8,1152]{2,1,0:T(8,128)S(1)} %get-tuple-element.22), channel_id=1, source_target_pairs={{0,2},{2,0},{4,6},{6,4},{8,10},{10,8},{12,14},{14,12},{1,3},{3,1},... | collective-permute-start | bytes 774152 | tf_op jit(solution)/shard_map/ppermute | solution.py:426
  8.1 17.0 %collective-permute-start.6 = (f32[7,8,1152]{2,1,0:T(8,128)S(1)}, f32[7,8,1152]{2,1,0:T(8,128)S(1)}, u32[]{:S(2)}, u32[]{:S(2)}) collective-permute-start(f32[7,8,1152]{2,1,0:T(8,128)S(1)} %get-tuple-element.23), channel_id=1, source_target_pairs={{2,4},{4,2},{6,8},{8,6},{10,12},{12,10},{3,5},{5,3},{7,9},{9,7},{1... | collective-permute-start | bytes 774152 | tf_op jit(solution)/shard_map/ppermute | solution.py:429
  12.6 4.5 %copy-start.2 = (f32[2,4,1152]{2,1,0:T(4,128)S(1)}, f32[2,4,1152]{2,1,0:T(4,128)}, u32[]{:S(2)}) copy-start(f32[2,4,1152]{2,1,0:T(4,128)} %c.3) | copy-start | bytes 110596
  12.7 9.6 %copy-start.1 = (f32[16,2,4,1152]{3,2,1,0:T(4,128)S(1)}, f32[16,2,4,1152]{3,2,1,0:T(4,128)}, u32[]{:S(2)}) copy-start(f32[16,2,4,1152]{3,2,1,0:T(4,128)} %x.5) | copy-start | bytes 1769476
  12.7 12.8 %collective-permute-start.3 = (f32[6,8,1152]{2,1,0:T(8,128)S(1)}, f32[6,8,1152]{2,1,0:T(8,128)S(1)}, u32[]{:S(2)}, u32[]{:S(2)}) collective-permute-start(f32[6,8,1152]{2,1,0:T(8,128)S(1)} %shard_map.123.relay), channel_id=1, source_target_pairs={{0,4},{4,8},{8,12},{6,2},{10,6},{14,10},{1,5},{5,9},{9,13},{7,3},{... | collective-permute-start | bytes 663560 | tf_op jit(solution)/shard_map/ppermute | solution.py:432
  17.2 5.1 %copy-start.4 = (f32[64]{0:T(128)S(1)}, f32[64]{0:T(128)}, u32[]{:S(2)}) copy-start(f32[64]{0:T(128)} %constant.8.clone.scale) | copy-start | bytes 772
  17.2 5.1 %collective-permute-start.2 = (f32[2,1152]{1,0:T(2,128)S(1)}, f32[2,1152]{1,0:T(2,128)S(1)}, u32[]{:S(2)}, u32[]{:S(2)}) collective-permute-start(f32[2,1152]{1,0:T(2,128)S(1)} %get-tuple-element.17), channel_id=1, source_target_pairs={{0,2},{2,4},{4,6},{6,8},{8,10},{10,12},{12,14},{1,3},{3,5},{5,7},{... | collective-permute-start | bytes 27656 | tf_op jit(solution)/shard_map/ppermute | solution.py:489
  25.4 1.7 %collective-permute-start.7 = (f32[9,2,4,1152]{3,2,1,0:T(4,128)S(1)}, f32[9,2,4,1152]{3,2,1,0:T(4,128)S(1)}, u32[]{:S(2)}, u32[]{:S(2)}) collective-permute-start(f32[9,2,4,1152]{3,2,1,0:T(4,128)S(1)} %shard_map.127.own), channel_id=1, source_target_pairs={{0,1},{1,0},{2,3},{3,2},{4,5},{5,4},{6,7},{7,6},{8,9},{9,8},{10,11... | collective-permute-start | bytes 995336 | tf_op jit(solution)/shard_map/ppermute | solution.py:435
  25.8 1.8 %collective-permute-start.4 = (f32[8,2,4,1152]{3,2,1,0:T(4,128)S(1)}, f32[8,2,4,1152]{3,2,1,0:T(4,128)S(1)}, u32[]{:S(2)}, u32[]{:S(2)}) collective-permute-start(f32[8,2,4,1152]{3,2,1,0:T(4,128)S(1)} %shard_map.126.own), channel_id=1, source_target_pairs={{0,1},{1,0},{2,3},{3,2},{4,5},{5,4},{6,7},{7,6},{8,9},{9,8},{10,11... | collective-permute-start | bytes 884744 | tf_op jit(solution)/shard_map/ppermute | solution.py:435

commit v10 on v8

--- a/solution.py
+++ b/solution.py
@@ -124,7 +124,8 @@
 
 
 def early_kernel(
-    fields, levels, last, scale, columns, c, x, t, zon_in, zon_t_in, mix, out, zon, zon_t, factor, ws
+    fields, levels, last, scale, columns, c, x, t, zon_in, zon_t_in,
+    mix, out, zon, zon_t, factor, south_rows, south_rows_t, ws,
 ):
     lat = lax.axis_index("lat")
     lons = x.shape[-1]
@@ -141,6 +142,29 @@
         for lev in range(LEVELS):
             out[r, lev] = w[lev * ROWS : (lev + 1) * ROWS]
 
+    for lev in range(LEVELS):
+        for r in range(3):
+            at = r * LEVELS + lev
+            south_rows_t[at : at + 1, :] = t[lev, r : r + 1, :]
+            for i in range(fields):
+                south_rows[at, i : i + 1, :] = x[i, lev, r : r + 1, :]
+        for chunk in range(lons // LANE):
+            lane = lanes(chunk)
+            weights = [out[r + 3, lev, :, lane] for r in range(ROWS)]
+
+            def with_own_rows(total, row_at):
+                for r, w in enumerate(weights):
+                    total = total + w * jnp.broadcast_to(row_at(r), total.shape)
+                return total
+
+            zon_t[lev, :, lane] = with_own_rows(
+                zon_t_in[lev, :, lane], lambda r: t[lev, r : r + 1, lane]
+            )
+            for i in range(fields):
+                zon[i, lev, :, lane] = with_own_rows(
+                    zon_in[i, lev, :, lane], lambda r: x[i, lev, r : r + 1, lane]
+                )
+
     def pole(rows):
         for k, (_, at) in enumerate(rows):
             ws[k] = stacked(out.at[at])
@@ -176,14 +200,28 @@
         pole([(ROWS - d, ROWS + 2 + d) for d in range(1, 4)])
 
 
-def patch_kernel(factor, near, far, weights_in, weights):
+def patch_kernel(factor, near, far, weights, south_rows, south_rows_t, low, delta, delta_t):
     block = 3 * LEVELS
     rows = slice(block, block + LEVELS)
     below = jnp.where(parity() == 1, near[block, rows, :], far[block, rows, :])
-    for r, part in enumerate(face_weights(below)):
-        part = factor[...] * part
+    parts = [factor[...] * part for part in face_weights(below)]
+    for r in range(3):
         for lev in range(LEVELS):
-            weights[r, lev, 0:1, :] = weights[r, lev, 0:1, :] + part[lev : lev + 1]
+            w = weights[r, lev]
+            low[r, lev] = w
+            low[r, lev, 0:1, :] = w[0:1] + parts[r][lev : lev + 1]
+    total_t = None
+    for r in range(3):
+        term = parts[r + 3] * south_rows_t[LEVELS * r : LEVELS * (r + 1), :]
+        total_t = term if total_t is None else total_t + term
+    delta_t[...] = total_t
+    for lev in range(LEVELS):
+        total = None
+        for r in range(3):
+            v = south_rows[r * LEVELS + lev]
+            term = jnp.broadcast_to(parts[r + 3][lev : lev + 1], v.shape) * v
+            total = term if total is None else total + term
+        delta[lev] = total
 
 
 def zonal_kernel(
@@ -237,25 +275,26 @@
 
 def fin_kernel(skip, count, direct, *refs):
     if direct:
-        x, zon, near, far, w, t, zon_t, adv = refs
+        base, near, far, w, low, delta, base_t, delta_t, adv = refs
     else:
-        x, zon, near, far, w, adv = refs
+        base, near, far, w, low, delta, adv = refs
     chunks = w.shape[-1] // LANE
+    first_row = lax.broadcasted_iota(jnp.int32, (ROWS, LANE), 0) == 0
 
     def body(odd):
         for lev in range(LEVELS):
             for chunk in range(chunks):
                 lane = lanes(chunk)
-                weights = [w[r, lev, :, lane] for r in range(ROWS + 6)]
-
-                def total_of(total, own_row, near_row, far_row):
-                    for r in range(-3, ROWS + 3):
-                        if 0 <= r < ROWS:
-                            v = own_row(r)
-                        else:
-                            d = -r if r < 0 else r - ROWS + 1
-                            v = near_row(d) if (r < 0) == odd else far_row(d)
-                        total = total + weights[r + 3] * jnp.broadcast_to(v, total.shape)
+                sides = [
+                    (low[3 - d, lev, :, lane], w[ROWS + 2 + d, lev, :, lane]) for d in range(1, 4)
+                ]
+
+                def total_of(total, row_0, near_row, far_row):
+                    total = total + jnp.where(first_row, jnp.broadcast_to(row_0, total.shape), 0.0)
+                    for d, (south, north) in enumerate(sides, 1):
+                        for weight, is_near in ((south, odd), (north, not odd)):
+                            v = near_row(d) if is_near else far_row(d)
+                            total = total + weight * jnp.broadcast_to(v, total.shape)
                     return total
 
                 def gathered(ref, f):
@@ -277,15 +316,15 @@
 
                 for f in range(count):
                     adv[f, lev, :, lane] = total_of(
-                        zon[skip + f, lev, :, lane],
-                        lambda r: x[skip + f, lev, r : r + 1, lane],
+                        base[skip + f, lev, :, lane],
+                        delta[lev, skip + f : skip + f + 1, lane],
                         gathered(near, f) if direct else swapped(near, f),
                         gathered(far, f),
                     )
                 if direct:
                     adv[count, lev, :, lane] = total_of(
-                        zon_t[lev, :, lane],
-                        lambda r: t[lev, r : r + 1, lane],
+                        base_t[lev, :, lane],
+                        delta_t[lev : lev + 1, lane],
                         gathered_t(near),
                         gathered_t(far),
                     )
@@ -476,7 +515,7 @@
         jnp.concatenate([peer_columns, columns], -1),
     )
 
-    mix, weights, zon, zon_t, factor = call(
+    mix, weights, base, base_t, factor, south_rows, south_rows_t = call(
         functools.partial(early_kernel, fields, levels, bands - 1),
         [
             (levels, 2 * LEVELS, ROWS, lons),
@@ -484,30 +523,30 @@
             x.shape,
             t.shape,
             (LEVELS, lons),
+            (3 * LEVELS, fields, lons),
+            (3 * LEVELS, lons),
         ],
         [(3, LEVELS * ROWS, lons)],
         [smem] + [vmem] * 6,
         cost=COST["early"],
-        aliases={5: 2, 6: 3},
     )(scale, columns, c, x, t, zon, zon_t)
-    weights = call(
+    low, delta, delta_t = call(
         patch_kernel,
-        weights.shape,
+        [(3, LEVELS, ROWS, lons), (LEVELS, fields, lons), (LEVELS, lons)],
         cost=COST["patch"],
-        aliases={3: 0},
-    )(factor, near_b, far_b, weights)
+    )(factor, near_b, far_b, weights, south_rows, south_rows_t)
 
     adv_b = call(
         functools.partial(fin_kernel, 0, direct, True),
         (direct + 1,) + x.shape[1:],
         cost=COST["fin_b"],
-    )(x, zon, near_b, far_b, weights, t, zon_t)
+    )(base, near_b, far_b, weights, low, delta, base_t, delta_t)
     peer_b = other_core(adv_b)
     adv_a = call(
         functools.partial(fin_kernel, direct, swapped, False),
         (swapped,) + x.shape[1:],
         cost=COST["fin_a"],
-    )(x, zon, near_a, far_a, weights)
+    )(base, near_a, far_a, weights, low, delta)
     peer_a = other_core(adv_a)
 
     anywhere = pl.BlockSpec(memory_space=pl.ANY)

time: 26.2 us -> 26 us (level)
  waiting for transfers between devices: 7.28 us -> 6.77 us
  Pallas kernels: 6.55 us -> 6.87 us
    pallas_call x1, Pallas kernels: 1.82 us -> 2.33 us  [on_device(): call(functools.partial(early_kernel, fields, levels, bands - 1), [(levels...]
    ppermute x2, waiting for transfers between devices: 6.28 us -> 5.77 us  [swap(): return lax.ppermute(v, 'lat', pairs)]
  transfers between devices with their start and end apart: 7 -> 7, of which waited for: 4 -> 4; matrix products, arithmetic and copies ran while one was open for 1% -> 1% of each run, Pallas kernels for 22% -> 23%
where the time goes in v10:
time: 26 us; the launch traced here: 25.7 us
  starting transfers between devices  9.29 us (36%)
  Pallas kernels  6.87 us (26%)
  waiting for transfers between devices  6.77 us (26%)
  local copies, waits for them, and re-layouts  1.74 us (7%)
  between operations  0.84 us (3%)
    ppermute x2, waiting for transfers between devices, swap(): return lax.ppermute(v, 'lat', pairs)  5.77 us
    ppermute x1, starting transfers between devices, pass_on(): return lax.ppermute(v, 'lat', relays)  4.19 us
    ppermute x2, starting transfers between devices, swap(): return lax.ppermute(v, 'lat', pairs)  3.75 us
    pallas_call x1, Pallas kernels, on_device(): call(functools.partial(zonal_kernel, fields), [x.shape, t.shape, direct_s...  2.5 us
    pallas_call x1, Pallas kernels, on_device(): call(functools.partial(early_kernel, fields, levels, bands - 1), [(levels...  2.33 us
    unnamed x22, local copies, waits for them, and re-layouts  1.74 us
    ppermute x3, waiting for transfers between devices, other_core(): return lax.ppermute(v, 'lev', cores)  1 us
    pallas_call x1, Pallas kernels, on_device(): call(functools.partial(remap_last_kernel, levels), [x.shape, t.shape, t.s...  0.9 us
  transfers between devices with their start and end apart: 7, of which 4 were waited for; matrix products, arithmetic and copies ran while one was open for 1% of the time, Pallas kernels for 23%

profile of v10, /device:TPU:0, one launch (start us, length us, event | category | flops | bytes accessed | tf_op | source)
XLA Modules:
  0.0 25.7 jit_solution(14180384497841998553)
XLA Ops:
  0.6 0.0 copy-start
  0.6 1.1 %copy-done = f32[16,2,4,1152]{3,2,1,0:T(4,128)S(1)} copy-done((f32[16,2,4,1152]{3,2,1,0:T(4,128)S(1)}, f32[16,2,4,1152]{3,2,1,0:T(4,128)}, u32[]{:S(2)}) %copy-start) | copy-done | bytes 589848
  1.7 0.0 copy-start.2
  1.7 0.0 copy-start.3
  1.7 0.0 copy-start.5
  1.7 0.0 copy-start.6
  1.7 0.0 copy-start.7
  1.7 0.0 copy-start.8
  1.7 0.0 copy-start.9
  1.7 0.0 copy-start.10
  1.8 3.0 %collective-permute-start.1 = (f32[8,2,4,1152]{3,2,1,0:T(4,128)S(1)}, f32[8,2,4,1152]{3,2,1,0:T(4,128)S(1)}, u32[]{:S(2)}, u32[]{:S(2)}) collective-permute-start(f32[8,2,4,1152]{3,2,1,0:T(4,128)S(1)} %shard_map.123), channel_id=1, source_target_pairs={{0,2},{2,0},{4,6},{6,4},{8,10},{10,8},{12,14},{14,12},{1,3},{3,1},... | collective-permute-start | bytes 884744 | tf_op jit(solution)/shard_map/ppermute | solution.py:459
  4.8 0.0 copy-done.2
  4.8 0.0 copy-done.3
  4.8 0.0 copy-done.5
  4.8 0.0 copy-done.6
  4.8 0.0 copy-done.7
  4.8 0.0 copy-done.8
  4.8 0.0 copy-done.9
  4.8 0.0 copy-done.10
  4.8 2.5 %shard_map.121 = (f32[16,2,4,1152]{3,2,1,0:T(4,128)S(1)}, f32[2,4,1152]{2,1,0:T(4,128)S(1)}, f32[7,8,1152]{2,1,0:T(8,128)S(1)}, f32[7,8,1152]{2,1,0:T(8,128)S(1)}, f32[13,4,576]{2,1,0:T(4,128)S(1)}) custom-call(f32[16,2,4,1152]{3,2,1,0:T(4,128)S(1)} %copy-done, f32[2,4,1152]{2,1,0:T(4,128)S(1)} %copy-done.2, s32[2,4,1152]{2,1,0:T(4,128)S(1)} %copy-done.8, ...), custom_call_target="tpu_custom_call" | custom-call | flops 10000000000 | bytes 1000 | tf_op jit(solution)/shard_map/pallas_call | solution.py:483
  7.3 0.1 collective-permute-start
  7.4 0.7 %collective-permute-start.3 = (f32[7,8,1152]{2,1,0:T(8,128)S(1)}, f32[7,8,1152]{2,1,0:T(8,128)S(1)}, u32[]{:S(2)}, u32[]{:S(2)}) collective-permute-start(f32[7,8,1152]{2,1,0:T(8,128)S(1)} %get-tuple-element.26), channel_id=1, source_target_pairs={{0,2},{2,0},{4,6},{6,4},{8,10},{10,8},{12,14},{14,12},{1,3},{3,1},... | collective-permute-start | bytes 774152 | tf_op jit(solution)/shard_map/ppermute | solution.py:459
  8.2 0.7 %collective-permute-start.4 = (f32[7,8,1152]{2,1,0:T(8,128)S(1)}, f32[7,8,1152]{2,1,0:T(8,128)S(1)}, u32[]{:S(2)}, u32[]{:S(2)}) collective-permute-start(f32[7,8,1152]{2,1,0:T(8,128)S(1)} %get-tuple-element.27), channel_id=1, source_target_pairs={{2,4},{4,2},{6,8},{8,6},{10,12},{12,10},{3,5},{5,3},{7,9},{9,7},{1... | collective-permute-start | bytes 774152 | tf_op jit(solution)/shard_map/ppermute | solution.py:462
  8.9 3.8 %collective-permute-done.1.swapped.refs_1_ = f32[8,2,4,1152]{3,2,1,0:T(4,128)S(1)} collective-permute-done((f32[8,2,4,1152]{3,2,1,0:T(4,128)S(1)}, f32[8,2,4,1152]{3,2,1,0:T(4,128)S(1)}, u32[]{:S(2)}, u32[]{:S(2)}) %collective-permute-start.1) | collective-permute-done | bytes 294944 | tf_op jit(solution)/shard_map/ppermute | solution.py:459
  12.6 0.0 copy-start.1
  12.6 0.1 shard_map.124
  12.7 4.2 %collective-permute-start.2 = (f32[6,8,1152]{2,1,0:T(8,128)S(1)}, f32[6,8,1152]{2,1,0:T(8,128)S(1)}, u32[]{:S(2)}, u32[]{:S(2)}) collective-permute-start(f32[6,8,1152]{2,1,0:T(8,128)S(1)} %shard_map.124), channel_id=1, source_target_pairs={{0,4},{4,8},{8,12},{6,2},{10,6},{14,10},{1,5},{5,9},{9,13},{7,3},{... | collective-permute-start | bytes 663560 | tf_op jit(solution)/shard_map/ppermute | solution.py:465
  16.9 0.0 collective-permute-done
  16.9 0.2 maximum_select_fusion.columns
  17.1 0.0 copy-start.4
  17.1 0.0 copy-done.1
  17.1 0.6 %copy-done.4 = f32[64]{0:T(128)S(1)} copy-done((f32[64]{0:T(128)S(1)}, f32[64]{0:T(128)}, u32[]{:S(2)}) %copy-start.4) | copy-done | bytes 280
  17.8 2.3 %shard_map.122 = (f32[4,4,4,1152]{3,2,1,0:T(4,128)S(1)}, f32[10,2,4,1152]{3,2,1,0:T(4,128)S(1)}, f32[16,2,4,1152]{3,2,1,0:T(4,128)S(1)}, f32[2,4,1152]{2,1,0:T(4...) custom-call(f32[64]{0:T(128)S(1)} %copy-done.4, ...), custom_call_target="tpu_custom_call" | custom-call | flops 1000000 | bytes 1000 | tf_op jit(solution)/shard_map/pallas_call | solution.py:518
  20.1 2.0 %collective-permute-done.3.near.refs_1_ = f32[7,8,1152]{2,1,0:T(8,128)S(1)} collective-permute-done((f32[7,8,1152]{2,1,0:T(8,128)S(1)}, f32[7,8,1152]{2,1,0:T(8,128)S(1)}, u32[]{:S(2)}, u32[]{:S(2)}) %collective-permute-start.3) | collective-permute-done | bytes 258080 | tf_op jit(solution)/shard_map/ppermute | solution.py:459
  22.1 0.0 collective-permute-done.4.far.refs_2_
  22.1 0.1 shard_map.125
  22.3 0.3 %shard_map.127.own = f32[9,2,4,1152]{3,2,1,0:T(4,128)S(1)} custom-call(f32[16,2,4,1152]{3,2,1,0:T(4,128)S(1)} %get-tuple-element.23.refs_0_, f32[7,8,1152]{2,1,0:T(8,128)S(1)} %collective-permute-done.3.near.refs_1_, f32[7,8,1152]{2,1,0:T(8,128)S(1)} %collective-permute-done.4.far.refs_2_, f32[10,2,4,1152]{3,2,1,0:T(4,128)S(1)} %get-tuple-element.24.weights.refs_3_, ...), custom_call_target="tpu_custom_call" | custom-call | flops 1000000 | bytes 1000 | tf_op jit(solution)/shard_map/pallas_call | solution.py:539
  22.6 0.1 collective-permute-start.6
  22.7 0.0 collective-permute-done.2.refs_2_
  22.7 0.3 %shard_map.126.own = f32[8,2,4,1152]{3,2,1,0:T(4,128)S(1)} custom-call(f32[16,2,4,1152]{3,2,1,0:T(4,128)S(1)} %get-tuple-element.23.refs_0_, f32[8,2,4,1152]{3,2,1,0:T(4,128)S(1)} %collective-permute-done.1.swapped.refs_1_, f32[6,8,1152]{2,1,0:T(8,128)S(1)} %collective-permute-done.2.refs_2_, f32[10,2,4,1152]{3,2,1,0:T(4,128)S(1)} %get-tuple-element.24.weights.refs_3_, ...), custom_call_target="tpu_custom_call" | custom-call | flops 1000000 | bytes 1000 | tf_op jit(solution)/shard_map/pallas_call | solution.py:545
  23.1 0.5 %collective-permute-start.5 = (f32[8,2,4,1152]{3,2,1,0:T(4,128)S(1)}, f32[8,2,4,1152]{3,2,1,0:T(4,128)S(1)}, u32[]{:S(2)}, u32[]{:S(2)}) collective-permute-start(f32[8,2,4,1152]{3,2,1,0:T(4,128)S(1)} %shard_map.126.own), channel_id=1, source_target_pairs={{0,1},{1,0},{2,3},{3,2},{4,5},{5,4},{6,7},{7,6},{8,9},{9,8},{10,11... | collective-permute-start | bytes 884744 | tf_op jit(solution)/shard_map/ppermute | solution.py:468
  23.6 0.7 %collective-permute-done.6.peer = f32[9,2,4,1152]{3,2,1,0:T(4,128)S(1)} collective-permute-done((f32[9,2,4,1152]{3,2,1,0:T(4,128)S(1)}, f32[9,2,4,1152]{3,2,1,0:T(4,128)S(1)}, u32[]{:S(2)}, u32[]{:S(2)}) %collective-permute-start.6) | collective-permute-done | bytes 331808 | tf_op jit(solution)/shard_map/ppermute | solution.py:468
  24.3 0.2 shard_map.128
  24.5 0.3 %collective-permute-done.5.peer = f32[8,2,4,1152]{3,2,1,0:T(4,128)S(1)} collective-permute-done((f32[8,2,4,1152]{3,2,1,0:T(4,128)S(1)}, f32[8,2,4,1152]{3,2,1,0:T(4,128)S(1)}, u32[]{:S(2)}, u32[]{:S(2)}) %collective-permute-start.5) | collective-permute-done | bytes 294944 | tf_op jit(solution)/shard_map/ppermute | solution.py:468
  24.8 0.9 %shard_map.129 = (f32[16,2,4,1152]{3,2,1,0:T(4,128)}, f32[2,4,1152]{2,1,0:T(4,128)}, f32[2,4,1152]{2,1,0:T(4,128)}) custom-call(f32[8,2,4,1152]{3,2,1,0:T(4,128)S(1)} %shard_map.126.own, f32[8,2,4,1152]{3,2,1,0:T(4,128)S(1)} %collective-permute-done.5.peer, f32[4,4,4,1152]{3,2,1,0:T(4,128)S(1)} %get-tuple-element.32.weights, ...), custom_call_target="tpu_custom_call" | custom-call | flops 1000000 | bytes 1000 | tf_op jit(solution)/shard_map/pallas_call | solution.py:558
  (1 shorter events, 0.0 us)
Async XLA Ops:
  0.6 1.1 %copy-start = (f32[16,2,4,1152]{3,2,1,0:T(4,128)S(1)}, f32[16,2,4,1152]{3,2,1,0:T(4,128)}, u32[]{:S(2)}) copy-start(f32[16,2,4,1152]{3,2,1,0:T(4,128)} %x.5) | copy-start | bytes 1769476
  1.7 3.1 %copy-start.2 = (f32[2,4,1152]{2,1,0:T(4,128)S(1)}, f32[2,4,1152]{2,1,0:T(4,128)}, u32[]{:S(2)}) copy-start(f32[2,4,1152]{2,1,0:T(4,128)} %t.3) | copy-start | bytes 110596
  1.7 3.1 %copy-start.3 = (f32[2,4,1152]{2,1,0:T(4,128)S(1)}, f32[2,4,1152]{2,1,0:T(4,128)}, u32[]{:S(2)}) copy-start(f32[2,4,1152]{2,1,0:T(4,128)} %c.3) | copy-start | bytes 110596
  1.7 3.1 %copy-start.5 = (s32[4,4,576]{2,1,0:T(4,128)S(1)}, s32[4,4,576]{2,1,0:T(4,128)}, u32[]{:S(2)}) copy-start(s32[4,4,576]{2,1,0:T(4,128)} %upper.1) | copy-start | bytes 110596
  1.7 3.1 %copy-start.6 = (f32[4,4,576]{2,1,0:T(4,128)S(1)}, f32[4,4,576]{2,1,0:T(4,128)}, u32[]{:S(2)}) copy-start(f32[4,4,576]{2,1,0:T(4,128)} %share.1) | copy-start | bytes 110596
  1.7 3.1 %copy-start.7 = (f32[4,4,576]{2,1,0:T(4,128)S(1)}, f32[4,4,576]{2,1,0:T(4,128)}, u32[]{:S(2)}) copy-start(f32[4,4,576]{2,1,0:T(4,128)} %quotient.1) | copy-start | bytes 110596
  1.7 3.1 %copy-start.8 = (s32[2,4,1152]{2,1,0:T(4,128)S(1)}, s32[2,4,1152]{2,1,0:T(4,128)}, u32[]{:S(2)}) copy-start(s32[2,4,1152]{2,1,0:T(4,128)} %n.1) | copy-start | bytes 110596
  1.7 3.1 %copy-start.9 = (f32[2,4,1152]{2,1,0:T(4,128)S(1)}, f32[2,4,1152]{2,1,0:T(4,128)}, u32[]{:S(2)}) copy-start(f32[2,4,1152]{2,1,0:T(4,128)} %f.1) | copy-start | bytes 110596
  1.7 3.1 %copy-start.10 = (f32[4,576]{1,0:T(4,128)S(1)}, f32[4,576]{1,0:T(4,128)}, u32[]{:S(2)}) copy-start(f32[4,576]{1,0:T(4,128)} %ground.1) | copy-start | bytes 27652
  1.8 10.8 %collective-permute-start.1 = (f32[8,2,4,1152]{3,2,1,0:T(4,128)S(1)}, f32[8,2,4,1152]{3,2,1,0:T(4,128)S(1)}, u32[]{:S(2)}, u32[]{:S(2)}) collective-permute-start(f32[8,2,4,1152]{3,2,1,0:T(4,128)S(1)} %shard_map.123), channel_id=1, source_target_pairs={{0,2},{2,0},{4,6},{6,4},{8,10},{10,8},{12,14},{14,12},{1,3},{3,1},... | collective-permute-start | bytes 884744 | tf_op jit(solution)/shard_map/ppermute | solution.py:459
  7.3 9.6 %collective-permute-start = (f32[13,4,576]{2,1,0:T(4,128)S(1)}, f32[13,4,576]{2,1,0:T(4,128)S(1)}, u32[]{:S(2)}, u32[]{:S(2)}) collective-permute-start(f32[13,4,576]{2,1,0:T(4,128)S(1)} %get-tuple-element.20), channel_id=1, source_target_pairs={{0,1},{1,0},{2,3},{3,2},{4,5},{5,4},{6,7},{7,6},{8,9},{9,8},{10,11... | collective-permute-start | bytes 359432 | tf_op jit(solution)/shard_map/ppermute | solution.py:468
  7.4 14.7 %collective-permute-start.3 = (f32[7,8,1152]{2,1,0:T(8,128)S(1)}, f32[7,8,1152]{2,1,0:T(8,128)S(1)}, u32[]{:S(2)}, u32[]{:S(2)}) collective-permute-start(f32[7,8,1152]{2,1,0:T(8,128)S(1)} %get-tuple-element.26), channel_id=1, source_target_pairs={{0,2},{2,0},{4,6},{6,4},{8,10},{10,8},{12,14},{14,12},{1,3},{3,1},... | collective-permute-start | bytes 774152 | tf_op jit(solution)/shard_map/ppermute | solution.py:459
  8.2 13.9 %collective-permute-start.4 = (f32[7,8,1152]{2,1,0:T(8,128)S(1)}, f32[7,8,1152]{2,1,0:T(8,128)S(1)}, u32[]{:S(2)}, u32[]{:S(2)}) collective-permute-start(f32[7,8,1152]{2,1,0:T(8,128)S(1)} %get-tuple-element.27), channel_id=1, source_target_pairs={{2,4},{4,2},{6,8},{8,6},{10,12},{12,10},{3,5},{5,3},{7,9},{9,7},{1... | collective-permute-start | bytes 774152 | tf_op jit(solution)/shard_map/ppermute | solution.py:462
  12.6 4.5 %copy-start.1 = (f32[16,2,4,1152]{3,2,1,0:T(4,128)S(1)}, f32[16,2,4,1152]{3,2,1,0:T(4,128)}, u32[]{:S(2)}) copy-start(f32[16,2,4,1152]{3,2,1,0:T(4,128)} %x.5) | copy-start | bytes 1769476
  12.7 10.0 %collective-permute-start.2 = (f32[6,8,1152]{2,1,0:T(8,128)S(1)}, f32[6,8,1152]{2,1,0:T(8,128)S(1)}, u32[]{:S(2)}, u32[]{:S(2)}) collective-permute-start(f32[6,8,1152]{2,1,0:T(8,128)S(1)} %shard_map.124), channel_id=1, source_target_pairs={{0,4},{4,8},{8,12},{6,2},{10,6},{14,10},{1,5},{5,9},{9,13},{7,3},{... | collective-permute-start | bytes 663560 | tf_op jit(solution)/shard_map/ppermute | solution.py:465
  17.1 0.7 %copy-start.4 = (f32[64]{0:T(128)S(1)}, f32[64]{0:T(128)}, u32[]{:S(2)}) copy-start(f32[64]{0:T(128)} %constant.8.clone.scale) | copy-start | bytes 772
  22.6 1.7 %collective-permute-start.6 = (f32[9,2,4,1152]{3,2,1,0:T(4,128)S(1)}, f32[9,2,4,1152]{3,2,1,0:T(4,128)S(1)}, u32[]{:S(2)}, u32[]{:S(2)}) collective-permute-start(f32[9,2,4,1152]{3,2,1,0:T(4,128)S(1)} %shard_map.127.own), channel_id=1, source_target_pairs={{0,1},{1,0},{2,3},{3,2},{4,5},{5,4},{6,7},{7,6},{8,9},{9,8},{10,11... | collective-permute-start | bytes 995336 | tf_op jit(solution)/shard_map/ppermute | solution.py:468
  23.1 1.7 %collective-permute-start.5 = (f32[8,2,4,1152]{3,2,1,0:T(4,128)S(1)}, f32[8,2,4,1152]{3,2,1,0:T(4,128)S(1)}, u32[]{:S(2)}, u32[]{:S(2)}) collective-permute-start(f32[8,2,4,1152]{3,2,1,0:T(4,128)S(1)} %shard_map.126.own), channel_id=1, source_target_pairs={{0,1},{1,0},{2,3},{3,2},{4,5},{5,4},{6,7},{7,6},{8,9},{9,8},{10,11... | collective-permute-start | bytes 884744 | tf_op jit(solution)/shard_map/ppermute | solution.py:468

commit v11 on v10

--- a/solution.py
+++ b/solution.py
@@ -402,13 +402,13 @@
         copy.start()
         copies.append(copy)
 
-    half = count // 2
-    for start in (0, half):
-        send(first.at[pl.ds(start, half)], out.at[pl.ds(start, half)])
+    piece = count // 1
+    for start in range(0, count, piece):
+        send(first.at[pl.ds(start, piece)], out.at[pl.ds(start, piece)])
     mine = group * LEVELS
     send(thick.at[pl.ds(mine, LEVELS)], out_phi)
     send(thick.at[pl.ds(levels + mine, LEVELS)], out_t)
-    step = 2
+    step = 4
     for start in range(0, buffer.shape[0], step):
         blend(own, peer, weights, buffer, range(start, start + step))
         send(buffer.at[pl.ds(start, step)], out.at[pl.ds(count + start, step)])
@@ -558,7 +558,7 @@
     return call(
         functools.partial(remap_last_kernel, levels),
         [x.shape, t.shape, t.shape],
-        [(swapped,) + x.shape[1:], pltpu.SemaphoreType.DMA((4 + swapped // 2,))],
+        [(swapped,) + x.shape[1:], pltpu.SemaphoreType.DMA((2 + 1 + swapped // 4,))],
         cost=COST["last"],
         out_specs=(anywhere,) * 3,
     )(adv_a, peer_a, mix, first, thick)

time: 26 us -> 26 us (level)
  no operation moved by 1% of the time
where the time goes in v11:
time: 26 us; the launch traced here: 25.7 us
  starting transfers between devices  9.29 us (36%)
  Pallas kernels  6.85 us (26%)
  waiting for transfers between devices  6.77 us (26%)
  local copies, waits for them, and re-layouts  1.74 us (7%)
  between operations  0.84 us (3%)
    ppermute x2, waiting for transfers between devices, swap(): return lax.ppermute(v, 'lat', pairs)  5.77 us
    ppermute x1, starting transfers between devices, pass_on(): return lax.ppermute(v, 'lat', relays)  4.19 us
    ppermute x2, starting transfers between devices, swap(): return lax.ppermute(v, 'lat', pairs)  3.75 us
    pallas_call x1, Pallas kernels, on_device(): call(functools.partial(zonal_kernel, fields), [x.shape, t.shape, direct_s...  2.5 us
    pallas_call x1, Pallas kernels, on_device(): call(functools.partial(early_kernel, fields, levels, bands - 1), [(levels...  2.33 us
    unnamed x22, local copies, waits for them, and re-layouts  1.74 us
    ppermute x3, waiting for transfers between devices, other_core(): return lax.ppermute(v, 'lev', cores)  1 us
    pallas_call x1, Pallas kernels, on_device(): call(functools.partial(remap_last_kernel, levels), [x.shape, t.shape, t.s...  0.87 us
  transfers between devices with their start and end apart: 7, of which 4 were waited for; matrix products, arithmetic and copies ran while one was open for 1% of the time, Pallas kernels for 23%

profile of v11, /device:TPU:0, one launch (start us, length us, event | category | flops | bytes accessed | tf_op | source)
XLA Modules:
  0.0 25.7 jit_solution(14089525131599194321)
XLA Ops:
  0.6 0.0 copy-start
  0.6 1.1 %copy-done = f32[16,2,4,1152]{3,2,1,0:T(4,128)S(1)} copy-done((f32[16,2,4,1152]{3,2,1,0:T(4,128)S(1)}, f32[16,2,4,1152]{3,2,1,0:T(4,128)}, u32[]{:S(2)}) %copy-start) | copy-done | bytes 589848
  1.7 0.0 copy-start.2
  1.7 0.0 copy-start.3
  1.7 0.0 copy-start.5
  1.7 0.0 copy-start.6
  1.7 0.0 copy-start.7
  1.7 0.0 copy-start.8
  1.7 0.0 copy-start.9
  1.7 0.0 copy-start.10
  1.8 3.0 %collective-permute-start.1 = (f32[8,2,4,1152]{3,2,1,0:T(4,128)S(1)}, f32[8,2,4,1152]{3,2,1,0:T(4,128)S(1)}, u32[]{:S(2)}, u32[]{:S(2)}) collective-permute-start(f32[8,2,4,1152]{3,2,1,0:T(4,128)S(1)} %shard_map.123), channel_id=1, source_target_pairs={{0,2},{2,0},{4,6},{6,4},{8,10},{10,8},{12,14},{14,12},{1,3},{3,1},... | collective-permute-start | bytes 884744 | tf_op jit(solution)/shard_map/ppermute | solution.py:459
  4.8 0.0 copy-done.2
  4.8 0.0 copy-done.3
  4.8 0.0 copy-done.5
  4.8 0.0 copy-done.6
  4.8 0.0 copy-done.7
  4.8 0.0 copy-done.8
  4.8 0.0 copy-done.9
  4.8 0.0 copy-done.10
  4.8 2.5 %shard_map.121 = (f32[16,2,4,1152]{3,2,1,0:T(4,128)S(1)}, f32[2,4,1152]{2,1,0:T(4,128)S(1)}, f32[7,8,1152]{2,1,0:T(8,128)S(1)}, f32[7,8,1152]{2,1,0:T(8,128)S(1)}, f32[13,4,576]{2,1,0:T(4,128)S(1)}) custom-call(f32[16,2,4,1152]{3,2,1,0:T(4,128)S(1)} %copy-done, f32[2,4,1152]{2,1,0:T(4,128)S(1)} %copy-done.2, s32[2,4,1152]{2,1,0:T(4,128)S(1)} %copy-done.8, ...), custom_call_target="tpu_custom_call" | custom-call | flops 10000000000 | bytes 1000 | tf_op jit(solution)/shard_map/pallas_call | solution.py:483
  7.3 0.1 collective-permute-start
  7.4 0.7 %collective-permute-start.3 = (f32[7,8,1152]{2,1,0:T(8,128)S(1)}, f32[7,8,1152]{2,1,0:T(8,128)S(1)}, u32[]{:S(2)}, u32[]{:S(2)}) collective-permute-start(f32[7,8,1152]{2,1,0:T(8,128)S(1)} %get-tuple-element.26), channel_id=1, source_target_pairs={{0,2},{2,0},{4,6},{6,4},{8,10},{10,8},{12,14},{14,12},{1,3},{3,1},... | collective-permute-start | bytes 774152 | tf_op jit(solution)/shard_map/ppermute | solution.py:459
  8.2 0.7 %collective-permute-start.4 = (f32[7,8,1152]{2,1,0:T(8,128)S(1)}, f32[7,8,1152]{2,1,0:T(8,128)S(1)}, u32[]{:S(2)}, u32[]{:S(2)}) collective-permute-start(f32[7,8,1152]{2,1,0:T(8,128)S(1)} %get-tuple-element.27), channel_id=1, source_target_pairs={{2,4},{4,2},{6,8},{8,6},{10,12},{12,10},{3,5},{5,3},{7,9},{9,7},{1... | collective-permute-start | bytes 774152 | tf_op jit(solution)/shard_map/ppermute | solution.py:462
  8.9 3.8 %collective-permute-done.1.swapped.refs_1_ = f32[8,2,4,1152]{3,2,1,0:T(4,128)S(1)} collective-permute-done((f32[8,2,4,1152]{3,2,1,0:T(4,128)S(1)}, f32[8,2,4,1152]{3,2,1,0:T(4,128)S(1)}, u32[]{:S(2)}, u32[]{:S(2)}) %collective-permute-start.1) | collective-permute-done | bytes 294944 | tf_op jit(solution)/shard_map/ppermute | solution.py:459
  12.6 0.0 copy-start.1
  12.6 0.1 shard_map.124
  12.7 4.2 %collective-permute-start.2 = (f32[6,8,1152]{2,1,0:T(8,128)S(1)}, f32[6,8,1152]{2,1,0:T(8,128)S(1)}, u32[]{:S(2)}, u32[]{:S(2)}) collective-permute-start(f32[6,8,1152]{2,1,0:T(8,128)S(1)} %shard_map.124), channel_id=1, source_target_pairs={{0,4},{4,8},{8,12},{6,2},{10,6},{14,10},{1,5},{5,9},{9,13},{7,3},{... | collective-permute-start | bytes 663560 | tf_op jit(solution)/shard_map/ppermute | solution.py:465
  16.9 0.0 collective-permute-done
  16.9 0.2 maximum_select_fusion.columns
  17.1 0.0 copy-start.4
  17.1 0.0 copy-done.1
  17.1 0.6 %copy-done.4 = f32[64]{0:T(128)S(1)} copy-done((f32[64]{0:T(128)S(1)}, f32[64]{0:T(128)}, u32[]{:S(2)}) %copy-start.4) | copy-done | bytes 280
  17.8 2.3 %shard_map.122 = (f32[4,4,4,1152]{3,2,1,0:T(4,128)S(1)}, f32[10,2,4,1152]{3,2,1,0:T(4,128)S(1)}, f32[16,2,4,1152]{3,2,1,0:T(4,128)S(1)}, f32[2,4,1152]{2,1,0:T(4...) custom-call(f32[64]{0:T(128)S(1)} %copy-done.4, ...), custom_call_target="tpu_custom_call" | custom-call | flops 1000000 | bytes 1000 | tf_op jit(solution)/shard_map/pallas_call | solution.py:518
  20.1 2.0 %collective-permute-done.3.near.refs_1_ = f32[7,8,1152]{2,1,0:T(8,128)S(1)} collective-permute-done((f32[7,8,1152]{2,1,0:T(8,128)S(1)}, f32[7,8,1152]{2,1,0:T(8,128)S(1)}, u32[]{:S(2)}, u32[]{:S(2)}) %collective-permute-start.3) | collective-permute-done | bytes 258080 | tf_op jit(solution)/shard_map/ppermute | solution.py:459
  22.1 0.0 collective-permute-done.4.far.refs_2_
  22.1 0.1 shard_map.125
  22.3 0.3 %shard_map.127.own = f32[9,2,4,1152]{3,2,1,0:T(4,128)S(1)} custom-call(f32[16,2,4,1152]{3,2,1,0:T(4,128)S(1)} %get-tuple-element.23.refs_0_, f32[7,8,1152]{2,1,0:T(8,128)S(1)} %collective-permute-done.3.near.refs_1_, f32[7,8,1152]{2,1,0:T(8,128)S(1)} %collective-permute-done.4.far.refs_2_, f32[10,2,4,1152]{3,2,1,0:T(4,128)S(1)} %get-tuple-element.24.weights.refs_3_, ...), custom_call_target="tpu_custom_call" | custom-call | flops 1000000 | bytes 1000 | tf_op jit(solution)/shard_map/pallas_call | solution.py:539
  22.6 0.1 collective-permute-start.6
  22.7 0.0 collective-permute-done.2.refs_2_
  22.7 0.3 %shard_map.126.own = f32[8,2,4,1152]{3,2,1,0:T(4,128)S(1)} custom-call(f32[16,2,4,1152]{3,2,1,0:T(4,128)S(1)} %get-tuple-element.23.refs_0_, f32[8,2,4,1152]{3,2,1,0:T(4,128)S(1)} %collective-permute-done.1.swapped.refs_1_, f32[6,8,1152]{2,1,0:T(8,128)S(1)} %collective-permute-done.2.refs_2_, f32[10,2,4,1152]{3,2,1,0:T(4,128)S(1)} %get-tuple-element.24.weights.refs_3_, ...), custom_call_target="tpu_custom_call" | custom-call | flops 1000000 | bytes 1000 | tf_op jit(solution)/shard_map/pallas_call | solution.py:545
  23.1 0.5 %collective-permute-start.5 = (f32[8,2,4,1152]{3,2,1,0:T(4,128)S(1)}, f32[8,2,4,1152]{3,2,1,0:T(4,128)S(1)}, u32[]{:S(2)}, u32[]{:S(2)}) collective-permute-start(f32[8,2,4,1152]{3,2,1,0:T(4,128)S(1)} %shard_map.126.own), channel_id=1, source_target_pairs={{0,1},{1,0},{2,3},{3,2},{4,5},{5,4},{6,7},{7,6},{8,9},{9,8},{10,11... | collective-permute-start | bytes 884744 | tf_op jit(solution)/shard_map/ppermute | solution.py:468
  23.6 0.7 %collective-permute-done.6.peer = f32[9,2,4,1152]{3,2,1,0:T(4,128)S(1)} collective-permute-done((f32[9,2,4,1152]{3,2,1,0:T(4,128)S(1)}, f32[9,2,4,1152]{3,2,1,0:T(4,128)S(1)}, u32[]{:S(2)}, u32[]{:S(2)}) %collective-permute-start.6) | collective-permute-done | bytes 331808 | tf_op jit(solution)/shard_map/ppermute | solution.py:468
  24.3 0.2 shard_map.128
  24.5 0.3 %collective-permute-done.5.peer = f32[8,2,4,1152]{3,2,1,0:T(4,128)S(1)} collective-permute-done((f32[8,2,4,1152]{3,2,1,0:T(4,128)S(1)}, f32[8,2,4,1152]{3,2,1,0:T(4,128)S(1)}, u32[]{:S(2)}, u32[]{:S(2)}) %collective-permute-start.5) | collective-permute-done | bytes 294944 | tf_op jit(solution)/shard_map/ppermute | solution.py:468
  24.8 0.9 %shard_map.129 = (f32[16,2,4,1152]{3,2,1,0:T(4,128)}, f32[2,4,1152]{2,1,0:T(4,128)}, f32[2,4,1152]{2,1,0:T(4,128)}) custom-call(f32[8,2,4,1152]{3,2,1,0:T(4,128)S(1)} %shard_map.126.own, f32[8,2,4,1152]{3,2,1,0:T(4,128)S(1)} %collective-permute-done.5.peer, f32[4,4,4,1152]{3,2,1,0:T(4,128)S(1)} %get-tuple-element.32.weights, ...), custom_call_target="tpu_custom_call" | custom-call | flops 1000000 | bytes 1000 | tf_op jit(solution)/shard_map/pallas_call | solution.py:558
  (1 shorter events, 0.0 us)
Async XLA Ops:
  0.6 1.1 %copy-start = (f32[16,2,4,1152]{3,2,1,0:T(4,128)S(1)}, f32[16,2,4,1152]{3,2,1,0:T(4,128)}, u32[]{:S(2)}) copy-start(f32[16,2,4,1152]{3,2,1,0:T(4,128)} %x.5) | copy-start | bytes 1769476
  1.7 3.1 %copy-start.2 = (f32[2,4,1152]{2,1,0:T(4,128)S(1)}, f32[2,4,1152]{2,1,0:T(4,128)}, u32[]{:S(2)}) copy-start(f32[2,4,1152]{2,1,0:T(4,128)} %t.3) | copy-start | bytes 110596
  1.7 3.1 %copy-start.3 = (f32[2,4,1152]{2,1,0:T(4,128)S(1)}, f32[2,4,1152]{2,1,0:T(4,128)}, u32[]{:S(2)}) copy-start(f32[2,4,1152]{2,1,0:T(4,128)} %c.3) | copy-start | bytes 110596
  1.7 3.1 %copy-start.5 = (s32[4,4,576]{2,1,0:T(4,128)S(1)}, s32[4,4,576]{2,1,0:T(4,128)}, u32[]{:S(2)}) copy-start(s32[4,4,576]{2,1,0:T(4,128)} %upper.1) | copy-start | bytes 110596
  1.7 3.1 %copy-start.6 = (f32[4,4,576]{2,1,0:T(4,128)S(1)}, f32[4,4,576]{2,1,0:T(4,128)}, u32[]{:S(2)}) copy-start(f32[4,4,576]{2,1,0:T(4,128)} %share.1) | copy-start | bytes 110596
  1.7 3.1 %copy-start.7 = (f32[4,4,576]{2,1,0:T(4,128)S(1)}, f32[4,4,576]{2,1,0:T(4,128)}, u32[]{:S(2)}) copy-start(f32[4,4,576]{2,1,0:T(4,128)} %quotient.1) | copy-start | bytes 110596
  1.7 3.1 %copy-start.8 = (s32[2,4,1152]{2,1,0:T(4,128)S(1)}, s32[2,4,1152]{2,1,0:T(4,128)}, u32[]{:S(2)}) copy-start(s32[2,4,1152]{2,1,0:T(4,128)} %n.1) | copy-start | bytes 110596
  1.7 3.1 %copy-start.9 = (f32[2,4,1152]{2,1,0:T(4,128)S(1)}, f32[2,4,1152]{2,1,0:T(4,128)}, u32[]{:S(2)}) copy-start(f32[2,4,1152]{2,1,0:T(4,128)} %f.1) | copy-start | bytes 110596
  1.7 3.1 %copy-start.10 = (f32[4,576]{1,0:T(4,128)S(1)}, f32[4,576]{1,0:T(4,128)}, u32[]{:S(2)}) copy-start(f32[4,576]{1,0:T(4,128)} %ground.1) | copy-start | bytes 27652
  1.8 10.8 %collective-permute-start.1 = (f32[8,2,4,1152]{3,2,1,0:T(4,128)S(1)}, f32[8,2,4,1152]{3,2,1,0:T(4,128)S(1)}, u32[]{:S(2)}, u32[]{:S(2)}) collective-permute-start(f32[8,2,4,1152]{3,2,1,0:T(4,128)S(1)} %shard_map.123), channel_id=1, source_target_pairs={{0,2},{2,0},{4,6},{6,4},{8,10},{10,8},{12,14},{14,12},{1,3},{3,1},... | collective-permute-start | bytes 884744 | tf_op jit(solution)/shard_map/ppermute | solution.py:459
  7.3 9.6 %collective-permute-start = (f32[13,4,576]{2,1,0:T(4,128)S(1)}, f32[13,4,576]{2,1,0:T(4,128)S(1)}, u32[]{:S(2)}, u32[]{:S(2)}) collective-permute-start(f32[13,4,576]{2,1,0:T(4,128)S(1)} %get-tuple-element.20), channel_id=1, source_target_pairs={{0,1},{1,0},{2,3},{3,2},{4,5},{5,4},{6,7},{7,6},{8,9},{9,8},{10,11... | collective-permute-start | bytes 359432 | tf_op jit(solution)/shard_map/ppermute | solution.py:468
  7.4 14.7 %collective-permute-start.3 = (f32[7,8,1152]{2,1,0:T(8,128)S(1)}, f32[7,8,1152]{2,1,0:T(8,128)S(1)}, u32[]{:S(2)}, u32[]{:S(2)}) collective-permute-start(f32[7,8,1152]{2,1,0:T(8,128)S(1)} %get-tuple-element.26), channel_id=1, source_target_pairs={{0,2},{2,0},{4,6},{6,4},{8,10},{10,8},{12,14},{14,12},{1,3},{3,1},... | collective-permute-start | bytes 774152 | tf_op jit(solution)/shard_map/ppermute | solution.py:459
  8.2 13.9 %collective-permute-start.4 = (f32[7,8,1152]{2,1,0:T(8,128)S(1)}, f32[7,8,1152]{2,1,0:T(8,128)S(1)}, u32[]{:S(2)}, u32[]{:S(2)}) collective-permute-start(f32[7,8,1152]{2,1,0:T(8,128)S(1)} %get-tuple-element.27), channel_id=1, source_target_pairs={{2,4},{4,2},{6,8},{8,6},{10,12},{12,10},{3,5},{5,3},{7,9},{9,7},{1... | collective-permute-start | bytes 774152 | tf_op jit(solution)/shard_map/ppermute | solution.py:462
  12.6 4.5 %copy-start.1 = (f32[16,2,4,1152]{3,2,1,0:T(4,128)S(1)}, f32[16,2,4,1152]{3,2,1,0:T(4,128)}, u32[]{:S(2)}) copy-start(f32[16,2,4,1152]{3,2,1,0:T(4,128)} %x.5) | copy-start | bytes 1769476
  12.7 10.0 %collective-permute-start.2 = (f32[6,8,1152]{2,1,0:T(8,128)S(1)}, f32[6,8,1152]{2,1,0:T(8,128)S(1)}, u32[]{:S(2)}, u32[]{:S(2)}) collective-permute-start(f32[6,8,1152]{2,1,0:T(8,128)S(1)} %shard_map.124), channel_id=1, source_target_pairs={{0,4},{4,8},{8,12},{6,2},{10,6},{14,10},{1,5},{5,9},{9,13},{7,3},{... | collective-permute-start | bytes 663560 | tf_op jit(solution)/shard_map/ppermute | solution.py:465
  17.1 0.7 %copy-start.4 = (f32[64]{0:T(128)S(1)}, f32[64]{0:T(128)}, u32[]{:S(2)}) copy-start(f32[64]{0:T(128)} %constant.8.clone.scale) | copy-start | bytes 772
  22.6 1.7 %collective-permute-start.6 = (f32[9,2,4,1152]{3,2,1,0:T(4,128)S(1)}, f32[9,2,4,1152]{3,2,1,0:T(4,128)S(1)}, u32[]{:S(2)}, u32[]{:S(2)}) collective-permute-start(f32[9,2,4,1152]{3,2,1,0:T(4,128)S(1)} %shard_map.127.own), channel_id=1, source_target_pairs={{0,1},{1,0},{2,3},{3,2},{4,5},{5,4},{6,7},{7,6},{8,9},{9,8},{10,11... | collective-permute-start | bytes 995336 | tf_op jit(solution)/shard_map/ppermute | solution.py:468
  23.1 1.7 %collective-permute-start.5 = (f32[8,2,4,1152]{3,2,1,0:T(4,128)S(1)}, f32[8,2,4,1152]{3,2,1,0:T(4,128)S(1)}, u32[]{:S(2)}, u32[]{:S(2)}) collective-permute-start(f32[8,2,4,1152]{3,2,1,0:T(4,128)S(1)} %shard_map.126.own), channel_id=1, source_target_pairs={{0,1},{1,0},{2,3},{3,2},{4,5},{5,4},{6,7},{7,6},{8,9},{9,8},{10,11... | collective-permute-start | bytes 884744 | tf_op jit(solution)/shard_map/ppermute | solution.py:468

commit v12 on v11

--- a/solution.py
+++ b/solution.py
@@ -124,8 +124,8 @@
 
 
 def early_kernel(
-    fields, levels, last, scale, columns, c, x, t, zon_in, zon_t_in,
-    mix, out, zon, zon_t, factor, south_rows, south_rows_t, ws,
+    fields, levels, last, scale, columns, c, x, t, zon_in, zon_t_in, swapped,
+    mix, out, zon, zon_t, factor, south_rows, south_rows_t, south_near, ws,
 ):
     lat = lax.axis_index("lat")
     lons = x.shape[-1]
@@ -165,6 +165,29 @@
                     zon_in[i, lev, :, lane], lambda r: x[i, lev, r : r + 1, lane]
                 )
 
+    def near_terms(odd):
+        count = swapped.shape[0]
+        skip = fields - count
+        rows = side_rows(odd)
+        for lev in range(LEVELS):
+            for d, row in enumerate(rows, 1):
+                at = (3 - d) * LEVELS + lev
+                for i in range(count):
+                    south_near[at, i : i + 1, :] = (
+                        swapped[i, lev, row : row + 1, :] if odd else jnp.zeros((1, lons), jnp.float32)
+                    )
+            for chunk in range(lons // LANE):
+                lane = lanes(chunk)
+                weights = [out[3 - d if odd else ROWS + 2 + d, lev, :, lane] for d in range(1, 4)]
+                for i in range(count):
+                    total = zon[skip + i, lev, :, lane]
+                    for w, row in zip(weights, rows):
+                        v = swapped[i, lev, row : row + 1, lane]
+                        total = total + w * jnp.broadcast_to(v, total.shape)
+                    zon[skip + i, lev, :, lane] = total
+
+    both(lax.rem(lat, 2), near_terms)
+
     def pole(rows):
         for k, (_, at) in enumerate(rows):
             ws[k] = stacked(out.at[at])
@@ -200,7 +223,9 @@
         pole([(ROWS - d, ROWS + 2 + d) for d in range(1, 4)])
 
 
-def patch_kernel(factor, near, far, weights, south_rows, south_rows_t, low, delta, delta_t):
+def patch_kernel(
+    factor, near, far, weights, south_rows, south_rows_t, south_near, low, delta, delta_t
+):
     block = 3 * LEVELS
     rows = slice(block, block + LEVELS)
     below = jnp.where(parity() == 1, near[block, rows, :], far[block, rows, :])
@@ -222,6 +247,12 @@
             term = jnp.broadcast_to(parts[r + 3][lev : lev + 1], v.shape) * v
             total = term if total is None else total + term
         delta[lev] = total
+        skip = total.shape[0] - south_near.shape[1]
+        total = total[skip:]
+        for r in range(3):
+            v = south_near[r * LEVELS + lev]
+            total = total + jnp.broadcast_to(parts[r][lev : lev + 1], v.shape) * v
+        delta[lev, skip:, :] = total
 
 
 def zonal_kernel(
@@ -277,7 +308,7 @@
     if direct:
         base, near, far, w, low, delta, base_t, delta_t, adv = refs
     else:
-        base, near, far, w, low, delta, adv = refs
+        base, far, w, low, delta, adv = refs
     chunks = w.shape[-1] // LANE
     first_row = lax.broadcasted_iota(jnp.int32, (ROWS, LANE), 0) == 0
 
@@ -293,19 +324,14 @@
                     total = total + jnp.where(first_row, jnp.broadcast_to(row_0, total.shape), 0.0)
                     for d, (south, north) in enumerate(sides, 1):
                         for weight, is_near in ((south, odd), (north, not odd)):
+                            if is_near and near_row is None:
+                                continue
                             v = near_row(d) if is_near else far_row(d)
                             total = total + weight * jnp.broadcast_to(v, total.shape)
                     return total
 
                 def gathered(ref, f):
                     return lambda d: ref[(d - 1) * LEVELS + lev, f : f + 1, lane]
-
-                def swapped(ref, f):
-                    def row_at(d):
-                        row = side_rows(odd)[d - 1]
-                        return ref[f, lev, row : row + 1, lane]
-
-                    return row_at
 
                 def gathered_t(ref):
                     def row_at(d):
@@ -318,7 +344,7 @@
                     adv[f, lev, :, lane] = total_of(
                         base[skip + f, lev, :, lane],
                         delta[lev, skip + f : skip + f + 1, lane],
-                        gathered(near, f) if direct else swapped(near, f),
+                        gathered(near, f) if direct else None,
                         gathered(far, f),
                     )
                 if direct:
@@ -402,9 +428,7 @@
         copy.start()
         copies.append(copy)
 
-    piece = count // 1
-    for start in range(0, count, piece):
-        send(first.at[pl.ds(start, piece)], out.at[pl.ds(start, piece)])
+    send(first, out.at[pl.ds(0, count)])
     mine = group * LEVELS
     send(thick.at[pl.ds(mine, LEVELS)], out_phi)
     send(thick.at[pl.ds(levels + mine, LEVELS)], out_t)
@@ -515,7 +539,7 @@
         jnp.concatenate([peer_columns, columns], -1),
     )
 
-    mix, weights, base, base_t, factor, south_rows, south_rows_t = call(
+    mix, weights, base, base_t, factor, south_rows, south_rows_t, south_near = call(
         functools.partial(early_kernel, fields, levels, bands - 1),
         [
             (levels, 2 * LEVELS, ROWS, lons),
@@ -525,16 +549,17 @@
             (LEVELS, lons),
             (3 * LEVELS, fields, lons),
             (3 * LEVELS, lons),
+            (3 * LEVELS, swapped, lons),
         ],
         [(3, LEVELS * ROWS, lons)],
-        [smem] + [vmem] * 6,
+        [smem] + [vmem] * 7,
         cost=COST["early"],
-    )(scale, columns, c, x, t, zon, zon_t)
+    )(scale, columns, c, x, t, zon, zon_t, near_a)
     low, delta, delta_t = call(
         patch_kernel,
         [(3, LEVELS, ROWS, lons), (LEVELS, fields, lons), (LEVELS, lons)],
         cost=COST["patch"],
-    )(factor, near_b, far_b, weights, south_rows, south_rows_t)
+    )(factor, near_b, far_b, weights, south_rows, south_rows_t, south_near)
 
     adv_b = call(
         functools.partial(fin_kernel, 0, direct, True),
@@ -546,7 +571,7 @@
         functools.partial(fin_kernel, direct, swapped, False),
         (swapped,) + x.shape[1:],
         cost=COST["fin_a"],
-    )(base, near_a, far_a, weights, low, delta)
+    )(base, far_a, weights, low, delta)
     peer_a = other_core(adv_a)
 
     anywhere = pl.BlockSpec(memory_space=pl.ANY)
@@ -558,7 +583,7 @@
     return call(
         functools.partial(remap_last_kernel, levels),
         [x.shape, t.shape, t.shape],
-        [(swapped,) + x.shape[1:], pltpu.SemaphoreType.DMA((2 + 1 + swapped // 4,))],
+        [(swapped,) + x.shape[1:], pltpu.SemaphoreType.DMA((3 + swapped // 4,))],
         cost=COST["last"],
         out_specs=(anywhere,) * 3,
     )(adv_a, peer_a, mix, first, thick)

time: 26 us -> 26 us (level)
  transfers between devices with their start and end apart: 7 -> 7, of which waited for: 4 -> 4; matrix products, arithmetic and copies ran while one was open for 1% -> 1% of each run, Pallas kernels for 23% -> 24%
where the time goes in v12:
time: 26 us; the launch traced here: 25.7 us
  starting transfers between devices  9.29 us (36%)
  Pallas kernels  7.02 us (27%)
  waiting for transfers between devices  6.59 us (25%)
  local copies, waits for them, and re-layouts  1.74 us (7%)
  between operations  0.83 us (3%)
    ppermute x2, waiting for transfers between devices, swap(): return lax.ppermute(v, 'lat', pairs)  5.56 us
    ppermute x1, starting transfers between devices, pass_on(): return lax.ppermute(v, 'lat', relays)  4.19 us
    ppermute x2, starting transfers between devices, swap(): return lax.ppermute(v, 'lat', pairs)  3.75 us
    pallas_call x1, Pallas kernels, on_device(): call(functools.partial(early_kernel, fields, levels, bands - 1), [(levels...  2.54 us
    pallas_call x1, Pallas kernels, on_device(): call(functools.partial(zonal_kernel, fields), [x.shape, t.shape, direct_s...  2.5 us
    unnamed x22, local copies, waits for them, and re-layouts  1.74 us
    ppermute x3, waiting for transfers between devices, other_core(): return lax.ppermute(v, 'lev', cores)  1.02 us
    pallas_call x1, Pallas kernels, on_device(): call(functools.partial(remap_last_kernel, levels), [x.shape, t.shape, t.s...  0.87 us
  transfers between devices with their start and end apart: 7, of which 4 were waited for; matrix products, arithmetic and copies ran while one was open for 1% of the time, Pallas kernels for 24%

profile of v12, /device:TPU:0, one launch (start us, length us, event | category | flops | bytes accessed | tf_op | source)
XLA Modules:
  0.0 25.7 jit_solution(14620700755738565159)
XLA Ops:
  0.6 0.0 copy-start
  0.6 1.1 %copy-done = f32[16,2,4,1152]{3,2,1,0:T(4,128)S(1)} copy-done((f32[16,2,4,1152]{3,2,1,0:T(4,128)S(1)}, f32[16,2,4,1152]{3,2,1,0:T(4,128)}, u32[]{:S(2)}) %copy-start) | copy-done | bytes 589848
  1.7 0.0 copy-start.2
  1.7 0.0 copy-start.3
  1.7 0.0 copy-start.5
  1.7 0.0 copy-start.6
  1.7 0.0 copy-start.7
  1.7 0.0 copy-start.8
  1.7 0.0 copy-start.9
  1.7 0.0 copy-start.10
  1.8 3.0 %collective-permute-start.1 = (f32[8,2,4,1152]{3,2,1,0:T(4,128)S(1)}, f32[8,2,4,1152]{3,2,1,0:T(4,128)S(1)}, u32[]{:S(2)}, u32[]{:S(2)}) collective-permute-start(f32[8,2,4,1152]{3,2,1,0:T(4,128)S(1)} %shard_map.122), channel_id=1, source_target_pairs={{0,2},{2,0},{4,6},{6,4},{8,10},{10,8},{12,14},{14,12},{1,3},{3,1},... | collective-permute-start | bytes 884744 | tf_op jit(solution)/shard_map/ppermute | solution.py:483
  4.8 0.0 copy-done.2
  4.8 0.0 copy-done.3
  4.8 0.0 copy-done.5
  4.8 0.0 copy-done.6
  4.8 0.0 copy-done.7
  4.8 0.0 copy-done.8
  4.8 0.0 copy-done.9
  4.8 0.0 copy-done.10
  4.8 2.5 %shard_map.121 = (f32[16,2,4,1152]{3,2,1,0:T(4,128)S(1)}, f32[2,4,1152]{2,1,0:T(4,128)S(1)}, f32[7,8,1152]{2,1,0:T(8,128)S(1)}, f32[7,8,1152]{2,1,0:T(8,128)S(1)}, f32[13,4,576]{2,1,0:T(4,128)S(1)}) custom-call(f32[16,2,4,1152]{3,2,1,0:T(4,128)S(1)} %copy-done, f32[2,4,1152]{2,1,0:T(4,128)S(1)} %copy-done.2, s32[2,4,1152]{2,1,0:T(4,128)S(1)} %copy-done.8, ...), custom_call_target="tpu_custom_call" | custom-call | flops 10000000000 | bytes 1000 | tf_op jit(solution)/shard_map/pallas_call | solution.py:507
  7.3 0.1 collective-permute-start
  7.4 0.7 %collective-permute-start.3 = (f32[7,8,1152]{2,1,0:T(8,128)S(1)}, f32[7,8,1152]{2,1,0:T(8,128)S(1)}, u32[]{:S(2)}, u32[]{:S(2)}) collective-permute-start(f32[7,8,1152]{2,1,0:T(8,128)S(1)} %get-tuple-element.27), channel_id=1, source_target_pairs={{0,2},{2,0},{4,6},{6,4},{8,10},{10,8},{12,14},{14,12},{1,3},{3,1},... | collective-permute-start | bytes 774152 | tf_op jit(solution)/shard_map/ppermute | solution.py:483
  8.2 0.7 %collective-permute-start.4 = (f32[7,8,1152]{2,1,0:T(8,128)S(1)}, f32[7,8,1152]{2,1,0:T(8,128)S(1)}, u32[]{:S(2)}, u32[]{:S(2)}) collective-permute-start(f32[7,8,1152]{2,1,0:T(8,128)S(1)} %get-tuple-element.28), channel_id=1, source_target_pairs={{2,4},{4,2},{6,8},{8,6},{10,12},{12,10},{3,5},{5,3},{7,9},{9,7},{1... | collective-permute-start | bytes 774152 | tf_op jit(solution)/shard_map/ppermute | solution.py:486
  8.9 3.8 %collective-permute-done.1.swapped = f32[8,2,4,1152]{3,2,1,0:T(4,128)S(1)} collective-permute-done((f32[8,2,4,1152]{3,2,1,0:T(4,128)S(1)}, f32[8,2,4,1152]{3,2,1,0:T(4,128)S(1)}, u32[]{:S(2)}, u32[]{:S(2)}) %collective-permute-start.1) | collective-permute-done | bytes 294944 | tf_op jit(solution)/shard_map/ppermute | solution.py:483
  12.6 0.0 copy-start.1
  12.6 0.1 shard_map.124
  12.7 4.2 %collective-permute-start.2 = (f32[6,8,1152]{2,1,0:T(8,128)S(1)}, f32[6,8,1152]{2,1,0:T(8,128)S(1)}, u32[]{:S(2)}, u32[]{:S(2)}) collective-permute-start(f32[6,8,1152]{2,1,0:T(8,128)S(1)} %shard_map.124), channel_id=1, source_target_pairs={{0,4},{4,8},{8,12},{6,2},{10,6},{14,10},{1,5},{5,9},{9,13},{7,3},{... | collective-permute-start | bytes 663560 | tf_op jit(solution)/shard_map/ppermute | solution.py:489
  16.9 0.0 collective-permute-done
  16.9 0.2 maximum_select_fusion.columns
  17.1 0.0 copy-start.4
  17.1 0.0 copy-done.1
  17.1 0.6 %copy-done.4 = f32[64]{0:T(128)S(1)} copy-done((f32[64]{0:T(128)S(1)}, f32[64]{0:T(128)}, u32[]{:S(2)}) %copy-start.4) | copy-done | bytes 280
  17.8 2.5 %shard_map.123 = (f32[4,4,4,1152]{3,2,1,0:T(4,128)S(1)}, f32[10,2,4,1152]{3,2,1,0:T(4,128)S(1)}, f32[16,2,4,1152]{3,2,1,0:T(4,128)S(1)}, f32[2,4,1152]{2,1,0:T(4...) custom-call(f32[64]{0:T(128)S(1)} %copy-done.4, ...), custom_call_target="tpu_custom_call" | custom-call | flops 1000000 | bytes 1000 | tf_op jit(solution)/shard_map/pallas_call | solution.py:542
  20.3 1.8 %collective-permute-done.3.near.refs_1_ = f32[7,8,1152]{2,1,0:T(8,128)S(1)} collective-permute-done((f32[7,8,1152]{2,1,0:T(8,128)S(1)}, f32[7,8,1152]{2,1,0:T(8,128)S(1)}, u32[]{:S(2)}, u32[]{:S(2)}) %collective-permute-start.3) | collective-permute-done | bytes 258080 | tf_op jit(solution)/shard_map/ppermute | solution.py:483
  22.1 0.0 collective-permute-done.4.far.refs_2_
  22.1 0.2 shard_map.125
  22.3 0.4 %shard_map.127.own = f32[9,2,4,1152]{3,2,1,0:T(4,128)S(1)} custom-call(f32[16,2,4,1152]{3,2,1,0:T(4,128)S(1)} %get-tuple-element.24.refs_0_, f32[7,8,1152]{2,1,0:T(8,128)S(1)} %collective-permute-done.3.near.refs_1_, f32[7,8,1152]{2,1,0:T(8,128)S(1)} %collective-permute-done.4.far.refs_2_, f32[10,2,4,1152]{3,2,1,0:T(4,128)S(1)} %get-tuple-element.25.weights.refs_2_.refs_3_, ...), custom_call_target="tpu_custom_call" | custom-call | flops 1000000 | bytes 1000 | tf_op jit(solution)/shard_map/pallas_call | solution.py:564
  22.7 0.1 collective-permute-start.6
  22.8 0.0 collective-permute-done.2.refs_1_
  22.8 0.2 shard_map.126.own
  23.0 0.5 %collective-permute-start.5 = (f32[8,2,4,1152]{3,2,1,0:T(4,128)S(1)}, f32[8,2,4,1152]{3,2,1,0:T(4,128)S(1)}, u32[]{:S(2)}, u32[]{:S(2)}) collective-permute-start(f32[8,2,4,1152]{3,2,1,0:T(4,128)S(1)} %shard_map.126.own), channel_id=1, source_target_pairs={{0,1},{1,0},{2,3},{3,2},{4,5},{5,4},{6,7},{7,6},{8,9},{9,8},{10,11... | collective-permute-start | bytes 884744 | tf_op jit(solution)/shard_map/ppermute | solution.py:492
  23.6 0.8 %collective-permute-done.6.peer = f32[9,2,4,1152]{3,2,1,0:T(4,128)S(1)} collective-permute-done((f32[9,2,4,1152]{3,2,1,0:T(4,128)S(1)}, f32[9,2,4,1152]{3,2,1,0:T(4,128)S(1)}, u32[]{:S(2)}, u32[]{:S(2)}) %collective-permute-start.6) | collective-permute-done | bytes 331808 | tf_op jit(solution)/shard_map/ppermute | solution.py:492
  24.4 0.2 shard_map.128
  24.6 0.2 collective-permute-done.5.peer
  24.8 0.9 %shard_map.129 = (f32[16,2,4,1152]{3,2,1,0:T(4,128)}, f32[2,4,1152]{2,1,0:T(4,128)}, f32[2,4,1152]{2,1,0:T(4,128)}) custom-call(f32[8,2,4,1152]{3,2,1,0:T(4,128)S(1)} %shard_map.126.own, f32[8,2,4,1152]{3,2,1,0:T(4,128)S(1)} %collective-permute-done.5.peer, f32[4,4,4,1152]{3,2,1,0:T(4,128)S(1)} %get-tuple-element.34.weights, ...), custom_call_target="tpu_custom_call" | custom-call | flops 1000000 | bytes 1000 | tf_op jit(solution)/shard_map/pallas_call | solution.py:583
  (1 shorter events, 0.0 us)
Async XLA Ops:
  0.6 1.1 %copy-start = (f32[16,2,4,1152]{3,2,1,0:T(4,128)S(1)}, f32[16,2,4,1152]{3,2,1,0:T(4,128)}, u32[]{:S(2)}) copy-start(f32[16,2,4,1152]{3,2,1,0:T(4,128)} %x.5) | copy-start | bytes 1769476
  1.7 3.1 %copy-start.2 = (f32[2,4,1152]{2,1,0:T(4,128)S(1)}, f32[2,4,1152]{2,1,0:T(4,128)}, u32[]{:S(2)}) copy-start(f32[2,4,1152]{2,1,0:T(4,128)} %t.3) | copy-start | bytes 110596
  1.7 3.1 %copy-start.3 = (f32[2,4,1152]{2,1,0:T(4,128)S(1)}, f32[2,4,1152]{2,1,0:T(4,128)}, u32[]{:S(2)}) copy-start(f32[2,4,1152]{2,1,0:T(4,128)} %c.3) | copy-start | bytes 110596
  1.7 3.1 %copy-start.5 = (s32[4,4,576]{2,1,0:T(4,128)S(1)}, s32[4,4,576]{2,1,0:T(4,128)}, u32[]{:S(2)}) copy-start(s32[4,4,576]{2,1,0:T(4,128)} %upper.1) | copy-start | bytes 110596
  1.7 3.1 %copy-start.6 = (f32[4,4,576]{2,1,0:T(4,128)S(1)}, f32[4,4,576]{2,1,0:T(4,128)}, u32[]{:S(2)}) copy-start(f32[4,4,576]{2,1,0:T(4,128)} %share.1) | copy-start | bytes 110596
  1.7 3.1 %copy-start.7 = (f32[4,4,576]{2,1,0:T(4,128)S(1)}, f32[4,4,576]{2,1,0:T(4,128)}, u32[]{:S(2)}) copy-start(f32[4,4,576]{2,1,0:T(4,128)} %quotient.1) | copy-start | bytes 110596
  1.7 3.1 %copy-start.8 = (s32[2,4,1152]{2,1,0:T(4,128)S(1)}, s32[2,4,1152]{2,1,0:T(4,128)}, u32[]{:S(2)}) copy-start(s32[2,4,1152]{2,1,0:T(4,128)} %n.1) | copy-start | bytes 110596
  1.7 3.1 %copy-start.9 = (f32[2,4,1152]{2,1,0:T(4,128)S(1)}, f32[2,4,1152]{2,1,0:T(4,128)}, u32[]{:S(2)}) copy-start(f32[2,4,1152]{2,1,0:T(4,128)} %f.1) | copy-start | bytes 110596
  1.7 3.1 %copy-start.10 = (f32[4,576]{1,0:T(4,128)S(1)}, f32[4,576]{1,0:T(4,128)}, u32[]{:S(2)}) copy-start(f32[4,576]{1,0:T(4,128)} %ground.1) | copy-start | bytes 27652
  1.8 10.8 %collective-permute-start.1 = (f32[8,2,4,1152]{3,2,1,0:T(4,128)S(1)}, f32[8,2,4,1152]{3,2,1,0:T(4,128)S(1)}, u32[]{:S(2)}, u32[]{:S(2)}) collective-permute-start(f32[8,2,4,1152]{3,2,1,0:T(4,128)S(1)} %shard_map.122), channel_id=1, source_target_pairs={{0,2},{2,0},{4,6},{6,4},{8,10},{10,8},{12,14},{14,12},{1,3},{3,1},... | collective-permute-start | bytes 884744 | tf_op jit(solution)/shard_map/ppermute | solution.py:483
  7.3 9.6 %collective-permute-start = (f32[13,4,576]{2,1,0:T(4,128)S(1)}, f32[13,4,576]{2,1,0:T(4,128)S(1)}, u32[]{:S(2)}, u32[]{:S(2)}) collective-permute-start(f32[13,4,576]{2,1,0:T(4,128)S(1)} %get-tuple-element.21), channel_id=1, source_target_pairs={{0,1},{1,0},{2,3},{3,2},{4,5},{5,4},{6,7},{7,6},{8,9},{9,8},{10,11... | collective-permute-start | bytes 359432 | tf_op jit(solution)/shard_map/ppermute | solution.py:492
  7.4 14.7 %collective-permute-start.3 = (f32[7,8,1152]{2,1,0:T(8,128)S(1)}, f32[7,8,1152]{2,1,0:T(8,128)S(1)}, u32[]{:S(2)}, u32[]{:S(2)}) collective-permute-start(f32[7,8,1152]{2,1,0:T(8,128)S(1)} %get-tuple-element.27), channel_id=1, source_target_pairs={{0,2},{2,0},{4,6},{6,4},{8,10},{10,8},{12,14},{14,12},{1,3},{3,1},... | collective-permute-start | bytes 774152 | tf_op jit(solution)/shard_map/ppermute | solution.py:483
  8.2 13.9 %collective-permute-start.4 = (f32[7,8,1152]{2,1,0:T(8,128)S(1)}, f32[7,8,1152]{2,1,0:T(8,128)S(1)}, u32[]{:S(2)}, u32[]{:S(2)}) collective-permute-start(f32[7,8,1152]{2,1,0:T(8,128)S(1)} %get-tuple-element.28), channel_id=1, source_target_pairs={{2,4},{4,2},{6,8},{8,6},{10,12},{12,10},{3,5},{5,3},{7,9},{9,7},{1... | collective-permute-start | bytes 774152 | tf_op jit(solution)/shard_map/ppermute | solution.py:486
  12.6 4.5 %copy-start.1 = (f32[16,2,4,1152]{3,2,1,0:T(4,128)S(1)}, f32[16,2,4,1152]{3,2,1,0:T(4,128)}, u32[]{:S(2)}) copy-start(f32[16,2,4,1152]{3,2,1,0:T(4,128)} %x.5) | copy-start | bytes 1769476
  12.7 10.1 %collective-permute-start.2 = (f32[6,8,1152]{2,1,0:T(8,128)S(1)}, f32[6,8,1152]{2,1,0:T(8,128)S(1)}, u32[]{:S(2)}, u32[]{:S(2)}) collective-permute-start(f32[6,8,1152]{2,1,0:T(8,128)S(1)} %shard_map.124), channel_id=1, source_target_pairs={{0,4},{4,8},{8,12},{6,2},{10,6},{14,10},{1,5},{5,9},{9,13},{7,3},{... | collective-permute-start | bytes 663560 | tf_op jit(solution)/shard_map/ppermute | solution.py:489
  17.1 0.7 %copy-start.4 = (f32[64]{0:T(128)S(1)}, f32[64]{0:T(128)}, u32[]{:S(2)}) copy-start(f32[64]{0:T(128)} %constant.8.clone.scale) | copy-start | bytes 772
  22.7 1.7 %collective-permute-start.6 = (f32[9,2,4,1152]{3,2,1,0:T(4,128)S(1)}, f32[9,2,4,1152]{3,2,1,0:T(4,128)S(1)}, u32[]{:S(2)}, u32[]{:S(2)}) collective-permute-start(f32[9,2,4,1152]{3,2,1,0:T(4,128)S(1)} %shard_map.127.own), channel_id=1, source_target_pairs={{0,1},{1,0},{2,3},{3,2},{4,5},{5,4},{6,7},{7,6},{8,9},{9,8},{10,11... | collective-permute-start | bytes 995336 | tf_op jit(solution)/shard_map/ppermute | solution.py:492
  23.0 1.8 %collective-permute-start.5 = (f32[8,2,4,1152]{3,2,1,0:T(4,128)S(1)}, f32[8,2,4,1152]{3,2,1,0:T(4,128)S(1)}, u32[]{:S(2)}, u32[]{:S(2)}) collective-permute-start(f32[8,2,4,1152]{3,2,1,0:T(4,128)S(1)} %shard_map.126.own), channel_id=1, source_target_pairs={{0,1},{1,0},{2,3},{3,2},{4,5},{5,4},{6,7},{7,6},{8,9},{9,8},{10,11... | collective-permute-start | bytes 884744 | tf_op jit(solution)/shard_map/ppermute | solution.py:492
